TPU v7x, 32 devices: a whole 2x2x4 slice. The times are simulated.
32 devices in a mesh: tile: 16 (over z, y, x), frame: 2 (over core).
Axes of the slice: x: 2, y: 2, z: 4, core: 2. Of those that a mesh axis runs over, the one named last changes fastest.
Arguments:
- latents: bfloat16 [64, 2, 104, 384], P('tile', 'frame'), may hold values from -80 to 80
- row_video: int32 [64], replicated, may hold values from 0 to 1, never falling along the last dimension, each value on 1 to 48 neighbouring positions
- video_cols: int32 [2], replicated, may hold values from 52 to 104, as said below
- first_gain: float32 [384], replicated, may hold values from 0.5 to 1.5
- first_shift: float32 [384], replicated, may hold values from -3 to 3
- conv_weight: bfloat16 [3, 3, 3, 384, 384], replicated, may hold values from -0.0625 to 0.0625
- conv_bias: float32 [384], replicated, may hold values from -3 to 3
- second_gain: float32 [384], replicated, may hold values from 0.5 to 1.5
- second_shift: float32 [384], replicated, may hold values from -3 to 3
- triple_weight: bfloat16 [384, 1152], replicated, may hold values from -0.55 to 0.55
- triple_bias: float32 [1152], replicated, may hold values from -3 to 3
- output_weight: bfloat16 [384, 384], replicated, may hold values from -0.3125 to 0.3125
- output_bias: float32 [384], replicated, may hold values from -3 to 3
- upsample_weight: bfloat16 [3, 3, 384, 192], replicated, may hold values from -0.109375 to 0.109375
- upsample_bias: float32 [192], replicated, may hold values from -3 to 3
Outputs:
- decoded: bfloat16 [128, 2, 208, 192], P('tile', 'frame')
Inputs may be any that keep to these rules, and one draw needn't show every extreme that they name: `row_video`: video numbers never fall along the rows; every video has 1 to 48 rows. `video_cols`: one video has all 104 columns.
All inputs are finite; a program needn't handle non-finite values.
Results may differ from a plain program's by a relative error of at most 0.013.
The roundings to bfloat16 on the way count: a program that leaves them out, or rounds other values in their place, can miss the bound.
Values may be sent and summed in bfloat16 or wider, within the bound.
No kernel may reach another device: no remote copies, remote signals or barrier semaphores. Data moves between devices by JAX's collectives and lax.ppermute only.
A program may use at most 128 MiB of HBM per device.

v0:
```python
import functools
import math

import jax
import jax.numpy as jnp
from jax import lax
from jax.experimental import pallas as pl
from jax.experimental.pallas import tpu as pltpu
from jax.sharding import PartitionSpec as P

GROUPS = 32
EPSILON = 1e-05
MASKED = -1e30
LOWEST = -5e29
HIGHEST = lax.Precision.HIGHEST
SLOTS = 8
ROWS_OF_TILE = 4
LANES = 128
VMEM_BYTES = 24 * 1024 * 1024
CONV_VMEM_BYTES = 50 * 1024 * 1024
F32 = jnp.float32
BF16 = jnp.bfloat16

SMEM_SPEC = pl.BlockSpec(memory_space=pltpu.SMEM)
VMEM_SPEC = pl.BlockSpec(memory_space=pltpu.VMEM)
HBM_SPEC = pl.BlockSpec(memory_space=pltpu.HBM)


def cost(microseconds):
    return pl.CostEstimate(
        flops=int(microseconds * 1.1e9), bytes_accessed=0, transcendentals=0
    )


def params():
    return pltpu.CompilerParams(vmem_limit_bytes=VMEM_BYTES)


def member_matrix(channels):
    per_group = channels // GROUPS
    group = lax.broadcasted_iota(jnp.int32, (LANES, channels), 0) * per_group
    channel = lax.broadcasted_iota(jnp.int32, (LANES, channels), 1)
    return jnp.where((channel >= group) & (channel < group + per_group), 1.0, 0.0).astype(F32)


def to_groups(values, member):
    return lax.dot_general(
        values, member, (((1,), (1,)), ((), ())), precision=HIGHEST, preferred_element_type=F32
    )


def to_channels(values, member):
    return jnp.dot(values, member, precision=HIGHEST, preferred_element_type=F32)


class Info:
    def __init__(self, ref, rows):
        self.ref, self.rows = ref, rows
        self.videos = ref.shape[0] - 1 - rows

    def tile(self):
        return self.ref[0]

    def label(self, row):
        inside = (row >= 0) & (row < self.rows)
        return jnp.where(inside, self.ref[1 + jnp.clip(row, 0, self.rows - 1)], -1)

    def width(self, label):
        return jnp.where(label >= 0, self.ref[1 + self.rows + jnp.maximum(label, 0)], 0)

    def window(self, first, count):
        labels = [self.label(first + r) for r in range(count)]
        return labels, [self.width(label) for label in labels]


def pick(table, label, videos):
    chosen = table[0:1]
    for video in range(1, videos):
        chosen = jnp.where(label == video, table[video : video + 1], chosen)
    return chosen


def norm_tables(stats_ref, gain_ref):
    member = member_matrix(gain_ref.shape[1])
    counts = jnp.maximum(stats_ref[0], 1.0)
    scale = lax.rsqrt(stats_ref[2] / counts + EPSILON)
    return to_channels(stats_ref[1], member), to_channels(scale, member) * gain_ref[...]


def write_stats(out_ref, rows, labels, widths, videos, channels):
    member = member_matrix(channels)
    per_group = channels // GROUPS
    cols = rows[0].shape[0]
    slot = lax.broadcasted_iota(jnp.int32, (SLOTS, 1), 0)
    column = lax.broadcasted_iota(jnp.int32, (cols, 1), 0)
    sums = jnp.zeros((SLOTS, channels), F32)
    counts = jnp.zeros((SLOTS, 1), F32)
    for index, row in enumerate(rows):
        sums = jnp.where(slot == index, jnp.sum(row, axis=0, keepdims=True), sums)
        counts = jnp.where(slot == index, (widths[index] * per_group).astype(F32), counts)
    means = to_groups(sums, member) / jnp.maximum(counts, 1.0)
    means_wide = to_channels(means, member)
    squares = jnp.zeros((SLOTS, channels), F32)
    for index, row in enumerate(rows):
        centered = jnp.where(column < widths[index], row - means_wide[index : index + 1], 0.0)
        squares = jnp.where(
            slot == index, jnp.sum(centered * centered, axis=0, keepdims=True), squares
        )
    spreads = to_groups(squares, member)
    out_ref[...] = jnp.zeros(out_ref.shape, F32)
    for video in range(videos):
        total = jnp.zeros((1, LANES), F32)
        count = jnp.zeros((1, LANES), F32)
        for index in range(len(rows)):
            mine = labels[index] == video
            row_count = counts[index : index + 1]
            total = total + jnp.where(mine, means[index : index + 1] * row_count, 0.0)
            count = count + jnp.where(mine, row_count, 0.0)
        mean = total / jnp.maximum(count, 1.0)
        spread = jnp.zeros((1, LANES), F32)
        for index in range(len(rows)):
            off = means[index : index + 1] - mean
            part = spreads[index : index + 1] + counts[index : index + 1] * off * off
            spread = spread + jnp.where(labels[index] == video, part, 0.0)
        out_ref[0, video : video + 1, :] = count
        out_ref[1, video : video + 1, :] = mean
        out_ref[2, video : video + 1, :] = spread


def build_columns(columns_ref, row_refs):
    padded = columns_ref.shape[0] // len(row_refs)
    for index, row in enumerate(row_refs):
        cells = row().astype(F32)
        count, channels = cells.shape
        cells = jnp.concatenate([cells, jnp.zeros((padded - count, channels), F32)], axis=0)
        start = index * padded
        columns_ref[start : start + padded, 0:channels] = pltpu.roll(cells, 1, 0).astype(BF16)
        columns_ref[start : start + padded, channels : 2 * channels] = cells.astype(BF16)
        columns_ref[start : start + padded, 2 * channels : 3 * channels] = pltpu.roll(
            cells, padded - 1, 0
        ).astype(BF16)


def stats_kernel(rows, info_ref, latents_ref, out_ref):
    info = Info(info_ref, rows)
    row_count, cols, channels = latents_ref.shape
    labels, widths = info.window(info.tile() * row_count, row_count)
    column = lax.broadcasted_iota(jnp.int32, (cols, 1), 0)
    cells = [
        jnp.where(column < widths[r], latents_ref[r].astype(F32), 0.0) for r in range(row_count)
    ]
    write_stats(out_ref, cells, labels, widths, info.videos, channels)


def rims(info, inner_ref, outer_ref):
    odd = lax.rem(info.tile(), 2) == 1
    inner, outer = inner_ref[0].astype(F32), outer_ref[0].astype(F32)
    return jnp.where(odd, inner, outer), jnp.where(odd, outer, inner)


def hidden_kernel(
    rows, info_ref, inner_ref, latents_ref, outer_ref, stats_ref, gain_ref, shift_ref, out_ref,
    source_ref,
):
    info = Info(info_ref, rows)
    row_count, cols, _ = latents_ref.shape
    labels, widths = info.window(info.tile() * row_count - 1, row_count + 2)
    means, scales = norm_tables(stats_ref, gain_ref)
    column = lax.broadcasted_iota(jnp.int32, (cols, 1), 0)
    above, below = rims(info, inner_ref, outer_ref)
    sources = [above] + [latents_ref[r].astype(F32) for r in range(row_count)] + [below]
    for r, source in enumerate(sources):
        mean = pick(means, labels[r], info.videos)
        scale = pick(scales, labels[r], info.videos)
        normed = (source - mean) * scale + shift_ref[...]
        active = normed / (1.0 + jnp.exp(-normed))
        active = jnp.where(column < widths[r], active, 0.0)
        rest = jnp.zeros((out_ref.shape[1] - cols, active.shape[1]), F32)
        out_ref[r] = jnp.concatenate([active, rest], axis=0).astype(BF16)
    source_ref[...] = latents_ref[...]


def hold_kernel(taps, weight_ref, held_ref, sems):
    channels = weight_ref.shape[-1]
    copies = [
        pltpu.make_async_copy(
            weight_ref.at[2 - depth // 3, depth % 3, side],
            held_ref.at[pl.ds(depth * channels, channels), pl.ds(side * channels, channels)],
            sems.at[side, depth],
        )
        for side in range(3)
        for depth in range(3 * taps)
    ]
    for copy in copies:
        copy.start()
    for copy in copies:
        copy.wait()


def conv_kernel(rows, taps, info_ref, *rest):
    hidden_refs, rest = rest[:taps], rest[taps:]
    latents_ref, bias_ref, held_ref, own_ref, stats_ref, inputs_ref = rest
    row_count, cols, channels = latents_ref.shape
    info = Info(info_ref, rows)
    padded = hidden_refs[0].shape[1]
    labels, widths = info.window(info.tile() * row_count - 1, row_count + 2)
    for back, hidden_ref in enumerate(hidden_refs):
        for tap in range(3):
            lanes = slice((3 * back + tap) * channels, (3 * back + tap + 1) * channels)
            for r in range(row_count):
                block = hidden_ref[r + tap]
                if tap != 1:
                    same = labels[r + tap] == labels[r + 1]
                    block = jnp.where(same, block, jnp.zeros_like(block))
                inputs_ref[r * padded : (r + 1) * padded, lanes] = block
    product = jnp.dot(inputs_ref[...], held_ref[...], preferred_element_type=F32)
    column = lax.broadcasted_iota(jnp.int32, (cols, 1), 0)
    cells = []
    for r in range(row_count):
        lines = slice(r * padded, (r + 1) * padded)
        branch = pltpu.roll(product[lines, 0:channels], 1, 0)
        branch = branch + product[lines, channels : 2 * channels]
        branch = branch + pltpu.roll(product[lines, 2 * channels :], padded - 1, 0)
        value = latents_ref[r].astype(F32) + branch[:cols] + bias_ref[...]
        value = jnp.where(column < widths[r + 1], value, 0.0).astype(BF16)
        cells.append(value.astype(F32))
    for pair in range(row_count // 2):
        own_ref[pair] = jnp.concatenate(cells[2 * pair : 2 * pair + 2], axis=0).astype(BF16)
    write_stats(stats_ref, cells, labels[1:-1], widths[1:-1], info.videos, channels)


def split_rows(pairs_ref):
    cols = pairs_ref.shape[1] // 2
    cells = []
    for pair in range(pairs_ref.shape[0]):
        both = pairs_ref[pair].astype(F32)
        cells += [both[:cols], both[cols:]]
    return cells


def query_kernel(
    rows, info_ref, own_ref, other_ref, stats_ref, gain_ref, shift_ref, weight_ref, bias_ref,
    *out_refs,
):
    info = Info(info_ref, rows)
    pairs, double, channels = own_ref.shape
    cols = double // 2
    row_count = 2 * pairs
    span = row_count * cols
    means, scales = norm_tables(stats_ref, gain_ref)
    column = lax.broadcasted_iota(jnp.int32, (cols, 1), 0)
    cells = []
    for tile, pairs_ref in ((info.tile(), own_ref), (info.tile() ^ 1, other_ref)):
        labels, widths = info.window(tile * row_count, row_count)
        for r, values in enumerate(split_rows(pairs_ref)):
            mean = pick(means, labels[r], info.videos)
            scale = pick(scales, labels[r], info.videos)
            normed = (values - mean) * scale + shift_ref[...]
            cells.append(jnp.where(column < widths[r], normed, 0.0))
    cells = jnp.concatenate(cells, axis=0).astype(BF16)
    queries = (
        jnp.dot(cells, weight_ref[:, 0:channels], preferred_element_type=F32)
        + bias_ref[:, 0:channels]
    ).astype(BF16)
    factor = channels ** (-0.5) * math.log2(math.e)
    turned = lax.dot_general(
        queries, weight_ref[:, channels : 2 * channels], (((1,), (1,)), ((), ())),
        preferred_element_type=F32,
    )
    turned = (turned * factor).astype(BF16)
    constant = jnp.sum(
        queries.astype(F32) * bias_ref[:, channels : 2 * channels], axis=1, keepdims=True
    )
    constant = jnp.broadcast_to(constant * factor, (2 * span, LANES))
    for side in range(2):
        out_refs[2 * side][...] = turned[side * span : (side + 1) * span]
        out_refs[2 * side + 1][...] = constant[side * span : (side + 1) * span]


def key_codes(info, masks, span, cols):
    row_count = span // cols
    position = lax.broadcasted_iota(jnp.int32, (1, len(masks) * span), 1)
    codes = jnp.full((1, len(masks) * span), -2.0, F32)
    for index, mask in enumerate(masks):
        near, widths = info.window((info.tile() ^ (2 * mask)) * row_count, row_count)
        for r in range(row_count):
            start = index * span + r * cols
            inside = (position >= start) & (position < start + widths[r])
            codes = jnp.where(inside, near[r].astype(F32), codes)
    return codes


def query_codes(info, tile, span, cols):
    row_count = span // cols
    labels, _ = info.window(tile * row_count, row_count)
    return jnp.concatenate(
        [jnp.zeros((cols, 1), F32) + label.astype(F32) for label in labels], axis=0
    )


def scores_of(queries, keys, codes, query_code):
    scores = lax.dot_general(
        queries, keys, (((1,), (1,)), ((), ())), preferred_element_type=F32
    )
    return jnp.where(codes == query_code, scores, MASKED)


def mean_and_level(peak, denominator, total):
    some = denominator > 0.0
    safe = jnp.where(some, denominator, 1.0)
    return total / safe, jnp.where(some, peak + jnp.log2(safe), LOWEST)


def attend_yours_kernel(rows, masks, first, last, info_ref, *rest):
    stats_ref, gain_ref, shift_ref, queries_ref, constant_ref, *rest = rest
    block_refs, rest = rest[: len(masks)], rest[len(masks) :]
    if not first:
        old_peak_ref, old_sum_ref, old_total_ref, *rest = rest
    keys_ref, *out_refs = rest
    info = Info(info_ref, rows)
    span, channels = queries_ref.shape
    pairs, double, _ = block_refs[0].shape
    cols = double // 2
    row_count = 2 * pairs
    tile = info.tile()
    means, scales = norm_tables(stats_ref, gain_ref)
    for index, (mask, block_ref) in enumerate(zip(masks, block_refs)):
        near, _ = info.window((tile ^ (2 * mask)) * row_count, row_count)
        for pair in range(pairs):
            both = block_ref[pair].astype(F32)
            halves = []
            for half in range(2):
                label = near[2 * pair + half]
                mean = pick(means, label, info.videos)
                scale = pick(scales, label, info.videos)
                values = both[half * cols : (half + 1) * cols]
                halves.append((values - mean) * scale + shift_ref[...])
            start = index * span + pair * double
            keys_ref[start : start + double, :] = jnp.concatenate(halves, axis=0).astype(BF16)
    constant = constant_ref[:, 0:1]
    scores = scores_of(
        queries_ref[...], keys_ref[...], key_codes(info, masks, span, cols),
        query_codes(info, tile ^ 1, span, cols),
    )
    peak = jnp.maximum(LOWEST, jnp.max(scores, axis=1, keepdims=True) + constant)
    if not first:
        largest = old_peak_ref[:, 0:1]
        peak = jnp.maximum(largest, peak)
    weights = jnp.exp2(scores - (peak - constant))
    denominator = jnp.sum(weights, axis=1, keepdims=True)
    total = jnp.dot(weights.astype(BF16), keys_ref[...], preferred_element_type=F32)
    if not first:
        factor = jnp.exp2(largest - peak)
        denominator = old_sum_ref[:, 0:1] * factor + denominator
        total = old_total_ref[...] * factor + total
    if not last:
        peak_ref, sum_ref, total_ref = out_refs
        peak_ref[...] = jnp.broadcast_to(peak, peak_ref.shape)
        sum_ref[...] = jnp.broadcast_to(denominator, sum_ref.shape)
        total_ref[...] = total
        return
    (sent_ref,) = out_refs
    mean, level = mean_and_level(peak, denominator, total)
    sent_ref[0:span, :] = mean.astype(BF16)
    slots = sent_ref.shape[0] - span
    slot = lax.broadcasted_iota(jnp.int32, (slots, 1), 0)
    packed = jnp.zeros((slots, LANES), F32)
    for r in range(row_count):
        left = level[r * cols : (r + 1) * cols]
        left = jnp.sum(jnp.where(diagonal(cols), left, 0.0), axis=0, keepdims=True)
        for part in range(3):
            rounded = left.astype(BF16).astype(F32)
            packed = jnp.where(slot == 3 * r + part, rounded, packed)
            left = left - rounded
    sent_ref[span:, 0:LANES] = packed.astype(BF16)
    sent_ref[span:, LANES:] = jnp.zeros((slots, channels - LANES), BF16)


def attend_mine_kernel(rows, groups, info_ref, queries_ref, constant_ref, *rest):
    key_refs, (mean_ref, level_ref) = rest[: len(groups)], rest[len(groups) :]
    info = Info(info_ref, rows)
    span = queries_ref.shape[0]
    cols = span // ROWS_OF_TILE
    query_code = query_codes(info, info.tile(), span, cols)
    constant = constant_ref[:, 0:1]
    peak = jnp.full((span, 1), LOWEST, F32)
    scores = []
    for masks, key_ref in zip(groups, key_refs):
        codes = key_codes(info, masks, span, cols)
        scores.append(scores_of(queries_ref[...], key_ref[...], codes, query_code))
        peak = jnp.maximum(peak, jnp.max(scores[-1], axis=1, keepdims=True) + constant)
    denominator, total = 0.0, 0.0
    for part, key_ref in zip(scores, key_refs):
        weights = jnp.exp2(part - (peak - constant))
        denominator = denominator + jnp.sum(weights, axis=1, keepdims=True)
        total = total + jnp.dot(
            weights.astype(BF16), key_ref[...], preferred_element_type=F32
        )
    mean, level = mean_and_level(peak, denominator, total)
    mean_ref[...] = mean
    level_ref[...] = jnp.broadcast_to(level, level_ref.shape)


def diagonal(cols):
    return lax.broadcasted_iota(jnp.int32, (cols, LANES), 0) == lax.broadcasted_iota(
        jnp.int32, (cols, LANES), 1
    )


def finish_kernel(
    rows, info_ref, mean_ref, level_ref, received_ref, own_ref, triple_ref, triple_bias_ref,
    output_ref, output_bias_ref, out_ref, inner_ref, outer_ref,
):
    info = Info(info_ref, rows)
    row_count, cols, channels = out_ref.shape
    span = row_count * cols
    _, widths = info.window(info.tile() * row_count, row_count)
    received = received_ref[0:span, :].astype(F32)
    levels = received_ref[span:, 0:LANES].astype(F32)
    yours = []
    for r in range(row_count):
        level = levels[3 * r : 3 * r + 1] + levels[3 * r + 1 : 3 * r + 2]
        level = level + levels[3 * r + 2 : 3 * r + 3]
        yours.append(jnp.sum(jnp.where(diagonal(cols), level, 0.0), axis=1, keepdims=True))
    yours = jnp.concatenate(yours, axis=0)
    mine = level_ref[:, 0:1]
    peak = jnp.maximum(mine, yours)
    weight, other_weight = jnp.exp2(mine - peak), jnp.exp2(yours - peak)
    share = weight / (weight + other_weight)
    mean_cell = (mean_ref[...] * share + received * (1.0 - share)).astype(BF16)
    mixed = (
        jnp.dot(mean_cell, triple_ref[:, 2 * channels :], preferred_element_type=F32)
        + triple_bias_ref[:, 2 * channels :]
    ).astype(BF16)
    attended = jnp.dot(mixed, output_ref[...], preferred_element_type=F32) + output_bias_ref[...]
    column = lax.broadcasted_iota(jnp.int32, (cols, 1), 0)
    for r, before in enumerate(split_rows(own_ref)):
        value = before + attended[r * cols : (r + 1) * cols]
        value = jnp.where(column < widths[r], value, 0.0)
        out_ref[r] = value.astype(BF16)
        if r == 0:
            top = value
    odd = lax.rem(info.tile(), 2) == 1
    inner_ref[0] = jnp.where(odd, top, value).astype(BF16)
    outer_ref[0] = jnp.where(odd, value, top).astype(BF16)


def fold_kernel(weight_ref, out_ref):
    channels = weight_ref.shape[-1]
    wide = [[weight_ref[a, b].astype(F32) for b in range(3)] for a in range(3)]

    def both(upper, lower):
        return [x + y for x, y in zip(upper, lower)]

    phases = [[wide[0], both(wide[1], wide[2])], [both(wide[0], wide[1]), wide[2]]]
    for down in range(2):
        for tap in range(2):
            left, middle, right = phases[down][tap]
            out_ref[down, tap, 0, :, 0:channels] = left.astype(BF16)
            out_ref[down, tap, 0, :, channels:] = (middle + right).astype(BF16)
            out_ref[down, tap, 1, :, 0:channels] = (left + middle).astype(BF16)
            out_ref[down, tap, 1, :, channels:] = right.astype(BF16)


def upsample_kernel(
    rows, info_ref, inner_ref, own_ref, outer_ref, weight_ref, bias_ref, out_ref, columns_ref,
    wide_ref,
):
    info = Info(info_ref, rows)
    row_count, cols, channels = own_ref.shape
    near_rows = row_count + 2
    padded = columns_ref.shape[0] // near_rows
    parts_out = wide_ref.shape[0]
    out_channels = out_ref.shape[-1]
    labels, widths = info.window(info.tile() * row_count - 1, near_rows)
    above, below = rims(info, inner_ref, outer_ref)
    sources = [lambda: above]
    sources += [functools.partial(own_ref.__getitem__, r) for r in range(row_count)]
    sources += [lambda: below]
    build_columns(columns_ref, sources)
    span = row_count * padded
    wide_column = lax.broadcasted_iota(jnp.int32, (2 * cols, 1), 0)
    for down in range(2):
        for right in range(2):
            lanes = slice(right * channels, (right + 2) * channels)
            products = [
                lax.dot_general(
                    columns_ref[(down + tap) * padded : (down + tap) * padded + span, lanes],
                    weight_ref[down, tap, right],
                    (((1,), (1,)), ((), ())),
                    preferred_element_type=F32,
                )
                for tap in range(2)
            ]
            rim, same = products[down], products[1 - down]
            for r in range(row_count):
                lo, hi = r * padded, r * padded + cols
                near = labels[r + 2 * down]
                value = same[lo:hi] + jnp.where(near == labels[r + 1], rim[lo:hi], 0.0)
                for part in range(parts_out):
                    part_lo, part_hi = part * LANES, min((part + 1) * LANES, out_channels)
                    piece = value[:, part_lo:part_hi]
                    if part_hi - part_lo < LANES:
                        missing = LANES - (part_hi - part_lo)
                        piece = jnp.concatenate([piece, jnp.zeros((cols, missing), F32)], axis=1)
                    wide_ref[part, 2 * r + down, pl.ds(right, cols, 2), :] = piece
    for r in range(2 * row_count):
        valid = wide_column < 2 * widths[r // 2 + 1]
        for part in range(parts_out):
            lo, hi = part * LANES, min((part + 1) * LANES, out_channels)
            value = wide_ref[part, r, :, 0 : hi - lo] + bias_ref[:, lo:hi]
            out_ref[r, :, lo:hi] = jnp.where(valid, value, 0.0).astype(BF16)


def merge_stats(mine, other):
    count = mine[0] + other[0]
    safe = jnp.maximum(count, 1.0)
    off = other[1] - mine[1]
    mean = mine[1] + off * (other[0] / safe)
    spread = mine[2] + other[2] + off * off * (mine[0] * other[0] / safe)
    return jnp.stack([count, mean, spread])


def exchange(array, tiles, mask, among=None):
    moves = [(i, i ^ mask) for i in range(tiles) if among is None or among(i)]
    return lax.ppermute(array, "tile", moves)


def merge_round(stats, tiles, masks):
    parts = [stats] + [exchange(stats, tiles, mask) for mask in masks]
    while len(parts) > 1:
        parts = [merge_stats(*parts[i : i + 2]) for i in range(0, len(parts), 2)]
    return parts[0]


def merge_masks(tiles):
    bits = [1 << i for i in range(tiles.bit_length() - 1)]
    pairs = [bits[i : i + 2] for i in range(0, len(bits), 2)]
    return [[p[0], p[1], p[0] ^ p[1]] if len(p) == 2 else p for p in pairs]


def shards(
    tiles,
    frames,
    latents,
    row_video,
    video_cols,
    first_gain,
    first_shift,
    conv_weight,
    conv_bias,
    second_gain,
    second_shift,
    triple_weight,
    triple_bias,
    output_weight,
    output_bias,
    upsample_weight,
    upsample_bias,
):
    row_count, frame_count, cols, channels = latents.shape
    assert frame_count == 1 and row_count == ROWS_OF_TILE and tiles % 4 == 0
    out_channels = upsample_weight.shape[-1]
    rows = row_count * tiles
    cells = row_count * cols
    padded = -(-(cols + 1) // 16) * 16
    near_rows = row_count + 2
    source = latents.reshape(row_count, cols, channels)
    tile = lax.axis_index("tile").astype(jnp.int32)
    info = jnp.concatenate([jnp.reshape(tile, (1,)), row_video, video_cols])

    def row(vector):
        return vector.reshape(1, -1)

    def shape(*dims, dtype=BF16):
        return jax.ShapeDtypeStruct(dims, dtype)

    def call(kernel, operands, out_shape, scratch=(), **kwargs):
        many = isinstance(out_shape, tuple)
        return pl.pallas_call(
            kernel,
            out_shape=out_shape,
            in_specs=[SMEM_SPEC] + [VMEM_SPEC] * len(operands),
            out_specs=(VMEM_SPEC,) * len(out_shape) if many else VMEM_SPEC,
            scratch_shapes=list(scratch),
            compiler_params=params(),
            **kwargs,
        )(info, *operands)

    outer_moves = [(i, i - 1 if i % 2 == 0 else i + 1) for i in range(tiles)]
    outer_moves = [(i, j) for i, j in outer_moves if 0 <= j < tiles]
    odd = tile % 2 == 1
    stats_shape = shape(3, SLOTS, LANES, dtype=F32)
    stats = call(
        functools.partial(stats_kernel, rows), [source], stats_shape,
        cost_estimate=cost(1.5), name="first_stats",
    )
    inner = exchange(jnp.where(odd, source[:1], source[row_count - 1 :]), tiles, 1)
    outer = lax.ppermute(
        jnp.where(odd, source[row_count - 1 :], source[:1]), "tile", outer_moves
    )
    taps = min(3, frames)
    held = pl.pallas_call(
        functools.partial(hold_kernel, taps),
        out_shape=shape(3 * taps * channels, 3 * channels),
        in_specs=[HBM_SPEC],
        out_specs=VMEM_SPEC,
        scratch_shapes=[pltpu.SemaphoreType.DMA((3, 3 * taps))],
        compiler_params=pltpu.CompilerParams(vmem_limit_bytes=CONV_VMEM_BYTES),
        cost_estimate=cost(1.0 * taps),
        name="hold",
    )(conv_weight)
    rounds = merge_masks(tiles)
    for index, masks in enumerate(rounds):
        stats = merge_round(stats, tiles, masks)
        if index == 0:
            stats, held = lax.optimization_barrier((stats, held))
    hidden, source = call(
        functools.partial(hidden_kernel, rows),
        [inner, source, outer, stats, row(first_gain), row(first_shift)],
        (shape(near_rows, padded, channels), shape(row_count, cols, channels)),
        cost_estimate=cost(1.3),
        name="hidden",
    )

    context = [hidden] + [
        lax.ppermute(hidden, "frame", [(i, i + by) for i in range(frames - by)])
        for by in range(1, taps)
    ]

    pairs = row_count // 2
    pair_shape = shape(pairs, 2 * cols, channels)
    own, stats = pl.pallas_call(
        functools.partial(conv_kernel, rows, taps),
        out_shape=(pair_shape, stats_shape),
        in_specs=[SMEM_SPEC] + [VMEM_SPEC] * (taps + 3),
        out_specs=(VMEM_SPEC, VMEM_SPEC),
        scratch_shapes=[
            pltpu.VMEM((row_count * padded, 3 * taps * channels), BF16),
        ],
        compiler_params=params(),
        cost_estimate=cost(2.5 * taps),
        name="conv",
    )(info, *context, source, row(conv_bias), held)

    blocks = {0: own}
    neighbour = [(i, i ^ 1) for i in range(tiles)]
    if tiles == 16 and video_cols.shape[0] == 2:
        def middle(t):
            return t // 4 in (1, 2)

        stats = merge_round(stats, tiles, rounds[1])
        other = exchange(own, tiles, 1)
        blocks[1] = exchange(own, tiles, 2)
        blocks[2] = exchange(own, tiles, 4)
        blocks[6] = exchange(own, tiles, 12, middle)
        stats, other, blocks[1], blocks[2], blocks[6] = lax.optimization_barrier(
            (stats, other, blocks[1], blocks[2], blocks[6])
        )
        stats = merge_round(stats, tiles, rounds[0])
        inward = exchange(blocks[2], tiles, 12, middle)
        outward = exchange(blocks[6], tiles, 4, middle)
        blocks[4] = jnp.where((tile // 4 == 1) | (tile // 4 == 2), inward, outward)
        blocks[7] = exchange(blocks[6], tiles, 2, middle)
        blocks[5] = exchange(blocks[4], tiles, 2)
        passed, blocks[4] = lax.optimization_barrier((blocks[1], blocks[4]))
        blocks[3] = exchange(passed, tiles, 4)
        groups = [[0, 1, 2, 6], [4], [7, 3, 5]]
    else:
        for masks in rounds:
            stats = merge_round(stats, tiles, masks)
        other = exchange(own, tiles, 1)
        for mask in range(1, tiles // 2):
            blocks[mask] = exchange(own, tiles, 2 * mask)
        groups = [list(range(i, i + 4)) for i in range(0, tiles // 2, 4)]
    gain, shift = row(second_gain), row(second_shift)
    query_shapes = (shape(cells, channels), shape(cells, LANES, dtype=F32))
    mine_queries, mine_constant, queries, constant = call(
        functools.partial(query_kernel, rows),
        [own, other, stats, gain, shift, triple_weight, row(triple_bias)],
        query_shapes * 2,
        cost_estimate=cost(1.9),
        name="queries",
    )

    level_shape = shape(cells, LANES, dtype=F32)
    total_shape = shape(cells, channels, dtype=F32)
    state, keys = (), []
    for index, masks in enumerate(groups):
        last = index == len(groups) - 1
        outs = (shape(len(masks) * cells, channels),)
        outs += (shape(cells + 16, channels),) if last else (level_shape, level_shape, total_shape)
        normed, *state = call(
            functools.partial(attend_yours_kernel, rows, tuple(masks), index == 0, last),
            [stats, gain, shift, queries, constant] + [blocks[m] for m in masks] + list(state),
            outs,
            cost_estimate=cost(1.0 * len(masks)),
            name="attend_yours",
        )
        keys.append(normed)
    (sent,) = state
    received = lax.ppermute(sent, "tile", neighbour)
    sent, mine_queries, upsample_weight = lax.optimization_barrier(
        (sent, mine_queries, upsample_weight)
    )
    mean, level = call(
        functools.partial(attend_mine_kernel, rows, tuple(tuple(masks) for masks in groups)),
        [mine_queries, mine_constant] + keys,
        (total_shape, level_shape),
        cost_estimate=cost(6.0),
        name="attend_mine",
    )
    folded = pl.pallas_call(
        fold_kernel,
        out_shape=shape(2, 2, 2, out_channels, 2 * channels),
        in_specs=[VMEM_SPEC],
        out_specs=VMEM_SPEC,
        compiler_params=params(),
        cost_estimate=cost(0.5),
        name="fold",
    )(jnp.swapaxes(upsample_weight, 2, 3))

    rim_shape = shape(1, cols, channels)
    attended, inner, outer = call(
        functools.partial(finish_kernel, rows),
        [
            mean, level, received, own, triple_weight, row(triple_bias), output_weight,
            row(output_bias),
        ],
        (shape(row_count, cols, channels), rim_shape, rim_shape),
        cost_estimate=cost(1.4),
        name="finish",
    )
    outer = lax.ppermute(outer, "tile", outer_moves)
    inner = exchange(inner, tiles, 1)
    decoded = call(
        functools.partial(upsample_kernel, rows),
        [inner, attended, outer, folded, row(upsample_bias)],
        shape(2 * row_count, 2 * cols, out_channels),
        scratch=[
            pltpu.VMEM((near_rows * padded, 3 * channels), BF16),
            pltpu.VMEM((-(-out_channels // LANES), 2 * row_count, 2 * cols, LANES), F32),
        ],
        cost_estimate=cost(2.3),
        name="upsample",
    )
    return decoded.reshape(2 * row_count, 1, 2 * cols, out_channels)


def solution(mesh):
    sizes = dict(mesh.shape)
    in_specs = (P("tile", "frame", None, None),) + (P(),) * 14
    out_specs = P("tile", "frame", None, None)
    body = functools.partial(shards, sizes["tile"], sizes["frame"])
    return jax.shard_map(body, mesh=mesh, in_specs=in_specs, out_specs=out_specs, check_vma=False)
```

profile of v0, /device:TPU:8, one launch (start us, length us, event | category | flops | bytes accessed | tf_op | source)
XLA Modules:
  0.0 102.5 jit_solution(1810404774590663737)
XLA Ops:
  1.7 1.8 %first_stats.1 = f32[3,8,128]{2,1,0:T(8,128)S(1)} custom-call(s32[67]{0:T(128)S(1)} %pad_add_fusion.info_ref, bf16[4,104,384]{2,1,0:T(8,128)(2,1)S(1)} %bitcast.11), custom_call_target="tpu_custom_call" | custom-call | flops 1650000000 | tf_op jit(solution)/shard_map/first_stats/pallas_call | solution.py:580
  7.2 5.0 %hold.1.rest_4_ = bf16[2304,1152]{1,0:T(8,128)(2,1)} custom-call(bf16[3,3,3,384,384]{4,3,2,1,0:T(8,128)(2,1)} %weight_ref.2), custom_call_target="tpu_custom_call" | custom-call | flops 2200000000 | tf_op jit(solution)/shard_map/hold/pallas_call | solution.py:603
  12.3 3.0 %collective-permute-start.6 = (f32[3,8,128]{2,1,0:T(8,128)S(1)}, f32[3,8,128]{2,1,0:T(8,128)S(1)}, u32[]{:S(2)}, u32[]{:S(2)}) collective-permute-start(f32[3,8,128]{2,1,0:T(8,128)S(1)} %pad_maximum_fusion), channel_id=1, source_target_pairs={{0,16},{2,18},{4,20},{6,22},{8,24},{10,26},{12,28},{14,30},{16,0},... | collective-permute-start | bytes 36872 | tf_op jit(solution)/shard_map/ppermute | solution.py:526
  15.8 1.6 %collective-permute-start = (bf16[1,104,384]{2,1,0:T(8,128)(2,1)S(1)}, bf16[1,104,384]{2,1,0:T(8,128)(2,1)S(1)}, u32[]{:S(2)}, u32[]{:S(2)}) collective-permute-start(bf16[1,104,384]{2,1,0:T(8,128)(2,1)S(1)} %get-tuple-element.86), channel_id=1, source_target_pairs={{0,2},{2,0},{4,6},{6,4},{8,10},{10,8},{12,14},{14,12},{16,18},{18,... | collective-permute-start | bytes 239624 | tf_op jit(solution)/shard_map/ppermute | solution.py:526
  17.4 4.2 %collective-permute-start.1 = (bf16[1,104,384]{2,1,0:T(8,128)(2,1)S(1)}, bf16[1,104,384]{2,1,0:T(8,128)(2,1)S(1)}, u32[]{:S(2)}, u32[]{:S(2)}) collective-permute-start(bf16[1,104,384]{2,1,0:T(8,128)(2,1)S(1)} %get-tuple-element.85), channel_id=1, source_target_pairs={{2,4},{4,2},{6,8},{8,6},{10,12},{12,10},{14,16},{16,14},{18,20},{2... | collective-permute-start | bytes 239624 | tf_op jit(solution)/shard_map/ppermute | solution.py:599
  21.7 3.8 %collective-permute-done.1.outer_ref = bf16[1,104,384]{2,1,0:T(8,128)(2,1)S(1)} collective-permute-done((bf16[1,104,384]{2,1,0:T(8,128)(2,1)S(1)}, bf16[1,104,384]{2,1,0:T(8,128)(2,1)S(1)}, u32[]{:S(2)}, u32[]{:S(2)}) %collective-permute-start.1) | collective-permute-done | bytes 79904 | tf_op jit(solution)/shard_map/ppermute | solution.py:599
  29.6 5.1 %conv.1 = (bf16[2,208,384]{2,1,0:T(8,128)(2,1)S(1)}, f32[3,8,128]{2,1,0:T(8,128)S(1)}) custom-call(s32[67]{0:T(128)S(1)} %pad_add_fusion.info_ref, bf16[6,112,384]{2,1,0:T(8,128)(2,1)S(1)} %get-tuple-element.40.rest_0_, bf16[6,112,384]{2,1,0:T(8,128)(2,1)S(1)} %collective-permute-done.8.rest_1_, bf16[4,104,384]{2,1,0:T(8,128)(2,1)S(1)} %get-tuple-element.41.rest_2_, ...), custom_call_target="tpu_custom_call" | custom-call | flops 5500000256 | tf_op jit(solution)/shard_map/conv/pallas_call | solution.py:633
  34.7 3.5 %collective-permute-start.10 = (f32[3,8,128]{2,1,0:T(8,128)S(1)}, f32[3,8,128]{2,1,0:T(8,128)S(1)}, u32[]{:S(2)}, u32[]{:S(2)}) collective-permute-start(f32[3,8,128]{2,1,0:T(8,128)S(1)} %get-tuple-element.43), channel_id=1, source_target_pairs={{0,16},{2,18},{4,20},{6,22},{8,24},{10,26},{12,28},{14,30},{16,0},... | collective-permute-start | bytes 36872 | tf_op jit(solution)/shard_map/ppermute | solution.py:526
  41.9 3.3 %collective-permute-start.15 = (bf16[2,208,384]{2,1,0:T(8,128)(2,1)S(1)}, bf16[2,208,384]{2,1,0:T(8,128)(2,1)S(1)}, u32[]{:S(2)}, u32[]{:S(2)}) collective-permute-start(bf16[2,208,384]{2,1,0:T(8,128)(2,1)S(1)} %get-tuple-element.44.own_ref.rest_5_), channel_id=1, source_target_pairs={{8,16},{10,18},{12,20},{14,22},{16,8},{18,10},{20,12},{22,14},{9,1... | collective-permute-start | bytes 958472 | tf_op jit(solution)/shard_map/ppermute | solution.py:526
  45.3 3.6 %collective-permute-done.12.other_ref = bf16[2,208,384]{2,1,0:T(8,128)(2,1)S(1)} collective-permute-done((bf16[2,208,384]{2,1,0:T(8,128)(2,1)S(1)}, bf16[2,208,384]{2,1,0:T(8,128)(2,1)S(1)}, u32[]{:S(2)}, u32[]{:S(2)}) %collective-permute-start.12) | collective-permute-done | bytes 319520 | tf_op jit(solution)/shard_map/ppermute | solution.py:526
  49.6 2.6 %collective-permute-done.15.rest_8_ = bf16[2,208,384]{2,1,0:T(8,128)(2,1)S(1)} collective-permute-done((bf16[2,208,384]{2,1,0:T(8,128)(2,1)S(1)}, bf16[2,208,384]{2,1,0:T(8,128)(2,1)S(1)}, u32[]{:S(2)}, u32[]{:S(2)}) %collective-permute-start.15) | collective-permute-done | bytes 319520 | tf_op jit(solution)/shard_map/ppermute | solution.py:526
  57.0 2.6 %collective-permute-start.19 = (bf16[2,208,384]{2,1,0:T(8,128)(2,1)S(1)}, bf16[2,208,384]{2,1,0:T(8,128)(2,1)S(1)}, u32[]{:S(2)}, u32[]{:S(2)}) collective-permute-start(bf16[2,208,384]{2,1,0:T(8,128)(2,1)S(1)} %collective-permute-done.15.rest_8_), channel_id=1, source_target_pairs={{8,12},{10,14},{12,8},{14,10},{16,20},{18,22},{20,16},{22,18},{9,1... | collective-permute-start | bytes 958472 | tf_op jit(solution)/shard_map/ppermute | solution.py:526
  59.6 3.8 %collective-permute-start.20 = (bf16[2,208,384]{2,1,0:T(8,128)(2,1)S(1)}, bf16[2,208,384]{2,1,0:T(8,128)(2,1)S(1)}, u32[]{:S(2)}, u32[]{:S(2)}) collective-permute-start(bf16[2,208,384]{2,1,0:T(8,128)(2,1)S(1)} %collective-permute-done.14.rest_7_), channel_id=1, source_target_pairs={{8,16},{10,18},{12,20},{14,22},{16,8},{18,10},{20,12},{22,14},{9,1... | collective-permute-start | bytes 958472 | tf_op jit(solution)/shard_map/ppermute | solution.py:526
  63.6 1.9 %queries.1 = (bf16[416,384]{1,0:T(8,128)(2,1)S(1)}, f32[416,128]{1,0:T(8,128)S(1)}, bf16[416,384]{1,0:T(8,128)(2,1)S(1)}, f32[416,128]{1,0:T(8,128)S(1)}) custom-call(s32[67]{0:T(128)S(1)} %pad_add_fusion.info_ref, bf16[2,208,384]{2,1,0:T(8,128)(2,1)S(1)} %get-tuple-element.44.own_ref.rest_5_, bf16[2,208,384]{2,1,0:T(8,128)(2,1)S(1)} %collective-permute-done.12.other_ref, ...), custom_call_target="tpu_custom_call" | custom-call | flops 2090000000 | tf_op jit(solution)/shard_map/queries/pallas_call | solution.py:580
  65.4 3.1 %collective-permute-done.20 = bf16[2,208,384]{2,1,0:T(8,128)(2,1)S(1)} collective-permute-done((bf16[2,208,384]{2,1,0:T(8,128)(2,1)S(1)}, bf16[2,208,384]{2,1,0:T(8,128)(2,1)S(1)}, u32[]{:S(2)}, u32[]{:S(2)}) %collective-permute-start.20) | collective-permute-done | bytes 319520 | tf_op jit(solution)/shard_map/ppermute | solution.py:526
  70.0 3.4 %attend_yours.3 = (bf16[1664,384]{1,0:T(8,128)(2,1)S(1)}, f32[416,128]{1,0:T(8,128)S(1)}, f32[416,128]{1,0:T(8,128)S(1)}, f32[416,384]{1,0:T(8,128)S(1)}) custom-call(s32[67]{0:T(128)S(1)} %pad_add_fusion.info_ref, f32[3,8,128]{2,1,0:T(8,128)S(1)} %pad_maximum_fusion.3.stats_ref.rest_0_, f32[1,384]{1,0:T(1,128)S(1)} %reshape.85.gain_ref.rest_1_, ...), custom_call_target="tpu_custom_call" | custom-call | flops 4400000000 | tf_op jit(solution)/shard_map/attend_yours/pallas_call | solution.py:580
  73.4 2.3 %attend_yours.4 = (bf16[416,384]{1,0:T(8,128)(2,1)S(1)}, f32[416,128]{1,0:T(8,128)S(1)}, f32[416,128]{1,0:T(8,128)S(1)}, f32[416,384]{1,0:T(8,128)S(1)}) custom-call(s32[67]{0:T(128)S(1)} %pad_add_fusion.info_ref, f32[3,8,128]{2,1,0:T(8,128)S(1)} %pad_maximum_fusion.3.stats_ref.rest_0_, f32[1,384]{1,0:T(1,128)S(1)} %reshape.85.gain_ref.rest_1_, ...), custom_call_target="tpu_custom_call" | custom-call | flops 1100000000 | tf_op jit(solution)/shard_map/attend_yours/pallas_call | solution.py:580
  77.0 3.0 %attend_yours.5 = (bf16[1248,384]{1,0:T(8,128)(2,1)S(1)}, bf16[432,384]{1,0:T(8,128)(2,1)S(1)}) custom-call(s32[67]{0:T(128)S(1)} %pad_add_fusion.info_ref, f32[3,8,128]{2,1,0:T(8,128)S(1)} %pad_maximum_fusion.3.stats_ref.rest_0_, f32[1,384]{1,0:T(1,128)S(1)} %reshape.85.gain_ref.rest_1_, f32[1,384]{1,0:T(1,128)S(1)} %reshape.86.shift_ref.rest_2_, ...), custom_call_target="tpu_custom_call" | custom-call | flops 3300000000 | tf_op jit(solution)/shard_map/attend_yours/pallas_call | solution.py:580
  81.1 4.9 %attend_mine.1 = (f32[416,384]{1,0:T(8,128)S(1)}, f32[416,128]{1,0:T(8,128)S(1)}) custom-call(s32[67]{0:T(128)S(1)} %pad_add_fusion.info_ref, bf16[416,384]{1,0:T(8,128)(2,1)S(1)} %get-tuple-element.62.queries_ref, f32[416,128]{1,0:T(8,128)S(1)} %get-tuple-element.63.constant_ref, bf16[1664,384]{1,0:T(8,128)(2,1)S(1)} %get-tuple-element.64.rest_0_, ...), custom_call_target="tpu_custom_call" | custom-call | flops 6600000000 | tf_op jit(solution)/shard_map/attend_mine/pallas_call | solution.py:580
  86.0 2.0 %collective-permute-done.24.received_ref = bf16[432,384]{1,0:T(8,128)(2,1)S(1)} collective-permute-done((bf16[432,384]{1,0:T(8,128)(2,1)S(1)}, bf16[432,384]{1,0:T(8,128)(2,1)S(1)}, u32[]{:S(2)}, u32[]{:S(2)}) %collective-permute-start.24) | collective-permute-done | bytes 331808 | tf_op jit(solution)/shard_map/ppermute | solution.py:702
  88.0 1.6 %finish.1 = (bf16[4,104,384]{2,1,0:T(8,128)(2,1)S(1)}, bf16[1,104,384]{2,1,0:T(8,128)(2,1)S(1)}, bf16[1,104,384]{2,1,0:T(8,128)(2,1)S(1)}) custom-call(s32[67]{0:T(128)S(1)} %pad_add_fusion.info_ref, f32[416,384]{1,0:T(8,128)S(1)} %get-tuple-element.67.mean_ref, f32[416,128]{1,0:T(8,128)S(1)} %get-tuple-element.68.level_ref, ...), custom_call_target="tpu_custom_call" | custom-call | flops 1540000000 | tf_op jit(solution)/shard_map/finish/pallas_call | solution.py:580
  90.8 3.2 %collective-permute-start.26 = (bf16[1,104,384]{2,1,0:T(8,128)(2,1)S(1)}, bf16[1,104,384]{2,1,0:T(8,128)(2,1)S(1)}, u32[]{:S(2)}, u32[]{:S(2)}) collective-permute-start(bf16[1,104,384]{2,1,0:T(8,128)(2,1)S(1)} %get-tuple-element.71), channel_id=1, source_target_pairs={{2,4},{4,2},{6,8},{8,6},{10,12},{12,10},{14,16},{16,14},{18,20},{2... | collective-permute-start | bytes 239624 | tf_op jit(solution)/shard_map/ppermute | solution.py:734
  94.5 4.4 %collective-permute-done.26.outer_ref = bf16[1,104,384]{2,1,0:T(8,128)(2,1)S(1)} collective-permute-done((bf16[1,104,384]{2,1,0:T(8,128)(2,1)S(1)}, bf16[1,104,384]{2,1,0:T(8,128)(2,1)S(1)}, u32[]{:S(2)}, u32[]{:S(2)}) %collective-permute-start.26) | collective-permute-done | bytes 79904 | tf_op jit(solution)/shard_map/ppermute | solution.py:734
  98.9 2.3 %upsample.1 = bf16[8,208,192]{2,1,0:T(8,128)(2,1)S(1)} custom-call(s32[67]{0:T(128)S(1)} %pad_add_fusion.info_ref, bf16[1,104,384]{2,1,0:T(8,128)(2,1)S(1)} %collective-permute-done.25.inner_ref, bf16[4,104,384]{2,1,0:T(8,128)(2,1)S(1)} %get-tuple-element.70.own_ref, bf16[1,104,384]{2,1,0:T(8,128)(2,1)S(1)} %collective-permute-done.26.outer_ref, ...), custom_call_target="tpu_custom_call" | custom-call | flops 2529999872 | tf_op jit(solution)/shard_map/upsample/pallas_call | solution.py:580
  (93 shorter events, 25.9 us)
Async XLA Ops:
  3.6 8.5 %collective-permute-start.2 = (f32[3,8,128]{2,1,0:T(8,128)S(1)}, f32[3,8,128]{2,1,0:T(8,128)S(1)}, u32[]{:S(2)}, u32[]{:S(2)}) collective-permute-start(f32[3,8,128]{2,1,0:T(8,128)S(1)} %first_stats.1), channel_id=1, source_target_pairs={{0,2},{2,0},{4,6},{6,4},{8,10},{10,8},{12,14},{14,12},{16,18},{18,... | collective-permute-start | bytes 36872 | tf_op jit(solution)/shard_map/ppermute | solution.py:526
  5.2 7.0 %collective-permute-start.3 = (f32[3,8,128]{2,1,0:T(8,128)S(1)}, f32[3,8,128]{2,1,0:T(8,128)S(1)}, u32[]{:S(2)}, u32[]{:S(2)}) collective-permute-start(f32[3,8,128]{2,1,0:T(8,128)S(1)} %first_stats.1), channel_id=1, source_target_pairs={{0,4},{2,6},{4,0},{6,2},{8,12},{10,14},{12,8},{14,10},{16,20},{18,... | collective-permute-start | bytes 36872 | tf_op jit(solution)/shard_map/ppermute | solution.py:526
  6.7 5.5 %collective-permute-start.4 = (f32[3,8,128]{2,1,0:T(8,128)S(1)}, f32[3,8,128]{2,1,0:T(8,128)S(1)}, u32[]{:S(2)}, u32[]{:S(2)}) collective-permute-start(f32[3,8,128]{2,1,0:T(8,128)S(1)} %first_stats.1), channel_id=1, source_target_pairs={{0,6},{2,4},{4,2},{6,0},{8,14},{10,12},{12,10},{14,8},{16,22},{18,... | collective-permute-start | bytes 36872 | tf_op jit(solution)/shard_map/ppermute | solution.py:526
  12.2 9.4 %collective-permute-start.5 = (f32[3,8,128]{2,1,0:T(8,128)S(1)}, f32[3,8,128]{2,1,0:T(8,128)S(1)}, u32[]{:S(2)}, u32[]{:S(2)}) collective-permute-start(f32[3,8,128]{2,1,0:T(8,128)S(1)} %pad_maximum_fusion), channel_id=1, source_target_pairs={{0,8},{2,10},{4,12},{6,14},{8,0},{10,2},{12,4},{14,6},{16,24},{18,... | collective-permute-start | bytes 36872 | tf_op jit(solution)/shard_map/ppermute | solution.py:526
  12.3 9.3 %collective-permute-start.6 = (f32[3,8,128]{2,1,0:T(8,128)S(1)}, f32[3,8,128]{2,1,0:T(8,128)S(1)}, u32[]{:S(2)}, u32[]{:S(2)}) collective-permute-start(f32[3,8,128]{2,1,0:T(8,128)S(1)} %pad_maximum_fusion), channel_id=1, source_target_pairs={{0,16},{2,18},{4,20},{6,22},{8,24},{10,26},{12,28},{14,30},{16,0},... | collective-permute-start | bytes 36872 | tf_op jit(solution)/shard_map/ppermute | solution.py:526
  15.3 6.3 %collective-permute-start.7 = (f32[3,8,128]{2,1,0:T(8,128)S(1)}, f32[3,8,128]{2,1,0:T(8,128)S(1)}, u32[]{:S(2)}, u32[]{:S(2)}) collective-permute-start(f32[3,8,128]{2,1,0:T(8,128)S(1)} %pad_maximum_fusion), channel_id=1, source_target_pairs={{0,24},{2,26},{4,28},{6,30},{8,16},{10,18},{12,20},{14,22},{16,8},... | collective-permute-start | bytes 36872 | tf_op jit(solution)/shard_map/ppermute | solution.py:526
  15.8 5.9 %collective-permute-start = (bf16[1,104,384]{2,1,0:T(8,128)(2,1)S(1)}, bf16[1,104,384]{2,1,0:T(8,128)(2,1)S(1)}, u32[]{:S(2)}, u32[]{:S(2)}) collective-permute-start(bf16[1,104,384]{2,1,0:T(8,128)(2,1)S(1)} %get-tuple-element.86), channel_id=1, source_target_pairs={{0,2},{2,0},{4,6},{6,4},{8,10},{10,8},{12,14},{14,12},{16,18},{18,... | collective-permute-start | bytes 239624 | tf_op jit(solution)/shard_map/ppermute | solution.py:526
  17.4 8.1 %collective-permute-start.1 = (bf16[1,104,384]{2,1,0:T(8,128)(2,1)S(1)}, bf16[1,104,384]{2,1,0:T(8,128)(2,1)S(1)}, u32[]{:S(2)}, u32[]{:S(2)}) collective-permute-start(bf16[1,104,384]{2,1,0:T(8,128)(2,1)S(1)} %get-tuple-element.85), channel_id=1, source_target_pairs={{2,4},{4,2},{6,8},{8,6},{10,12},{12,10},{14,16},{16,14},{18,20},{2... | collective-permute-start | bytes 239624 | tf_op jit(solution)/shard_map/ppermute | solution.py:599
  34.7 6.5 %collective-permute-start.10 = (f32[3,8,128]{2,1,0:T(8,128)S(1)}, f32[3,8,128]{2,1,0:T(8,128)S(1)}, u32[]{:S(2)}, u32[]{:S(2)}) collective-permute-start(f32[3,8,128]{2,1,0:T(8,128)S(1)} %get-tuple-element.43), channel_id=1, source_target_pairs={{0,16},{2,18},{4,20},{6,22},{8,24},{10,26},{12,28},{14,30},{16,0},... | collective-permute-start | bytes 36872 | tf_op jit(solution)/shard_map/ppermute | solution.py:526
  38.2 7.1 %collective-permute-start.9 = (f32[3,8,128]{2,1,0:T(8,128)S(1)}, f32[3,8,128]{2,1,0:T(8,128)S(1)}, u32[]{:S(2)}, u32[]{:S(2)}) collective-permute-start(f32[3,8,128]{2,1,0:T(8,128)S(1)} %get-tuple-element.43), channel_id=1, source_target_pairs={{0,8},{2,10},{4,12},{6,14},{8,0},{10,2},{12,4},{14,6},{16,24},{18,... | collective-permute-start | bytes 36872 | tf_op jit(solution)/shard_map/ppermute | solution.py:526
  39.7 9.2 %collective-permute-start.12 = (bf16[2,208,384]{2,1,0:T(8,128)(2,1)S(1)}, bf16[2,208,384]{2,1,0:T(8,128)(2,1)S(1)}, u32[]{:S(2)}, u32[]{:S(2)}) collective-permute-start(bf16[2,208,384]{2,1,0:T(8,128)(2,1)S(1)} %get-tuple-element.44.own_ref.rest_5_), channel_id=1, source_target_pairs={{0,2},{2,0},{4,6},{6,4},{8,10},{10,8},{12,14},{14,12},{16,18},{18,... | collective-permute-start | bytes 958472 | tf_op jit(solution)/shard_map/ppermute | solution.py:526
  39.8 9.2 %collective-permute-start.13 = (bf16[2,208,384]{2,1,0:T(8,128)(2,1)S(1)}, bf16[2,208,384]{2,1,0:T(8,128)(2,1)S(1)}, u32[]{:S(2)}, u32[]{:S(2)}) collective-permute-start(bf16[2,208,384]{2,1,0:T(8,128)(2,1)S(1)} %get-tuple-element.44.own_ref.rest_5_), channel_id=1, source_target_pairs={{0,4},{2,6},{4,0},{6,2},{8,12},{10,14},{12,8},{14,10},{16,20},{18,... | collective-permute-start | bytes 958472 | tf_op jit(solution)/shard_map/ppermute | solution.py:526
  41.2 8.4 %collective-permute-start.14 = (bf16[2,208,384]{2,1,0:T(8,128)(2,1)S(1)}, bf16[2,208,384]{2,1,0:T(8,128)(2,1)S(1)}, u32[]{:S(2)}, u32[]{:S(2)}) collective-permute-start(bf16[2,208,384]{2,1,0:T(8,128)(2,1)S(1)} %get-tuple-element.44.own_ref.rest_5_), channel_id=1, source_target_pairs={{0,8},{2,10},{4,12},{6,14},{8,0},{10,2},{12,4},{14,6},{16,24},{18,... | collective-permute-start | bytes 958472 | tf_op jit(solution)/shard_map/ppermute | solution.py:526
  41.9 10.3 %collective-permute-start.15 = (bf16[2,208,384]{2,1,0:T(8,128)(2,1)S(1)}, bf16[2,208,384]{2,1,0:T(8,128)(2,1)S(1)}, u32[]{:S(2)}, u32[]{:S(2)}) collective-permute-start(bf16[2,208,384]{2,1,0:T(8,128)(2,1)S(1)} %get-tuple-element.44.own_ref.rest_5_), channel_id=1, source_target_pairs={{8,16},{10,18},{12,20},{14,22},{16,8},{18,10},{20,12},{22,14},{9,1... | collective-permute-start | bytes 958472 | tf_op jit(solution)/shard_map/ppermute | solution.py:526
  52.2 7.5 %collective-permute-start.16 = (f32[3,8,128]{2,1,0:T(8,128)S(1)}, f32[3,8,128]{2,1,0:T(8,128)S(1)}, u32[]{:S(2)}, u32[]{:S(2)}) collective-permute-start(f32[3,8,128]{2,1,0:T(8,128)S(1)} %pad_maximum_fusion.2), channel_id=1, source_target_pairs={{0,2},{2,0},{4,6},{6,4},{8,10},{10,8},{12,14},{14,12},{16,18},{18,... | collective-permute-start | bytes 36872 | tf_op jit(solution)/shard_map/ppermute | solution.py:526
  53.2 10.3 %collective-permute-start.17 = (f32[3,8,128]{2,1,0:T(8,128)S(1)}, f32[3,8,128]{2,1,0:T(8,128)S(1)}, u32[]{:S(2)}, u32[]{:S(2)}) collective-permute-start(f32[3,8,128]{2,1,0:T(8,128)S(1)} %pad_maximum_fusion.2), channel_id=1, source_target_pairs={{0,4},{2,6},{4,0},{6,2},{8,12},{10,14},{12,8},{14,10},{16,20},{18,... | collective-permute-start | bytes 36872 | tf_op jit(solution)/shard_map/ppermute | solution.py:526
  54.6 8.9 %collective-permute-start.18 = (f32[3,8,128]{2,1,0:T(8,128)S(1)}, f32[3,8,128]{2,1,0:T(8,128)S(1)}, u32[]{:S(2)}, u32[]{:S(2)}) collective-permute-start(f32[3,8,128]{2,1,0:T(8,128)S(1)} %pad_maximum_fusion.2), channel_id=1, source_target_pairs={{0,6},{2,4},{4,2},{6,0},{8,14},{10,12},{12,10},{14,8},{16,22},{18,... | collective-permute-start | bytes 36872 | tf_op jit(solution)/shard_map/ppermute | solution.py:526
  55.7 12.8 %collective-permute-start.21 = (bf16[2,208,384]{2,1,0:T(8,128)(2,1)S(1)}, bf16[2,208,384]{2,1,0:T(8,128)(2,1)S(1)}, u32[]{:S(2)}, u32[]{:S(2)}) collective-permute-start(bf16[2,208,384]{2,1,0:T(8,128)(2,1)S(1)} %collective-permute-done.15.rest_8_), channel_id=1, source_target_pairs={{8,0},{10,2},{12,4},{14,6},{16,24},{18,26},{20,28},{22,30},{9,1},{... | collective-permute-start | bytes 958472 | tf_op jit(solution)/shard_map/ppermute | solution.py:526
  57.0 18.7 %collective-permute-start.19 = (bf16[2,208,384]{2,1,0:T(8,128)(2,1)S(1)}, bf16[2,208,384]{2,1,0:T(8,128)(2,1)S(1)}, u32[]{:S(2)}, u32[]{:S(2)}) collective-permute-start(bf16[2,208,384]{2,1,0:T(8,128)(2,1)S(1)} %collective-permute-done.15.rest_8_), channel_id=1, source_target_pairs={{8,12},{10,14},{12,8},{14,10},{16,20},{18,22},{20,16},{22,18},{9,1... | collective-permute-start | bytes 958472 | tf_op jit(solution)/shard_map/ppermute | solution.py:526
  59.6 8.9 %collective-permute-start.20 = (bf16[2,208,384]{2,1,0:T(8,128)(2,1)S(1)}, bf16[2,208,384]{2,1,0:T(8,128)(2,1)S(1)}, u32[]{:S(2)}, u32[]{:S(2)}) collective-permute-start(bf16[2,208,384]{2,1,0:T(8,128)(2,1)S(1)} %collective-permute-done.14.rest_7_), channel_id=1, source_target_pairs={{8,16},{10,18},{12,20},{14,22},{16,8},{18,10},{20,12},{22,14},{9,1... | collective-permute-start | bytes 958472 | tf_op jit(solution)/shard_map/ppermute | solution.py:526
  68.6 8.4 %collective-permute-start.23 = (bf16[2,208,384]{2,1,0:T(8,128)(2,1)S(1)}, bf16[2,208,384]{2,1,0:T(8,128)(2,1)S(1)}, u32[]{:S(2)}, u32[]{:S(2)}) collective-permute-start(bf16[2,208,384]{2,1,0:T(8,128)(2,1)S(1)} %broadcast_select_fusion.rest_5_), channel_id=1, source_target_pairs={{0,4},{2,6},{4,0},{6,2},{8,12},{10,14},{12,8},{14,10},{16,20},{18,... | collective-permute-start | bytes 958472 | tf_op jit(solution)/shard_map/ppermute | solution.py:526
  70.0 7.0 %collective-permute-start.22 = (bf16[2,208,384]{2,1,0:T(8,128)(2,1)S(1)}, bf16[2,208,384]{2,1,0:T(8,128)(2,1)S(1)}, u32[]{:S(2)}, u32[]{:S(2)}) collective-permute-start(bf16[2,208,384]{2,1,0:T(8,128)(2,1)S(1)} %collective-permute-done.13.rest_6_), channel_id=1, source_target_pairs={{0,8},{2,10},{4,12},{6,14},{8,0},{10,2},{12,4},{14,6},{16,24},{18,... | collective-permute-start | bytes 958472 | tf_op jit(solution)/shard_map/ppermute | solution.py:526
  80.0 8.0 %collective-permute-start.24 = (bf16[432,384]{1,0:T(8,128)(2,1)S(1)}, bf16[432,384]{1,0:T(8,128)(2,1)S(1)}, u32[]{:S(2)}, u32[]{:S(2)}) collective-permute-start(bf16[432,384]{1,0:T(8,128)(2,1)S(1)} %get-tuple-element.60), channel_id=1, source_target_pairs={{0,2},{2,0},{4,6},{6,4},{8,10},{10,8},{12,14},{14,12},{16,18},{18,... | collective-permute-start | bytes 995336 | tf_op jit(solution)/shard_map/ppermute | solution.py:702
  90.8 8.1 %collective-permute-start.26 = (bf16[1,104,384]{2,1,0:T(8,128)(2,1)S(1)}, bf16[1,104,384]{2,1,0:T(8,128)(2,1)S(1)}, u32[]{:S(2)}, u32[]{:S(2)}) collective-permute-start(bf16[1,104,384]{2,1,0:T(8,128)(2,1)S(1)} %get-tuple-element.71), channel_id=1, source_target_pairs={{2,4},{4,2},{6,8},{8,6},{10,12},{12,10},{14,16},{16,14},{18,20},{2... | collective-permute-start | bytes 239624 | tf_op jit(solution)/shard_map/ppermute | solution.py:734
  (17 other events, 235.3 us)
where the time goes:
time: 103 us; the launch traced here: 102 us
  starting transfers between devices  42.4 us (41%)
  Pallas kernels  33.2 us (32%)
  waiting for transfers between devices  23.1 us (22%)
  local copies, waits for them, and re-layouts  2.33 us (2%)
    ppermute x23, starting transfers between devices, exchange(): return lax.ppermute(array, 'tile', moves)  32.6 us
    pallas_call x9, Pallas kernels, call(): pl.pallas_call(kernel, out_shape=out_shape, in_specs=[SMEM_SPEC] + [VMEM_...  22.6 us
    ppermute x23, waiting for transfers between devices, exchange(): return lax.ppermute(array, 'tile', moves)  11.5 us
    pallas_call x1, Pallas kernels, shards(): pl.pallas_call(functools.partial(conv_kernel, rows, taps), out_shape=(pai...  5.07 us
    pallas_call x1, Pallas kernels, shards(): pl.pallas_call(functools.partial(hold_kernel, taps), out_shape=shape(3 *...  4.97 us
    ppermute x1, waiting for transfers between devices, shards(): outer = lax.ppermute(outer, 'tile', outer_moves)  4.35 us
    ppermute x1, starting transfers between devices, shards(): lax.ppermute(jnp.where(odd, source[row_count - 1:], source[:1]), 'tile',...  4.17 us
    ppermute x1, waiting for transfers between devices, shards(): lax.ppermute(jnp.where(odd, source[row_count - 1:], source[:1]), 'tile',...  3.76 us
  transfers between devices with their start and end apart: 27, of which 10 were waited for; matrix products, arithmetic and copies ran while one was open for 0% of the time, Pallas kernels for 18%

commit v1 on v0

--- a/solution.py
+++ b/solution.py
@@ -17,7 +17,6 @@
 ROWS_OF_TILE = 4
 LANES = 128
 VMEM_BYTES = 24 * 1024 * 1024
-CONV_VMEM_BYTES = 50 * 1024 * 1024
 F32 = jnp.float32
 BF16 = jnp.bfloat16
 
@@ -180,26 +179,9 @@
     source_ref[...] = latents_ref[...]
 
 
-def hold_kernel(taps, weight_ref, held_ref, sems):
-    channels = weight_ref.shape[-1]
-    copies = [
-        pltpu.make_async_copy(
-            weight_ref.at[2 - depth // 3, depth % 3, side],
-            held_ref.at[pl.ds(depth * channels, channels), pl.ds(side * channels, channels)],
-            sems.at[side, depth],
-        )
-        for side in range(3)
-        for depth in range(3 * taps)
-    ]
-    for copy in copies:
-        copy.start()
-    for copy in copies:
-        copy.wait()
-
-
 def conv_kernel(rows, taps, info_ref, *rest):
     hidden_refs, rest = rest[:taps], rest[taps:]
-    latents_ref, bias_ref, held_ref, own_ref, stats_ref, inputs_ref = rest
+    latents_ref, bias_ref, weight_ref, own_ref, stats_ref, inputs_ref, held_ref = rest
     row_count, cols, channels = latents_ref.shape
     info = Info(info_ref, rows)
     padded = hidden_refs[0].shape[1]
@@ -213,6 +195,11 @@
                     same = labels[r + tap] == labels[r + 1]
                     block = jnp.where(same, block, jnp.zeros_like(block))
                 inputs_ref[r * padded : (r + 1) * padded, lanes] = block
+    for depth in range(3 * taps):
+        for side in range(3):
+            held_ref[
+                depth * channels : (depth + 1) * channels, side * channels : (side + 1) * channels
+            ] = weight_ref[2 - depth // 3, depth % 3, side]
     product = jnp.dot(inputs_ref[...], held_ref[...], preferred_element_type=F32)
     column = lax.broadcasted_iota(jnp.int32, (cols, 1), 0)
     cells = []
@@ -238,25 +225,17 @@
     return cells
 
 
-def query_kernel(
-    rows, info_ref, own_ref, other_ref, stats_ref, gain_ref, shift_ref, weight_ref, bias_ref,
-    *out_refs,
-):
-    info = Info(info_ref, rows)
-    pairs, double, channels = own_ref.shape
+def turned_queries(info, tile, pairs_ref, means, scales, shift_ref, weight_ref, bias_ref):
+    pairs, double, channels = pairs_ref.shape
     cols = double // 2
-    row_count = 2 * pairs
-    span = row_count * cols
-    means, scales = norm_tables(stats_ref, gain_ref)
     column = lax.broadcasted_iota(jnp.int32, (cols, 1), 0)
+    labels, widths = info.window(tile * 2 * pairs, 2 * pairs)
     cells = []
-    for tile, pairs_ref in ((info.tile(), own_ref), (info.tile() ^ 1, other_ref)):
-        labels, widths = info.window(tile * row_count, row_count)
-        for r, values in enumerate(split_rows(pairs_ref)):
-            mean = pick(means, labels[r], info.videos)
-            scale = pick(scales, labels[r], info.videos)
-            normed = (values - mean) * scale + shift_ref[...]
-            cells.append(jnp.where(column < widths[r], normed, 0.0))
+    for r, values in enumerate(split_rows(pairs_ref)):
+        mean = pick(means, labels[r], info.videos)
+        scale = pick(scales, labels[r], info.videos)
+        normed = (values - mean) * scale + shift_ref[...]
+        cells.append(jnp.where(column < widths[r], normed, 0.0))
     cells = jnp.concatenate(cells, axis=0).astype(BF16)
     queries = (
         jnp.dot(cells, weight_ref[:, 0:channels], preferred_element_type=F32)
@@ -267,14 +246,25 @@
         queries, weight_ref[:, channels : 2 * channels], (((1,), (1,)), ((), ())),
         preferred_element_type=F32,
     )
-    turned = (turned * factor).astype(BF16)
     constant = jnp.sum(
         queries.astype(F32) * bias_ref[:, channels : 2 * channels], axis=1, keepdims=True
     )
-    constant = jnp.broadcast_to(constant * factor, (2 * span, LANES))
-    for side in range(2):
-        out_refs[2 * side][...] = turned[side * span : (side + 1) * span]
-        out_refs[2 * side + 1][...] = constant[side * span : (side + 1) * span]
+    return (turned * factor).astype(BF16), constant * factor
+
+
+def query_kernel(
+    rows, info_ref, other_ref, stats_ref, gain_ref, shift_ref, weight_ref, bias_ref, queries_ref,
+    constant_ref, means_ref, scales_ref,
+):
+    info = Info(info_ref, rows)
+    means, scales = norm_tables(stats_ref, gain_ref)
+    means_ref[...] = means
+    scales_ref[...] = scales
+    queries, constant = turned_queries(
+        info, info.tile() ^ 1, other_ref, means, scales, shift_ref, weight_ref, bias_ref
+    )
+    queries_ref[...] = queries
+    constant_ref[...] = jnp.broadcast_to(constant, constant_ref.shape)
 
 
 def key_codes(info, masks, span, cols):
@@ -312,7 +302,7 @@
 
 
 def attend_yours_kernel(rows, masks, first, last, info_ref, *rest):
-    stats_ref, gain_ref, shift_ref, queries_ref, constant_ref, *rest = rest
+    means_ref, scales_ref, shift_ref, queries_ref, constant_ref, *rest = rest
     block_refs, rest = rest[: len(masks)], rest[len(masks) :]
     if not first:
         old_peak_ref, old_sum_ref, old_total_ref, *rest = rest
@@ -323,7 +313,7 @@
     cols = double // 2
     row_count = 2 * pairs
     tile = info.tile()
-    means, scales = norm_tables(stats_ref, gain_ref)
+    means, scales = means_ref[...], scales_ref[...]
     for index, (mask, block_ref) in enumerate(zip(masks, block_refs)):
         near, _ = info.window((tile ^ (2 * mask)) * row_count, row_count)
         for pair in range(pairs):
@@ -376,18 +366,23 @@
     sent_ref[span:, LANES:] = jnp.zeros((slots, channels - LANES), BF16)
 
 
-def attend_mine_kernel(rows, groups, info_ref, queries_ref, constant_ref, *rest):
+def attend_mine_kernel(
+    rows, groups, info_ref, own_ref, means_ref, scales_ref, shift_ref, weight_ref, bias_ref, *rest
+):
     key_refs, (mean_ref, level_ref) = rest[: len(groups)], rest[len(groups) :]
     info = Info(info_ref, rows)
-    span = queries_ref.shape[0]
+    span = mean_ref.shape[0]
+    queries, constant = turned_queries(
+        info, info.tile(), own_ref, means_ref[...], scales_ref[...], shift_ref, weight_ref,
+        bias_ref,
+    )
     cols = span // ROWS_OF_TILE
     query_code = query_codes(info, info.tile(), span, cols)
-    constant = constant_ref[:, 0:1]
     peak = jnp.full((span, 1), LOWEST, F32)
     scores = []
     for masks, key_ref in zip(groups, key_refs):
         codes = key_codes(info, masks, span, cols)
-        scores.append(scores_of(queries_ref[...], key_ref[...], codes, query_code))
+        scores.append(scores_of(queries, key_ref[...], codes, query_code))
         peak = jnp.maximum(peak, jnp.max(scores[-1], axis=1, keepdims=True) + constant)
     denominator, total = 0.0, 0.0
     for part, key_ref in zip(scores, key_refs):
@@ -600,21 +595,11 @@
         jnp.where(odd, source[row_count - 1 :], source[:1]), "tile", outer_moves
     )
     taps = min(3, frames)
-    held = pl.pallas_call(
-        functools.partial(hold_kernel, taps),
-        out_shape=shape(3 * taps * channels, 3 * channels),
-        in_specs=[HBM_SPEC],
-        out_specs=VMEM_SPEC,
-        scratch_shapes=[pltpu.SemaphoreType.DMA((3, 3 * taps))],
-        compiler_params=pltpu.CompilerParams(vmem_limit_bytes=CONV_VMEM_BYTES),
-        cost_estimate=cost(1.0 * taps),
-        name="hold",
-    )(conv_weight)
     rounds = merge_masks(tiles)
     for index, masks in enumerate(rounds):
         stats = merge_round(stats, tiles, masks)
         if index == 0:
-            stats, held = lax.optimization_barrier((stats, held))
+            stats, inner, outer = lax.optimization_barrier((stats, inner, outer))
     hidden, source = call(
         functools.partial(hidden_kernel, rows),
         [inner, source, outer, stats, row(first_gain), row(first_shift)],
@@ -637,11 +622,12 @@
         out_specs=(VMEM_SPEC, VMEM_SPEC),
         scratch_shapes=[
             pltpu.VMEM((row_count * padded, 3 * taps * channels), BF16),
+            pltpu.VMEM((3 * taps * channels, 3 * channels), BF16),
         ],
         compiler_params=params(),
         cost_estimate=cost(2.5 * taps),
         name="conv",
-    )(info, *context, source, row(conv_bias), held)
+    )(info, *context, source, row(conv_bias), conv_weight)
 
     blocks = {0: own}
     neighbour = [(i, i ^ 1) for i in range(tiles)]
@@ -650,14 +636,13 @@
             return t // 4 in (1, 2)
 
         stats = merge_round(stats, tiles, rounds[1])
-        other = exchange(own, tiles, 1)
-        blocks[1] = exchange(own, tiles, 2)
         blocks[2] = exchange(own, tiles, 4)
         blocks[6] = exchange(own, tiles, 12, middle)
-        stats, other, blocks[1], blocks[2], blocks[6] = lax.optimization_barrier(
-            (stats, other, blocks[1], blocks[2], blocks[6])
-        )
         stats = merge_round(stats, tiles, rounds[0])
+        own_xy, stats = lax.optimization_barrier((own, stats))
+        other = exchange(own_xy, tiles, 1)
+        blocks[1] = exchange(own_xy, tiles, 2)
+        other, blocks[1] = lax.optimization_barrier((other, blocks[1]))
         inward = exchange(blocks[2], tiles, 12, middle)
         outward = exchange(blocks[6], tiles, 4, middle)
         blocks[4] = jnp.where((tile // 4 == 1) | (tile // 4 == 2), inward, outward)
@@ -665,7 +650,7 @@
         blocks[5] = exchange(blocks[4], tiles, 2)
         passed, blocks[4] = lax.optimization_barrier((blocks[1], blocks[4]))
         blocks[3] = exchange(passed, tiles, 4)
-        groups = [[0, 1, 2, 6], [4], [7, 3, 5]]
+        groups = [[0, 1, 2, 6], [4, 7, 3, 5]]
     else:
         for masks in rounds:
             stats = merge_round(stats, tiles, masks)
@@ -674,15 +659,14 @@
             blocks[mask] = exchange(own, tiles, 2 * mask)
         groups = [list(range(i, i + 4)) for i in range(0, tiles // 2, 4)]
     gain, shift = row(second_gain), row(second_shift)
-    query_shapes = (shape(cells, channels), shape(cells, LANES, dtype=F32))
-    mine_queries, mine_constant, queries, constant = call(
+    table_shape = shape(SLOTS, channels, dtype=F32)
+    queries, constant, means, scales = call(
         functools.partial(query_kernel, rows),
-        [own, other, stats, gain, shift, triple_weight, row(triple_bias)],
-        query_shapes * 2,
-        cost_estimate=cost(1.9),
+        [other, stats, gain, shift, triple_weight, row(triple_bias)],
+        (shape(cells, channels), shape(cells, LANES, dtype=F32), table_shape, table_shape),
+        cost_estimate=cost(1.5),
         name="queries",
     )
-
     level_shape = shape(cells, LANES, dtype=F32)
     total_shape = shape(cells, channels, dtype=F32)
     state, keys = (), []
@@ -692,20 +676,18 @@
         outs += (shape(cells + 16, channels),) if last else (level_shape, level_shape, total_shape)
         normed, *state = call(
             functools.partial(attend_yours_kernel, rows, tuple(masks), index == 0, last),
-            [stats, gain, shift, queries, constant] + [blocks[m] for m in masks] + list(state),
+            [means, scales, shift, queries, constant] + [blocks[m] for m in masks] + list(state),
             outs,
-            cost_estimate=cost(1.0 * len(masks)),
+            cost_estimate=cost(0.9 * len(masks)),
             name="attend_yours",
         )
         keys.append(normed)
     (sent,) = state
     received = lax.ppermute(sent, "tile", neighbour)
-    sent, mine_queries, upsample_weight = lax.optimization_barrier(
-        (sent, mine_queries, upsample_weight)
-    )
+    sent, own_late, upsample_weight = lax.optimization_barrier((sent, own, upsample_weight))
     mean, level = call(
         functools.partial(attend_mine_kernel, rows, tuple(tuple(masks) for masks in groups)),
-        [mine_queries, mine_constant] + keys,
+        [own_late, means, scales, shift, triple_weight, row(triple_bias)] + keys,
         (total_shape, level_shape),
         cost_estimate=cost(6.0),
         name="attend_mine",

time: 103 us -> 99.3 us (0.964)
  Pallas kernels: 33.2 us -> 25.5 us
  local copies, waits for them, and re-layouts: 2.33 us -> 5.56 us
  waiting for transfers between devices: 23.1 us -> 25.7 us
  starting transfers between devices: 42.4 us -> 40.5 us
    pallas_call x1 -> x0, Pallas kernels: 4.97 us -> none  [shards(): pl.pallas_call(functools.partial(hold_kernel, taps), out_shape=shape(3 *...]
    unnamed x28, local copies, waits for them, and re-layouts: 1.06 us -> 4.28 us
    ppermute x23, waiting for transfers between devices: 11.5 us -> 14.4 us  [exchange(): return lax.ppermute(array, 'tile', moves)]
    pallas_call x9 -> x8, Pallas kernels: 22.6 us -> 19.8 us  [call(): pl.pallas_call(kernel, out_shape=out_shape, in_specs=[SMEM_SPEC] + [VMEM_...]
    ppermute x23, starting transfers between devices: 32.6 us -> 30.7 us  [exchange(): return lax.ppermute(array, 'tile', moves)]
    ppermute x1, waiting for transfers between devices: 4.35 us -> 3.02 us  [shards(): outer = lax.ppermute(outer, 'tile', outer_moves)]
    ppermute x1, starting transfers between devices: 3.2 us -> 4.52 us  [shards(): outer = lax.ppermute(outer, 'tile', outer_moves)]
    ppermute x1, waiting for transfers between devices: 3.76 us -> 4.85 us  [shards(): lax.ppermute(jnp.where(odd, source[row_count - 1:], source[:1]), 'tile',...]
  transfers between devices with their start and end apart: 27 -> 27, of which waited for: 10 -> 14; matrix products, arithmetic and copies ran while one was open for 0% -> 0% of each run, Pallas kernels for 18% -> 11%
where the time goes in v1:
time: 99.3 us; the launch traced here: 98.7 us
  starting transfers between devices  40.5 us (41%)
  waiting for transfers between devices  25.7 us (26%)
  Pallas kernels  25.5 us (26%)
  local copies, waits for them, and re-layouts  5.56 us (6%)
    ppermute x23, starting transfers between devices, exchange(): return lax.ppermute(array, 'tile', moves)  30.7 us
    pallas_call x8, Pallas kernels, call(): pl.pallas_call(kernel, out_shape=out_shape, in_specs=[SMEM_SPEC] + [VMEM_...  19.8 us
    ppermute x23, waiting for transfers between devices, exchange(): return lax.ppermute(array, 'tile', moves)  14.4 us
    pallas_call x1, Pallas kernels, shards(): pl.pallas_call(functools.partial(conv_kernel, rows, taps), out_shape=(pai...  5.22 us
    ppermute x1, waiting for transfers between devices, shards(): lax.ppermute(jnp.where(odd, source[row_count - 1:], source[:1]), 'tile',...  4.85 us
    ppermute x1, starting transfers between devices, shards(): outer = lax.ppermute(outer, 'tile', outer_moves)  4.52 us
    unnamed x28, local copies, waits for them, and re-layouts  4.28 us
    ppermute x1, starting transfers between devices, shards(): lax.ppermute(jnp.where(odd, source[row_count - 1:], source[:1]), 'tile',...  3.27 us
  transfers between devices with their start and end apart: 27, of which 14 were waited for; matrix products, arithmetic and copies ran while one was open for 0% of the time, Pallas kernels for 11%

profile of v1, /device:TPU:8, one launch (start us, length us, event | category | flops | bytes accessed | tf_op | source)
XLA Modules:
  0.0 98.7 jit_solution(18313404738466787284)
XLA Ops:
  1.7 1.8 %first_stats.1 = f32[3,8,128]{2,1,0:T(8,128)S(1)} custom-call(s32[67]{0:T(128)S(1)} %pad_add_fusion.info_ref, bf16[4,104,384]{2,1,0:T(8,128)(2,1)S(1)} %bitcast.11), custom_call_target="tpu_custom_call" | custom-call | flops 1650000000 | tf_op jit(solution)/shard_map/first_stats/pallas_call | solution.py:575
  3.5 2.5 %collective-permute-start.2 = (f32[3,8,128]{2,1,0:T(8,128)S(1)}, f32[3,8,128]{2,1,0:T(8,128)S(1)}, u32[]{:S(2)}, u32[]{:S(2)}) collective-permute-start(f32[3,8,128]{2,1,0:T(8,128)S(1)} %first_stats.1), channel_id=1, source_target_pairs={{0,6},{2,4},{4,2},{6,0},{8,14},{10,12},{12,10},{14,8},{16,22},{18,... | collective-permute-start | bytes 36872 | tf_op jit(solution)/shard_map/ppermute | solution.py:521
  8.7 3.3 %collective-permute-start.4 = (bf16[1,104,384]{2,1,0:T(8,128)(2,1)S(1)}, bf16[1,104,384]{2,1,0:T(8,128)(2,1)S(1)}, u32[]{:S(2)}, u32[]{:S(2)}) collective-permute-start(bf16[1,104,384]{2,1,0:T(8,128)(2,1)S(1)} %get-tuple-element.76), channel_id=1, source_target_pairs={{2,4},{4,2},{6,8},{8,6},{10,12},{12,10},{14,16},{16,14},{18,20},{2... | collective-permute-start | bytes 239624 | tf_op jit(solution)/shard_map/ppermute | solution.py:594
  12.1 4.9 %collective-permute-done.4.outer_ref = bf16[1,104,384]{2,1,0:T(8,128)(2,1)S(1)} collective-permute-done((bf16[1,104,384]{2,1,0:T(8,128)(2,1)S(1)}, bf16[1,104,384]{2,1,0:T(8,128)(2,1)S(1)}, u32[]{:S(2)}, u32[]{:S(2)}) %collective-permute-start.4) | collective-permute-done | bytes 79904 | tf_op jit(solution)/shard_map/ppermute | solution.py:594
  21.0 2.1 %collective-permute-done.6 = f32[3,8,128]{2,1,0:T(8,128)S(1)} collective-permute-done((f32[3,8,128]{2,1,0:T(8,128)S(1)}, f32[3,8,128]{2,1,0:T(8,128)S(1)}, u32[]{:S(2)}, u32[]{:S(2)}) %collective-permute-start.6) | collective-permute-done | bytes 12320 | tf_op jit(solution)/shard_map/ppermute | solution.py:521
  27.4 3.3 %copy-done.3 = bf16[3,3,3,384,384]{4,3,2,1,0:T(8,128)(2,1)S(1)} copy-done((bf16[3,3,3,384,384]{4,3,2,1,0:T(8,128)(2,1)S(1)}, bf16[3,3,3,384,384]{4,3,2,1,0:T(8,128)(2,1)}, u32[]{:S(2)}) %copy-start.3) | copy-done | bytes 7962648
  30.7 5.2 %conv.1 = (bf16[2,208,384]{2,1,0:T(8,128)(2,1)S(1)}, f32[3,8,128]{2,1,0:T(8,128)S(1)}) custom-call(s32[67]{0:T(128)S(1)} %pad_add_fusion.info_ref, bf16[6,112,384]{2,1,0:T(8,128)(2,1)S(1)} %get-tuple-element.38.rest_0_, bf16[6,112,384]{2,1,0:T(8,128)(2,1)S(1)} %collective-permute-done.8.rest_1_, bf16[4,104,384]{2,1,0:T(8,128)(2,1)S(1)} %get-tuple-element.39.rest_2_, ...), custom_call_target="tpu_custom_call" | custom-call | flops 5500000256 | tf_op jit(solution)/shard_map/conv/pallas_call | solution.py:618
  35.9 3.0 %collective-permute-start.11 = (f32[3,8,128]{2,1,0:T(8,128)S(1)}, f32[3,8,128]{2,1,0:T(8,128)S(1)}, u32[]{:S(2)}, u32[]{:S(2)}) collective-permute-start(f32[3,8,128]{2,1,0:T(8,128)S(1)} %get-tuple-element.41), channel_id=1, source_target_pairs={{0,24},{2,26},{4,28},{6,30},{8,16},{10,18},{12,20},{14,22},{16,8},... | collective-permute-start | bytes 36872 | tf_op jit(solution)/shard_map/ppermute | solution.py:521
  38.8 1.8 %collective-permute-start.10 = (f32[3,8,128]{2,1,0:T(8,128)S(1)}, f32[3,8,128]{2,1,0:T(8,128)S(1)}, u32[]{:S(2)}, u32[]{:S(2)}) collective-permute-start(f32[3,8,128]{2,1,0:T(8,128)S(1)} %get-tuple-element.41), channel_id=1, source_target_pairs={{0,16},{2,18},{4,20},{6,22},{8,24},{10,26},{12,28},{14,30},{16,0},... | collective-permute-start | bytes 36872 | tf_op jit(solution)/shard_map/ppermute | solution.py:521
  40.6 2.8 %collective-permute-done.10 = f32[3,8,128]{2,1,0:T(8,128)S(1)} collective-permute-done((f32[3,8,128]{2,1,0:T(8,128)S(1)}, f32[3,8,128]{2,1,0:T(8,128)S(1)}, u32[]{:S(2)}, u32[]{:S(2)}) %collective-permute-start.10) | collective-permute-done | bytes 12320 | tf_op jit(solution)/shard_map/ppermute | solution.py:521
  45.4 2.5 %collective-permute-start.12 = (f32[3,8,128]{2,1,0:T(8,128)S(1)}, f32[3,8,128]{2,1,0:T(8,128)S(1)}, u32[]{:S(2)}, u32[]{:S(2)}) collective-permute-start(f32[3,8,128]{2,1,0:T(8,128)S(1)} %pad_maximum_fusion.2), channel_id=1, source_target_pairs={{0,2},{2,0},{4,6},{6,4},{8,10},{10,8},{12,14},{14,12},{16,18},{18,... | collective-permute-start | bytes 36872 | tf_op jit(solution)/shard_map/ppermute | solution.py:521
  48.1 3.5 %collective-permute-start.19 = (bf16[2,208,384]{2,1,0:T(8,128)(2,1)S(1)}, bf16[2,208,384]{2,1,0:T(8,128)(2,1)S(1)}, u32[]{:S(2)}, u32[]{:S(2)}) collective-permute-start(bf16[2,208,384]{2,1,0:T(8,128)(2,1)S(1)} %get-tuple-element.56.rest_5_.own_ref), channel_id=1, source_target_pairs={{8,16},{10,18},{12,20},{14,22},{16,8},{18,10},{20,12},{22,14},{9,1... | collective-permute-start | bytes 958472 | tf_op jit(solution)/shard_map/ppermute | solution.py:521
  52.3 3.2 %collective-permute-done.17.rest_7_ = bf16[2,208,384]{2,1,0:T(8,128)(2,1)S(1)} collective-permute-done((bf16[2,208,384]{2,1,0:T(8,128)(2,1)S(1)}, bf16[2,208,384]{2,1,0:T(8,128)(2,1)S(1)}, u32[]{:S(2)}, u32[]{:S(2)}) %collective-permute-start.17) | collective-permute-done | bytes 319520 | tf_op jit(solution)/shard_map/ppermute | solution.py:521
  55.5 2.2 %collective-permute-start.18 = (bf16[2,208,384]{2,1,0:T(8,128)(2,1)S(1)}, bf16[2,208,384]{2,1,0:T(8,128)(2,1)S(1)}, u32[]{:S(2)}, u32[]{:S(2)}) collective-permute-start(bf16[2,208,384]{2,1,0:T(8,128)(2,1)S(1)} %collective-permute-done.17.rest_7_), channel_id=1, source_target_pairs={{8,16},{10,18},{12,20},{14,22},{16,8},{18,10},{20,12},{22,14},{9,1... | collective-permute-start | bytes 958472 | tf_op jit(solution)/shard_map/ppermute | solution.py:521
  59.2 2.6 %collective-permute-start.21 = (bf16[2,208,384]{2,1,0:T(8,128)(2,1)S(1)}, bf16[2,208,384]{2,1,0:T(8,128)(2,1)S(1)}, u32[]{:S(2)}, u32[]{:S(2)}) collective-permute-start(bf16[2,208,384]{2,1,0:T(8,128)(2,1)S(1)} %collective-permute-done.19.rest_8_), channel_id=1, source_target_pairs={{8,12},{10,14},{12,8},{14,10},{16,20},{18,22},{20,16},{22,18},{9,1... | collective-permute-start | bytes 958472 | tf_op jit(solution)/shard_map/ppermute | solution.py:521
  65.0 2.2 %collective-permute-start.22 = (bf16[2,208,384]{2,1,0:T(8,128)(2,1)S(1)}, bf16[2,208,384]{2,1,0:T(8,128)(2,1)S(1)}, u32[]{:S(2)}, u32[]{:S(2)}) collective-permute-start(bf16[2,208,384]{2,1,0:T(8,128)(2,1)S(1)} %collective-permute-done.16.rest_6_), channel_id=1, source_target_pairs={{0,8},{2,10},{4,12},{6,14},{8,0},{10,2},{12,4},{14,6},{16,24},{18,... | collective-permute-start | bytes 958472 | tf_op jit(solution)/shard_map/ppermute | solution.py:521
  67.2 3.0 %attend_yours.2 = (bf16[1664,384]{1,0:T(8,128)(2,1)S(1)}, f32[416,128]{1,0:T(8,128)S(1)}, f32[416,128]{1,0:T(8,128)S(1)}, f32[416,384]{1,0:T(8,128)S(1)}) custom-call(s32[67]{0:T(128)S(1)} %pad_add_fusion.info_ref, f32[8,384]{1,0:T(8,128)S(1)} %get-tuple-element.45.rest_0_.means_ref, f32[8,384]{1,0:T(8,128)S(1)} %get-tuple-element.46.rest_1_.scales_ref, ...), custom_call_target="tpu_custom_call" | custom-call | flops 3960000000 | tf_op jit(solution)/shard_map/attend_yours/pallas_call | solution.py:575
  72.2 2.1 %collective-permute-done.23.rest_8_ = bf16[2,208,384]{2,1,0:T(8,128)(2,1)S(1)} collective-permute-done((bf16[2,208,384]{2,1,0:T(8,128)(2,1)S(1)}, bf16[2,208,384]{2,1,0:T(8,128)(2,1)S(1)}, u32[]{:S(2)}, u32[]{:S(2)}) %collective-permute-start.23) | collective-permute-done | bytes 319520 | tf_op jit(solution)/shard_map/ppermute | solution.py:521
  74.3 3.0 %attend_yours.3 = (bf16[1664,384]{1,0:T(8,128)(2,1)S(1)}, bf16[432,384]{1,0:T(8,128)(2,1)S(1)}) custom-call(s32[67]{0:T(128)S(1)} %pad_add_fusion.info_ref, f32[8,384]{1,0:T(8,128)S(1)} %get-tuple-element.45.rest_0_.means_ref, f32[8,384]{1,0:T(8,128)S(1)} %get-tuple-element.46.rest_1_.scales_ref, f32[1,384]{1,0:T(1,128)S(1)} %reshape.87.shift_ref.rest_2_, ...), custom_call_target="tpu_custom_call" | custom-call | flops 3960000000 | tf_op jit(solution)/shard_map/attend_yours/pallas_call | solution.py:575
  77.9 5.4 %attend_mine.1 = (f32[416,384]{1,0:T(8,128)S(1)}, f32[416,128]{1,0:T(8,128)S(1)}) custom-call(s32[67]{0:T(128)S(1)} %pad_add_fusion.info_ref, bf16[2,208,384]{2,1,0:T(8,128)(2,1)S(1)} %get-tuple-element.56.rest_5_.own_ref, f32[8,384]{1,0:T(8,128)S(1)} %get-tuple-element.45.rest_0_.means_ref, f32[8,384]{1,0:T(8,128)S(1)} %get-tuple-element.46.rest_1_.scales_ref, ...), custom_call_target="tpu_custom_call" | custom-call | flops 6600000000 | tf_op jit(solution)/shard_map/attend_mine/pallas_call | solution.py:575
  83.3 2.0 %collective-permute-done.24.received_ref = bf16[432,384]{1,0:T(8,128)(2,1)S(1)} collective-permute-done((bf16[432,384]{1,0:T(8,128)(2,1)S(1)}, bf16[432,384]{1,0:T(8,128)(2,1)S(1)}, u32[]{:S(2)}, u32[]{:S(2)}) %collective-permute-start.24) | collective-permute-done | bytes 331808 | tf_op jit(solution)/shard_map/ppermute | solution.py:686
  87.0 4.5 %collective-permute-start.26 = (bf16[1,104,384]{2,1,0:T(8,128)(2,1)S(1)}, bf16[1,104,384]{2,1,0:T(8,128)(2,1)S(1)}, u32[]{:S(2)}, u32[]{:S(2)}) collective-permute-start(bf16[1,104,384]{2,1,0:T(8,128)(2,1)S(1)} %get-tuple-element.63), channel_id=1, source_target_pairs={{2,4},{4,2},{6,8},{8,6},{10,12},{12,10},{14,16},{16,14},{18,20},{2... | collective-permute-start | bytes 239624 | tf_op jit(solution)/shard_map/ppermute | solution.py:716
  92.0 3.0 %collective-permute-done.26.outer_ref = bf16[1,104,384]{2,1,0:T(8,128)(2,1)S(1)} collective-permute-done((bf16[1,104,384]{2,1,0:T(8,128)(2,1)S(1)}, bf16[1,104,384]{2,1,0:T(8,128)(2,1)S(1)}, u32[]{:S(2)}, u32[]{:S(2)}) %collective-permute-start.26) | collective-permute-done | bytes 79904 | tf_op jit(solution)/shard_map/ppermute | solution.py:716
  95.1 2.3 %upsample.1 = bf16[8,208,192]{2,1,0:T(8,128)(2,1)S(1)} custom-call(s32[67]{0:T(128)S(1)} %pad_add_fusion.info_ref, bf16[1,104,384]{2,1,0:T(8,128)(2,1)S(1)} %collective-permute-done.25.inner_ref, bf16[4,104,384]{2,1,0:T(8,128)(2,1)S(1)} %get-tuple-element.62.own_ref, bf16[1,104,384]{2,1,0:T(8,128)(2,1)S(1)} %collective-permute-done.26.outer_ref, ...), custom_call_target="tpu_custom_call" | custom-call | flops 2529999872 | tf_op jit(solution)/shard_map/upsample/pallas_call | solution.py:575
  (91 shorter events, 26.2 us)
Async XLA Ops:
  3.5 8.4 %collective-permute-start.2 = (f32[3,8,128]{2,1,0:T(8,128)S(1)}, f32[3,8,128]{2,1,0:T(8,128)S(1)}, u32[]{:S(2)}, u32[]{:S(2)}) collective-permute-start(f32[3,8,128]{2,1,0:T(8,128)S(1)} %first_stats.1), channel_id=1, source_target_pairs={{0,6},{2,4},{4,2},{6,0},{8,14},{10,12},{12,10},{14,8},{16,22},{18,... | collective-permute-start | bytes 36872 | tf_op jit(solution)/shard_map/ppermute | solution.py:521
  6.1 5.9 %collective-permute-start.1 = (f32[3,8,128]{2,1,0:T(8,128)S(1)}, f32[3,8,128]{2,1,0:T(8,128)S(1)}, u32[]{:S(2)}, u32[]{:S(2)}) collective-permute-start(f32[3,8,128]{2,1,0:T(8,128)S(1)} %first_stats.1), channel_id=1, source_target_pairs={{0,4},{2,6},{4,0},{6,2},{8,12},{10,14},{12,8},{14,10},{16,20},{18,... | collective-permute-start | bytes 36872 | tf_op jit(solution)/shard_map/ppermute | solution.py:521
  6.6 5.4 %collective-permute-start = (f32[3,8,128]{2,1,0:T(8,128)S(1)}, f32[3,8,128]{2,1,0:T(8,128)S(1)}, u32[]{:S(2)}, u32[]{:S(2)}) collective-permute-start(f32[3,8,128]{2,1,0:T(8,128)S(1)} %first_stats.1), channel_id=1, source_target_pairs={{0,2},{2,0},{4,6},{6,4},{8,10},{10,8},{12,14},{14,12},{16,18},{18,... | collective-permute-start | bytes 36872 | tf_op jit(solution)/shard_map/ppermute | solution.py:521
  7.1 4.9 %collective-permute-start.3 = (bf16[1,104,384]{2,1,0:T(8,128)(2,1)S(1)}, bf16[1,104,384]{2,1,0:T(8,128)(2,1)S(1)}, u32[]{:S(2)}, u32[]{:S(2)}) collective-permute-start(bf16[1,104,384]{2,1,0:T(8,128)(2,1)S(1)} %get-tuple-element.77), channel_id=1, source_target_pairs={{0,2},{2,0},{4,6},{6,4},{8,10},{10,8},{12,14},{14,12},{16,18},{18,... | collective-permute-start | bytes 239624 | tf_op jit(solution)/shard_map/ppermute | solution.py:521
  8.7 8.2 %collective-permute-start.4 = (bf16[1,104,384]{2,1,0:T(8,128)(2,1)S(1)}, bf16[1,104,384]{2,1,0:T(8,128)(2,1)S(1)}, u32[]{:S(2)}, u32[]{:S(2)}) collective-permute-start(bf16[1,104,384]{2,1,0:T(8,128)(2,1)S(1)} %get-tuple-element.76), channel_id=1, source_target_pairs={{2,4},{4,2},{6,8},{8,6},{10,12},{12,10},{14,16},{16,14},{18,20},{2... | collective-permute-start | bytes 239624 | tf_op jit(solution)/shard_map/ppermute | solution.py:594
  16.9 4.1 %collective-permute-start.7 = (f32[3,8,128]{2,1,0:T(8,128)S(1)}, f32[3,8,128]{2,1,0:T(8,128)S(1)}, u32[]{:S(2)}, u32[]{:S(2)}) collective-permute-start(f32[3,8,128]{2,1,0:T(8,128)S(1)} %pad_maximum_fusion), channel_id=1, source_target_pairs={{0,24},{2,26},{4,28},{6,30},{8,16},{10,18},{12,20},{14,22},{16,8},... | collective-permute-start | bytes 36872 | tf_op jit(solution)/shard_map/ppermute | solution.py:521
  18.5 4.6 %collective-permute-start.6 = (f32[3,8,128]{2,1,0:T(8,128)S(1)}, f32[3,8,128]{2,1,0:T(8,128)S(1)}, u32[]{:S(2)}, u32[]{:S(2)}) collective-permute-start(f32[3,8,128]{2,1,0:T(8,128)S(1)} %pad_maximum_fusion), channel_id=1, source_target_pairs={{0,16},{2,18},{4,20},{6,22},{8,24},{10,26},{12,28},{14,30},{16,0},... | collective-permute-start | bytes 36872 | tf_op jit(solution)/shard_map/ppermute | solution.py:521
  35.9 4.8 %collective-permute-start.11 = (f32[3,8,128]{2,1,0:T(8,128)S(1)}, f32[3,8,128]{2,1,0:T(8,128)S(1)}, u32[]{:S(2)}, u32[]{:S(2)}) collective-permute-start(f32[3,8,128]{2,1,0:T(8,128)S(1)} %get-tuple-element.41), channel_id=1, source_target_pairs={{0,24},{2,26},{4,28},{6,30},{8,16},{10,18},{12,20},{14,22},{16,8},... | collective-permute-start | bytes 36872 | tf_op jit(solution)/shard_map/ppermute | solution.py:521
  38.8 4.6 %collective-permute-start.10 = (f32[3,8,128]{2,1,0:T(8,128)S(1)}, f32[3,8,128]{2,1,0:T(8,128)S(1)}, u32[]{:S(2)}, u32[]{:S(2)}) collective-permute-start(f32[3,8,128]{2,1,0:T(8,128)S(1)} %get-tuple-element.41), channel_id=1, source_target_pairs={{0,16},{2,18},{4,20},{6,22},{8,24},{10,26},{12,28},{14,30},{16,0},... | collective-permute-start | bytes 36872 | tf_op jit(solution)/shard_map/ppermute | solution.py:521
  44.4 7.1 %collective-permute-start.14 = (f32[3,8,128]{2,1,0:T(8,128)S(1)}, f32[3,8,128]{2,1,0:T(8,128)S(1)}, u32[]{:S(2)}, u32[]{:S(2)}) collective-permute-start(f32[3,8,128]{2,1,0:T(8,128)S(1)} %pad_maximum_fusion.2), channel_id=1, source_target_pairs={{0,6},{2,4},{4,2},{6,0},{8,14},{10,12},{12,10},{14,8},{16,22},{18,... | collective-permute-start | bytes 36872 | tf_op jit(solution)/shard_map/ppermute | solution.py:521
  44.5 7.1 %collective-permute-start.13 = (f32[3,8,128]{2,1,0:T(8,128)S(1)}, f32[3,8,128]{2,1,0:T(8,128)S(1)}, u32[]{:S(2)}, u32[]{:S(2)}) collective-permute-start(f32[3,8,128]{2,1,0:T(8,128)S(1)} %pad_maximum_fusion.2), channel_id=1, source_target_pairs={{0,4},{2,6},{4,0},{6,2},{8,12},{10,14},{12,8},{14,10},{16,20},{18,... | collective-permute-start | bytes 36872 | tf_op jit(solution)/shard_map/ppermute | solution.py:521
  45.4 6.1 %collective-permute-start.12 = (f32[3,8,128]{2,1,0:T(8,128)S(1)}, f32[3,8,128]{2,1,0:T(8,128)S(1)}, u32[]{:S(2)}, u32[]{:S(2)}) collective-permute-start(f32[3,8,128]{2,1,0:T(8,128)S(1)} %pad_maximum_fusion.2), channel_id=1, source_target_pairs={{0,2},{2,0},{4,6},{6,4},{8,10},{10,8},{12,14},{14,12},{16,18},{18,... | collective-permute-start | bytes 36872 | tf_op jit(solution)/shard_map/ppermute | solution.py:521
  47.9 7.5 %collective-permute-start.17 = (bf16[2,208,384]{2,1,0:T(8,128)(2,1)S(1)}, bf16[2,208,384]{2,1,0:T(8,128)(2,1)S(1)}, u32[]{:S(2)}, u32[]{:S(2)}) collective-permute-start(bf16[2,208,384]{2,1,0:T(8,128)(2,1)S(1)} %get-tuple-element.56.rest_5_.own_ref), channel_id=1, source_target_pairs={{0,8},{2,10},{4,12},{6,14},{8,0},{10,2},{12,4},{14,6},{16,24},{18,... | collective-permute-start | bytes 958472 | tf_op jit(solution)/shard_map/ppermute | solution.py:521
  48.1 9.7 %collective-permute-start.19 = (bf16[2,208,384]{2,1,0:T(8,128)(2,1)S(1)}, bf16[2,208,384]{2,1,0:T(8,128)(2,1)S(1)}, u32[]{:S(2)}, u32[]{:S(2)}) collective-permute-start(bf16[2,208,384]{2,1,0:T(8,128)(2,1)S(1)} %get-tuple-element.56.rest_5_.own_ref), channel_id=1, source_target_pairs={{8,16},{10,18},{12,20},{14,22},{16,8},{18,10},{20,12},{22,14},{9,1... | collective-permute-start | bytes 958472 | tf_op jit(solution)/shard_map/ppermute | solution.py:521
  51.6 10.2 %collective-permute-start.15 = (bf16[2,208,384]{2,1,0:T(8,128)(2,1)S(1)}, bf16[2,208,384]{2,1,0:T(8,128)(2,1)S(1)}, u32[]{:S(2)}, u32[]{:S(2)}) collective-permute-start(bf16[2,208,384]{2,1,0:T(8,128)(2,1)S(1)} %get-tuple-element.56.rest_5_.own_ref), channel_id=1, source_target_pairs={{0,2},{2,0},{4,6},{6,4},{8,10},{10,8},{12,14},{14,12},{16,18},{18,... | collective-permute-start | bytes 958472 | tf_op jit(solution)/shard_map/ppermute | solution.py:521
  51.7 10.0 %collective-permute-start.16 = (bf16[2,208,384]{2,1,0:T(8,128)(2,1)S(1)}, bf16[2,208,384]{2,1,0:T(8,128)(2,1)S(1)}, u32[]{:S(2)}, u32[]{:S(2)}) collective-permute-start(bf16[2,208,384]{2,1,0:T(8,128)(2,1)S(1)} %get-tuple-element.56.rest_5_.own_ref), channel_id=1, source_target_pairs={{0,4},{2,6},{4,0},{6,2},{8,12},{10,14},{12,8},{14,10},{16,20},{18,... | collective-permute-start | bytes 958472 | tf_op jit(solution)/shard_map/ppermute | solution.py:521
  55.5 8.9 %collective-permute-start.18 = (bf16[2,208,384]{2,1,0:T(8,128)(2,1)S(1)}, bf16[2,208,384]{2,1,0:T(8,128)(2,1)S(1)}, u32[]{:S(2)}, u32[]{:S(2)}) collective-permute-start(bf16[2,208,384]{2,1,0:T(8,128)(2,1)S(1)} %collective-permute-done.17.rest_7_), channel_id=1, source_target_pairs={{8,16},{10,18},{12,20},{14,22},{16,8},{18,10},{20,12},{22,14},{9,1... | collective-permute-start | bytes 958472 | tf_op jit(solution)/shard_map/ppermute | solution.py:521
  57.8 6.8 %collective-permute-start.20 = (bf16[2,208,384]{2,1,0:T(8,128)(2,1)S(1)}, bf16[2,208,384]{2,1,0:T(8,128)(2,1)S(1)}, u32[]{:S(2)}, u32[]{:S(2)}) collective-permute-start(bf16[2,208,384]{2,1,0:T(8,128)(2,1)S(1)} %collective-permute-done.19.rest_8_), channel_id=1, source_target_pairs={{8,0},{10,2},{12,4},{14,6},{16,24},{18,26},{20,28},{22,30},{9,1},{... | collective-permute-start | bytes 958472 | tf_op jit(solution)/shard_map/ppermute | solution.py:521
  59.2 11.7 %collective-permute-start.21 = (bf16[2,208,384]{2,1,0:T(8,128)(2,1)S(1)}, bf16[2,208,384]{2,1,0:T(8,128)(2,1)S(1)}, u32[]{:S(2)}, u32[]{:S(2)}) collective-permute-start(bf16[2,208,384]{2,1,0:T(8,128)(2,1)S(1)} %collective-permute-done.19.rest_8_), channel_id=1, source_target_pairs={{8,12},{10,14},{12,8},{14,10},{16,20},{18,22},{20,16},{22,18},{9,1... | collective-permute-start | bytes 958472 | tf_op jit(solution)/shard_map/ppermute | solution.py:521
  64.6 9.7 %collective-permute-start.23 = (bf16[2,208,384]{2,1,0:T(8,128)(2,1)S(1)}, bf16[2,208,384]{2,1,0:T(8,128)(2,1)S(1)}, u32[]{:S(2)}, u32[]{:S(2)}) collective-permute-start(bf16[2,208,384]{2,1,0:T(8,128)(2,1)S(1)} %broadcast_select_fusion.rest_5_), channel_id=1, source_target_pairs={{0,4},{2,6},{4,0},{6,2},{8,12},{10,14},{12,8},{14,10},{16,20},{18,... | collective-permute-start | bytes 958472 | tf_op jit(solution)/shard_map/ppermute | solution.py:521
  65.0 7.1 %collective-permute-start.22 = (bf16[2,208,384]{2,1,0:T(8,128)(2,1)S(1)}, bf16[2,208,384]{2,1,0:T(8,128)(2,1)S(1)}, u32[]{:S(2)}, u32[]{:S(2)}) collective-permute-start(bf16[2,208,384]{2,1,0:T(8,128)(2,1)S(1)} %collective-permute-done.16.rest_6_), channel_id=1, source_target_pairs={{0,8},{2,10},{4,12},{6,14},{8,0},{10,2},{12,4},{14,6},{16,24},{18,... | collective-permute-start | bytes 958472 | tf_op jit(solution)/shard_map/ppermute | solution.py:521
  77.3 8.0 %collective-permute-start.24 = (bf16[432,384]{1,0:T(8,128)(2,1)S(1)}, bf16[432,384]{1,0:T(8,128)(2,1)S(1)}, u32[]{:S(2)}, u32[]{:S(2)}) collective-permute-start(bf16[432,384]{1,0:T(8,128)(2,1)S(1)} %get-tuple-element.55), channel_id=1, source_target_pairs={{0,2},{2,0},{4,6},{6,4},{8,10},{10,8},{12,14},{14,12},{16,18},{18,... | collective-permute-start | bytes 995336 | tf_op jit(solution)/shard_map/ppermute | solution.py:686
  86.7 5.3 %collective-permute-start.25 = (bf16[1,104,384]{2,1,0:T(8,128)(2,1)S(1)}, bf16[1,104,384]{2,1,0:T(8,128)(2,1)S(1)}, u32[]{:S(2)}, u32[]{:S(2)}) collective-permute-start(bf16[1,104,384]{2,1,0:T(8,128)(2,1)S(1)} %get-tuple-element.61), channel_id=1, source_target_pairs={{0,2},{2,0},{4,6},{6,4},{8,10},{10,8},{12,14},{14,12},{16,18},{18,... | collective-permute-start | bytes 239624 | tf_op jit(solution)/shard_map/ppermute | solution.py:521
  87.0 8.1 %collective-permute-start.26 = (bf16[1,104,384]{2,1,0:T(8,128)(2,1)S(1)}, bf16[1,104,384]{2,1,0:T(8,128)(2,1)S(1)}, u32[]{:S(2)}, u32[]{:S(2)}) collective-permute-start(bf16[1,104,384]{2,1,0:T(8,128)(2,1)S(1)} %get-tuple-element.63), channel_id=1, source_target_pairs={{2,4},{4,2},{6,8},{8,6},{10,12},{12,10},{14,16},{16,14},{18,20},{2... | collective-permute-start | bytes 239624 | tf_op jit(solution)/shard_map/ppermute | solution.py:716
  (17 other events, 223.3 us)

commit v2 on v1

--- a/solution.py
+++ b/solution.py
@@ -17,6 +17,7 @@
 ROWS_OF_TILE = 4
 LANES = 128
 VMEM_BYTES = 24 * 1024 * 1024
+HIDDEN_VMEM_BYTES = 46 * 1024 * 1024
 F32 = jnp.float32
 BF16 = jnp.bfloat16
 
@@ -158,9 +159,21 @@
 
 
 def hidden_kernel(
-    rows, info_ref, inner_ref, latents_ref, outer_ref, stats_ref, gain_ref, shift_ref, out_ref,
-    source_ref,
+    rows, info_ref, inner_ref, latents_ref, outer_ref, stats_ref, gain_ref, shift_ref, weight_ref,
+    out_ref, source_ref, held_ref, sems,
 ):
+    channels = weight_ref.shape[-1]
+    copies = [
+        pltpu.make_async_copy(
+            weight_ref.at[2 - depth // 3, depth % 3, side],
+            held_ref.at[pl.ds(depth * channels, channels), pl.ds(side * channels, channels)],
+            sems.at[side, depth],
+        )
+        for side in range(3)
+        for depth in range(held_ref.shape[0] // channels)
+    ]
+    for copy in copies:
+        copy.start()
     info = Info(info_ref, rows)
     row_count, cols, _ = latents_ref.shape
     labels, widths = info.window(info.tile() * row_count - 1, row_count + 2)
@@ -177,11 +190,13 @@
         rest = jnp.zeros((out_ref.shape[1] - cols, active.shape[1]), F32)
         out_ref[r] = jnp.concatenate([active, rest], axis=0).astype(BF16)
     source_ref[...] = latents_ref[...]
+    for copy in copies:
+        copy.wait()
 
 
 def conv_kernel(rows, taps, info_ref, *rest):
     hidden_refs, rest = rest[:taps], rest[taps:]
-    latents_ref, bias_ref, weight_ref, own_ref, stats_ref, inputs_ref, held_ref = rest
+    latents_ref, bias_ref, held_ref, own_ref, stats_ref, inputs_ref = rest
     row_count, cols, channels = latents_ref.shape
     info = Info(info_ref, rows)
     padded = hidden_refs[0].shape[1]
@@ -195,11 +210,6 @@
                     same = labels[r + tap] == labels[r + 1]
                     block = jnp.where(same, block, jnp.zeros_like(block))
                 inputs_ref[r * padded : (r + 1) * padded, lanes] = block
-    for depth in range(3 * taps):
-        for side in range(3):
-            held_ref[
-                depth * channels : (depth + 1) * channels, side * channels : (side + 1) * channels
-            ] = weight_ref[2 - depth // 3, depth % 3, side]
     product = jnp.dot(inputs_ref[...], held_ref[...], preferred_element_type=F32)
     column = lax.broadcasted_iota(jnp.int32, (cols, 1), 0)
     cells = []
@@ -596,17 +606,24 @@
     )
     taps = min(3, frames)
     rounds = merge_masks(tiles)
-    for index, masks in enumerate(rounds):
+    for index, masks in enumerate(reversed(rounds)):
         stats = merge_round(stats, tiles, masks)
         if index == 0:
             stats, inner, outer = lax.optimization_barrier((stats, inner, outer))
-    hidden, source = call(
+    hidden, source, held = pl.pallas_call(
         functools.partial(hidden_kernel, rows),
-        [inner, source, outer, stats, row(first_gain), row(first_shift)],
-        (shape(near_rows, padded, channels), shape(row_count, cols, channels)),
-        cost_estimate=cost(1.3),
+        out_shape=(
+            shape(near_rows, padded, channels),
+            shape(row_count, cols, channels),
+            shape(3 * taps * channels, 3 * channels),
+        ),
+        in_specs=[SMEM_SPEC] + [VMEM_SPEC] * 6 + [HBM_SPEC],
+        out_specs=(VMEM_SPEC,) * 3,
+        scratch_shapes=[pltpu.SemaphoreType.DMA((3, 3 * taps))],
+        compiler_params=pltpu.CompilerParams(vmem_limit_bytes=HIDDEN_VMEM_BYTES),
+        cost_estimate=cost(2.0),
         name="hidden",
-    )
+    )(info, inner, source, outer, stats, row(first_gain), row(first_shift), conv_weight)
 
     context = [hidden] + [
         lax.ppermute(hidden, "frame", [(i, i + by) for i in range(frames - by)])
@@ -622,12 +639,11 @@
         out_specs=(VMEM_SPEC, VMEM_SPEC),
         scratch_shapes=[
             pltpu.VMEM((row_count * padded, 3 * taps * channels), BF16),
-            pltpu.VMEM((3 * taps * channels, 3 * channels), BF16),
         ],
         compiler_params=params(),
         cost_estimate=cost(2.5 * taps),
         name="conv",
-    )(info, *context, source, row(conv_bias), conv_weight)
+    )(info, *context, source, row(conv_bias), held)
 
     blocks = {0: own}
     neighbour = [(i, i ^ 1) for i in range(tiles)]

time: 99.3 us -> 99.8 us (level)
  starting transfers between devices: 40.5 us -> 45.6 us
  local copies, waits for them, and re-layouts: 5.56 us -> 2.29 us
  waiting for transfers between devices: 25.7 us -> 22.6 us
  Pallas kernels: 25.5 us -> 27.6 us
    ppermute x23, starting transfers between devices: 30.7 us -> 35 us  [exchange(): return lax.ppermute(array, 'tile', moves)]
    pallas_call x0 -> x1, Pallas kernels: none -> 3.55 us  [shards(): pl.pallas_call(functools.partial(hidden_kernel, rows), out_shape=(shape(n...]
    unnamed x28 -> x26, local copies, waits for them, and re-layouts: 4.28 us -> 1.02 us
    ppermute x23, waiting for transfers between devices: 14.4 us -> 12.2 us  [exchange(): return lax.ppermute(array, 'tile', moves)]
    pallas_call x8 -> x7, Pallas kernels: 19.8 us -> 18.5 us  [call(): pl.pallas_call(kernel, out_shape=out_shape, in_specs=[SMEM_SPEC] + [VMEM_...]
    ppermute x1, waiting for transfers between devices: 4.85 us -> 3.82 us  [shards(): lax.ppermute(jnp.where(odd, source[row_count - 1:], source[:1]), 'tile',...]
  transfers between devices with their start and end apart: 27 -> 27, of which waited for: 14 -> 15; matrix products, arithmetic and copies ran while one was open for 0% -> 0% of each run, Pallas kernels for 11% -> 10%
where the time goes in v2:
time: 99.8 us; the launch traced here: 99.5 us
  starting transfers between devices  45.6 us (46%)
  Pallas kernels  27.6 us (28%)
  waiting for transfers between devices  22.6 us (23%)
  local copies, waits for them, and re-layouts  2.29 us (2%)
    ppermute x23, starting transfers between devices, exchange(): return lax.ppermute(array, 'tile', moves)  35 us
    pallas_call x7, Pallas kernels, call(): pl.pallas_call(kernel, out_shape=out_shape, in_specs=[SMEM_SPEC] + [VMEM_...  18.5 us
    ppermute x23, waiting for transfers between devices, exchange(): return lax.ppermute(array, 'tile', moves)  12.2 us
    pallas_call x1, Pallas kernels, shards(): pl.pallas_call(functools.partial(conv_kernel, rows, taps), out_shape=(pai...  5.06 us
    ppermute x1, starting transfers between devices, shards(): lax.ppermute(jnp.where(odd, source[row_count - 1:], source[:1]), 'tile',...  4.17 us
    ppermute x1, waiting for transfers between devices, shards(): lax.ppermute(jnp.where(odd, source[row_count - 1:], source[:1]), 'tile',...  3.82 us
    ppermute x1, waiting for transfers between devices, shards(): outer = lax.ppermute(outer, 'tile', outer_moves)  3.8 us
    ppermute x1, starting transfers between devices, shards(): outer = lax.ppermute(outer, 'tile', outer_moves)  3.75 us
  transfers between devices with their start and end apart: 27, of which 15 were waited for; matrix products, arithmetic and copies ran while one was open for 0% of the time, Pallas kernels for 10%

profile of v2, /device:TPU:8, one launch (start us, length us, event | category | flops | bytes accessed | tf_op | source)
XLA Modules:
  0.0 99.5 jit_solution(8952895955342369745)
XLA Ops:
  1.7 1.8 %first_stats.1 = f32[3,8,128]{2,1,0:T(8,128)S(1)} custom-call(s32[67]{0:T(128)S(1)} %pad_add_fusion.info_ref, bf16[4,104,384]{2,1,0:T(8,128)(2,1)S(1)} %bitcast.11), custom_call_target="tpu_custom_call" | custom-call | flops 1650000000 | tf_op jit(solution)/shard_map/first_stats/pallas_call | solution.py:585
  3.6 3.0 %collective-permute-start.1 = (f32[3,8,128]{2,1,0:T(8,128)S(1)}, f32[3,8,128]{2,1,0:T(8,128)S(1)}, u32[]{:S(2)}, u32[]{:S(2)}) collective-permute-start(f32[3,8,128]{2,1,0:T(8,128)S(1)} %first_stats.1), channel_id=1, source_target_pairs={{0,16},{2,18},{4,20},{6,22},{8,24},{10,26},{12,28},{14,30},{16,0},... | collective-permute-start | bytes 36872 | tf_op jit(solution)/shard_map/ppermute | solution.py:531
  8.7 4.2 %collective-permute-start.4 = (bf16[1,104,384]{2,1,0:T(8,128)(2,1)S(1)}, bf16[1,104,384]{2,1,0:T(8,128)(2,1)S(1)}, u32[]{:S(2)}, u32[]{:S(2)}) collective-permute-start(bf16[1,104,384]{2,1,0:T(8,128)(2,1)S(1)} %get-tuple-element.78), channel_id=1, source_target_pairs={{2,4},{4,2},{6,8},{8,6},{10,12},{12,10},{14,16},{16,14},{18,20},{2... | collective-permute-start | bytes 239624 | tf_op jit(solution)/shard_map/ppermute | solution.py:604
  13.0 3.8 %collective-permute-done.4.outer_ref = bf16[1,104,384]{2,1,0:T(8,128)(2,1)S(1)} collective-permute-done((bf16[1,104,384]{2,1,0:T(8,128)(2,1)S(1)}, bf16[1,104,384]{2,1,0:T(8,128)(2,1)S(1)}, u32[]{:S(2)}, u32[]{:S(2)}) %collective-permute-start.4) | collective-permute-done | bytes 79904 | tf_op jit(solution)/shard_map/ppermute | solution.py:604
  16.8 2.1 %collective-permute-start.6 = (f32[3,8,128]{2,1,0:T(8,128)S(1)}, f32[3,8,128]{2,1,0:T(8,128)S(1)}, u32[]{:S(2)}, u32[]{:S(2)}) collective-permute-start(f32[3,8,128]{2,1,0:T(8,128)S(1)} %pad_maximum_fusion), channel_id=1, source_target_pairs={{0,4},{2,6},{4,0},{6,2},{8,12},{10,14},{12,8},{14,10},{16,20},{18,... | collective-permute-start | bytes 36872 | tf_op jit(solution)/shard_map/ppermute | solution.py:531
  20.5 2.9 %collective-permute-done.7 = f32[3,8,128]{2,1,0:T(8,128)S(1)} collective-permute-done((f32[3,8,128]{2,1,0:T(8,128)S(1)}, f32[3,8,128]{2,1,0:T(8,128)S(1)}, u32[]{:S(2)}, u32[]{:S(2)}) %collective-permute-start.7) | collective-permute-done | bytes 12320 | tf_op jit(solution)/shard_map/ppermute | solution.py:531
  23.5 3.5 %hidden.1 = (bf16[6,112,384]{2,1,0:T(8,128)(2,1)S(1)}, bf16[4,104,384]{2,1,0:T(8,128)(2,1)S(1)}, bf16[2304,1152]{1,0:T(8,128)(2,1)S(1)}) custom-call(s32[67]{0:T(128)S(1)} %pad_add_fusion.info_ref, bf16[1,104,384]{2,1,0:T(8,128)(2,1)S(1)} %collective-permute-done.3.inner_ref, bf16[4,104,384]{2,1,0:T(8,128)(2,1)S(1)} %bitcast.12, ...), custom_call_target="tpu_custom_call" | custom-call | flops 2200000000 | tf_op jit(solution)/shard_map/hidden/pallas_call | solution.py:613
  29.9 5.1 %conv.1 = (bf16[2,208,384]{2,1,0:T(8,128)(2,1)S(1)}, f32[3,8,128]{2,1,0:T(8,128)S(1)}) custom-call(s32[67]{0:T(128)S(1)} %pad_add_fusion.info_ref, bf16[6,112,384]{2,1,0:T(8,128)(2,1)S(1)} %get-tuple-element.39.rest_0_, bf16[6,112,384]{2,1,0:T(8,128)(2,1)S(1)} %collective-permute-done.8.rest_1_, bf16[4,104,384]{2,1,0:T(8,128)(2,1)S(1)} %get-tuple-element.40.rest_2_, ...), custom_call_target="tpu_custom_call" | custom-call | flops 5500000256 | tf_op jit(solution)/shard_map/conv/pallas_call | solution.py:635
  34.9 2.1 %collective-permute-start.10 = (f32[3,8,128]{2,1,0:T(8,128)S(1)}, f32[3,8,128]{2,1,0:T(8,128)S(1)}, u32[]{:S(2)}, u32[]{:S(2)}) collective-permute-start(f32[3,8,128]{2,1,0:T(8,128)S(1)} %get-tuple-element.43), channel_id=1, source_target_pairs={{0,16},{2,18},{4,20},{6,22},{8,24},{10,26},{12,28},{14,30},{16,0},... | collective-permute-start | bytes 36872 | tf_op jit(solution)/shard_map/ppermute | solution.py:531
  37.8 1.6 %collective-permute-start.9 = (f32[3,8,128]{2,1,0:T(8,128)S(1)}, f32[3,8,128]{2,1,0:T(8,128)S(1)}, u32[]{:S(2)}, u32[]{:S(2)}) collective-permute-start(f32[3,8,128]{2,1,0:T(8,128)S(1)} %get-tuple-element.43), channel_id=1, source_target_pairs={{0,8},{2,10},{4,12},{6,14},{8,0},{10,2},{12,4},{14,6},{16,24},{18,... | collective-permute-start | bytes 36872 | tf_op jit(solution)/shard_map/ppermute | solution.py:531
  45.1 2.0 %collective-permute-start.17 = (bf16[2,208,384]{2,1,0:T(8,128)(2,1)S(1)}, bf16[2,208,384]{2,1,0:T(8,128)(2,1)S(1)}, u32[]{:S(2)}, u32[]{:S(2)}) collective-permute-start(bf16[2,208,384]{2,1,0:T(8,128)(2,1)S(1)} %get-tuple-element.58.rest_5_.own_ref), channel_id=1, source_target_pairs={{0,8},{2,10},{4,12},{6,14},{8,0},{10,2},{12,4},{14,6},{16,24},{18,... | collective-permute-start | bytes 958472 | tf_op jit(solution)/shard_map/ppermute | solution.py:531
  47.1 3.0 %collective-permute-start.19 = (bf16[2,208,384]{2,1,0:T(8,128)(2,1)S(1)}, bf16[2,208,384]{2,1,0:T(8,128)(2,1)S(1)}, u32[]{:S(2)}, u32[]{:S(2)}) collective-permute-start(bf16[2,208,384]{2,1,0:T(8,128)(2,1)S(1)} %get-tuple-element.58.rest_5_.own_ref), channel_id=1, source_target_pairs={{8,16},{10,18},{12,20},{14,22},{16,8},{18,10},{20,12},{22,14},{9,1... | collective-permute-start | bytes 958472 | tf_op jit(solution)/shard_map/ppermute | solution.py:531
  52.9 3.0 %collective-permute-start.18 = (bf16[2,208,384]{2,1,0:T(8,128)(2,1)S(1)}, bf16[2,208,384]{2,1,0:T(8,128)(2,1)S(1)}, u32[]{:S(2)}, u32[]{:S(2)}) collective-permute-start(bf16[2,208,384]{2,1,0:T(8,128)(2,1)S(1)} %collective-permute-done.17.rest_7_), channel_id=1, source_target_pairs={{8,16},{10,18},{12,20},{14,22},{16,8},{18,10},{20,12},{22,14},{9,1... | collective-permute-start | bytes 958472 | tf_op jit(solution)/shard_map/ppermute | solution.py:531
  55.9 1.7 %collective-permute-done.19.rest_8_ = bf16[2,208,384]{2,1,0:T(8,128)(2,1)S(1)} collective-permute-done((bf16[2,208,384]{2,1,0:T(8,128)(2,1)S(1)}, bf16[2,208,384]{2,1,0:T(8,128)(2,1)S(1)}, u32[]{:S(2)}, u32[]{:S(2)}) %collective-permute-start.19) | collective-permute-done | bytes 319520 | tf_op jit(solution)/shard_map/ppermute | solution.py:531
  59.0 2.8 %collective-permute-start.21 = (bf16[2,208,384]{2,1,0:T(8,128)(2,1)S(1)}, bf16[2,208,384]{2,1,0:T(8,128)(2,1)S(1)}, u32[]{:S(2)}, u32[]{:S(2)}) collective-permute-start(bf16[2,208,384]{2,1,0:T(8,128)(2,1)S(1)} %collective-permute-done.19.rest_8_), channel_id=1, source_target_pairs={{8,12},{10,14},{12,8},{14,10},{16,20},{18,22},{20,16},{22,18},{9,1... | collective-permute-start | bytes 958472 | tf_op jit(solution)/shard_map/ppermute | solution.py:531
  65.0 2.5 %collective-permute-start.22 = (bf16[2,208,384]{2,1,0:T(8,128)(2,1)S(1)}, bf16[2,208,384]{2,1,0:T(8,128)(2,1)S(1)}, u32[]{:S(2)}, u32[]{:S(2)}) collective-permute-start(bf16[2,208,384]{2,1,0:T(8,128)(2,1)S(1)} %collective-permute-done.16.rest_6_), channel_id=1, source_target_pairs={{0,8},{2,10},{4,12},{6,14},{8,0},{10,2},{12,4},{14,6},{16,24},{18,... | collective-permute-start | bytes 958472 | tf_op jit(solution)/shard_map/ppermute | solution.py:531
  67.4 3.0 %attend_yours.2 = (bf16[1664,384]{1,0:T(8,128)(2,1)S(1)}, f32[416,128]{1,0:T(8,128)S(1)}, f32[416,128]{1,0:T(8,128)S(1)}, f32[416,384]{1,0:T(8,128)S(1)}) custom-call(s32[67]{0:T(128)S(1)} %pad_add_fusion.info_ref, f32[8,384]{1,0:T(8,128)S(1)} %get-tuple-element.47.rest_0_.means_ref, f32[8,384]{1,0:T(8,128)S(1)} %get-tuple-element.48.rest_1_.scales_ref, ...), custom_call_target="tpu_custom_call" | custom-call | flops 3960000000 | tf_op jit(solution)/shard_map/attend_yours/pallas_call | solution.py:585
  70.6 1.8 %collective-permute-done.22.rest_7_ = bf16[2,208,384]{2,1,0:T(8,128)(2,1)S(1)} collective-permute-done((bf16[2,208,384]{2,1,0:T(8,128)(2,1)S(1)}, bf16[2,208,384]{2,1,0:T(8,128)(2,1)S(1)}, u32[]{:S(2)}, u32[]{:S(2)}) %collective-permute-start.22) | collective-permute-done | bytes 319520 | tf_op jit(solution)/shard_map/ppermute | solution.py:531
  72.4 1.6 %collective-permute-done.23.rest_8_ = bf16[2,208,384]{2,1,0:T(8,128)(2,1)S(1)} collective-permute-done((bf16[2,208,384]{2,1,0:T(8,128)(2,1)S(1)}, bf16[2,208,384]{2,1,0:T(8,128)(2,1)S(1)}, u32[]{:S(2)}, u32[]{:S(2)}) %collective-permute-start.23) | collective-permute-done | bytes 319520 | tf_op jit(solution)/shard_map/ppermute | solution.py:531
  74.0 3.0 %attend_yours.3 = (bf16[1664,384]{1,0:T(8,128)(2,1)S(1)}, bf16[432,384]{1,0:T(8,128)(2,1)S(1)}) custom-call(s32[67]{0:T(128)S(1)} %pad_add_fusion.info_ref, f32[8,384]{1,0:T(8,128)S(1)} %get-tuple-element.47.rest_0_.means_ref, f32[8,384]{1,0:T(8,128)S(1)} %get-tuple-element.48.rest_1_.scales_ref, f32[1,384]{1,0:T(1,128)S(1)} %reshape.87.shift_ref.rest_2_, ...), custom_call_target="tpu_custom_call" | custom-call | flops 3960000000 | tf_op jit(solution)/shard_map/attend_yours/pallas_call | solution.py:585
  78.3 5.4 %attend_mine.1 = (f32[416,384]{1,0:T(8,128)S(1)}, f32[416,128]{1,0:T(8,128)S(1)}) custom-call(s32[67]{0:T(128)S(1)} %pad_add_fusion.info_ref, bf16[2,208,384]{2,1,0:T(8,128)(2,1)S(1)} %get-tuple-element.58.rest_5_.own_ref, f32[8,384]{1,0:T(8,128)S(1)} %get-tuple-element.47.rest_0_.means_ref, f32[8,384]{1,0:T(8,128)S(1)} %get-tuple-element.48.rest_1_.scales_ref, ...), custom_call_target="tpu_custom_call" | custom-call | flops 6600000000 | tf_op jit(solution)/shard_map/attend_mine/pallas_call | solution.py:585
  87.8 3.8 %collective-permute-start.26 = (bf16[1,104,384]{2,1,0:T(8,128)(2,1)S(1)}, bf16[1,104,384]{2,1,0:T(8,128)(2,1)S(1)}, u32[]{:S(2)}, u32[]{:S(2)}) collective-permute-start(bf16[1,104,384]{2,1,0:T(8,128)(2,1)S(1)} %get-tuple-element.65), channel_id=1, source_target_pairs={{2,4},{4,2},{6,8},{8,6},{10,12},{12,10},{14,16},{16,14},{18,20},{2... | collective-permute-start | bytes 239624 | tf_op jit(solution)/shard_map/ppermute | solution.py:732
  92.1 3.8 %collective-permute-done.26.outer_ref = bf16[1,104,384]{2,1,0:T(8,128)(2,1)S(1)} collective-permute-done((bf16[1,104,384]{2,1,0:T(8,128)(2,1)S(1)}, bf16[1,104,384]{2,1,0:T(8,128)(2,1)S(1)}, u32[]{:S(2)}, u32[]{:S(2)}) %collective-permute-start.26) | collective-permute-done | bytes 79904 | tf_op jit(solution)/shard_map/ppermute | solution.py:732
  95.9 2.3 %upsample.1 = bf16[8,208,192]{2,1,0:T(8,128)(2,1)S(1)} custom-call(s32[67]{0:T(128)S(1)} %pad_add_fusion.info_ref, bf16[1,104,384]{2,1,0:T(8,128)(2,1)S(1)} %collective-permute-done.25.inner_ref, bf16[4,104,384]{2,1,0:T(8,128)(2,1)S(1)} %get-tuple-element.64.own_ref, bf16[1,104,384]{2,1,0:T(8,128)(2,1)S(1)} %collective-permute-done.26.outer_ref, ...), custom_call_target="tpu_custom_call" | custom-call | flops 2529999872 | tf_op jit(solution)/shard_map/upsample/pallas_call | solution.py:585
  (89 shorter events, 29.2 us)
Async XLA Ops:
  3.5 9.3 %collective-permute-start = (f32[3,8,128]{2,1,0:T(8,128)S(1)}, f32[3,8,128]{2,1,0:T(8,128)S(1)}, u32[]{:S(2)}, u32[]{:S(2)}) collective-permute-start(f32[3,8,128]{2,1,0:T(8,128)S(1)} %first_stats.1), channel_id=1, source_target_pairs={{0,8},{2,10},{4,12},{6,14},{8,0},{10,2},{12,4},{14,6},{16,24},{18,... | collective-permute-start | bytes 36872 | tf_op jit(solution)/shard_map/ppermute | solution.py:531
  3.6 9.3 %collective-permute-start.1 = (f32[3,8,128]{2,1,0:T(8,128)S(1)}, f32[3,8,128]{2,1,0:T(8,128)S(1)}, u32[]{:S(2)}, u32[]{:S(2)}) collective-permute-start(f32[3,8,128]{2,1,0:T(8,128)S(1)} %first_stats.1), channel_id=1, source_target_pairs={{0,16},{2,18},{4,20},{6,22},{8,24},{10,26},{12,28},{14,30},{16,0},... | collective-permute-start | bytes 36872 | tf_op jit(solution)/shard_map/ppermute | solution.py:531
  6.6 6.2 %collective-permute-start.2 = (f32[3,8,128]{2,1,0:T(8,128)S(1)}, f32[3,8,128]{2,1,0:T(8,128)S(1)}, u32[]{:S(2)}, u32[]{:S(2)}) collective-permute-start(f32[3,8,128]{2,1,0:T(8,128)S(1)} %first_stats.1), channel_id=1, source_target_pairs={{0,24},{2,26},{4,28},{6,30},{8,16},{10,18},{12,20},{14,22},{16,8},... | collective-permute-start | bytes 36872 | tf_op jit(solution)/shard_map/ppermute | solution.py:531
  7.1 5.8 %collective-permute-start.3 = (bf16[1,104,384]{2,1,0:T(8,128)(2,1)S(1)}, bf16[1,104,384]{2,1,0:T(8,128)(2,1)S(1)}, u32[]{:S(2)}, u32[]{:S(2)}) collective-permute-start(bf16[1,104,384]{2,1,0:T(8,128)(2,1)S(1)} %get-tuple-element.79), channel_id=1, source_target_pairs={{0,2},{2,0},{4,6},{6,4},{8,10},{10,8},{12,14},{14,12},{16,18},{18,... | collective-permute-start | bytes 239624 | tf_op jit(solution)/shard_map/ppermute | solution.py:531
  8.7 8.1 %collective-permute-start.4 = (bf16[1,104,384]{2,1,0:T(8,128)(2,1)S(1)}, bf16[1,104,384]{2,1,0:T(8,128)(2,1)S(1)}, u32[]{:S(2)}, u32[]{:S(2)}) collective-permute-start(bf16[1,104,384]{2,1,0:T(8,128)(2,1)S(1)} %get-tuple-element.78), channel_id=1, source_target_pairs={{2,4},{4,2},{6,8},{8,6},{10,12},{12,10},{14,16},{16,14},{18,20},{2... | collective-permute-start | bytes 239624 | tf_op jit(solution)/shard_map/ppermute | solution.py:604
  16.8 3.7 %collective-permute-start.5 = (f32[3,8,128]{2,1,0:T(8,128)S(1)}, f32[3,8,128]{2,1,0:T(8,128)S(1)}, u32[]{:S(2)}, u32[]{:S(2)}) collective-permute-start(f32[3,8,128]{2,1,0:T(8,128)S(1)} %pad_maximum_fusion), channel_id=1, source_target_pairs={{0,2},{2,0},{4,6},{6,4},{8,10},{10,8},{12,14},{14,12},{16,18},{18,... | collective-permute-start | bytes 36872 | tf_op jit(solution)/shard_map/ppermute | solution.py:531
  16.8 3.7 %collective-permute-start.6 = (f32[3,8,128]{2,1,0:T(8,128)S(1)}, f32[3,8,128]{2,1,0:T(8,128)S(1)}, u32[]{:S(2)}, u32[]{:S(2)}) collective-permute-start(f32[3,8,128]{2,1,0:T(8,128)S(1)} %pad_maximum_fusion), channel_id=1, source_target_pairs={{0,4},{2,6},{4,0},{6,2},{8,12},{10,14},{12,8},{14,10},{16,20},{18,... | collective-permute-start | bytes 36872 | tf_op jit(solution)/shard_map/ppermute | solution.py:531
  18.8 4.6 %collective-permute-start.7 = (f32[3,8,128]{2,1,0:T(8,128)S(1)}, f32[3,8,128]{2,1,0:T(8,128)S(1)}, u32[]{:S(2)}, u32[]{:S(2)}) collective-permute-start(f32[3,8,128]{2,1,0:T(8,128)S(1)} %pad_maximum_fusion), channel_id=1, source_target_pairs={{0,6},{2,4},{4,2},{6,0},{8,14},{10,12},{12,10},{14,8},{16,22},{18,... | collective-permute-start | bytes 36872 | tf_op jit(solution)/shard_map/ppermute | solution.py:531
  34.9 4.7 %collective-permute-start.10 = (f32[3,8,128]{2,1,0:T(8,128)S(1)}, f32[3,8,128]{2,1,0:T(8,128)S(1)}, u32[]{:S(2)}, u32[]{:S(2)}) collective-permute-start(f32[3,8,128]{2,1,0:T(8,128)S(1)} %get-tuple-element.43), channel_id=1, source_target_pairs={{0,16},{2,18},{4,20},{6,22},{8,24},{10,26},{12,28},{14,30},{16,0},... | collective-permute-start | bytes 36872 | tf_op jit(solution)/shard_map/ppermute | solution.py:531
  41.5 8.6 %collective-permute-start.12 = (f32[3,8,128]{2,1,0:T(8,128)S(1)}, f32[3,8,128]{2,1,0:T(8,128)S(1)}, u32[]{:S(2)}, u32[]{:S(2)}) collective-permute-start(f32[3,8,128]{2,1,0:T(8,128)S(1)} %pad_maximum_fusion.2), channel_id=1, source_target_pairs={{0,2},{2,0},{4,6},{6,4},{8,10},{10,8},{12,14},{14,12},{16,18},{18,... | collective-permute-start | bytes 36872 | tf_op jit(solution)/shard_map/ppermute | solution.py:531
  42.9 7.3 %collective-permute-start.13 = (f32[3,8,128]{2,1,0:T(8,128)S(1)}, f32[3,8,128]{2,1,0:T(8,128)S(1)}, u32[]{:S(2)}, u32[]{:S(2)}) collective-permute-start(f32[3,8,128]{2,1,0:T(8,128)S(1)} %pad_maximum_fusion.2), channel_id=1, source_target_pairs={{0,4},{2,6},{4,0},{6,2},{8,12},{10,14},{12,8},{14,10},{16,20},{18,... | collective-permute-start | bytes 36872 | tf_op jit(solution)/shard_map/ppermute | solution.py:531
  44.3 5.9 %collective-permute-start.14 = (f32[3,8,128]{2,1,0:T(8,128)S(1)}, f32[3,8,128]{2,1,0:T(8,128)S(1)}, u32[]{:S(2)}, u32[]{:S(2)}) collective-permute-start(f32[3,8,128]{2,1,0:T(8,128)S(1)} %pad_maximum_fusion.2), channel_id=1, source_target_pairs={{0,6},{2,4},{4,2},{6,0},{8,14},{10,12},{12,10},{14,8},{16,22},{18,... | collective-permute-start | bytes 36872 | tf_op jit(solution)/shard_map/ppermute | solution.py:531
  45.1 7.8 %collective-permute-start.17 = (bf16[2,208,384]{2,1,0:T(8,128)(2,1)S(1)}, bf16[2,208,384]{2,1,0:T(8,128)(2,1)S(1)}, u32[]{:S(2)}, u32[]{:S(2)}) collective-permute-start(bf16[2,208,384]{2,1,0:T(8,128)(2,1)S(1)} %get-tuple-element.58.rest_5_.own_ref), channel_id=1, source_target_pairs={{0,8},{2,10},{4,12},{6,14},{8,0},{10,2},{12,4},{14,6},{16,24},{18,... | collective-permute-start | bytes 958472 | tf_op jit(solution)/shard_map/ppermute | solution.py:531
  47.1 10.5 %collective-permute-start.19 = (bf16[2,208,384]{2,1,0:T(8,128)(2,1)S(1)}, bf16[2,208,384]{2,1,0:T(8,128)(2,1)S(1)}, u32[]{:S(2)}, u32[]{:S(2)}) collective-permute-start(bf16[2,208,384]{2,1,0:T(8,128)(2,1)S(1)} %get-tuple-element.58.rest_5_.own_ref), channel_id=1, source_target_pairs={{8,16},{10,18},{12,20},{14,22},{16,8},{18,10},{20,12},{22,14},{9,1... | collective-permute-start | bytes 958472 | tf_op jit(solution)/shard_map/ppermute | solution.py:531
  50.2 11.6 %collective-permute-start.15 = (bf16[2,208,384]{2,1,0:T(8,128)(2,1)S(1)}, bf16[2,208,384]{2,1,0:T(8,128)(2,1)S(1)}, u32[]{:S(2)}, u32[]{:S(2)}) collective-permute-start(bf16[2,208,384]{2,1,0:T(8,128)(2,1)S(1)} %get-tuple-element.58.rest_5_.own_ref), channel_id=1, source_target_pairs={{0,2},{2,0},{4,6},{6,4},{8,10},{10,8},{12,14},{14,12},{16,18},{18,... | collective-permute-start | bytes 958472 | tf_op jit(solution)/shard_map/ppermute | solution.py:531
  51.0 10.9 %collective-permute-start.16 = (bf16[2,208,384]{2,1,0:T(8,128)(2,1)S(1)}, bf16[2,208,384]{2,1,0:T(8,128)(2,1)S(1)}, u32[]{:S(2)}, u32[]{:S(2)}) collective-permute-start(bf16[2,208,384]{2,1,0:T(8,128)(2,1)S(1)} %get-tuple-element.58.rest_5_.own_ref), channel_id=1, source_target_pairs={{0,4},{2,6},{4,0},{6,2},{8,12},{10,14},{12,8},{14,10},{16,20},{18,... | collective-permute-start | bytes 958472 | tf_op jit(solution)/shard_map/ppermute | solution.py:531
  52.9 10.5 %collective-permute-start.18 = (bf16[2,208,384]{2,1,0:T(8,128)(2,1)S(1)}, bf16[2,208,384]{2,1,0:T(8,128)(2,1)S(1)}, u32[]{:S(2)}, u32[]{:S(2)}) collective-permute-start(bf16[2,208,384]{2,1,0:T(8,128)(2,1)S(1)} %collective-permute-done.17.rest_7_), channel_id=1, source_target_pairs={{8,16},{10,18},{12,20},{14,22},{16,8},{18,10},{20,12},{22,14},{9,1... | collective-permute-start | bytes 958472 | tf_op jit(solution)/shard_map/ppermute | solution.py:531
  57.6 7.0 %collective-permute-start.20 = (bf16[2,208,384]{2,1,0:T(8,128)(2,1)S(1)}, bf16[2,208,384]{2,1,0:T(8,128)(2,1)S(1)}, u32[]{:S(2)}, u32[]{:S(2)}) collective-permute-start(bf16[2,208,384]{2,1,0:T(8,128)(2,1)S(1)} %collective-permute-done.19.rest_8_), channel_id=1, source_target_pairs={{8,0},{10,2},{12,4},{14,6},{16,24},{18,26},{20,28},{22,30},{9,1},{... | collective-permute-start | bytes 958472 | tf_op jit(solution)/shard_map/ppermute | solution.py:531
  59.0 11.6 %collective-permute-start.21 = (bf16[2,208,384]{2,1,0:T(8,128)(2,1)S(1)}, bf16[2,208,384]{2,1,0:T(8,128)(2,1)S(1)}, u32[]{:S(2)}, u32[]{:S(2)}) collective-permute-start(bf16[2,208,384]{2,1,0:T(8,128)(2,1)S(1)} %collective-permute-done.19.rest_8_), channel_id=1, source_target_pairs={{8,12},{10,14},{12,8},{14,10},{16,20},{18,22},{20,16},{22,18},{9,1... | collective-permute-start | bytes 958472 | tf_op jit(solution)/shard_map/ppermute | solution.py:531
  64.6 9.4 %collective-permute-start.23 = (bf16[2,208,384]{2,1,0:T(8,128)(2,1)S(1)}, bf16[2,208,384]{2,1,0:T(8,128)(2,1)S(1)}, u32[]{:S(2)}, u32[]{:S(2)}) collective-permute-start(bf16[2,208,384]{2,1,0:T(8,128)(2,1)S(1)} %broadcast_select_fusion.rest_5_), channel_id=1, source_target_pairs={{0,4},{2,6},{4,0},{6,2},{8,12},{10,14},{12,8},{14,10},{16,20},{18,... | collective-permute-start | bytes 958472 | tf_op jit(solution)/shard_map/ppermute | solution.py:531
  65.0 7.4 %collective-permute-start.22 = (bf16[2,208,384]{2,1,0:T(8,128)(2,1)S(1)}, bf16[2,208,384]{2,1,0:T(8,128)(2,1)S(1)}, u32[]{:S(2)}, u32[]{:S(2)}) collective-permute-start(bf16[2,208,384]{2,1,0:T(8,128)(2,1)S(1)} %collective-permute-done.16.rest_6_), channel_id=1, source_target_pairs={{0,8},{2,10},{4,12},{6,14},{8,0},{10,2},{12,4},{14,6},{16,24},{18,... | collective-permute-start | bytes 958472 | tf_op jit(solution)/shard_map/ppermute | solution.py:531
  77.0 8.0 %collective-permute-start.24 = (bf16[432,384]{1,0:T(8,128)(2,1)S(1)}, bf16[432,384]{1,0:T(8,128)(2,1)S(1)}, u32[]{:S(2)}, u32[]{:S(2)}) collective-permute-start(bf16[432,384]{1,0:T(8,128)(2,1)S(1)} %get-tuple-element.57), channel_id=1, source_target_pairs={{0,2},{2,0},{4,6},{6,4},{8,10},{10,8},{12,14},{14,12},{16,18},{18,... | collective-permute-start | bytes 995336 | tf_op jit(solution)/shard_map/ppermute | solution.py:702
  86.5 5.6 %collective-permute-start.25 = (bf16[1,104,384]{2,1,0:T(8,128)(2,1)S(1)}, bf16[1,104,384]{2,1,0:T(8,128)(2,1)S(1)}, u32[]{:S(2)}, u32[]{:S(2)}) collective-permute-start(bf16[1,104,384]{2,1,0:T(8,128)(2,1)S(1)} %get-tuple-element.63), channel_id=1, source_target_pairs={{0,2},{2,0},{4,6},{6,4},{8,10},{10,8},{12,14},{14,12},{16,18},{18,... | collective-permute-start | bytes 239624 | tf_op jit(solution)/shard_map/ppermute | solution.py:531
  87.8 8.1 %collective-permute-start.26 = (bf16[1,104,384]{2,1,0:T(8,128)(2,1)S(1)}, bf16[1,104,384]{2,1,0:T(8,128)(2,1)S(1)}, u32[]{:S(2)}, u32[]{:S(2)}) collective-permute-start(bf16[1,104,384]{2,1,0:T(8,128)(2,1)S(1)} %get-tuple-element.65), channel_id=1, source_target_pairs={{2,4},{4,2},{6,8},{8,6},{10,12},{12,10},{14,16},{16,14},{18,20},{2... | collective-permute-start | bytes 239624 | tf_op jit(solution)/shard_map/ppermute | solution.py:732
  (16 other events, 229.6 us)

commit v3 on v1

--- a/solution.py
+++ b/solution.py
@@ -17,6 +17,7 @@
 ROWS_OF_TILE = 4
 LANES = 128
 VMEM_BYTES = 24 * 1024 * 1024
+HOLD_VMEM_BYTES = 46 * 1024 * 1024
 F32 = jnp.float32
 BF16 = jnp.bfloat16
 
@@ -158,7 +159,7 @@
 
 
 def hidden_kernel(
-    rows, info_ref, inner_ref, latents_ref, outer_ref, stats_ref, gain_ref, shift_ref, out_ref,
+    rows, info_ref, outer_ref, inner_ref, latents_ref, stats_ref, gain_ref, shift_ref, out_ref,
     source_ref,
 ):
     info = Info(info_ref, rows)
@@ -179,9 +180,26 @@
     source_ref[...] = latents_ref[...]
 
 
+def hold_kernel(taps, weight_ref, held_ref, sems):
+    channels = weight_ref.shape[-1]
+    copies = [
+        pltpu.make_async_copy(
+            weight_ref.at[2 - depth // 3, depth % 3, side],
+            held_ref.at[pl.ds(depth * channels, channels), pl.ds(side * channels, channels)],
+            sems.at[side, depth],
+        )
+        for side in range(3)
+        for depth in range(3 * taps)
+    ]
+    for copy in copies:
+        copy.start()
+    for copy in copies:
+        copy.wait()
+
+
 def conv_kernel(rows, taps, info_ref, *rest):
     hidden_refs, rest = rest[:taps], rest[taps:]
-    latents_ref, bias_ref, weight_ref, own_ref, stats_ref, inputs_ref, held_ref = rest
+    latents_ref, bias_ref, held_ref, own_ref, stats_ref, inputs_ref = rest
     row_count, cols, channels = latents_ref.shape
     info = Info(info_ref, rows)
     padded = hidden_refs[0].shape[1]
@@ -195,11 +213,6 @@
                     same = labels[r + tap] == labels[r + 1]
                     block = jnp.where(same, block, jnp.zeros_like(block))
                 inputs_ref[r * padded : (r + 1) * padded, lanes] = block
-    for depth in range(3 * taps):
-        for side in range(3):
-            held_ref[
-                depth * channels : (depth + 1) * channels, side * channels : (side + 1) * channels
-            ] = weight_ref[2 - depth // 3, depth % 3, side]
     product = jnp.dot(inputs_ref[...], held_ref[...], preferred_element_type=F32)
     column = lax.broadcasted_iota(jnp.int32, (cols, 1), 0)
     cells = []
@@ -458,7 +471,7 @@
 
 
 def upsample_kernel(
-    rows, info_ref, inner_ref, own_ref, outer_ref, weight_ref, bias_ref, out_ref, columns_ref,
+    rows, info_ref, outer_ref, inner_ref, own_ref, weight_ref, bias_ref, out_ref, columns_ref,
     wide_ref,
 ):
     info = Info(info_ref, rows)
@@ -590,19 +603,30 @@
         functools.partial(stats_kernel, rows), [source], stats_shape,
         cost_estimate=cost(1.5), name="first_stats",
     )
-    inner = exchange(jnp.where(odd, source[:1], source[row_count - 1 :]), tiles, 1)
     outer = lax.ppermute(
         jnp.where(odd, source[row_count - 1 :], source[:1]), "tile", outer_moves
     )
+    inner = exchange(jnp.where(odd, source[:1], source[row_count - 1 :]), tiles, 1)
+    stats, outer, inner = lax.optimization_barrier((stats, outer, inner))
     taps = min(3, frames)
+    held = pl.pallas_call(
+        functools.partial(hold_kernel, taps),
+        out_shape=shape(3 * taps * channels, 3 * channels),
+        in_specs=[HBM_SPEC],
+        out_specs=VMEM_SPEC,
+        scratch_shapes=[pltpu.SemaphoreType.DMA((3, 3 * taps))],
+        compiler_params=pltpu.CompilerParams(vmem_limit_bytes=HOLD_VMEM_BYTES),
+        cost_estimate=cost(1.5 * taps),
+        name="hold",
+    )(conv_weight)
     rounds = merge_masks(tiles)
-    for index, masks in enumerate(rounds):
+    for index, masks in enumerate(reversed(rounds)):
         stats = merge_round(stats, tiles, masks)
-        if index == 0:
-            stats, inner, outer = lax.optimization_barrier((stats, inner, outer))
+        if index == len(rounds) - 2:
+            stats, held = lax.optimization_barrier((stats, held))
     hidden, source = call(
         functools.partial(hidden_kernel, rows),
-        [inner, source, outer, stats, row(first_gain), row(first_shift)],
+        [outer, inner, source, stats, row(first_gain), row(first_shift)],
         (shape(near_rows, padded, channels), shape(row_count, cols, channels)),
         cost_estimate=cost(1.3),
         name="hidden",
@@ -622,12 +646,11 @@
         out_specs=(VMEM_SPEC, VMEM_SPEC),
         scratch_shapes=[
             pltpu.VMEM((row_count * padded, 3 * taps * channels), BF16),
-            pltpu.VMEM((3 * taps * channels, 3 * channels), BF16),
         ],
         compiler_params=params(),
         cost_estimate=cost(2.5 * taps),
         name="conv",
-    )(info, *context, source, row(conv_bias), conv_weight)
+    )(info, *context, source, row(conv_bias), held)
 
     blocks = {0: own}
     neighbour = [(i, i ^ 1) for i in range(tiles)]
@@ -639,17 +662,17 @@
         blocks[2] = exchange(own, tiles, 4)
         blocks[6] = exchange(own, tiles, 12, middle)
         stats = merge_round(stats, tiles, rounds[0])
-        own_xy, stats = lax.optimization_barrier((own, stats))
+        stats, own_xy = lax.optimization_barrier((stats, own))
+        inward = exchange(blocks[2], tiles, 12, middle)
+        outward = exchange(blocks[6], tiles, 4, middle)
         other = exchange(own_xy, tiles, 1)
         blocks[1] = exchange(own_xy, tiles, 2)
         other, blocks[1] = lax.optimization_barrier((other, blocks[1]))
-        inward = exchange(blocks[2], tiles, 12, middle)
-        outward = exchange(blocks[6], tiles, 4, middle)
         blocks[4] = jnp.where((tile // 4 == 1) | (tile // 4 == 2), inward, outward)
-        blocks[7] = exchange(blocks[6], tiles, 2, middle)
+        passed, blocks[4] = lax.optimization_barrier((blocks[1], blocks[4]))
         blocks[5] = exchange(blocks[4], tiles, 2)
-        passed, blocks[4] = lax.optimization_barrier((blocks[1], blocks[4]))
         blocks[3] = exchange(passed, tiles, 4)
+        blocks[7] = exchange(passed, tiles, 12, middle)
         groups = [[0, 1, 2, 6], [4, 7, 3, 5]]
     else:
         for masks in rounds:
@@ -717,7 +740,7 @@
     inner = exchange(inner, tiles, 1)
     decoded = call(
         functools.partial(upsample_kernel, rows),
-        [inner, attended, outer, folded, row(upsample_bias)],
+        [outer, inner, attended, folded, row(upsample_bias)],
         shape(2 * row_count, 2 * cols, out_channels),
         scratch=[
             pltpu.VMEM((near_rows * padded, 3 * channels), BF16),

time: 99.3 us -> 98.6 us (level); the launches traced: 98.7 us -> 96.7 us
  waiting for transfers between devices: 25.7 us -> 22 us
  local copies, waits for them, and re-layouts: 5.56 us -> 2.32 us
  Pallas kernels: 25.5 us -> 27.9 us
  starting transfers between devices: 40.5 us -> 42.1 us
    ppermute x1, waiting for transfers between devices: 4.85 us -> 0.01 us  [shards(): lax.ppermute(jnp.where(odd, source[row_count - 1:], source[:1]), 'tile',...]
    unnamed x28 -> x26, local copies, waits for them, and re-layouts: 4.28 us -> 1.05 us
    ppermute x23, waiting for transfers between devices: 14.4 us -> 17.3 us  [exchange(): return lax.ppermute(array, 'tile', moves)]
    pallas_call x0 -> x1, Pallas kernels: none -> 2.63 us  [shards(): pl.pallas_call(functools.partial(hold_kernel, taps), out_shape=shape(3 *...]
    ppermute x1, waiting for transfers between devices: 2.05 us -> 0.56 us  [shards(): received = lax.ppermute(sent, 'tile', neighbour)]
  transfers between devices with their start and end apart: 27 -> 27, of which waited for: 14 -> 19; matrix products, arithmetic and copies ran while one was open for 0% -> 1% of each run, Pallas kernels for 11% -> 15%
where the time goes in v3:
time: 98.6 us; the launch traced here: 96.7 us
  starting transfers between devices  42.1 us (43%)
  Pallas kernels  27.9 us (28%)
  waiting for transfers between devices  22 us (22%)
  local copies, waits for them, and re-layouts  2.32 us (2%)
  other arithmetic  1.89 us (2%)
    ppermute x23, starting transfers between devices, exchange(): return lax.ppermute(array, 'tile', moves)  30.4 us
    pallas_call x8, Pallas kernels, call(): pl.pallas_call(kernel, out_shape=out_shape, in_specs=[SMEM_SPEC] + [VMEM_...  19.8 us
    ppermute x23, waiting for transfers between devices, exchange(): return lax.ppermute(array, 'tile', moves)  17.3 us
    pallas_call x1, Pallas kernels, shards(): pl.pallas_call(functools.partial(conv_kernel, rows, taps), out_shape=(pai...  5.03 us
    ppermute x1, starting transfers between devices, shards(): outer = lax.ppermute(outer, 'tile', outer_moves)  4.82 us
    ppermute x1, starting transfers between devices, shards(): lax.ppermute(jnp.where(odd, source[row_count - 1:], source[:1]), 'tile',...  4.24 us
    ppermute x1, waiting for transfers between devices, shards(): outer = lax.ppermute(outer, 'tile', outer_moves)  2.73 us
    pallas_call x1, Pallas kernels, shards(): pl.pallas_call(functools.partial(hold_kernel, taps), out_shape=shape(3 *...  2.63 us
  transfers between devices with their start and end apart: 27, of which 19 were waited for; matrix products, arithmetic and copies ran while one was open for 1% of the time, Pallas kernels for 15%

profile of v3, /device:TPU:8, one launch (start us, length us, event | category | flops | bytes accessed | tf_op | source)
XLA Modules:
  0.0 96.7 jit_solution(7041723851895991402)
XLA Ops:
  0.9 4.2 %collective-permute-start = (bf16[1,104,384]{2,1,0:T(8,128)(2,1)S(1)}, bf16[1,104,384]{2,1,0:T(8,128)(2,1)S(1)}, u32[]{:S(2)}, u32[]{:S(2)}) collective-permute-start(bf16[1,104,384]{2,1,0:T(8,128)(2,1)S(1)} %get-tuple-element.81), channel_id=1, source_target_pairs={{2,4},{4,2},{6,8},{8,6},{10,12},{12,10},{14,16},{16,14},{18,20},{2... | collective-permute-start | bytes 239624 | tf_op jit(solution)/shard_map/ppermute | solution.py:606
  7.6 1.8 %first_stats.1 = f32[3,8,128]{2,1,0:T(8,128)S(1)} custom-call(s32[67]{0:T(128)S(1)} %pad_add_fusion.info_ref, bf16[4,104,384]{2,1,0:T(8,128)(2,1)S(1)} %bitcast.11), custom_call_target="tpu_custom_call" | custom-call | flops 1650000000 | tf_op jit(solution)/shard_map/first_stats/pallas_call | solution.py:588
  10.1 2.9 %collective-permute-start.3 = (f32[3,8,128]{2,1,0:T(8,128)S(1)}, f32[3,8,128]{2,1,0:T(8,128)S(1)}, u32[]{:S(2)}, u32[]{:S(2)}) collective-permute-start(f32[3,8,128]{2,1,0:T(8,128)S(1)} %first_stats.1), channel_id=1, source_target_pairs={{0,16},{2,18},{4,20},{6,22},{8,24},{10,26},{12,28},{14,30},{16,0},... | collective-permute-start | bytes 36872 | tf_op jit(solution)/shard_map/ppermute | solution.py:534
  13.4 2.6 %hold.1.rest_4_ = bf16[2304,1152]{1,0:T(8,128)(2,1)S(1)} custom-call(bf16[3,3,3,384,384]{4,3,2,1,0:T(8,128)(2,1)} %weight_ref.3), custom_call_target="tpu_custom_call" | custom-call | flops 3300000000 | tf_op jit(solution)/shard_map/hold/pallas_call | solution.py:612
  16.7 1.6 %collective-permute-start.5 = (f32[3,8,128]{2,1,0:T(8,128)S(1)}, f32[3,8,128]{2,1,0:T(8,128)S(1)}, u32[]{:S(2)}, u32[]{:S(2)}) collective-permute-start(f32[3,8,128]{2,1,0:T(8,128)S(1)} %pad_maximum_fusion), channel_id=1, source_target_pairs={{0,2},{2,0},{4,6},{6,4},{8,10},{10,8},{12,14},{14,12},{16,18},{18,... | collective-permute-start | bytes 36872 | tf_op jit(solution)/shard_map/ppermute | solution.py:534
  20.5 1.6 %collective-permute-done.6 = f32[3,8,128]{2,1,0:T(8,128)S(1)} collective-permute-done((f32[3,8,128]{2,1,0:T(8,128)S(1)}, f32[3,8,128]{2,1,0:T(8,128)S(1)}, u32[]{:S(2)}, u32[]{:S(2)}) %collective-permute-start.6) | collective-permute-done | bytes 12320 | tf_op jit(solution)/shard_map/ppermute | solution.py:534
  22.0 1.5 %collective-permute-done.7 = f32[3,8,128]{2,1,0:T(8,128)S(1)} collective-permute-done((f32[3,8,128]{2,1,0:T(8,128)S(1)}, f32[3,8,128]{2,1,0:T(8,128)S(1)}, u32[]{:S(2)}, u32[]{:S(2)}) %collective-permute-start.7) | collective-permute-done | bytes 12320 | tf_op jit(solution)/shard_map/ppermute | solution.py:534
  27.8 5.0 %conv.1 = (bf16[2,208,384]{2,1,0:T(8,128)(2,1)S(1)}, f32[3,8,128]{2,1,0:T(8,128)S(1)}) custom-call(s32[67]{0:T(128)S(1)} %pad_add_fusion.info_ref, bf16[6,112,384]{2,1,0:T(8,128)(2,1)S(1)} %get-tuple-element.41.rest_0_, bf16[6,112,384]{2,1,0:T(8,128)(2,1)S(1)} %collective-permute-done.8.rest_1_, bf16[4,104,384]{2,1,0:T(8,128)(2,1)S(1)} %get-tuple-element.42.rest_2_, ...), custom_call_target="tpu_custom_call" | custom-call | flops 5500000256 | tf_op jit(solution)/shard_map/conv/pallas_call | solution.py:642
  32.8 2.5 %collective-permute-start.10 = (f32[3,8,128]{2,1,0:T(8,128)S(1)}, f32[3,8,128]{2,1,0:T(8,128)S(1)}, u32[]{:S(2)}, u32[]{:S(2)}) collective-permute-start(f32[3,8,128]{2,1,0:T(8,128)S(1)} %get-tuple-element.44), channel_id=1, source_target_pairs={{0,16},{2,18},{4,20},{6,22},{8,24},{10,26},{12,28},{14,30},{16,0},... | collective-permute-start | bytes 36872 | tf_op jit(solution)/shard_map/ppermute | solution.py:534
  35.3 1.9 %collective-permute-start.11 = (f32[3,8,128]{2,1,0:T(8,128)S(1)}, f32[3,8,128]{2,1,0:T(8,128)S(1)}, u32[]{:S(2)}, u32[]{:S(2)}) collective-permute-start(f32[3,8,128]{2,1,0:T(8,128)S(1)} %get-tuple-element.44), channel_id=1, source_target_pairs={{0,24},{2,26},{4,28},{6,30},{8,16},{10,18},{12,20},{14,22},{16,8},... | collective-permute-start | bytes 36872 | tf_op jit(solution)/shard_map/ppermute | solution.py:534
  37.4 1.6 %collective-permute-done.11 = f32[3,8,128]{2,1,0:T(8,128)S(1)} collective-permute-done((f32[3,8,128]{2,1,0:T(8,128)S(1)}, f32[3,8,128]{2,1,0:T(8,128)S(1)}, u32[]{:S(2)}, u32[]{:S(2)}) %collective-permute-start.11) | collective-permute-done | bytes 12320 | tf_op jit(solution)/shard_map/ppermute | solution.py:534
  39.0 1.9 %collective-permute-done.9 = f32[3,8,128]{2,1,0:T(8,128)S(1)} collective-permute-done((f32[3,8,128]{2,1,0:T(8,128)S(1)}, f32[3,8,128]{2,1,0:T(8,128)S(1)}, u32[]{:S(2)}, u32[]{:S(2)}) %collective-permute-start.9) | collective-permute-done | bytes 12320 | tf_op jit(solution)/shard_map/ppermute | solution.py:534
  44.9 3.0 %collective-permute-start.19 = (bf16[2,208,384]{2,1,0:T(8,128)(2,1)S(1)}, bf16[2,208,384]{2,1,0:T(8,128)(2,1)S(1)}, u32[]{:S(2)}, u32[]{:S(2)}) collective-permute-start(bf16[2,208,384]{2,1,0:T(8,128)(2,1)S(1)} %get-tuple-element.60.rest_5_.own_ref), channel_id=1, source_target_pairs={{8,16},{10,18},{12,20},{14,22},{16,8},{18,10},{20,12},{22,14},{9,1... | collective-permute-start | bytes 958472 | tf_op jit(solution)/shard_map/ppermute | solution.py:534
  51.8 2.3 %collective-permute-start.18 = (bf16[2,208,384]{2,1,0:T(8,128)(2,1)S(1)}, bf16[2,208,384]{2,1,0:T(8,128)(2,1)S(1)}, u32[]{:S(2)}, u32[]{:S(2)}) collective-permute-start(bf16[2,208,384]{2,1,0:T(8,128)(2,1)S(1)} %collective-permute-done.17.rest_7_), channel_id=1, source_target_pairs={{8,16},{10,18},{12,20},{14,22},{16,8},{18,10},{20,12},{22,14},{9,1... | collective-permute-start | bytes 958472 | tf_op jit(solution)/shard_map/ppermute | solution.py:534
  56.9 1.5 %queries.1 = (bf16[416,384]{1,0:T(8,128)(2,1)S(1)}, f32[416,128]{1,0:T(8,128)S(1)}, f32[8,384]{1,0:T(8,128)S(1)}, f32[8,384]{1,0:T(8,128)S(1)}) custom-call(s32[67]{0:T(128)S(1)} %pad_add_fusion.info_ref, bf16[2,208,384]{2,1,0:T(8,128)(2,1)S(1)} %collective-permute-done.15.other_ref, f32[3,8,128]{2,1,0:T(8,128)S(1)} %pad_maximum_fusion.3.stats_ref, ...), custom_call_target="tpu_custom_call" | custom-call | flops 1650000000 | tf_op jit(solution)/shard_map/queries/pallas_call | solution.py:588
  58.4 2.7 %collective-permute-done.18 = bf16[2,208,384]{2,1,0:T(8,128)(2,1)S(1)} collective-permute-done((bf16[2,208,384]{2,1,0:T(8,128)(2,1)S(1)}, bf16[2,208,384]{2,1,0:T(8,128)(2,1)S(1)}, u32[]{:S(2)}, u32[]{:S(2)}) %collective-permute-start.18) | collective-permute-done | bytes 319520 | tf_op jit(solution)/shard_map/ppermute | solution.py:534
  61.3 3.7 %collective-permute-start.21 = (bf16[2,208,384]{2,1,0:T(8,128)(2,1)S(1)}, bf16[2,208,384]{2,1,0:T(8,128)(2,1)S(1)}, u32[]{:S(2)}, u32[]{:S(2)}) collective-permute-start(bf16[2,208,384]{2,1,0:T(8,128)(2,1)S(1)} %collective-permute-done.16.rest_6_), channel_id=1, source_target_pairs={{8,16},{10,18},{12,20},{14,22},{16,8},{18,10},{20,12},{22,14},{9,1... | collective-permute-start | bytes 958472 | tf_op jit(solution)/shard_map/ppermute | solution.py:534
  66.5 3.0 %attend_yours.2 = (bf16[1664,384]{1,0:T(8,128)(2,1)S(1)}, f32[416,128]{1,0:T(8,128)S(1)}, f32[416,128]{1,0:T(8,128)S(1)}, f32[416,384]{1,0:T(8,128)S(1)}) custom-call(s32[67]{0:T(128)S(1)} %pad_add_fusion.info_ref, f32[8,384]{1,0:T(8,128)S(1)} %get-tuple-element.49.rest_0_.means_ref, f32[8,384]{1,0:T(8,128)S(1)} %get-tuple-element.50.rest_1_.scales_ref, ...), custom_call_target="tpu_custom_call" | custom-call | flops 3960000000 | tf_op jit(solution)/shard_map/attend_yours/pallas_call | solution.py:588
  70.2 1.9 %collective-permute-done.22.rest_7_ = bf16[2,208,384]{2,1,0:T(8,128)(2,1)S(1)} collective-permute-done((bf16[2,208,384]{2,1,0:T(8,128)(2,1)S(1)}, bf16[2,208,384]{2,1,0:T(8,128)(2,1)S(1)}, u32[]{:S(2)}, u32[]{:S(2)}) %collective-permute-start.22) | collective-permute-done | bytes 319520 | tf_op jit(solution)/shard_map/ppermute | solution.py:534
  72.2 3.0 %attend_yours.3 = (bf16[1664,384]{1,0:T(8,128)(2,1)S(1)}, bf16[432,384]{1,0:T(8,128)(2,1)S(1)}) custom-call(s32[67]{0:T(128)S(1)} %pad_add_fusion.info_ref, f32[8,384]{1,0:T(8,128)S(1)} %get-tuple-element.49.rest_0_.means_ref, f32[8,384]{1,0:T(8,128)S(1)} %get-tuple-element.50.rest_1_.scales_ref, f32[1,384]{1,0:T(1,128)S(1)} %reshape.87.shift_ref.rest_2_, ...), custom_call_target="tpu_custom_call" | custom-call | flops 3960000000 | tf_op jit(solution)/shard_map/attend_yours/pallas_call | solution.py:588
  76.4 5.4 %attend_mine.1 = (f32[416,384]{1,0:T(8,128)S(1)}, f32[416,128]{1,0:T(8,128)S(1)}) custom-call(s32[67]{0:T(128)S(1)} %pad_add_fusion.info_ref, bf16[2,208,384]{2,1,0:T(8,128)(2,1)S(1)} %get-tuple-element.60.rest_5_.own_ref, f32[8,384]{1,0:T(8,128)S(1)} %get-tuple-element.49.rest_0_.means_ref, f32[8,384]{1,0:T(8,128)S(1)} %get-tuple-element.50.rest_1_.scales_ref, ...), custom_call_target="tpu_custom_call" | custom-call | flops 6600000000 | tf_op jit(solution)/shard_map/attend_mine/pallas_call | solution.py:588
  83.8 4.8 %collective-permute-start.25 = (bf16[1,104,384]{2,1,0:T(8,128)(2,1)S(1)}, bf16[1,104,384]{2,1,0:T(8,128)(2,1)S(1)}, u32[]{:S(2)}, u32[]{:S(2)}) collective-permute-start(bf16[1,104,384]{2,1,0:T(8,128)(2,1)S(1)} %get-tuple-element.65), channel_id=1, source_target_pairs={{2,4},{4,2},{6,8},{8,6},{10,12},{12,10},{14,16},{16,14},{18,20},{2... | collective-permute-start | bytes 239624 | tf_op jit(solution)/shard_map/ppermute | solution.py:739
  89.2 2.7 %collective-permute-done.25.outer_ref = bf16[1,104,384]{2,1,0:T(8,128)(2,1)S(1)} collective-permute-done((bf16[1,104,384]{2,1,0:T(8,128)(2,1)S(1)}, bf16[1,104,384]{2,1,0:T(8,128)(2,1)S(1)}, u32[]{:S(2)}, u32[]{:S(2)}) %collective-permute-start.25) | collective-permute-done | bytes 79904 | tf_op jit(solution)/shard_map/ppermute | solution.py:739
  93.1 2.4 %upsample.1 = bf16[8,208,192]{2,1,0:T(8,128)(2,1)S(1)} custom-call(s32[67]{0:T(128)S(1)} %pad_add_fusion.info_ref, bf16[1,104,384]{2,1,0:T(8,128)(2,1)S(1)} %collective-permute-done.25.outer_ref, bf16[1,104,384]{2,1,0:T(8,128)(2,1)S(1)} %collective-permute-done.26.inner_ref, bf16[4,104,384]{2,1,0:T(8,128)(2,1)S(1)} %get-tuple-element.67.own_ref, ...), custom_call_target="tpu_custom_call" | custom-call | flops 2529999872 | tf_op jit(solution)/shard_map/upsample/pallas_call | solution.py:588
  (90 shorter events, 30.7 us)
Async XLA Ops:
  0.9 8.6 %collective-permute-start = (bf16[1,104,384]{2,1,0:T(8,128)(2,1)S(1)}, bf16[1,104,384]{2,1,0:T(8,128)(2,1)S(1)}, u32[]{:S(2)}, u32[]{:S(2)}) collective-permute-start(bf16[1,104,384]{2,1,0:T(8,128)(2,1)S(1)} %get-tuple-element.81), channel_id=1, source_target_pairs={{2,4},{4,2},{6,8},{8,6},{10,12},{12,10},{14,16},{16,14},{18,20},{2... | collective-permute-start | bytes 239624 | tf_op jit(solution)/shard_map/ppermute | solution.py:606
  5.2 4.7 %collective-permute-start.1 = (bf16[1,104,384]{2,1,0:T(8,128)(2,1)S(1)}, bf16[1,104,384]{2,1,0:T(8,128)(2,1)S(1)}, u32[]{:S(2)}, u32[]{:S(2)}) collective-permute-start(bf16[1,104,384]{2,1,0:T(8,128)(2,1)S(1)} %get-tuple-element.80), channel_id=1, source_target_pairs={{0,2},{2,0},{4,6},{6,4},{8,10},{10,8},{12,14},{14,12},{16,18},{18,... | collective-permute-start | bytes 239624 | tf_op jit(solution)/shard_map/ppermute | solution.py:534
  9.9 6.1 %collective-permute-start.2 = (f32[3,8,128]{2,1,0:T(8,128)S(1)}, f32[3,8,128]{2,1,0:T(8,128)S(1)}, u32[]{:S(2)}, u32[]{:S(2)}) collective-permute-start(f32[3,8,128]{2,1,0:T(8,128)S(1)} %first_stats.1), channel_id=1, source_target_pairs={{0,8},{2,10},{4,12},{6,14},{8,0},{10,2},{12,4},{14,6},{16,24},{18,... | collective-permute-start | bytes 36872 | tf_op jit(solution)/shard_map/ppermute | solution.py:534
  10.1 6.0 %collective-permute-start.3 = (f32[3,8,128]{2,1,0:T(8,128)S(1)}, f32[3,8,128]{2,1,0:T(8,128)S(1)}, u32[]{:S(2)}, u32[]{:S(2)}) collective-permute-start(f32[3,8,128]{2,1,0:T(8,128)S(1)} %first_stats.1), channel_id=1, source_target_pairs={{0,16},{2,18},{4,20},{6,22},{8,24},{10,26},{12,28},{14,30},{16,0},... | collective-permute-start | bytes 36872 | tf_op jit(solution)/shard_map/ppermute | solution.py:534
  13.0 3.7 %collective-permute-start.4 = (f32[3,8,128]{2,1,0:T(8,128)S(1)}, f32[3,8,128]{2,1,0:T(8,128)S(1)}, u32[]{:S(2)}, u32[]{:S(2)}) collective-permute-start(f32[3,8,128]{2,1,0:T(8,128)S(1)} %first_stats.1), channel_id=1, source_target_pairs={{0,24},{2,26},{4,28},{6,30},{8,16},{10,18},{12,20},{14,22},{16,8},... | collective-permute-start | bytes 36872 | tf_op jit(solution)/shard_map/ppermute | solution.py:534
  16.7 3.8 %collective-permute-start.5 = (f32[3,8,128]{2,1,0:T(8,128)S(1)}, f32[3,8,128]{2,1,0:T(8,128)S(1)}, u32[]{:S(2)}, u32[]{:S(2)}) collective-permute-start(f32[3,8,128]{2,1,0:T(8,128)S(1)} %pad_maximum_fusion), channel_id=1, source_target_pairs={{0,2},{2,0},{4,6},{6,4},{8,10},{10,8},{12,14},{14,12},{16,18},{18,... | collective-permute-start | bytes 36872 | tf_op jit(solution)/shard_map/ppermute | solution.py:534
  19.0 4.6 %collective-permute-start.7 = (f32[3,8,128]{2,1,0:T(8,128)S(1)}, f32[3,8,128]{2,1,0:T(8,128)S(1)}, u32[]{:S(2)}, u32[]{:S(2)}) collective-permute-start(f32[3,8,128]{2,1,0:T(8,128)S(1)} %pad_maximum_fusion), channel_id=1, source_target_pairs={{0,6},{2,4},{4,2},{6,0},{8,14},{10,12},{12,10},{14,8},{16,22},{18,... | collective-permute-start | bytes 36872 | tf_op jit(solution)/shard_map/ppermute | solution.py:534
  32.8 4.6 %collective-permute-start.10 = (f32[3,8,128]{2,1,0:T(8,128)S(1)}, f32[3,8,128]{2,1,0:T(8,128)S(1)}, u32[]{:S(2)}, u32[]{:S(2)}) collective-permute-start(f32[3,8,128]{2,1,0:T(8,128)S(1)} %get-tuple-element.44), channel_id=1, source_target_pairs={{0,16},{2,18},{4,20},{6,22},{8,24},{10,26},{12,28},{14,30},{16,0},... | collective-permute-start | bytes 36872 | tf_op jit(solution)/shard_map/ppermute | solution.py:534
  35.3 3.7 %collective-permute-start.11 = (f32[3,8,128]{2,1,0:T(8,128)S(1)}, f32[3,8,128]{2,1,0:T(8,128)S(1)}, u32[]{:S(2)}, u32[]{:S(2)}) collective-permute-start(f32[3,8,128]{2,1,0:T(8,128)S(1)} %get-tuple-element.44), channel_id=1, source_target_pairs={{0,24},{2,26},{4,28},{6,30},{8,16},{10,18},{12,20},{14,22},{16,8},... | collective-permute-start | bytes 36872 | tf_op jit(solution)/shard_map/ppermute | solution.py:534
  40.9 7.0 %collective-permute-start.12 = (f32[3,8,128]{2,1,0:T(8,128)S(1)}, f32[3,8,128]{2,1,0:T(8,128)S(1)}, u32[]{:S(2)}, u32[]{:S(2)}) collective-permute-start(f32[3,8,128]{2,1,0:T(8,128)S(1)} %pad_maximum_fusion.2), channel_id=1, source_target_pairs={{0,2},{2,0},{4,6},{6,4},{8,10},{10,8},{12,14},{14,12},{16,18},{18,... | collective-permute-start | bytes 36872 | tf_op jit(solution)/shard_map/ppermute | solution.py:534
  42.4 5.5 %collective-permute-start.13 = (f32[3,8,128]{2,1,0:T(8,128)S(1)}, f32[3,8,128]{2,1,0:T(8,128)S(1)}, u32[]{:S(2)}, u32[]{:S(2)}) collective-permute-start(f32[3,8,128]{2,1,0:T(8,128)S(1)} %pad_maximum_fusion.2), channel_id=1, source_target_pairs={{0,4},{2,6},{4,0},{6,2},{8,12},{10,14},{12,8},{14,10},{16,20},{18,... | collective-permute-start | bytes 36872 | tf_op jit(solution)/shard_map/ppermute | solution.py:534
  43.3 4.6 %collective-permute-start.14 = (f32[3,8,128]{2,1,0:T(8,128)S(1)}, f32[3,8,128]{2,1,0:T(8,128)S(1)}, u32[]{:S(2)}, u32[]{:S(2)}) collective-permute-start(f32[3,8,128]{2,1,0:T(8,128)S(1)} %pad_maximum_fusion.2), channel_id=1, source_target_pairs={{0,6},{2,4},{4,2},{6,0},{8,14},{10,12},{12,10},{14,8},{16,22},{18,... | collective-permute-start | bytes 36872 | tf_op jit(solution)/shard_map/ppermute | solution.py:534
  44.5 7.3 %collective-permute-start.17 = (bf16[2,208,384]{2,1,0:T(8,128)(2,1)S(1)}, bf16[2,208,384]{2,1,0:T(8,128)(2,1)S(1)}, u32[]{:S(2)}, u32[]{:S(2)}) collective-permute-start(bf16[2,208,384]{2,1,0:T(8,128)(2,1)S(1)} %get-tuple-element.60.rest_5_.own_ref), channel_id=1, source_target_pairs={{0,8},{2,10},{4,12},{6,14},{8,0},{10,2},{12,4},{14,6},{16,24},{18,... | collective-permute-start | bytes 958472 | tf_op jit(solution)/shard_map/ppermute | solution.py:534
  44.9 10.6 %collective-permute-start.19 = (bf16[2,208,384]{2,1,0:T(8,128)(2,1)S(1)}, bf16[2,208,384]{2,1,0:T(8,128)(2,1)S(1)}, u32[]{:S(2)}, u32[]{:S(2)}) collective-permute-start(bf16[2,208,384]{2,1,0:T(8,128)(2,1)S(1)} %get-tuple-element.60.rest_5_.own_ref), channel_id=1, source_target_pairs={{8,16},{10,18},{12,20},{14,22},{16,8},{18,10},{20,12},{22,14},{9,1... | collective-permute-start | bytes 958472 | tf_op jit(solution)/shard_map/ppermute | solution.py:534
  48.0 8.9 %collective-permute-start.15 = (bf16[2,208,384]{2,1,0:T(8,128)(2,1)S(1)}, bf16[2,208,384]{2,1,0:T(8,128)(2,1)S(1)}, u32[]{:S(2)}, u32[]{:S(2)}) collective-permute-start(bf16[2,208,384]{2,1,0:T(8,128)(2,1)S(1)} %get-tuple-element.60.rest_5_.own_ref), channel_id=1, source_target_pairs={{0,2},{2,0},{4,6},{6,4},{8,10},{10,8},{12,14},{14,12},{16,18},{18,... | collective-permute-start | bytes 958472 | tf_op jit(solution)/shard_map/ppermute | solution.py:534
  49.5 7.4 %collective-permute-start.16 = (bf16[2,208,384]{2,1,0:T(8,128)(2,1)S(1)}, bf16[2,208,384]{2,1,0:T(8,128)(2,1)S(1)}, u32[]{:S(2)}, u32[]{:S(2)}) collective-permute-start(bf16[2,208,384]{2,1,0:T(8,128)(2,1)S(1)} %get-tuple-element.60.rest_5_.own_ref), channel_id=1, source_target_pairs={{0,4},{2,6},{4,0},{6,2},{8,12},{10,14},{12,8},{14,10},{16,20},{18,... | collective-permute-start | bytes 958472 | tf_op jit(solution)/shard_map/ppermute | solution.py:534
  51.8 9.4 %collective-permute-start.18 = (bf16[2,208,384]{2,1,0:T(8,128)(2,1)S(1)}, bf16[2,208,384]{2,1,0:T(8,128)(2,1)S(1)}, u32[]{:S(2)}, u32[]{:S(2)}) collective-permute-start(bf16[2,208,384]{2,1,0:T(8,128)(2,1)S(1)} %collective-permute-done.17.rest_7_), channel_id=1, source_target_pairs={{8,16},{10,18},{12,20},{14,22},{16,8},{18,10},{20,12},{22,14},{9,1... | collective-permute-start | bytes 958472 | tf_op jit(solution)/shard_map/ppermute | solution.py:534
  55.5 5.8 %collective-permute-start.20 = (bf16[2,208,384]{2,1,0:T(8,128)(2,1)S(1)}, bf16[2,208,384]{2,1,0:T(8,128)(2,1)S(1)}, u32[]{:S(2)}, u32[]{:S(2)}) collective-permute-start(bf16[2,208,384]{2,1,0:T(8,128)(2,1)S(1)} %collective-permute-done.19.rest_8_), channel_id=1, source_target_pairs={{8,0},{10,2},{12,4},{14,6},{16,24},{18,26},{20,28},{22,30},{9,1},{... | collective-permute-start | bytes 958472 | tf_op jit(solution)/shard_map/ppermute | solution.py:534
  61.3 8.9 %collective-permute-start.21 = (bf16[2,208,384]{2,1,0:T(8,128)(2,1)S(1)}, bf16[2,208,384]{2,1,0:T(8,128)(2,1)S(1)}, u32[]{:S(2)}, u32[]{:S(2)}) collective-permute-start(bf16[2,208,384]{2,1,0:T(8,128)(2,1)S(1)} %collective-permute-done.16.rest_6_), channel_id=1, source_target_pairs={{8,16},{10,18},{12,20},{14,22},{16,8},{18,10},{20,12},{22,14},{9,1... | collective-permute-start | bytes 958472 | tf_op jit(solution)/shard_map/ppermute | solution.py:534
  65.0 7.1 %collective-permute-start.22 = (bf16[2,208,384]{2,1,0:T(8,128)(2,1)S(1)}, bf16[2,208,384]{2,1,0:T(8,128)(2,1)S(1)}, u32[]{:S(2)}, u32[]{:S(2)}) collective-permute-start(bf16[2,208,384]{2,1,0:T(8,128)(2,1)S(1)} %collective-permute-done.16.rest_6_), channel_id=1, source_target_pairs={{0,8},{2,10},{4,12},{6,14},{8,0},{10,2},{12,4},{14,6},{16,24},{18,... | collective-permute-start | bytes 958472 | tf_op jit(solution)/shard_map/ppermute | solution.py:534
  65.1 7.1 %collective-permute-start.23 = (bf16[2,208,384]{2,1,0:T(8,128)(2,1)S(1)}, bf16[2,208,384]{2,1,0:T(8,128)(2,1)S(1)}, u32[]{:S(2)}, u32[]{:S(2)}) collective-permute-start(bf16[2,208,384]{2,1,0:T(8,128)(2,1)S(1)} %broadcast_select_fusion.rest_5_), channel_id=1, source_target_pairs={{0,4},{2,6},{4,0},{6,2},{8,12},{10,14},{12,8},{14,10},{16,20},{18,... | collective-permute-start | bytes 958472 | tf_op jit(solution)/shard_map/ppermute | solution.py:534
  75.2 7.2 %collective-permute-start.24 = (bf16[432,384]{1,0:T(8,128)(2,1)S(1)}, bf16[432,384]{1,0:T(8,128)(2,1)S(1)}, u32[]{:S(2)}, u32[]{:S(2)}) collective-permute-start(bf16[432,384]{1,0:T(8,128)(2,1)S(1)} %get-tuple-element.59), channel_id=1, source_target_pairs={{0,2},{2,0},{4,6},{6,4},{8,10},{10,8},{12,14},{14,12},{16,18},{18,... | collective-permute-start | bytes 995336 | tf_op jit(solution)/shard_map/ppermute | solution.py:709
  83.8 8.2 %collective-permute-start.25 = (bf16[1,104,384]{2,1,0:T(8,128)(2,1)S(1)}, bf16[1,104,384]{2,1,0:T(8,128)(2,1)S(1)}, u32[]{:S(2)}, u32[]{:S(2)}) collective-permute-start(bf16[1,104,384]{2,1,0:T(8,128)(2,1)S(1)} %get-tuple-element.65), channel_id=1, source_target_pairs={{2,4},{4,2},{6,8},{8,6},{10,12},{12,10},{14,16},{16,14},{18,20},{2... | collective-permute-start | bytes 239624 | tf_op jit(solution)/shard_map/ppermute | solution.py:739
  88.6 4.5 %collective-permute-start.26 = (bf16[1,104,384]{2,1,0:T(8,128)(2,1)S(1)}, bf16[1,104,384]{2,1,0:T(8,128)(2,1)S(1)}, u32[]{:S(2)}, u32[]{:S(2)}) collective-permute-start(bf16[1,104,384]{2,1,0:T(8,128)(2,1)S(1)} %get-tuple-element.66), channel_id=1, source_target_pairs={{0,2},{2,0},{4,6},{6,4},{8,10},{10,8},{12,14},{14,12},{16,18},{18,... | collective-permute-start | bytes 239624 | tf_op jit(solution)/shard_map/ppermute | solution.py:534
  (16 other events, 216.6 us)

commit v4 on v3

--- a/solution.py
+++ b/solution.py
@@ -152,7 +152,7 @@
     write_stats(out_ref, cells, labels, widths, info.videos, channels)
 
 
-def rims(info, inner_ref, outer_ref):
+def rims(info, outer_ref, inner_ref):
     odd = lax.rem(info.tile(), 2) == 1
     inner, outer = inner_ref[0].astype(F32), outer_ref[0].astype(F32)
     return jnp.where(odd, inner, outer), jnp.where(odd, outer, inner)
@@ -167,7 +167,7 @@
     labels, widths = info.window(info.tile() * row_count - 1, row_count + 2)
     means, scales = norm_tables(stats_ref, gain_ref)
     column = lax.broadcasted_iota(jnp.int32, (cols, 1), 0)
-    above, below = rims(info, inner_ref, outer_ref)
+    above, below = rims(info, outer_ref, inner_ref)
     sources = [above] + [latents_ref[r].astype(F32) for r in range(row_count)] + [below]
     for r, source in enumerate(sources):
         mean = pick(means, labels[r], info.videos)
@@ -470,54 +470,97 @@
             out_ref[down, tap, 1, :, channels:] = right.astype(BF16)
 
 
+def spread_columns(wide_ref, value, row, right):
+    cols, channels = value.shape
+    for part in range(wide_ref.shape[0]):
+        lo, hi = part * LANES, min((part + 1) * LANES, channels)
+        piece = value[:, lo:hi]
+        if hi - lo < LANES:
+            piece = jnp.concatenate([piece, jnp.zeros((cols, LANES - hi + lo), F32)], axis=1)
+        wide_ref[part, row, pl.ds(right, cols, 2), :] = piece
+
+
+def phase_product(columns, weight):
+    return lax.dot_general(
+        columns, weight, (((1,), (1,)), ((), ())), preferred_element_type=F32
+    )
+
+
 def upsample_kernel(
-    rows, info_ref, outer_ref, inner_ref, own_ref, weight_ref, bias_ref, out_ref, columns_ref,
-    wide_ref,
+    rows, info_ref, own_ref, weight_ref, bias_ref, out_ref, open_ref, columns_ref, wide_ref
 ):
     info = Info(info_ref, rows)
     row_count, cols, channels = own_ref.shape
-    near_rows = row_count + 2
-    padded = columns_ref.shape[0] // near_rows
+    padded = columns_ref.shape[0] // row_count
     parts_out = wide_ref.shape[0]
     out_channels = out_ref.shape[-1]
-    labels, widths = info.window(info.tile() * row_count - 1, near_rows)
-    above, below = rims(info, inner_ref, outer_ref)
-    sources = [lambda: above]
-    sources += [functools.partial(own_ref.__getitem__, r) for r in range(row_count)]
-    sources += [lambda: below]
-    build_columns(columns_ref, sources)
-    span = row_count * padded
+    labels, widths = info.window(info.tile() * row_count, row_count)
+    build_columns(
+        columns_ref, [functools.partial(own_ref.__getitem__, r) for r in range(row_count)]
+    )
+    inner_rows = (row_count - 1) * padded
     wide_column = lax.broadcasted_iota(jnp.int32, (2 * cols, 1), 0)
     for down in range(2):
         for right in range(2):
             lanes = slice(right * channels, (right + 2) * channels)
-            products = [
-                lax.dot_general(
-                    columns_ref[(down + tap) * padded : (down + tap) * padded + span, lanes],
-                    weight_ref[down, tap, right],
-                    (((1,), (1,)), ((), ())),
-                    preferred_element_type=F32,
-                )
-                for tap in range(2)
-            ]
-            rim, same = products[down], products[1 - down]
+            same = phase_product(columns_ref[:, lanes], weight_ref[down, 1 - down, right])
+            start = down * padded
+            rim = phase_product(
+                columns_ref[start : start + inner_rows, lanes], weight_ref[down, down, right]
+            )
             for r in range(row_count):
-                lo, hi = r * padded, r * padded + cols
-                near = labels[r + 2 * down]
-                value = same[lo:hi] + jnp.where(near == labels[r + 1], rim[lo:hi], 0.0)
-                for part in range(parts_out):
-                    part_lo, part_hi = part * LANES, min((part + 1) * LANES, out_channels)
-                    piece = value[:, part_lo:part_hi]
-                    if part_hi - part_lo < LANES:
-                        missing = LANES - (part_hi - part_lo)
-                        piece = jnp.concatenate([piece, jnp.zeros((cols, missing), F32)], axis=1)
-                    wide_ref[part, 2 * r + down, pl.ds(right, cols, 2), :] = piece
-    for r in range(2 * row_count):
-        valid = wide_column < 2 * widths[r // 2 + 1]
+                value = same[r * padded : r * padded + cols]
+                near = r - 1 + 2 * down
+                if 0 <= near < row_count:
+                    lo = (near - down) * padded
+                    value = value + jnp.where(
+                        labels[near] == labels[r], rim[lo : lo + cols], 0.0
+                    )
+                spread_columns(wide_ref, value, 2 * r + down, right)
+    for part in range(parts_out):
+        open_ref[part, 0] = wide_ref[part, 0]
+        open_ref[part, 1] = wide_ref[part, 2 * row_count - 1]
+    for r in range(1, 2 * row_count - 1):
+        valid = wide_column < 2 * widths[r // 2]
         for part in range(parts_out):
             lo, hi = part * LANES, min((part + 1) * LANES, out_channels)
             value = wide_ref[part, r, :, 0 : hi - lo] + bias_ref[:, lo:hi]
-            out_ref[r, :, lo:hi] = jnp.where(valid, value, 0.0).astype(BF16)
+            out_ref[r - 1, :, lo:hi] = jnp.where(valid, value, 0.0).astype(BF16)
+
+
+def close_kernel(
+    rows, info_ref, outer_ref, inner_ref, middle_ref, open_ref, weight_ref, bias_ref, out_ref,
+    columns_ref, wide_ref,
+):
+    info = Info(info_ref, rows)
+    wide_rows, wide_cols, out_channels = out_ref.shape
+    row_count, cols = wide_rows // 2, wide_cols // 2
+    channels = outer_ref.shape[-1]
+    padded = columns_ref.shape[0] // 2
+    labels, widths = info.window(info.tile() * row_count - 1, row_count + 2)
+    above, below = rims(info, outer_ref, inner_ref)
+    build_columns(columns_ref, [lambda: above, lambda: below])
+    wide_column = lax.broadcasted_iota(jnp.int32, (wide_cols, 1), 0)
+    for down in range(2):
+        for right in range(2):
+            lanes = slice(right * channels, (right + 2) * channels)
+            rim = phase_product(
+                columns_ref[down * padded : (down + 1) * padded, lanes],
+                weight_ref[down, down, right],
+            )
+            spread_columns(wide_ref, rim[:cols], down, right)
+    out_ref[1 : wide_rows - 1] = middle_ref[...]
+    for down in range(2):
+        rim_row, own_row = (row_count + 1, row_count) if down else (0, 1)
+        valid = wide_column < 2 * widths[own_row]
+        for part in range(wide_ref.shape[0]):
+            lo, hi = part * LANES, min((part + 1) * LANES, out_channels)
+            rim = jnp.where(
+                labels[rim_row] == labels[own_row], wide_ref[part, down, :, 0 : hi - lo], 0.0
+            )
+            value = open_ref[part, down, :, 0 : hi - lo] + rim + bias_ref[:, lo:hi]
+            value = jnp.where(valid, value, 0.0).astype(BF16)
+            out_ref[down * (wide_rows - 1), :, lo:hi] = value
 
 
 def merge_stats(mine, other):
@@ -534,11 +577,13 @@
     return lax.ppermute(array, "tile", moves)
 
 
-def merge_round(stats, tiles, masks):
+def merge_round(stats, tiles, masks, tied=()):
     parts = [stats] + [exchange(stats, tiles, mask) for mask in masks]
+    if tied:
+        parts[1], *tied = lax.optimization_barrier((parts[1], *tied))
     while len(parts) > 1:
         parts = [merge_stats(*parts[i : i + 2]) for i in range(0, len(parts), 2)]
-    return parts[0]
+    return (parts[0], *tied) if tied else parts[0]
 
 
 def merge_masks(tiles):
@@ -661,13 +706,14 @@
         stats = merge_round(stats, tiles, rounds[1])
         blocks[2] = exchange(own, tiles, 4)
         blocks[6] = exchange(own, tiles, 12, middle)
-        stats = merge_round(stats, tiles, rounds[0])
+        stats, blocks[2], blocks[6] = merge_round(
+            stats, tiles, rounds[0], (blocks[2], blocks[6])
+        )
         stats, own_xy = lax.optimization_barrier((stats, own))
         inward = exchange(blocks[2], tiles, 12, middle)
         outward = exchange(blocks[6], tiles, 4, middle)
         other = exchange(own_xy, tiles, 1)
         blocks[1] = exchange(own_xy, tiles, 2)
-        other, blocks[1] = lax.optimization_barrier((other, blocks[1]))
         blocks[4] = jnp.where((tile // 4 == 1) | (tile // 4 == 2), inward, outward)
         passed, blocks[4] = lax.optimization_barrier((blocks[1], blocks[4]))
         blocks[5] = exchange(blocks[4], tiles, 2)
@@ -738,16 +784,31 @@
     )
     outer = lax.ppermute(outer, "tile", outer_moves)
     inner = exchange(inner, tiles, 1)
+    parts_out = -(-out_channels // LANES)
+    middle, open_rows = call(
+        functools.partial(upsample_kernel, rows),
+        [attended, folded, row(upsample_bias)],
+        (
+            shape(2 * row_count - 2, 2 * cols, out_channels),
+            shape(parts_out, 2, 2 * cols, LANES, dtype=F32),
+        ),
+        scratch=[
+            pltpu.VMEM((row_count * padded, 3 * channels), BF16),
+            pltpu.VMEM((parts_out, 2 * row_count, 2 * cols, LANES), F32),
+        ],
+        cost_estimate=cost(2.0),
+        name="upsample",
+    )
     decoded = call(
-        functools.partial(upsample_kernel, rows),
-        [outer, inner, attended, folded, row(upsample_bias)],
+        functools.partial(close_kernel, rows),
+        [outer, inner, middle, open_rows, folded, row(upsample_bias)],
         shape(2 * row_count, 2 * cols, out_channels),
         scratch=[
-            pltpu.VMEM((near_rows * padded, 3 * channels), BF16),
-            pltpu.VMEM((-(-out_channels // LANES), 2 * row_count, 2 * cols, LANES), F32),
+            pltpu.VMEM((2 * padded, 3 * channels), BF16),
+            pltpu.VMEM((parts_out, 2, 2 * cols, LANES), F32),
         ],
-        cost_estimate=cost(2.3),
-        name="upsample",
+        cost_estimate=cost(1.0),
+        name="close",
     )
     return decoded.reshape(2 * row_count, 1, 2 * cols, out_channels)
 

time: 98.6 us -> 97.3 us (0.987)
  waiting for transfers between devices: 22 us -> 19.2 us
  Pallas kernels: 27.9 us -> 28.9 us
    ppermute x1, waiting for transfers between devices: 2.73 us -> 1.27 us  [shards(): outer = lax.ppermute(outer, 'tile', outer_moves)]
    pallas_call x8 -> x9, Pallas kernels: 19.8 us -> 20.8 us  [call(): pl.pallas_call(kernel, out_shape=out_shape, in_specs=[SMEM_SPEC] + [VMEM_...]
  transfers between devices with their start and end apart: 27 -> 27, of which waited for: 19 -> 15; matrix products, arithmetic and copies ran while one was open for 1% -> 1% of each run, Pallas kernels for 15% -> 18%
where the time goes in v4:
time: 97.3 us; the launch traced here: 95.7 us
  starting transfers between devices  42.5 us (44%)
  Pallas kernels  28.9 us (30%)
  waiting for transfers between devices  19.2 us (20%)
  local copies, waits for them, and re-layouts  2.73 us (3%)
  other arithmetic  1.89 us (2%)
    ppermute x23, starting transfers between devices, exchange(): return lax.ppermute(array, 'tile', moves)  30.8 us
    pallas_call x9, Pallas kernels, call(): pl.pallas_call(kernel, out_shape=out_shape, in_specs=[SMEM_SPEC] + [VMEM_...  20.8 us
    ppermute x23, waiting for transfers between devices, exchange(): return lax.ppermute(array, 'tile', moves)  16.4 us
    pallas_call x1, Pallas kernels, shards(): pl.pallas_call(functools.partial(conv_kernel, rows, taps), out_shape=(pai...  5.04 us
    ppermute x1, starting transfers between devices, shards(): outer = lax.ppermute(outer, 'tile', outer_moves)  4.67 us
    ppermute x1, starting transfers between devices, shards(): lax.ppermute(jnp.where(odd, source[row_count - 1:], source[:1]), 'tile',...  4.24 us
    pallas_call x1, Pallas kernels, shards(): pl.pallas_call(functools.partial(hold_kernel, taps), out_shape=shape(3 *...  2.63 us
  transfers between devices with their start and end apart: 27, of which 15 were waited for; matrix products, arithmetic and copies ran while one was open for 1% of the time, Pallas kernels for 18%

profile of v4, /device:TPU:8, one launch (start us, length us, event | category | flops | bytes accessed | tf_op | source)
XLA Modules:
  0.0 95.7 jit_solution(12373043084810093459)
XLA Ops:
  0.9 4.2 %collective-permute-start = (bf16[1,104,384]{2,1,0:T(8,128)(2,1)S(1)}, bf16[1,104,384]{2,1,0:T(8,128)(2,1)S(1)}, u32[]{:S(2)}, u32[]{:S(2)}) collective-permute-start(bf16[1,104,384]{2,1,0:T(8,128)(2,1)S(1)} %get-tuple-element.87), channel_id=1, source_target_pairs={{2,4},{4,2},{6,8},{8,6},{10,12},{12,10},{14,16},{16,14},{18,20},{2... | collective-permute-start | bytes 239624 | tf_op jit(solution)/shard_map/ppermute | solution.py:651
  7.6 1.8 %first_stats.1 = f32[3,8,128]{2,1,0:T(8,128)S(1)} custom-call(s32[67]{0:T(128)S(1)} %pad_add_fusion.info_ref, bf16[4,104,384]{2,1,0:T(8,128)(2,1)S(1)} %bitcast.11), custom_call_target="tpu_custom_call" | custom-call | flops 1650000000 | tf_op jit(solution)/shard_map/first_stats/pallas_call | solution.py:633
  10.1 2.9 %collective-permute-start.3 = (f32[3,8,128]{2,1,0:T(8,128)S(1)}, f32[3,8,128]{2,1,0:T(8,128)S(1)}, u32[]{:S(2)}, u32[]{:S(2)}) collective-permute-start(f32[3,8,128]{2,1,0:T(8,128)S(1)} %first_stats.1), channel_id=1, source_target_pairs={{0,16},{2,18},{4,20},{6,22},{8,24},{10,26},{12,28},{14,30},{16,0},... | collective-permute-start | bytes 36872 | tf_op jit(solution)/shard_map/ppermute | solution.py:577
  13.4 2.6 %hold.1.rest_4_ = bf16[2304,1152]{1,0:T(8,128)(2,1)S(1)} custom-call(bf16[3,3,3,384,384]{4,3,2,1,0:T(8,128)(2,1)} %weight_ref.3), custom_call_target="tpu_custom_call" | custom-call | flops 3300000000 | tf_op jit(solution)/shard_map/hold/pallas_call | solution.py:657
  16.7 1.6 %collective-permute-start.5 = (f32[3,8,128]{2,1,0:T(8,128)S(1)}, f32[3,8,128]{2,1,0:T(8,128)S(1)}, u32[]{:S(2)}, u32[]{:S(2)}) collective-permute-start(f32[3,8,128]{2,1,0:T(8,128)S(1)} %pad_maximum_fusion), channel_id=1, source_target_pairs={{0,2},{2,0},{4,6},{6,4},{8,10},{10,8},{12,14},{14,12},{16,18},{18,... | collective-permute-start | bytes 36872 | tf_op jit(solution)/shard_map/ppermute | solution.py:577
  20.5 1.6 %collective-permute-done.6 = f32[3,8,128]{2,1,0:T(8,128)S(1)} collective-permute-done((f32[3,8,128]{2,1,0:T(8,128)S(1)}, f32[3,8,128]{2,1,0:T(8,128)S(1)}, u32[]{:S(2)}, u32[]{:S(2)}) %collective-permute-start.6) | collective-permute-done | bytes 12320 | tf_op jit(solution)/shard_map/ppermute | solution.py:577
  22.0 1.5 %collective-permute-done.7 = f32[3,8,128]{2,1,0:T(8,128)S(1)} collective-permute-done((f32[3,8,128]{2,1,0:T(8,128)S(1)}, f32[3,8,128]{2,1,0:T(8,128)S(1)}, u32[]{:S(2)}, u32[]{:S(2)}) %collective-permute-start.7) | collective-permute-done | bytes 12320 | tf_op jit(solution)/shard_map/ppermute | solution.py:577
  27.8 5.0 %conv.1 = (bf16[2,208,384]{2,1,0:T(8,128)(2,1)S(1)}, f32[3,8,128]{2,1,0:T(8,128)S(1)}) custom-call(s32[67]{0:T(128)S(1)} %pad_add_fusion.info_ref, bf16[6,112,384]{2,1,0:T(8,128)(2,1)S(1)} %get-tuple-element.44.rest_0_, bf16[6,112,384]{2,1,0:T(8,128)(2,1)S(1)} %collective-permute-done.8.rest_1_, bf16[4,104,384]{2,1,0:T(8,128)(2,1)S(1)} %get-tuple-element.45.rest_2_, ...), custom_call_target="tpu_custom_call" | custom-call | flops 5500000256 | tf_op jit(solution)/shard_map/conv/pallas_call | solution.py:687
  32.8 2.5 %collective-permute-start.10 = (f32[3,8,128]{2,1,0:T(8,128)S(1)}, f32[3,8,128]{2,1,0:T(8,128)S(1)}, u32[]{:S(2)}, u32[]{:S(2)}) collective-permute-start(f32[3,8,128]{2,1,0:T(8,128)S(1)} %get-tuple-element.47), channel_id=1, source_target_pairs={{0,16},{2,18},{4,20},{6,22},{8,24},{10,26},{12,28},{14,30},{16,0},... | collective-permute-start | bytes 36872 | tf_op jit(solution)/shard_map/ppermute | solution.py:577
  35.3 1.9 %collective-permute-start.11 = (f32[3,8,128]{2,1,0:T(8,128)S(1)}, f32[3,8,128]{2,1,0:T(8,128)S(1)}, u32[]{:S(2)}, u32[]{:S(2)}) collective-permute-start(f32[3,8,128]{2,1,0:T(8,128)S(1)} %get-tuple-element.47), channel_id=1, source_target_pairs={{0,24},{2,26},{4,28},{6,30},{8,16},{10,18},{12,20},{14,22},{16,8},... | collective-permute-start | bytes 36872 | tf_op jit(solution)/shard_map/ppermute | solution.py:577
  37.2 2.0 %collective-permute-start.13 = (bf16[2,208,384]{2,1,0:T(8,128)(2,1)S(1)}, bf16[2,208,384]{2,1,0:T(8,128)(2,1)S(1)}, u32[]{:S(2)}, u32[]{:S(2)}) collective-permute-start(bf16[2,208,384]{2,1,0:T(8,128)(2,1)S(1)} %get-tuple-element.64.rest_5_.own_ref), channel_id=1, source_target_pairs={{0,8},{2,10},{4,12},{6,14},{8,0},{10,2},{12,4},{14,6},{16,24},{18,... | collective-permute-start | bytes 958472 | tf_op jit(solution)/shard_map/ppermute | solution.py:577
  39.2 2.0 %collective-permute-start.14 = (bf16[2,208,384]{2,1,0:T(8,128)(2,1)S(1)}, bf16[2,208,384]{2,1,0:T(8,128)(2,1)S(1)}, u32[]{:S(2)}, u32[]{:S(2)}) collective-permute-start(bf16[2,208,384]{2,1,0:T(8,128)(2,1)S(1)} %get-tuple-element.64.rest_5_.own_ref), channel_id=1, source_target_pairs={{8,16},{10,18},{12,20},{14,22},{16,8},{18,10},{20,12},{22,14},{9,1... | collective-permute-start | bytes 958472 | tf_op jit(solution)/shard_map/ppermute | solution.py:577
  45.1 1.6 %collective-permute-done.13.rest_7_ = bf16[2,208,384]{2,1,0:T(8,128)(2,1)S(1)} collective-permute-done((bf16[2,208,384]{2,1,0:T(8,128)(2,1)S(1)}, bf16[2,208,384]{2,1,0:T(8,128)(2,1)S(1)}, u32[]{:S(2)}, u32[]{:S(2)}) %collective-permute-start.13) | collective-permute-done | bytes 319520 | tf_op jit(solution)/shard_map/ppermute | solution.py:577
  46.7 3.1 %collective-permute-done.14.rest_8_ = bf16[2,208,384]{2,1,0:T(8,128)(2,1)S(1)} collective-permute-done((bf16[2,208,384]{2,1,0:T(8,128)(2,1)S(1)}, bf16[2,208,384]{2,1,0:T(8,128)(2,1)S(1)}, u32[]{:S(2)}, u32[]{:S(2)}) %collective-permute-start.14) | collective-permute-done | bytes 319520 | tf_op jit(solution)/shard_map/ppermute | solution.py:577
  49.8 2.2 %collective-permute-start.19 = (bf16[2,208,384]{2,1,0:T(8,128)(2,1)S(1)}, bf16[2,208,384]{2,1,0:T(8,128)(2,1)S(1)}, u32[]{:S(2)}, u32[]{:S(2)}) collective-permute-start(bf16[2,208,384]{2,1,0:T(8,128)(2,1)S(1)} %collective-permute-done.13.rest_7_), channel_id=1, source_target_pairs={{8,16},{10,18},{12,20},{14,22},{16,8},{18,10},{20,12},{22,14},{9,1... | collective-permute-start | bytes 958472 | tf_op jit(solution)/shard_map/ppermute | solution.py:577
  55.9 3.6 %collective-permute-done.19 = bf16[2,208,384]{2,1,0:T(8,128)(2,1)S(1)} collective-permute-done((bf16[2,208,384]{2,1,0:T(8,128)(2,1)S(1)}, bf16[2,208,384]{2,1,0:T(8,128)(2,1)S(1)}, u32[]{:S(2)}, u32[]{:S(2)}) %collective-permute-start.19) | collective-permute-done | bytes 319520 | tf_op jit(solution)/shard_map/ppermute | solution.py:577
  59.5 1.6 %collective-permute-done.18.rest_6_ = bf16[2,208,384]{2,1,0:T(8,128)(2,1)S(1)} collective-permute-done((bf16[2,208,384]{2,1,0:T(8,128)(2,1)S(1)}, bf16[2,208,384]{2,1,0:T(8,128)(2,1)S(1)}, u32[]{:S(2)}, u32[]{:S(2)}) %collective-permute-start.18) | collective-permute-done | bytes 319520 | tf_op jit(solution)/shard_map/ppermute | solution.py:577
  61.1 3.6 %collective-permute-start.21 = (bf16[2,208,384]{2,1,0:T(8,128)(2,1)S(1)}, bf16[2,208,384]{2,1,0:T(8,128)(2,1)S(1)}, u32[]{:S(2)}, u32[]{:S(2)}) collective-permute-start(bf16[2,208,384]{2,1,0:T(8,128)(2,1)S(1)} %collective-permute-done.18.rest_6_), channel_id=1, source_target_pairs={{8,16},{10,18},{12,20},{14,22},{16,8},{18,10},{20,12},{22,14},{9,1... | collective-permute-start | bytes 958472 | tf_op jit(solution)/shard_map/ppermute | solution.py:577
  66.3 1.5 %queries.1 = (bf16[416,384]{1,0:T(8,128)(2,1)S(1)}, f32[416,128]{1,0:T(8,128)S(1)}, f32[8,384]{1,0:T(8,128)S(1)}, f32[8,384]{1,0:T(8,128)S(1)}) custom-call(s32[67]{0:T(128)S(1)} %pad_add_fusion.info_ref, bf16[2,208,384]{2,1,0:T(8,128)(2,1)S(1)} %collective-permute-done.17.other_ref, f32[3,8,128]{2,1,0:T(8,128)S(1)} %pad_maximum_fusion.3.stats_ref, ...), custom_call_target="tpu_custom_call" | custom-call | flops 1650000000 | tf_op jit(solution)/shard_map/queries/pallas_call | solution.py:633
  67.8 3.0 %attend_yours.2 = (bf16[1664,384]{1,0:T(8,128)(2,1)S(1)}, f32[416,128]{1,0:T(8,128)S(1)}, f32[416,128]{1,0:T(8,128)S(1)}, f32[416,384]{1,0:T(8,128)S(1)}) custom-call(s32[67]{0:T(128)S(1)} %pad_add_fusion.info_ref, f32[8,384]{1,0:T(8,128)S(1)} %get-tuple-element.52.rest_0_.means_ref, f32[8,384]{1,0:T(8,128)S(1)} %get-tuple-element.53.rest_1_.scales_ref, ...), custom_call_target="tpu_custom_call" | custom-call | flops 3960000000 | tf_op jit(solution)/shard_map/attend_yours/pallas_call | solution.py:633
  71.9 3.0 %attend_yours.3 = (bf16[1664,384]{1,0:T(8,128)(2,1)S(1)}, bf16[432,384]{1,0:T(8,128)(2,1)S(1)}) custom-call(s32[67]{0:T(128)S(1)} %pad_add_fusion.info_ref, f32[8,384]{1,0:T(8,128)S(1)} %get-tuple-element.52.rest_0_.means_ref, f32[8,384]{1,0:T(8,128)S(1)} %get-tuple-element.53.rest_1_.scales_ref, f32[1,384]{1,0:T(1,128)S(1)} %reshape.88.shift_ref.rest_2_, ...), custom_call_target="tpu_custom_call" | custom-call | flops 3960000000 | tf_op jit(solution)/shard_map/attend_yours/pallas_call | solution.py:633
  76.4 5.4 %attend_mine.1 = (f32[416,384]{1,0:T(8,128)S(1)}, f32[416,128]{1,0:T(8,128)S(1)}) custom-call(s32[67]{0:T(128)S(1)} %pad_add_fusion.info_ref, bf16[2,208,384]{2,1,0:T(8,128)(2,1)S(1)} %get-tuple-element.64.rest_5_.own_ref, f32[8,384]{1,0:T(8,128)S(1)} %get-tuple-element.52.rest_0_.means_ref, f32[8,384]{1,0:T(8,128)S(1)} %get-tuple-element.53.rest_1_.scales_ref, ...), custom_call_target="tpu_custom_call" | custom-call | flops 6600000000 | tf_op jit(solution)/shard_map/attend_mine/pallas_call | solution.py:633
  84.2 4.7 %collective-permute-start.25 = (bf16[1,104,384]{2,1,0:T(8,128)(2,1)S(1)}, bf16[1,104,384]{2,1,0:T(8,128)(2,1)S(1)}, u32[]{:S(2)}, u32[]{:S(2)}) collective-permute-start(bf16[1,104,384]{2,1,0:T(8,128)(2,1)S(1)} %get-tuple-element.69), channel_id=1, source_target_pairs={{2,4},{4,2},{6,8},{8,6},{10,12},{12,10},{14,16},{16,14},{18,20},{2... | collective-permute-start | bytes 239624 | tf_op jit(solution)/shard_map/ppermute | solution.py:785
  88.9 2.2 %upsample.1 = (bf16[6,208,192]{2,1,0:T(8,128)(2,1)S(1)}, f32[2,2,208,128]{3,2,1,0:T(8,128)S(1)}) custom-call(s32[67]{0:T(128)S(1)} %pad_add_fusion.info_ref, bf16[4,104,384]{2,1,0:T(8,128)(2,1)S(1)} %get-tuple-element.71.own_ref, bf16[2,2,2,192,768]{4,3,2,1,0:T(8,128)(2,1)S(1)} %fold.1.weight_ref, f32[1,192]{1,0:T(1,128)S(1)} %bitcast.13), custom_call_target="tpu_custom_call" | custom-call | flops 2200000000 | tf_op jit(solution)/shard_map/upsample/pallas_call | solution.py:633
  (91 shorter events, 30.1 us)
Async XLA Ops:
  0.9 8.6 %collective-permute-start = (bf16[1,104,384]{2,1,0:T(8,128)(2,1)S(1)}, bf16[1,104,384]{2,1,0:T(8,128)(2,1)S(1)}, u32[]{:S(2)}, u32[]{:S(2)}) collective-permute-start(bf16[1,104,384]{2,1,0:T(8,128)(2,1)S(1)} %get-tuple-element.87), channel_id=1, source_target_pairs={{2,4},{4,2},{6,8},{8,6},{10,12},{12,10},{14,16},{16,14},{18,20},{2... | collective-permute-start | bytes 239624 | tf_op jit(solution)/shard_map/ppermute | solution.py:651
  5.2 4.7 %collective-permute-start.1 = (bf16[1,104,384]{2,1,0:T(8,128)(2,1)S(1)}, bf16[1,104,384]{2,1,0:T(8,128)(2,1)S(1)}, u32[]{:S(2)}, u32[]{:S(2)}) collective-permute-start(bf16[1,104,384]{2,1,0:T(8,128)(2,1)S(1)} %get-tuple-element.86), channel_id=1, source_target_pairs={{0,2},{2,0},{4,6},{6,4},{8,10},{10,8},{12,14},{14,12},{16,18},{18,... | collective-permute-start | bytes 239624 | tf_op jit(solution)/shard_map/ppermute | solution.py:577
  9.9 6.1 %collective-permute-start.2 = (f32[3,8,128]{2,1,0:T(8,128)S(1)}, f32[3,8,128]{2,1,0:T(8,128)S(1)}, u32[]{:S(2)}, u32[]{:S(2)}) collective-permute-start(f32[3,8,128]{2,1,0:T(8,128)S(1)} %first_stats.1), channel_id=1, source_target_pairs={{0,8},{2,10},{4,12},{6,14},{8,0},{10,2},{12,4},{14,6},{16,24},{18,... | collective-permute-start | bytes 36872 | tf_op jit(solution)/shard_map/ppermute | solution.py:577
  10.1 6.0 %collective-permute-start.3 = (f32[3,8,128]{2,1,0:T(8,128)S(1)}, f32[3,8,128]{2,1,0:T(8,128)S(1)}, u32[]{:S(2)}, u32[]{:S(2)}) collective-permute-start(f32[3,8,128]{2,1,0:T(8,128)S(1)} %first_stats.1), channel_id=1, source_target_pairs={{0,16},{2,18},{4,20},{6,22},{8,24},{10,26},{12,28},{14,30},{16,0},... | collective-permute-start | bytes 36872 | tf_op jit(solution)/shard_map/ppermute | solution.py:577
  16.7 3.8 %collective-permute-start.5 = (f32[3,8,128]{2,1,0:T(8,128)S(1)}, f32[3,8,128]{2,1,0:T(8,128)S(1)}, u32[]{:S(2)}, u32[]{:S(2)}) collective-permute-start(f32[3,8,128]{2,1,0:T(8,128)S(1)} %pad_maximum_fusion), channel_id=1, source_target_pairs={{0,2},{2,0},{4,6},{6,4},{8,10},{10,8},{12,14},{14,12},{16,18},{18,... | collective-permute-start | bytes 36872 | tf_op jit(solution)/shard_map/ppermute | solution.py:577
  19.0 4.6 %collective-permute-start.7 = (f32[3,8,128]{2,1,0:T(8,128)S(1)}, f32[3,8,128]{2,1,0:T(8,128)S(1)}, u32[]{:S(2)}, u32[]{:S(2)}) collective-permute-start(f32[3,8,128]{2,1,0:T(8,128)S(1)} %pad_maximum_fusion), channel_id=1, source_target_pairs={{0,6},{2,4},{4,2},{6,0},{8,14},{10,12},{12,10},{14,8},{16,22},{18,... | collective-permute-start | bytes 36872 | tf_op jit(solution)/shard_map/ppermute | solution.py:577
  32.8 8.4 %collective-permute-start.10 = (f32[3,8,128]{2,1,0:T(8,128)S(1)}, f32[3,8,128]{2,1,0:T(8,128)S(1)}, u32[]{:S(2)}, u32[]{:S(2)}) collective-permute-start(f32[3,8,128]{2,1,0:T(8,128)S(1)} %get-tuple-element.47), channel_id=1, source_target_pairs={{0,16},{2,18},{4,20},{6,22},{8,24},{10,26},{12,28},{14,30},{16,0},... | collective-permute-start | bytes 36872 | tf_op jit(solution)/shard_map/ppermute | solution.py:577
  35.3 6.0 %collective-permute-start.11 = (f32[3,8,128]{2,1,0:T(8,128)S(1)}, f32[3,8,128]{2,1,0:T(8,128)S(1)}, u32[]{:S(2)}, u32[]{:S(2)}) collective-permute-start(f32[3,8,128]{2,1,0:T(8,128)S(1)} %get-tuple-element.47), channel_id=1, source_target_pairs={{0,24},{2,26},{4,28},{6,30},{8,16},{10,18},{12,20},{14,22},{16,8},... | collective-permute-start | bytes 36872 | tf_op jit(solution)/shard_map/ppermute | solution.py:577
  37.2 4.1 %collective-permute-start.9 = (f32[3,8,128]{2,1,0:T(8,128)S(1)}, f32[3,8,128]{2,1,0:T(8,128)S(1)}, u32[]{:S(2)}, u32[]{:S(2)}) collective-permute-start(f32[3,8,128]{2,1,0:T(8,128)S(1)} %get-tuple-element.47), channel_id=1, source_target_pairs={{0,8},{2,10},{4,12},{6,14},{8,0},{10,2},{12,4},{14,6},{16,24},{18,... | collective-permute-start | bytes 36872 | tf_op jit(solution)/shard_map/ppermute | solution.py:577
  37.2 9.5 %collective-permute-start.13 = (bf16[2,208,384]{2,1,0:T(8,128)(2,1)S(1)}, bf16[2,208,384]{2,1,0:T(8,128)(2,1)S(1)}, u32[]{:S(2)}, u32[]{:S(2)}) collective-permute-start(bf16[2,208,384]{2,1,0:T(8,128)(2,1)S(1)} %get-tuple-element.64.rest_5_.own_ref), channel_id=1, source_target_pairs={{0,8},{2,10},{4,12},{6,14},{8,0},{10,2},{12,4},{14,6},{16,24},{18,... | collective-permute-start | bytes 958472 | tf_op jit(solution)/shard_map/ppermute | solution.py:577
  39.2 10.6 %collective-permute-start.14 = (bf16[2,208,384]{2,1,0:T(8,128)(2,1)S(1)}, bf16[2,208,384]{2,1,0:T(8,128)(2,1)S(1)}, u32[]{:S(2)}, u32[]{:S(2)}) collective-permute-start(bf16[2,208,384]{2,1,0:T(8,128)(2,1)S(1)} %get-tuple-element.64.rest_5_.own_ref), channel_id=1, source_target_pairs={{8,16},{10,18},{12,20},{14,22},{16,8},{18,10},{20,12},{22,14},{9,1... | collective-permute-start | bytes 958472 | tf_op jit(solution)/shard_map/ppermute | solution.py:577
  41.3 3.8 %collective-permute-start.12 = (f32[3,8,128]{2,1,0:T(8,128)S(1)}, f32[3,8,128]{2,1,0:T(8,128)S(1)}, u32[]{:S(2)}, u32[]{:S(2)}) collective-permute-start(f32[3,8,128]{2,1,0:T(8,128)S(1)} %pad_maximum_fusion.2), channel_id=1, source_target_pairs={{0,2},{2,0},{4,6},{6,4},{8,10},{10,8},{12,14},{14,12},{16,18},{18,... | collective-permute-start | bytes 36872 | tf_op jit(solution)/shard_map/ppermute | solution.py:577
  42.8 10.5 %collective-permute-start.15 = (f32[3,8,128]{2,1,0:T(8,128)S(1)}, f32[3,8,128]{2,1,0:T(8,128)S(1)}, u32[]{:S(2)}, u32[]{:S(2)}) collective-permute-start(f32[3,8,128]{2,1,0:T(8,128)S(1)} %pad_maximum_fusion.2), channel_id=1, source_target_pairs={{0,4},{2,6},{4,0},{6,2},{8,12},{10,14},{12,8},{14,10},{16,20},{18,... | collective-permute-start | bytes 36872 | tf_op jit(solution)/shard_map/ppermute | solution.py:577
  43.7 9.6 %collective-permute-start.16 = (f32[3,8,128]{2,1,0:T(8,128)S(1)}, f32[3,8,128]{2,1,0:T(8,128)S(1)}, u32[]{:S(2)}, u32[]{:S(2)}) collective-permute-start(f32[3,8,128]{2,1,0:T(8,128)S(1)} %pad_maximum_fusion.2), channel_id=1, source_target_pairs={{0,6},{2,4},{4,2},{6,0},{8,14},{10,12},{12,10},{14,8},{16,22},{18,... | collective-permute-start | bytes 36872 | tf_op jit(solution)/shard_map/ppermute | solution.py:577
  49.8 9.6 %collective-permute-start.19 = (bf16[2,208,384]{2,1,0:T(8,128)(2,1)S(1)}, bf16[2,208,384]{2,1,0:T(8,128)(2,1)S(1)}, u32[]{:S(2)}, u32[]{:S(2)}) collective-permute-start(bf16[2,208,384]{2,1,0:T(8,128)(2,1)S(1)} %collective-permute-done.13.rest_7_), channel_id=1, source_target_pairs={{8,16},{10,18},{12,20},{14,22},{16,8},{18,10},{20,12},{22,14},{9,1... | collective-permute-start | bytes 958472 | tf_op jit(solution)/shard_map/ppermute | solution.py:577
  52.0 7.4 %collective-permute-start.20 = (bf16[2,208,384]{2,1,0:T(8,128)(2,1)S(1)}, bf16[2,208,384]{2,1,0:T(8,128)(2,1)S(1)}, u32[]{:S(2)}, u32[]{:S(2)}) collective-permute-start(bf16[2,208,384]{2,1,0:T(8,128)(2,1)S(1)} %collective-permute-done.14.rest_8_), channel_id=1, source_target_pairs={{8,0},{10,2},{12,4},{14,6},{16,24},{18,26},{20,28},{22,30},{9,1},{... | collective-permute-start | bytes 958472 | tf_op jit(solution)/shard_map/ppermute | solution.py:577
  53.4 7.7 %collective-permute-start.18 = (bf16[2,208,384]{2,1,0:T(8,128)(2,1)S(1)}, bf16[2,208,384]{2,1,0:T(8,128)(2,1)S(1)}, u32[]{:S(2)}, u32[]{:S(2)}) collective-permute-start(bf16[2,208,384]{2,1,0:T(8,128)(2,1)S(1)} %get-tuple-element.64.rest_5_.own_ref), channel_id=1, source_target_pairs={{0,4},{2,6},{4,0},{6,2},{8,12},{10,14},{12,8},{14,10},{16,20},{18,... | collective-permute-start | bytes 958472 | tf_op jit(solution)/shard_map/ppermute | solution.py:577
  54.8 11.4 %collective-permute-start.17 = (bf16[2,208,384]{2,1,0:T(8,128)(2,1)S(1)}, bf16[2,208,384]{2,1,0:T(8,128)(2,1)S(1)}, u32[]{:S(2)}, u32[]{:S(2)}) collective-permute-start(bf16[2,208,384]{2,1,0:T(8,128)(2,1)S(1)} %get-tuple-element.64.rest_5_.own_ref), channel_id=1, source_target_pairs={{0,2},{2,0},{4,6},{6,4},{8,10},{10,8},{12,14},{14,12},{16,18},{18,... | collective-permute-start | bytes 958472 | tf_op jit(solution)/shard_map/ppermute | solution.py:577
  61.1 9.7 %collective-permute-start.21 = (bf16[2,208,384]{2,1,0:T(8,128)(2,1)S(1)}, bf16[2,208,384]{2,1,0:T(8,128)(2,1)S(1)}, u32[]{:S(2)}, u32[]{:S(2)}) collective-permute-start(bf16[2,208,384]{2,1,0:T(8,128)(2,1)S(1)} %collective-permute-done.18.rest_6_), channel_id=1, source_target_pairs={{8,16},{10,18},{12,20},{14,22},{16,8},{18,10},{20,12},{22,14},{9,1... | collective-permute-start | bytes 958472 | tf_op jit(solution)/shard_map/ppermute | solution.py:577
  64.8 7.1 %collective-permute-start.22 = (bf16[2,208,384]{2,1,0:T(8,128)(2,1)S(1)}, bf16[2,208,384]{2,1,0:T(8,128)(2,1)S(1)}, u32[]{:S(2)}, u32[]{:S(2)}) collective-permute-start(bf16[2,208,384]{2,1,0:T(8,128)(2,1)S(1)} %collective-permute-done.18.rest_6_), channel_id=1, source_target_pairs={{0,8},{2,10},{4,12},{6,14},{8,0},{10,2},{12,4},{14,6},{16,24},{18,... | collective-permute-start | bytes 958472 | tf_op jit(solution)/shard_map/ppermute | solution.py:577
  64.8 7.1 %collective-permute-start.23 = (bf16[2,208,384]{2,1,0:T(8,128)(2,1)S(1)}, bf16[2,208,384]{2,1,0:T(8,128)(2,1)S(1)}, u32[]{:S(2)}, u32[]{:S(2)}) collective-permute-start(bf16[2,208,384]{2,1,0:T(8,128)(2,1)S(1)} %broadcast_select_fusion.rest_5_), channel_id=1, source_target_pairs={{0,4},{2,6},{4,0},{6,2},{8,12},{10,14},{12,8},{14,10},{16,20},{18,... | collective-permute-start | bytes 958472 | tf_op jit(solution)/shard_map/ppermute | solution.py:577
  74.9 7.4 %collective-permute-start.24 = (bf16[432,384]{1,0:T(8,128)(2,1)S(1)}, bf16[432,384]{1,0:T(8,128)(2,1)S(1)}, u32[]{:S(2)}, u32[]{:S(2)}) collective-permute-start(bf16[432,384]{1,0:T(8,128)(2,1)S(1)} %get-tuple-element.63), channel_id=1, source_target_pairs={{0,2},{2,0},{4,6},{6,4},{8,10},{10,8},{12,14},{14,12},{16,18},{18,... | collective-permute-start | bytes 995336 | tf_op jit(solution)/shard_map/ppermute | solution.py:755
  84.2 8.2 %collective-permute-start.25 = (bf16[1,104,384]{2,1,0:T(8,128)(2,1)S(1)}, bf16[1,104,384]{2,1,0:T(8,128)(2,1)S(1)}, u32[]{:S(2)}, u32[]{:S(2)}) collective-permute-start(bf16[1,104,384]{2,1,0:T(8,128)(2,1)S(1)} %get-tuple-element.69), channel_id=1, source_target_pairs={{2,4},{4,2},{6,8},{8,6},{10,12},{12,10},{14,16},{16,14},{18,20},{2... | collective-permute-start | bytes 239624 | tf_op jit(solution)/shard_map/ppermute | solution.py:785
  88.8 4.5 %collective-permute-start.26 = (bf16[1,104,384]{2,1,0:T(8,128)(2,1)S(1)}, bf16[1,104,384]{2,1,0:T(8,128)(2,1)S(1)}, u32[]{:S(2)}, u32[]{:S(2)}) collective-permute-start(bf16[1,104,384]{2,1,0:T(8,128)(2,1)S(1)} %get-tuple-element.70), channel_id=1, source_target_pairs={{0,2},{2,0},{4,6},{6,4},{8,10},{10,8},{12,14},{14,12},{16,18},{18,... | collective-permute-start | bytes 239624 | tf_op jit(solution)/shard_map/ppermute | solution.py:577
  (16 other events, 212.8 us)

commit v5 on v4

--- a/solution.py
+++ b/solution.py
@@ -56,17 +56,20 @@
 class Info:
     def __init__(self, ref, rows):
         self.ref, self.rows = ref, rows
-        self.videos = ref.shape[0] - 1 - rows
+        self.videos = ref.shape[0] - 2 - rows
 
     def tile(self):
         return self.ref[0]
 
+    def frame(self):
+        return self.ref[1]
+
     def label(self, row):
         inside = (row >= 0) & (row < self.rows)
-        return jnp.where(inside, self.ref[1 + jnp.clip(row, 0, self.rows - 1)], -1)
+        return jnp.where(inside, self.ref[2 + jnp.clip(row, 0, self.rows - 1)], -1)
 
     def width(self, label):
-        return jnp.where(label >= 0, self.ref[1 + self.rows + jnp.maximum(label, 0)], 0)
+        return jnp.where(label >= 0, self.ref[2 + self.rows + jnp.maximum(label, 0)], 0)
 
     def window(self, first, count):
         labels = [self.label(first + r) for r in range(count)]
@@ -199,28 +202,38 @@
 
 def conv_kernel(rows, taps, info_ref, *rest):
     hidden_refs, rest = rest[:taps], rest[taps:]
-    latents_ref, bias_ref, held_ref, own_ref, stats_ref, inputs_ref = rest
+    latents_ref, bias_ref, held_ref, own_ref, stats_ref, inputs_ref, product_ref = rest
     row_count, cols, channels = latents_ref.shape
     info = Info(info_ref, rows)
     padded = hidden_refs[0].shape[1]
     labels, widths = info.window(info.tile() * row_count - 1, row_count + 2)
-    for back, hidden_ref in enumerate(hidden_refs):
-        for tap in range(3):
-            lanes = slice((3 * back + tap) * channels, (3 * back + tap + 1) * channels)
-            for r in range(row_count):
-                block = hidden_ref[r + tap]
-                if tap != 1:
-                    same = labels[r + tap] == labels[r + 1]
-                    block = jnp.where(same, block, jnp.zeros_like(block))
-                inputs_ref[r * padded : (r + 1) * padded, lanes] = block
-    product = jnp.dot(inputs_ref[...], held_ref[...], preferred_element_type=F32)
+    for active in range(1, taps + 1):
+        frames = info.frame() + 1
+
+        @pl.when(frames == active if active < taps else frames >= active)
+        def _(active=active):
+            for back in range(active):
+                for tap in range(3):
+                    depth = 3 * back + tap
+                    lanes = slice(depth * channels, (depth + 1) * channels)
+                    for r in range(row_count):
+                        block = hidden_refs[back][r + tap]
+                        if tap != 1:
+                            same = labels[r + tap] == labels[r + 1]
+                            block = jnp.where(same, block, jnp.zeros_like(block))
+                        inputs_ref[r * padded : (r + 1) * padded, lanes] = block
+            deep = 3 * active * channels
+            product_ref[...] = jnp.dot(
+                inputs_ref[:, 0:deep], held_ref[0:deep, :], preferred_element_type=F32
+            )
+
     column = lax.broadcasted_iota(jnp.int32, (cols, 1), 0)
     cells = []
     for r in range(row_count):
         lines = slice(r * padded, (r + 1) * padded)
-        branch = pltpu.roll(product[lines, 0:channels], 1, 0)
-        branch = branch + product[lines, channels : 2 * channels]
-        branch = branch + pltpu.roll(product[lines, 2 * channels :], padded - 1, 0)
+        branch = pltpu.roll(product_ref[lines, 0:channels], 1, 0)
+        branch = branch + product_ref[lines, channels : 2 * channels]
+        branch = branch + pltpu.roll(product_ref[lines, 2 * channels :], padded - 1, 0)
         value = latents_ref[r].astype(F32) + branch[:cols] + bias_ref[...]
         value = jnp.where(column < widths[r + 1], value, 0.0).astype(BF16)
         cells.append(value.astype(F32))
@@ -480,6 +493,14 @@
         wide_ref[part, row, pl.ds(right, cols, 2), :] = piece
 
 
+def write_turned(out_ref, row, part, value, width):
+    channels, cols = out_ref.shape[1:]
+    lo, hi = part * LANES, min((part + 1) * LANES, channels)
+    turned = value.T[0 : hi - lo, 0:cols]
+    column = lax.broadcasted_iota(jnp.int32, (1, cols), 1)
+    out_ref[row, lo:hi, :] = jnp.where(column < width, turned, 0.0).astype(BF16)
+
+
 def phase_product(columns, weight):
     return lax.dot_general(
         columns, weight, (((1,), (1,)), ((), ())), preferred_element_type=F32
@@ -493,13 +514,11 @@
     row_count, cols, channels = own_ref.shape
     padded = columns_ref.shape[0] // row_count
     parts_out = wide_ref.shape[0]
-    out_channels = out_ref.shape[-1]
     labels, widths = info.window(info.tile() * row_count, row_count)
     build_columns(
         columns_ref, [functools.partial(own_ref.__getitem__, r) for r in range(row_count)]
     )
     inner_rows = (row_count - 1) * padded
-    wide_column = lax.broadcasted_iota(jnp.int32, (2 * cols, 1), 0)
     for down in range(2):
         for right in range(2):
             lanes = slice(right * channels, (right + 2) * channels)
@@ -521,11 +540,9 @@
         open_ref[part, 0] = wide_ref[part, 0]
         open_ref[part, 1] = wide_ref[part, 2 * row_count - 1]
     for r in range(1, 2 * row_count - 1):
-        valid = wide_column < 2 * widths[r // 2]
         for part in range(parts_out):
-            lo, hi = part * LANES, min((part + 1) * LANES, out_channels)
-            value = wide_ref[part, r, :, 0 : hi - lo] + bias_ref[:, lo:hi]
-            out_ref[r - 1, :, lo:hi] = jnp.where(valid, value, 0.0).astype(BF16)
+            value = wide_ref[part, r] + bias_ref[:, part * LANES : (part + 1) * LANES]
+            write_turned(out_ref, r - 1, part, value, 2 * widths[r // 2])
 
 
 def close_kernel(
@@ -533,14 +550,13 @@
     columns_ref, wide_ref,
 ):
     info = Info(info_ref, rows)
-    wide_rows, wide_cols, out_channels = out_ref.shape
+    wide_rows, _, wide_cols = out_ref.shape
     row_count, cols = wide_rows // 2, wide_cols // 2
     channels = outer_ref.shape[-1]
     padded = columns_ref.shape[0] // 2
     labels, widths = info.window(info.tile() * row_count - 1, row_count + 2)
     above, below = rims(info, outer_ref, inner_ref)
     build_columns(columns_ref, [lambda: above, lambda: below])
-    wide_column = lax.broadcasted_iota(jnp.int32, (wide_cols, 1), 0)
     for down in range(2):
         for right in range(2):
             lanes = slice(right * channels, (right + 2) * channels)
@@ -552,15 +568,12 @@
     out_ref[1 : wide_rows - 1] = middle_ref[...]
     for down in range(2):
         rim_row, own_row = (row_count + 1, row_count) if down else (0, 1)
-        valid = wide_column < 2 * widths[own_row]
         for part in range(wide_ref.shape[0]):
-            lo, hi = part * LANES, min((part + 1) * LANES, out_channels)
-            rim = jnp.where(
-                labels[rim_row] == labels[own_row], wide_ref[part, down, :, 0 : hi - lo], 0.0
+            rim = jnp.where(labels[rim_row] == labels[own_row], wide_ref[part, down], 0.0)
+            value = open_ref[part, down] + rim + bias_ref[:, part * LANES : (part + 1) * LANES]
+            write_turned(
+                out_ref, down * (wide_rows - 1), part, value, 2 * widths[own_row]
             )
-            value = open_ref[part, down, :, 0 : hi - lo] + rim + bias_ref[:, lo:hi]
-            value = jnp.where(valid, value, 0.0).astype(BF16)
-            out_ref[down * (wide_rows - 1), :, lo:hi] = value
 
 
 def merge_stats(mine, other):
@@ -620,7 +633,8 @@
     near_rows = row_count + 2
     source = latents.reshape(row_count, cols, channels)
     tile = lax.axis_index("tile").astype(jnp.int32)
-    info = jnp.concatenate([jnp.reshape(tile, (1,)), row_video, video_cols])
+    frame = lax.axis_index("frame").astype(jnp.int32)
+    info = jnp.concatenate([jnp.stack([tile, frame]), row_video, video_cols])
 
     def row(vector):
         return vector.reshape(1, -1)
@@ -691,6 +705,7 @@
         out_specs=(VMEM_SPEC, VMEM_SPEC),
         scratch_shapes=[
             pltpu.VMEM((row_count * padded, 3 * taps * channels), BF16),
+            pltpu.VMEM((row_count * padded, 3 * channels), F32),
         ],
         compiler_params=params(),
         cost_estimate=cost(2.5 * taps),
@@ -785,32 +800,34 @@
     outer = lax.ppermute(outer, "tile", outer_moves)
     inner = exchange(inner, tiles, 1)
     parts_out = -(-out_channels // LANES)
+    wide_cols = -(-2 * cols // LANES) * LANES
+    wide_bias = jnp.pad(row(upsample_bias), ((0, 0), (0, -out_channels % LANES)))
     middle, open_rows = call(
         functools.partial(upsample_kernel, rows),
-        [attended, folded, row(upsample_bias)],
+        [attended, folded, wide_bias],
         (
-            shape(2 * row_count - 2, 2 * cols, out_channels),
-            shape(parts_out, 2, 2 * cols, LANES, dtype=F32),
+            shape(2 * row_count - 2, out_channels, 2 * cols),
+            shape(parts_out, 2, wide_cols, LANES, dtype=F32),
         ),
         scratch=[
             pltpu.VMEM((row_count * padded, 3 * channels), BF16),
-            pltpu.VMEM((parts_out, 2 * row_count, 2 * cols, LANES), F32),
+            pltpu.VMEM((parts_out, 2 * row_count, wide_cols, LANES), F32),
         ],
         cost_estimate=cost(2.0),
         name="upsample",
     )
     decoded = call(
         functools.partial(close_kernel, rows),
-        [outer, inner, middle, open_rows, folded, row(upsample_bias)],
-        shape(2 * row_count, 2 * cols, out_channels),
+        [outer, inner, middle, open_rows, folded, wide_bias],
+        shape(2 * row_count, out_channels, 2 * cols),
         scratch=[
             pltpu.VMEM((2 * padded, 3 * channels), BF16),
-            pltpu.VMEM((parts_out, 2, 2 * cols, LANES), F32),
+            pltpu.VMEM((parts_out, 2, wide_cols, LANES), F32),
         ],
         cost_estimate=cost(1.0),
         name="close",
     )
-    return decoded.reshape(2 * row_count, 1, 2 * cols, out_channels)
+    return jnp.swapaxes(decoded, 1, 2).reshape(2 * row_count, 1, 2 * cols, out_channels)
 
 
 def solution(mesh):

time: 97.3 us -> 98.8 us (1.015)
  waiting for transfers between devices: 19.2 us -> 22.5 us
  local copies, waits for them, and re-layouts: 2.73 us -> 1.49 us
    ppermute x23, waiting for transfers between devices: 16.4 us -> 19.5 us  [exchange(): return lax.ppermute(array, 'tile', moves)]
    pallas_call x1, Pallas kernels: 5.04 us -> 3.74 us  [shards(): pl.pallas_call(functools.partial(conv_kernel, rows, taps), out_shape=(pai...]
    reshape x1 -> x0, local copies, waits for them, and re-layouts: 1.25 us -> none  [shards(): return decoded.reshape(2 * row_count, 1, 2 * cols, out_channels)]
  transfers between devices with their start and end apart: 27 -> 27, of which waited for: 15 -> 16; matrix products, arithmetic and copies ran while one was open for 1% -> 1% of each run, Pallas kernels for 18% -> 18%
where the time goes in v5:
time: 98.8 us; the launch traced here: 97.2 us
  starting transfers between devices  42.4 us (43%)
  Pallas kernels  28.5 us (29%)
  waiting for transfers between devices  22.5 us (23%)
  other arithmetic  1.9 us (2%)
  local copies, waits for them, and re-layouts  1.49 us (2%)
    ppermute x23, starting transfers between devices, exchange(): return lax.ppermute(array, 'tile', moves)  30.9 us
    pallas_call x9, Pallas kernels, call(): pl.pallas_call(kernel, out_shape=out_shape, in_specs=[SMEM_SPEC] + [VMEM_...  21.7 us
    ppermute x23, waiting for transfers between devices, exchange(): return lax.ppermute(array, 'tile', moves)  19.5 us
    ppermute x1, starting transfers between devices, shards(): outer = lax.ppermute(outer, 'tile', outer_moves)  4.4 us
    ppermute x1, starting transfers between devices, shards(): lax.ppermute(jnp.where(odd, source[row_count - 1:], source[:1]), 'tile',...  4.24 us
    pallas_call x1, Pallas kernels, shards(): pl.pallas_call(functools.partial(conv_kernel, rows, taps), out_shape=(pai...  3.74 us
    pallas_call x1, Pallas kernels, shards(): pl.pallas_call(functools.partial(hold_kernel, taps), out_shape=shape(3 *...  2.63 us
  transfers between devices with their start and end apart: 27, of which 16 were waited for; matrix products, arithmetic and copies ran while one was open for 1% of the time, Pallas kernels for 18%

profile of v5, /device:TPU:8, one launch (start us, length us, event | category | flops | bytes accessed | tf_op | source)
XLA Modules:
  0.0 97.2 jit_solution(11299208086033007850)
XLA Ops:
  0.9 4.2 %collective-permute-start = (bf16[1,104,384]{2,1,0:T(8,128)(2,1)S(1)}, bf16[1,104,384]{2,1,0:T(8,128)(2,1)S(1)}, u32[]{:S(2)}, u32[]{:S(2)}) collective-permute-start(bf16[1,104,384]{2,1,0:T(8,128)(2,1)S(1)} %get-tuple-element.87), channel_id=1, source_target_pairs={{2,4},{4,2},{6,8},{8,6},{10,12},{12,10},{14,16},{16,14},{18,20},{2... | collective-permute-start | bytes 239624 | tf_op jit(solution)/shard_map/ppermute | solution.py:665
  7.6 1.8 %first_stats.1 = f32[3,8,128]{2,1,0:T(8,128)S(1)} custom-call(s32[68]{0:T(128)S(1)} %pad_add_fusion.info_ref, bf16[4,104,384]{2,1,0:T(8,128)(2,1)S(1)} %bitcast.15), custom_call_target="tpu_custom_call" | custom-call | flops 1650000000 | tf_op jit(solution)/shard_map/first_stats/pallas_call | solution.py:647
  10.1 2.9 %collective-permute-start.3 = (f32[3,8,128]{2,1,0:T(8,128)S(1)}, f32[3,8,128]{2,1,0:T(8,128)S(1)}, u32[]{:S(2)}, u32[]{:S(2)}) collective-permute-start(f32[3,8,128]{2,1,0:T(8,128)S(1)} %first_stats.1), channel_id=1, source_target_pairs={{0,16},{2,18},{4,20},{6,22},{8,24},{10,26},{12,28},{14,30},{16,0},... | collective-permute-start | bytes 36872 | tf_op jit(solution)/shard_map/ppermute | solution.py:590
  13.4 2.6 %hold.1.rest_4_ = bf16[2304,1152]{1,0:T(8,128)(2,1)S(1)} custom-call(bf16[3,3,3,384,384]{4,3,2,1,0:T(8,128)(2,1)} %weight_ref.3), custom_call_target="tpu_custom_call" | custom-call | flops 3300000000 | tf_op jit(solution)/shard_map/hold/pallas_call | solution.py:671
  16.7 1.6 %collective-permute-start.5 = (f32[3,8,128]{2,1,0:T(8,128)S(1)}, f32[3,8,128]{2,1,0:T(8,128)S(1)}, u32[]{:S(2)}, u32[]{:S(2)}) collective-permute-start(f32[3,8,128]{2,1,0:T(8,128)S(1)} %pad_maximum_fusion), channel_id=1, source_target_pairs={{0,2},{2,0},{4,6},{6,4},{8,10},{10,8},{12,14},{14,12},{16,18},{18,... | collective-permute-start | bytes 36872 | tf_op jit(solution)/shard_map/ppermute | solution.py:590
  20.5 1.6 %collective-permute-done.6 = f32[3,8,128]{2,1,0:T(8,128)S(1)} collective-permute-done((f32[3,8,128]{2,1,0:T(8,128)S(1)}, f32[3,8,128]{2,1,0:T(8,128)S(1)}, u32[]{:S(2)}, u32[]{:S(2)}) %collective-permute-start.6) | collective-permute-done | bytes 12320 | tf_op jit(solution)/shard_map/ppermute | solution.py:590
  22.0 1.5 %collective-permute-done.7 = f32[3,8,128]{2,1,0:T(8,128)S(1)} collective-permute-done((f32[3,8,128]{2,1,0:T(8,128)S(1)}, f32[3,8,128]{2,1,0:T(8,128)S(1)}, u32[]{:S(2)}, u32[]{:S(2)}) %collective-permute-start.7) | collective-permute-done | bytes 12320 | tf_op jit(solution)/shard_map/ppermute | solution.py:590
  27.8 3.7 %conv.1 = (bf16[2,208,384]{2,1,0:T(8,128)(2,1)S(1)}, f32[3,8,128]{2,1,0:T(8,128)S(1)}) custom-call(s32[68]{0:T(128)S(1)} %pad_add_fusion.info_ref, bf16[6,112,384]{2,1,0:T(8,128)(2,1)S(1)} %get-tuple-element.44.rest_0_, bf16[6,112,384]{2,1,0:T(8,128)(2,1)S(1)} %collective-permute-done.8.rest_1_, bf16[4,104,384]{2,1,0:T(8,128)(2,1)S(1)} %get-tuple-element.45.rest_2_, ...), custom_call_target="tpu_custom_call" | custom-call | flops 5500000256 | tf_op jit(solution)/shard_map/conv/pallas_call | solution.py:701
  31.5 2.5 %collective-permute-start.10 = (f32[3,8,128]{2,1,0:T(8,128)S(1)}, f32[3,8,128]{2,1,0:T(8,128)S(1)}, u32[]{:S(2)}, u32[]{:S(2)}) collective-permute-start(f32[3,8,128]{2,1,0:T(8,128)S(1)} %get-tuple-element.47), channel_id=1, source_target_pairs={{0,16},{2,18},{4,20},{6,22},{8,24},{10,26},{12,28},{14,30},{16,0},... | collective-permute-start | bytes 36872 | tf_op jit(solution)/shard_map/ppermute | solution.py:590
  34.0 1.9 %collective-permute-start.11 = (f32[3,8,128]{2,1,0:T(8,128)S(1)}, f32[3,8,128]{2,1,0:T(8,128)S(1)}, u32[]{:S(2)}, u32[]{:S(2)}) collective-permute-start(f32[3,8,128]{2,1,0:T(8,128)S(1)} %get-tuple-element.47), channel_id=1, source_target_pairs={{0,24},{2,26},{4,28},{6,30},{8,16},{10,18},{12,20},{14,22},{16,8},... | collective-permute-start | bytes 36872 | tf_op jit(solution)/shard_map/ppermute | solution.py:590
  36.0 2.0 %collective-permute-start.13 = (bf16[2,208,384]{2,1,0:T(8,128)(2,1)S(1)}, bf16[2,208,384]{2,1,0:T(8,128)(2,1)S(1)}, u32[]{:S(2)}, u32[]{:S(2)}) collective-permute-start(bf16[2,208,384]{2,1,0:T(8,128)(2,1)S(1)} %get-tuple-element.64.rest_5_.own_ref), channel_id=1, source_target_pairs={{0,8},{2,10},{4,12},{6,14},{8,0},{10,2},{12,4},{14,6},{16,24},{18,... | collective-permute-start | bytes 958472 | tf_op jit(solution)/shard_map/ppermute | solution.py:590
  38.0 2.0 %collective-permute-start.14 = (bf16[2,208,384]{2,1,0:T(8,128)(2,1)S(1)}, bf16[2,208,384]{2,1,0:T(8,128)(2,1)S(1)}, u32[]{:S(2)}, u32[]{:S(2)}) collective-permute-start(bf16[2,208,384]{2,1,0:T(8,128)(2,1)S(1)} %get-tuple-element.64.rest_5_.own_ref), channel_id=1, source_target_pairs={{8,16},{10,18},{12,20},{14,22},{16,8},{18,10},{20,12},{22,14},{9,1... | collective-permute-start | bytes 958472 | tf_op jit(solution)/shard_map/ppermute | solution.py:590
  43.8 2.7 %collective-permute-done.13.rest_7_ = bf16[2,208,384]{2,1,0:T(8,128)(2,1)S(1)} collective-permute-done((bf16[2,208,384]{2,1,0:T(8,128)(2,1)S(1)}, bf16[2,208,384]{2,1,0:T(8,128)(2,1)S(1)}, u32[]{:S(2)}, u32[]{:S(2)}) %collective-permute-start.13) | collective-permute-done | bytes 319520 | tf_op jit(solution)/shard_map/ppermute | solution.py:590
  46.5 3.3 %collective-permute-done.14.rest_8_ = bf16[2,208,384]{2,1,0:T(8,128)(2,1)S(1)} collective-permute-done((bf16[2,208,384]{2,1,0:T(8,128)(2,1)S(1)}, bf16[2,208,384]{2,1,0:T(8,128)(2,1)S(1)}, u32[]{:S(2)}, u32[]{:S(2)}) %collective-permute-start.14) | collective-permute-done | bytes 319520 | tf_op jit(solution)/shard_map/ppermute | solution.py:590
  49.8 2.2 %collective-permute-start.19 = (bf16[2,208,384]{2,1,0:T(8,128)(2,1)S(1)}, bf16[2,208,384]{2,1,0:T(8,128)(2,1)S(1)}, u32[]{:S(2)}, u32[]{:S(2)}) collective-permute-start(bf16[2,208,384]{2,1,0:T(8,128)(2,1)S(1)} %collective-permute-done.13.rest_7_), channel_id=1, source_target_pairs={{8,16},{10,18},{12,20},{14,22},{16,8},{18,10},{20,12},{22,14},{9,1... | collective-permute-start | bytes 958472 | tf_op jit(solution)/shard_map/ppermute | solution.py:590
  55.9 5.0 %collective-permute-done.19 = bf16[2,208,384]{2,1,0:T(8,128)(2,1)S(1)} collective-permute-done((bf16[2,208,384]{2,1,0:T(8,128)(2,1)S(1)}, bf16[2,208,384]{2,1,0:T(8,128)(2,1)S(1)}, u32[]{:S(2)}, u32[]{:S(2)}) %collective-permute-start.19) | collective-permute-done | bytes 319520 | tf_op jit(solution)/shard_map/ppermute | solution.py:590
  60.9 1.6 %collective-permute-done.18.rest_6_ = bf16[2,208,384]{2,1,0:T(8,128)(2,1)S(1)} collective-permute-done((bf16[2,208,384]{2,1,0:T(8,128)(2,1)S(1)}, bf16[2,208,384]{2,1,0:T(8,128)(2,1)S(1)}, u32[]{:S(2)}, u32[]{:S(2)}) %collective-permute-start.18) | collective-permute-done | bytes 319520 | tf_op jit(solution)/shard_map/ppermute | solution.py:590
  62.5 3.7 %collective-permute-start.21 = (bf16[2,208,384]{2,1,0:T(8,128)(2,1)S(1)}, bf16[2,208,384]{2,1,0:T(8,128)(2,1)S(1)}, u32[]{:S(2)}, u32[]{:S(2)}) collective-permute-start(bf16[2,208,384]{2,1,0:T(8,128)(2,1)S(1)} %collective-permute-done.18.rest_6_), channel_id=1, source_target_pairs={{8,16},{10,18},{12,20},{14,22},{16,8},{18,10},{20,12},{22,14},{9,1... | collective-permute-start | bytes 958472 | tf_op jit(solution)/shard_map/ppermute | solution.py:590
  69.2 3.0 %attend_yours.2 = (bf16[1664,384]{1,0:T(8,128)(2,1)S(1)}, f32[416,128]{1,0:T(8,128)S(1)}, f32[416,128]{1,0:T(8,128)S(1)}, f32[416,384]{1,0:T(8,128)S(1)}) custom-call(s32[68]{0:T(128)S(1)} %pad_add_fusion.info_ref, f32[8,384]{1,0:T(8,128)S(1)} %get-tuple-element.52.rest_0_.means_ref, f32[8,384]{1,0:T(8,128)S(1)} %get-tuple-element.53.rest_1_.scales_ref, ...), custom_call_target="tpu_custom_call" | custom-call | flops 3960000000 | tf_op jit(solution)/shard_map/attend_yours/pallas_call | solution.py:647
  74.0 3.0 %attend_yours.3 = (bf16[1664,384]{1,0:T(8,128)(2,1)S(1)}, bf16[432,384]{1,0:T(8,128)(2,1)S(1)}) custom-call(s32[68]{0:T(128)S(1)} %pad_add_fusion.info_ref, f32[8,384]{1,0:T(8,128)S(1)} %get-tuple-element.52.rest_0_.means_ref, f32[8,384]{1,0:T(8,128)S(1)} %get-tuple-element.53.rest_1_.scales_ref, f32[1,384]{1,0:T(1,128)S(1)} %reshape.83.shift_ref.rest_2_, ...), custom_call_target="tpu_custom_call" | custom-call | flops 3960000000 | tf_op jit(solution)/shard_map/attend_yours/pallas_call | solution.py:647
  78.5 5.4 %attend_mine.1 = (f32[416,384]{1,0:T(8,128)S(1)}, f32[416,128]{1,0:T(8,128)S(1)}) custom-call(s32[68]{0:T(128)S(1)} %pad_add_fusion.info_ref, bf16[2,208,384]{2,1,0:T(8,128)(2,1)S(1)} %get-tuple-element.64.rest_5_.own_ref, f32[8,384]{1,0:T(8,128)S(1)} %get-tuple-element.52.rest_0_.means_ref, f32[8,384]{1,0:T(8,128)S(1)} %get-tuple-element.53.rest_1_.scales_ref, ...), custom_call_target="tpu_custom_call" | custom-call | flops 6600000000 | tf_op jit(solution)/shard_map/attend_mine/pallas_call | solution.py:647
  86.2 4.4 %collective-permute-start.25 = (bf16[1,104,384]{2,1,0:T(8,128)(2,1)S(1)}, bf16[1,104,384]{2,1,0:T(8,128)(2,1)S(1)}, u32[]{:S(2)}, u32[]{:S(2)}) collective-permute-start(bf16[1,104,384]{2,1,0:T(8,128)(2,1)S(1)} %get-tuple-element.69), channel_id=1, source_target_pairs={{2,4},{4,2},{6,8},{8,6},{10,12},{12,10},{14,16},{16,14},{18,20},{2... | collective-permute-start | bytes 239624 | tf_op jit(solution)/shard_map/ppermute | solution.py:800
  90.7 2.2 %upsample.1 = (bf16[6,192,208]{2,1,0:T(8,128)(2,1)S(1)}, f32[2,2,256,128]{3,2,1,0:T(8,128)S(1)}) custom-call(s32[68]{0:T(128)S(1)} %pad_add_fusion.info_ref, bf16[4,104,384]{2,1,0:T(8,128)(2,1)S(1)} %get-tuple-element.71.own_ref, bf16[2,2,2,192,768]{4,3,2,1,0:T(8,128)(2,1)S(1)} %fold.1.weight_ref, f32[1,256]{1,0:T(1,128)S(1)} %pad.4.bias_ref), custom_call_target="tpu_custom_call" | custom-call | flops 2200000000 | tf_op jit(solution)/shard_map/upsample/pallas_call | solution.py:647
  95.1 2.1 %close.1 = bf16[8,192,208]{2,1,0:T(8,128)(2,1)} custom-call(s32[68]{0:T(128)S(1)} %pad_add_fusion.info_ref, bf16[1,104,384]{2,1,0:T(8,128)(2,1)S(1)} %collective-permute-done.25.outer_ref, bf16[1,104,384]{2,1,0:T(8,128)(2,1)S(1)} %collective-permute-done.26.inner_ref, bf16[6,192,208]{2,1,0:T(8,128)(2,1)S(1)} %get-tuple-element.73.middle_ref, ...), custom_call_target="tpu_custom_call" | custom-call | flops 1100000000 | tf_op jit(solution)/shard_map/close/pallas_call | solution.py:647
  (91 shorter events, 30.0 us)
Async XLA Ops:
  0.9 8.6 %collective-permute-start = (bf16[1,104,384]{2,1,0:T(8,128)(2,1)S(1)}, bf16[1,104,384]{2,1,0:T(8,128)(2,1)S(1)}, u32[]{:S(2)}, u32[]{:S(2)}) collective-permute-start(bf16[1,104,384]{2,1,0:T(8,128)(2,1)S(1)} %get-tuple-element.87), channel_id=1, source_target_pairs={{2,4},{4,2},{6,8},{8,6},{10,12},{12,10},{14,16},{16,14},{18,20},{2... | collective-permute-start | bytes 239624 | tf_op jit(solution)/shard_map/ppermute | solution.py:665
  5.2 4.7 %collective-permute-start.1 = (bf16[1,104,384]{2,1,0:T(8,128)(2,1)S(1)}, bf16[1,104,384]{2,1,0:T(8,128)(2,1)S(1)}, u32[]{:S(2)}, u32[]{:S(2)}) collective-permute-start(bf16[1,104,384]{2,1,0:T(8,128)(2,1)S(1)} %get-tuple-element.86), channel_id=1, source_target_pairs={{0,2},{2,0},{4,6},{6,4},{8,10},{10,8},{12,14},{14,12},{16,18},{18,... | collective-permute-start | bytes 239624 | tf_op jit(solution)/shard_map/ppermute | solution.py:590
  9.9 6.1 %collective-permute-start.2 = (f32[3,8,128]{2,1,0:T(8,128)S(1)}, f32[3,8,128]{2,1,0:T(8,128)S(1)}, u32[]{:S(2)}, u32[]{:S(2)}) collective-permute-start(f32[3,8,128]{2,1,0:T(8,128)S(1)} %first_stats.1), channel_id=1, source_target_pairs={{0,8},{2,10},{4,12},{6,14},{8,0},{10,2},{12,4},{14,6},{16,24},{18,... | collective-permute-start | bytes 36872 | tf_op jit(solution)/shard_map/ppermute | solution.py:590
  10.1 6.0 %collective-permute-start.3 = (f32[3,8,128]{2,1,0:T(8,128)S(1)}, f32[3,8,128]{2,1,0:T(8,128)S(1)}, u32[]{:S(2)}, u32[]{:S(2)}) collective-permute-start(f32[3,8,128]{2,1,0:T(8,128)S(1)} %first_stats.1), channel_id=1, source_target_pairs={{0,16},{2,18},{4,20},{6,22},{8,24},{10,26},{12,28},{14,30},{16,0},... | collective-permute-start | bytes 36872 | tf_op jit(solution)/shard_map/ppermute | solution.py:590
  16.7 3.8 %collective-permute-start.5 = (f32[3,8,128]{2,1,0:T(8,128)S(1)}, f32[3,8,128]{2,1,0:T(8,128)S(1)}, u32[]{:S(2)}, u32[]{:S(2)}) collective-permute-start(f32[3,8,128]{2,1,0:T(8,128)S(1)} %pad_maximum_fusion), channel_id=1, source_target_pairs={{0,2},{2,0},{4,6},{6,4},{8,10},{10,8},{12,14},{14,12},{16,18},{18,... | collective-permute-start | bytes 36872 | tf_op jit(solution)/shard_map/ppermute | solution.py:590
  19.0 4.6 %collective-permute-start.7 = (f32[3,8,128]{2,1,0:T(8,128)S(1)}, f32[3,8,128]{2,1,0:T(8,128)S(1)}, u32[]{:S(2)}, u32[]{:S(2)}) collective-permute-start(f32[3,8,128]{2,1,0:T(8,128)S(1)} %pad_maximum_fusion), channel_id=1, source_target_pairs={{0,6},{2,4},{4,2},{6,0},{8,14},{10,12},{12,10},{14,8},{16,22},{18,... | collective-permute-start | bytes 36872 | tf_op jit(solution)/shard_map/ppermute | solution.py:590
  31.5 8.4 %collective-permute-start.10 = (f32[3,8,128]{2,1,0:T(8,128)S(1)}, f32[3,8,128]{2,1,0:T(8,128)S(1)}, u32[]{:S(2)}, u32[]{:S(2)}) collective-permute-start(f32[3,8,128]{2,1,0:T(8,128)S(1)} %get-tuple-element.47), channel_id=1, source_target_pairs={{0,16},{2,18},{4,20},{6,22},{8,24},{10,26},{12,28},{14,30},{16,0},... | collective-permute-start | bytes 36872 | tf_op jit(solution)/shard_map/ppermute | solution.py:590
  34.0 6.0 %collective-permute-start.11 = (f32[3,8,128]{2,1,0:T(8,128)S(1)}, f32[3,8,128]{2,1,0:T(8,128)S(1)}, u32[]{:S(2)}, u32[]{:S(2)}) collective-permute-start(f32[3,8,128]{2,1,0:T(8,128)S(1)} %get-tuple-element.47), channel_id=1, source_target_pairs={{0,24},{2,26},{4,28},{6,30},{8,16},{10,18},{12,20},{14,22},{16,8},... | collective-permute-start | bytes 36872 | tf_op jit(solution)/shard_map/ppermute | solution.py:590
  35.9 4.1 %collective-permute-start.9 = (f32[3,8,128]{2,1,0:T(8,128)S(1)}, f32[3,8,128]{2,1,0:T(8,128)S(1)}, u32[]{:S(2)}, u32[]{:S(2)}) collective-permute-start(f32[3,8,128]{2,1,0:T(8,128)S(1)} %get-tuple-element.47), channel_id=1, source_target_pairs={{0,8},{2,10},{4,12},{6,14},{8,0},{10,2},{12,4},{14,6},{16,24},{18,... | collective-permute-start | bytes 36872 | tf_op jit(solution)/shard_map/ppermute | solution.py:590
  36.0 10.5 %collective-permute-start.13 = (bf16[2,208,384]{2,1,0:T(8,128)(2,1)S(1)}, bf16[2,208,384]{2,1,0:T(8,128)(2,1)S(1)}, u32[]{:S(2)}, u32[]{:S(2)}) collective-permute-start(bf16[2,208,384]{2,1,0:T(8,128)(2,1)S(1)} %get-tuple-element.64.rest_5_.own_ref), channel_id=1, source_target_pairs={{0,8},{2,10},{4,12},{6,14},{8,0},{10,2},{12,4},{14,6},{16,24},{18,... | collective-permute-start | bytes 958472 | tf_op jit(solution)/shard_map/ppermute | solution.py:590
  38.0 11.8 %collective-permute-start.14 = (bf16[2,208,384]{2,1,0:T(8,128)(2,1)S(1)}, bf16[2,208,384]{2,1,0:T(8,128)(2,1)S(1)}, u32[]{:S(2)}, u32[]{:S(2)}) collective-permute-start(bf16[2,208,384]{2,1,0:T(8,128)(2,1)S(1)} %get-tuple-element.64.rest_5_.own_ref), channel_id=1, source_target_pairs={{8,16},{10,18},{12,20},{14,22},{16,8},{18,10},{20,12},{22,14},{9,1... | collective-permute-start | bytes 958472 | tf_op jit(solution)/shard_map/ppermute | solution.py:590
  40.1 3.8 %collective-permute-start.12 = (f32[3,8,128]{2,1,0:T(8,128)S(1)}, f32[3,8,128]{2,1,0:T(8,128)S(1)}, u32[]{:S(2)}, u32[]{:S(2)}) collective-permute-start(f32[3,8,128]{2,1,0:T(8,128)S(1)} %pad_maximum_fusion.2), channel_id=1, source_target_pairs={{0,2},{2,0},{4,6},{6,4},{8,10},{10,8},{12,14},{14,12},{16,18},{18,... | collective-permute-start | bytes 36872 | tf_op jit(solution)/shard_map/ppermute | solution.py:590
  41.6 11.8 %collective-permute-start.15 = (f32[3,8,128]{2,1,0:T(8,128)S(1)}, f32[3,8,128]{2,1,0:T(8,128)S(1)}, u32[]{:S(2)}, u32[]{:S(2)}) collective-permute-start(f32[3,8,128]{2,1,0:T(8,128)S(1)} %pad_maximum_fusion.2), channel_id=1, source_target_pairs={{0,4},{2,6},{4,0},{6,2},{8,12},{10,14},{12,8},{14,10},{16,20},{18,... | collective-permute-start | bytes 36872 | tf_op jit(solution)/shard_map/ppermute | solution.py:590
  42.5 10.9 %collective-permute-start.16 = (f32[3,8,128]{2,1,0:T(8,128)S(1)}, f32[3,8,128]{2,1,0:T(8,128)S(1)}, u32[]{:S(2)}, u32[]{:S(2)}) collective-permute-start(f32[3,8,128]{2,1,0:T(8,128)S(1)} %pad_maximum_fusion.2), channel_id=1, source_target_pairs={{0,6},{2,4},{4,2},{6,0},{8,14},{10,12},{12,10},{14,8},{16,22},{18,... | collective-permute-start | bytes 36872 | tf_op jit(solution)/shard_map/ppermute | solution.py:590
  49.8 11.1 %collective-permute-start.19 = (bf16[2,208,384]{2,1,0:T(8,128)(2,1)S(1)}, bf16[2,208,384]{2,1,0:T(8,128)(2,1)S(1)}, u32[]{:S(2)}, u32[]{:S(2)}) collective-permute-start(bf16[2,208,384]{2,1,0:T(8,128)(2,1)S(1)} %collective-permute-done.13.rest_7_), channel_id=1, source_target_pairs={{8,16},{10,18},{12,20},{14,22},{16,8},{18,10},{20,12},{22,14},{9,1... | collective-permute-start | bytes 958472 | tf_op jit(solution)/shard_map/ppermute | solution.py:590
  52.0 8.9 %collective-permute-start.20 = (bf16[2,208,384]{2,1,0:T(8,128)(2,1)S(1)}, bf16[2,208,384]{2,1,0:T(8,128)(2,1)S(1)}, u32[]{:S(2)}, u32[]{:S(2)}) collective-permute-start(bf16[2,208,384]{2,1,0:T(8,128)(2,1)S(1)} %collective-permute-done.14.rest_8_), channel_id=1, source_target_pairs={{8,0},{10,2},{12,4},{14,6},{16,24},{18,26},{20,28},{22,30},{9,1},{... | collective-permute-start | bytes 958472 | tf_op jit(solution)/shard_map/ppermute | solution.py:590
  53.4 9.1 %collective-permute-start.18 = (bf16[2,208,384]{2,1,0:T(8,128)(2,1)S(1)}, bf16[2,208,384]{2,1,0:T(8,128)(2,1)S(1)}, u32[]{:S(2)}, u32[]{:S(2)}) collective-permute-start(bf16[2,208,384]{2,1,0:T(8,128)(2,1)S(1)} %get-tuple-element.64.rest_5_.own_ref), channel_id=1, source_target_pairs={{0,4},{2,6},{4,0},{6,2},{8,12},{10,14},{12,8},{14,10},{16,20},{18,... | collective-permute-start | bytes 958472 | tf_op jit(solution)/shard_map/ppermute | solution.py:590
  54.8 12.9 %collective-permute-start.17 = (bf16[2,208,384]{2,1,0:T(8,128)(2,1)S(1)}, bf16[2,208,384]{2,1,0:T(8,128)(2,1)S(1)}, u32[]{:S(2)}, u32[]{:S(2)}) collective-permute-start(bf16[2,208,384]{2,1,0:T(8,128)(2,1)S(1)} %get-tuple-element.64.rest_5_.own_ref), channel_id=1, source_target_pairs={{0,2},{2,0},{4,6},{6,4},{8,10},{10,8},{12,14},{14,12},{16,18},{18,... | collective-permute-start | bytes 958472 | tf_op jit(solution)/shard_map/ppermute | solution.py:590
  62.5 10.0 %collective-permute-start.21 = (bf16[2,208,384]{2,1,0:T(8,128)(2,1)S(1)}, bf16[2,208,384]{2,1,0:T(8,128)(2,1)S(1)}, u32[]{:S(2)}, u32[]{:S(2)}) collective-permute-start(bf16[2,208,384]{2,1,0:T(8,128)(2,1)S(1)} %collective-permute-done.18.rest_6_), channel_id=1, source_target_pairs={{8,16},{10,18},{12,20},{14,22},{16,8},{18,10},{20,12},{22,14},{9,1... | collective-permute-start | bytes 958472 | tf_op jit(solution)/shard_map/ppermute | solution.py:590
  66.2 7.8 %collective-permute-start.22 = (bf16[2,208,384]{2,1,0:T(8,128)(2,1)S(1)}, bf16[2,208,384]{2,1,0:T(8,128)(2,1)S(1)}, u32[]{:S(2)}, u32[]{:S(2)}) collective-permute-start(bf16[2,208,384]{2,1,0:T(8,128)(2,1)S(1)} %collective-permute-done.18.rest_6_), channel_id=1, source_target_pairs={{0,8},{2,10},{4,12},{6,14},{8,0},{10,2},{12,4},{14,6},{16,24},{18,... | collective-permute-start | bytes 958472 | tf_op jit(solution)/shard_map/ppermute | solution.py:590
  66.2 7.8 %collective-permute-start.23 = (bf16[2,208,384]{2,1,0:T(8,128)(2,1)S(1)}, bf16[2,208,384]{2,1,0:T(8,128)(2,1)S(1)}, u32[]{:S(2)}, u32[]{:S(2)}) collective-permute-start(bf16[2,208,384]{2,1,0:T(8,128)(2,1)S(1)} %broadcast_select_fusion.rest_5_), channel_id=1, source_target_pairs={{0,4},{2,6},{4,0},{6,2},{8,12},{10,14},{12,8},{14,10},{16,20},{18,... | collective-permute-start | bytes 958472 | tf_op jit(solution)/shard_map/ppermute | solution.py:590
  77.0 7.4 %collective-permute-start.24 = (bf16[432,384]{1,0:T(8,128)(2,1)S(1)}, bf16[432,384]{1,0:T(8,128)(2,1)S(1)}, u32[]{:S(2)}, u32[]{:S(2)}) collective-permute-start(bf16[432,384]{1,0:T(8,128)(2,1)S(1)} %get-tuple-element.63), channel_id=1, source_target_pairs={{0,2},{2,0},{4,6},{6,4},{8,10},{10,8},{12,14},{14,12},{16,18},{18,... | collective-permute-start | bytes 995336 | tf_op jit(solution)/shard_map/ppermute | solution.py:770
  86.2 8.2 %collective-permute-start.25 = (bf16[1,104,384]{2,1,0:T(8,128)(2,1)S(1)}, bf16[1,104,384]{2,1,0:T(8,128)(2,1)S(1)}, u32[]{:S(2)}, u32[]{:S(2)}) collective-permute-start(bf16[1,104,384]{2,1,0:T(8,128)(2,1)S(1)} %get-tuple-element.69), channel_id=1, source_target_pairs={{2,4},{4,2},{6,8},{8,6},{10,12},{12,10},{14,16},{16,14},{18,20},{2... | collective-permute-start | bytes 239624 | tf_op jit(solution)/shard_map/ppermute | solution.py:800
  90.7 4.5 %collective-permute-start.26 = (bf16[1,104,384]{2,1,0:T(8,128)(2,1)S(1)}, bf16[1,104,384]{2,1,0:T(8,128)(2,1)S(1)}, u32[]{:S(2)}, u32[]{:S(2)}) collective-permute-start(bf16[1,104,384]{2,1,0:T(8,128)(2,1)S(1)} %get-tuple-element.70), channel_id=1, source_target_pairs={{0,2},{2,0},{4,6},{6,4},{8,10},{10,8},{12,14},{14,12},{16,18},{18,... | collective-permute-start | bytes 239624 | tf_op jit(solution)/shard_map/ppermute | solution.py:590
  (16 other events, 236.1 us)

commit v6 on v5

--- a/solution.py
+++ b/solution.py
@@ -56,20 +56,17 @@
 class Info:
     def __init__(self, ref, rows):
         self.ref, self.rows = ref, rows
-        self.videos = ref.shape[0] - 2 - rows
+        self.videos = ref.shape[0] - 1 - rows
 
     def tile(self):
         return self.ref[0]
 
-    def frame(self):
-        return self.ref[1]
-
     def label(self, row):
         inside = (row >= 0) & (row < self.rows)
-        return jnp.where(inside, self.ref[2 + jnp.clip(row, 0, self.rows - 1)], -1)
+        return jnp.where(inside, self.ref[1 + jnp.clip(row, 0, self.rows - 1)], -1)
 
     def width(self, label):
-        return jnp.where(label >= 0, self.ref[2 + self.rows + jnp.maximum(label, 0)], 0)
+        return jnp.where(label >= 0, self.ref[1 + self.rows + jnp.maximum(label, 0)], 0)
 
     def window(self, first, count):
         labels = [self.label(first + r) for r in range(count)]
@@ -200,40 +197,50 @@
         copy.wait()
 
 
+def row_taps(info, hidden_refs, inputs_ref):
+    near_rows, padded, channels = hidden_refs[0].shape
+    row_count = near_rows - 2
+    labels, _ = info.window(info.tile() * row_count - 1, near_rows)
+    for back, hidden_ref in enumerate(hidden_refs):
+        for tap in range(3):
+            lanes = slice((3 * back + tap) * channels, (3 * back + tap + 1) * channels)
+            for r in range(row_count):
+                block = hidden_ref[r + tap]
+                if tap != 1:
+                    same = labels[r + tap] == labels[r + 1]
+                    block = jnp.where(same, block, jnp.zeros_like(block))
+                inputs_ref[r * padded : (r + 1) * padded, lanes] = block
+
+
+def own_conv_kernel(rows, info_ref, hidden_ref, held_ref, product_ref, inputs_ref):
+    row_taps(Info(info_ref, rows), [hidden_ref], inputs_ref)
+    depth = inputs_ref.shape[1]
+    product_ref[...] = jnp.dot(
+        inputs_ref[...], held_ref[0:depth, :], preferred_element_type=F32
+    )
+
+
 def conv_kernel(rows, taps, info_ref, *rest):
-    hidden_refs, rest = rest[:taps], rest[taps:]
-    latents_ref, bias_ref, held_ref, own_ref, stats_ref, inputs_ref, product_ref = rest
+    hidden_refs, rest = rest[: taps - 1], rest[taps - 1 :]
+    product_ref, latents_ref, bias_ref, held_ref, own_ref, stats_ref, *inputs_refs = rest
     row_count, cols, channels = latents_ref.shape
     info = Info(info_ref, rows)
-    padded = hidden_refs[0].shape[1]
+    padded = product_ref.shape[0] // row_count
     labels, widths = info.window(info.tile() * row_count - 1, row_count + 2)
-    for active in range(1, taps + 1):
-        frames = info.frame() + 1
-
-        @pl.when(frames == active if active < taps else frames >= active)
-        def _(active=active):
-            for back in range(active):
-                for tap in range(3):
-                    depth = 3 * back + tap
-                    lanes = slice(depth * channels, (depth + 1) * channels)
-                    for r in range(row_count):
-                        block = hidden_refs[back][r + tap]
-                        if tap != 1:
-                            same = labels[r + tap] == labels[r + 1]
-                            block = jnp.where(same, block, jnp.zeros_like(block))
-                        inputs_ref[r * padded : (r + 1) * padded, lanes] = block
-            deep = 3 * active * channels
-            product_ref[...] = jnp.dot(
-                inputs_ref[:, 0:deep], held_ref[0:deep, :], preferred_element_type=F32
-            )
-
+    product = product_ref[...]
+    if hidden_refs:
+        (inputs_ref,) = inputs_refs
+        row_taps(info, hidden_refs, inputs_ref)
+        product = product + jnp.dot(
+            inputs_ref[...], held_ref[3 * channels :, :], preferred_element_type=F32
+        )
     column = lax.broadcasted_iota(jnp.int32, (cols, 1), 0)
     cells = []
     for r in range(row_count):
         lines = slice(r * padded, (r + 1) * padded)
-        branch = pltpu.roll(product_ref[lines, 0:channels], 1, 0)
-        branch = branch + product_ref[lines, channels : 2 * channels]
-        branch = branch + pltpu.roll(product_ref[lines, 2 * channels :], padded - 1, 0)
+        branch = pltpu.roll(product[lines, 0:channels], 1, 0)
+        branch = branch + product[lines, channels : 2 * channels]
+        branch = branch + pltpu.roll(product[lines, 2 * channels :], padded - 1, 0)
         value = latents_ref[r].astype(F32) + branch[:cols] + bias_ref[...]
         value = jnp.where(column < widths[r + 1], value, 0.0).astype(BF16)
         cells.append(value.astype(F32))
@@ -633,8 +640,7 @@
     near_rows = row_count + 2
     source = latents.reshape(row_count, cols, channels)
     tile = lax.axis_index("tile").astype(jnp.int32)
-    frame = lax.axis_index("frame").astype(jnp.int32)
-    info = jnp.concatenate([jnp.stack([tile, frame]), row_video, video_cols])
+    info = jnp.concatenate([jnp.reshape(tile, (1,)), row_video, video_cols])
 
     def row(vector):
         return vector.reshape(1, -1)
@@ -691,26 +697,29 @@
         name="hidden",
     )
 
-    context = [hidden] + [
+    earlier = [
         lax.ppermute(hidden, "frame", [(i, i + by) for i in range(frames - by)])
         for by in range(1, taps)
     ]
-
     pairs = row_count // 2
     pair_shape = shape(pairs, 2 * cols, channels)
-    own, stats = pl.pallas_call(
+    product = call(
+        functools.partial(own_conv_kernel, rows),
+        [hidden, held],
+        shape(row_count * padded, 3 * channels, dtype=F32),
+        scratch=[pltpu.VMEM((row_count * padded, 3 * channels), BF16)],
+        cost_estimate=cost(2.2),
+        name="own_conv",
+    )
+    scratch = [pltpu.VMEM((row_count * padded, 3 * (taps - 1) * channels), BF16)]
+    own, stats = call(
         functools.partial(conv_kernel, rows, taps),
-        out_shape=(pair_shape, stats_shape),
-        in_specs=[SMEM_SPEC] + [VMEM_SPEC] * (taps + 3),
-        out_specs=(VMEM_SPEC, VMEM_SPEC),
-        scratch_shapes=[
-            pltpu.VMEM((row_count * padded, 3 * taps * channels), BF16),
-            pltpu.VMEM((row_count * padded, 3 * channels), F32),
-        ],
-        compiler_params=params(),
-        cost_estimate=cost(2.5 * taps),
+        earlier + [product, source, row(conv_bias), held],
+        (pair_shape, stats_shape),
+        scratch=scratch if taps > 1 else [],
+        cost_estimate=cost(1.5 + 2.0 * (taps - 1)),
         name="conv",
-    )(info, *context, source, row(conv_bias), held)
+    )
 
     blocks = {0: own}
     neighbour = [(i, i ^ 1) for i in range(tiles)]

time: 98.8 us -> 94.3 us (0.954)
  waiting for transfers between devices: 22.5 us -> 15 us
  Pallas kernels: 28.5 us -> 30.7 us
    ppermute x23, waiting for transfers between devices: 19.5 us -> 13.6 us  [exchange(): return lax.ppermute(array, 'tile', moves)]
    pallas_call x9 -> x11, Pallas kernels: 21.7 us -> 27.6 us  [call(): pl.pallas_call(kernel, out_shape=out_shape, in_specs=[SMEM_SPEC] + [VMEM_...]
    pallas_call x1 -> x0, Pallas kernels: 3.74 us -> none  [shards(): pl.pallas_call(functools.partial(conv_kernel, rows, taps), out_shape=(pai...]
    ppermute x1, waiting for transfers between devices: 1.45 us -> 0.01 us  [shards(): lax.ppermute(hidden, 'frame', [(i, i + by) for i in range(frames - by)])]
  transfers between devices with their start and end apart: 27 -> 27, of which waited for: 16 -> 15; matrix products, arithmetic and copies ran while one was open for 1% -> 1% of each run, Pallas kernels for 18% -> 21%
where the time goes in v6:
time: 94.3 us; the launch traced here: 92.4 us
  starting transfers between devices  43 us (46%)
  Pallas kernels  30.7 us (33%)
  waiting for transfers between devices  15 us (16%)
  other arithmetic  1.9 us (2%)
  local copies, waits for them, and re-layouts  1.3 us (1%)
    ppermute x23, starting transfers between devices, exchange(): return lax.ppermute(array, 'tile', moves)  31.7 us
    pallas_call x11, Pallas kernels, call(): pl.pallas_call(kernel, out_shape=out_shape, in_specs=[SMEM_SPEC] + [VMEM_...  27.6 us
    ppermute x23, waiting for transfers between devices, exchange(): return lax.ppermute(array, 'tile', moves)  13.6 us
    ppermute x1, starting transfers between devices, shards(): outer = lax.ppermute(outer, 'tile', outer_moves)  4.64 us
    ppermute x1, starting transfers between devices, shards(): lax.ppermute(jnp.where(odd, source[row_count - 1:], source[:1]), 'tile',...  4.24 us
    pallas_call x1, Pallas kernels, shards(): pl.pallas_call(functools.partial(hold_kernel, taps), out_shape=shape(3 *...  2.63 us
  transfers between devices with their start and end apart: 27, of which 15 were waited for; matrix products, arithmetic and copies ran while one was open for 1% of the time, Pallas kernels for 21%

profile of v6, /device:TPU:8, one launch (start us, length us, event | category | flops | bytes accessed | tf_op | source)
XLA Modules:
  0.0 92.4 jit_solution(11782550011629073468)
XLA Ops:
  0.9 4.2 %collective-permute-start = (bf16[1,104,384]{2,1,0:T(8,128)(2,1)S(1)}, bf16[1,104,384]{2,1,0:T(8,128)(2,1)S(1)}, u32[]{:S(2)}, u32[]{:S(2)}) collective-permute-start(bf16[1,104,384]{2,1,0:T(8,128)(2,1)S(1)} %get-tuple-element.87), channel_id=1, source_target_pairs={{2,4},{4,2},{6,8},{8,6},{10,12},{12,10},{14,16},{16,14},{18,20},{2... | collective-permute-start | bytes 239624 | tf_op jit(solution)/shard_map/ppermute | solution.py:671
  7.6 1.8 %first_stats.1 = f32[3,8,128]{2,1,0:T(8,128)S(1)} custom-call(s32[67]{0:T(128)S(1)} %pad_add_fusion.info_ref, bf16[4,104,384]{2,1,0:T(8,128)(2,1)S(1)} %bitcast.14), custom_call_target="tpu_custom_call" | custom-call | flops 1650000000 | tf_op jit(solution)/shard_map/first_stats/pallas_call | solution.py:653
  9.9 1.6 %collective-permute-start.4 = (f32[3,8,128]{2,1,0:T(8,128)S(1)}, f32[3,8,128]{2,1,0:T(8,128)S(1)}, u32[]{:S(2)}, u32[]{:S(2)}) collective-permute-start(f32[3,8,128]{2,1,0:T(8,128)S(1)} %first_stats.1), channel_id=1, source_target_pairs={{0,24},{2,26},{4,28},{6,30},{8,16},{10,18},{12,20},{14,22},{16,8},... | collective-permute-start | bytes 36872 | tf_op jit(solution)/shard_map/ppermute | solution.py:597
  12.5 1.5 %collective-permute-start.2 = (f32[3,8,128]{2,1,0:T(8,128)S(1)}, f32[3,8,128]{2,1,0:T(8,128)S(1)}, u32[]{:S(2)}, u32[]{:S(2)}) collective-permute-start(f32[3,8,128]{2,1,0:T(8,128)S(1)} %first_stats.1), channel_id=1, source_target_pairs={{0,8},{2,10},{4,12},{6,14},{8,0},{10,2},{12,4},{14,6},{16,24},{18,... | collective-permute-start | bytes 36872 | tf_op jit(solution)/shard_map/ppermute | solution.py:597
  14.0 2.6 %hold.1.held_ref.rest_4_ = bf16[2304,1152]{1,0:T(8,128)(2,1)S(1)} custom-call(bf16[3,3,3,384,384]{4,3,2,1,0:T(8,128)(2,1)} %weight_ref.3), custom_call_target="tpu_custom_call" | custom-call | flops 3300000000 | tf_op jit(solution)/shard_map/hold/pallas_call | solution.py:677
  16.7 1.5 %collective-permute-start.7 = (f32[3,8,128]{2,1,0:T(8,128)S(1)}, f32[3,8,128]{2,1,0:T(8,128)S(1)}, u32[]{:S(2)}, u32[]{:S(2)}) collective-permute-start(f32[3,8,128]{2,1,0:T(8,128)S(1)} %pad_maximum_fusion), channel_id=1, source_target_pairs={{0,6},{2,4},{4,2},{6,0},{8,14},{10,12},{12,10},{14,8},{16,22},{18,... | collective-permute-start | bytes 36872 | tf_op jit(solution)/shard_map/ppermute | solution.py:597
  26.0 2.2 %own_conv.1.rest_1_ = f32[448,1152]{1,0:T(8,128)S(1)} custom-call(s32[67]{0:T(128)S(1)} %pad_add_fusion.info_ref, bf16[6,112,384]{2,1,0:T(8,128)(2,1)S(1)} %get-tuple-element.44.hidden_ref, bf16[2304,1152]{1,0:T(8,128)(2,1)S(1)} %hold.1.held_ref.rest_4_), custom_call_target="tpu_custom_call" | custom-call | flops 2420000000 | tf_op jit(solution)/shard_map/own_conv/pallas_call | solution.py:653
  28.2 3.7 %conv.1 = (bf16[2,208,384]{2,1,0:T(8,128)(2,1)S(1)}, f32[3,8,128]{2,1,0:T(8,128)S(1)}) custom-call(s32[67]{0:T(128)S(1)} %pad_add_fusion.info_ref, bf16[6,112,384]{2,1,0:T(8,128)(2,1)S(1)} %collective-permute-done.8.rest_0_, f32[448,1152]{1,0:T(8,128)S(1)} %own_conv.1.rest_1_, bf16[4,104,384]{2,1,0:T(8,128)(2,1)S(1)} %get-tuple-element.46.rest_2_, ...), custom_call_target="tpu_custom_call" | custom-call | flops 3849999872 | tf_op jit(solution)/shard_map/conv/pallas_call | solution.py:653
  32.0 2.2 %collective-permute-start.11 = (f32[3,8,128]{2,1,0:T(8,128)S(1)}, f32[3,8,128]{2,1,0:T(8,128)S(1)}, u32[]{:S(2)}, u32[]{:S(2)}) collective-permute-start(f32[3,8,128]{2,1,0:T(8,128)S(1)} %get-tuple-element.47), channel_id=1, source_target_pairs={{0,24},{2,26},{4,28},{6,30},{8,16},{10,18},{12,20},{14,22},{16,8},... | collective-permute-start | bytes 36872 | tf_op jit(solution)/shard_map/ppermute | solution.py:597
  34.2 1.8 %collective-permute-start.10 = (f32[3,8,128]{2,1,0:T(8,128)S(1)}, f32[3,8,128]{2,1,0:T(8,128)S(1)}, u32[]{:S(2)}, u32[]{:S(2)}) collective-permute-start(f32[3,8,128]{2,1,0:T(8,128)S(1)} %get-tuple-element.47), channel_id=1, source_target_pairs={{0,16},{2,18},{4,20},{6,22},{8,24},{10,26},{12,28},{14,30},{16,0},... | collective-permute-start | bytes 36872 | tf_op jit(solution)/shard_map/ppermute | solution.py:597
  36.1 1.9 %collective-permute-start.13 = (bf16[2,208,384]{2,1,0:T(8,128)(2,1)S(1)}, bf16[2,208,384]{2,1,0:T(8,128)(2,1)S(1)}, u32[]{:S(2)}, u32[]{:S(2)}) collective-permute-start(bf16[2,208,384]{2,1,0:T(8,128)(2,1)S(1)} %get-tuple-element.64.rest_5_.own_ref), channel_id=1, source_target_pairs={{0,8},{2,10},{4,12},{6,14},{8,0},{10,2},{12,4},{14,6},{16,24},{18,... | collective-permute-start | bytes 958472 | tf_op jit(solution)/shard_map/ppermute | solution.py:597
  38.0 3.5 %collective-permute-start.14 = (bf16[2,208,384]{2,1,0:T(8,128)(2,1)S(1)}, bf16[2,208,384]{2,1,0:T(8,128)(2,1)S(1)}, u32[]{:S(2)}, u32[]{:S(2)}) collective-permute-start(bf16[2,208,384]{2,1,0:T(8,128)(2,1)S(1)} %get-tuple-element.64.rest_5_.own_ref), channel_id=1, source_target_pairs={{8,16},{10,18},{12,20},{14,22},{16,8},{18,10},{20,12},{22,14},{9,1... | collective-permute-start | bytes 958472 | tf_op jit(solution)/shard_map/ppermute | solution.py:597
  45.3 2.5 %collective-permute-done.14.rest_8_ = bf16[2,208,384]{2,1,0:T(8,128)(2,1)S(1)} collective-permute-done((bf16[2,208,384]{2,1,0:T(8,128)(2,1)S(1)}, bf16[2,208,384]{2,1,0:T(8,128)(2,1)S(1)}, u32[]{:S(2)}, u32[]{:S(2)}) %collective-permute-start.14) | collective-permute-done | bytes 319520 | tf_op jit(solution)/shard_map/ppermute | solution.py:597
  47.8 3.5 %collective-permute-start.19 = (bf16[2,208,384]{2,1,0:T(8,128)(2,1)S(1)}, bf16[2,208,384]{2,1,0:T(8,128)(2,1)S(1)}, u32[]{:S(2)}, u32[]{:S(2)}) collective-permute-start(bf16[2,208,384]{2,1,0:T(8,128)(2,1)S(1)} %collective-permute-done.13.rest_7_), channel_id=1, source_target_pairs={{8,16},{10,18},{12,20},{14,22},{16,8},{18,10},{20,12},{22,14},{9,1... | collective-permute-start | bytes 958472 | tf_op jit(solution)/shard_map/ppermute | solution.py:597
  55.0 1.8 %collective-permute-done.19 = bf16[2,208,384]{2,1,0:T(8,128)(2,1)S(1)} collective-permute-done((bf16[2,208,384]{2,1,0:T(8,128)(2,1)S(1)}, bf16[2,208,384]{2,1,0:T(8,128)(2,1)S(1)}, u32[]{:S(2)}, u32[]{:S(2)}) %collective-permute-start.19) | collective-permute-done | bytes 319520 | tf_op jit(solution)/shard_map/ppermute | solution.py:597
  57.2 2.6 %collective-permute-done.18.rest_6_ = bf16[2,208,384]{2,1,0:T(8,128)(2,1)S(1)} collective-permute-done((bf16[2,208,384]{2,1,0:T(8,128)(2,1)S(1)}, bf16[2,208,384]{2,1,0:T(8,128)(2,1)S(1)}, u32[]{:S(2)}, u32[]{:S(2)}) %collective-permute-start.18) | collective-permute-done | bytes 319520 | tf_op jit(solution)/shard_map/ppermute | solution.py:597
  59.7 2.5 %collective-permute-start.21 = (bf16[2,208,384]{2,1,0:T(8,128)(2,1)S(1)}, bf16[2,208,384]{2,1,0:T(8,128)(2,1)S(1)}, u32[]{:S(2)}, u32[]{:S(2)}) collective-permute-start(bf16[2,208,384]{2,1,0:T(8,128)(2,1)S(1)} %collective-permute-done.18.rest_6_), channel_id=1, source_target_pairs={{8,16},{10,18},{12,20},{14,22},{16,8},{18,10},{20,12},{22,14},{9,1... | collective-permute-start | bytes 958472 | tf_op jit(solution)/shard_map/ppermute | solution.py:597
  63.1 1.5 %queries.1 = (bf16[416,384]{1,0:T(8,128)(2,1)S(1)}, f32[416,128]{1,0:T(8,128)S(1)}, f32[8,384]{1,0:T(8,128)S(1)}, f32[8,384]{1,0:T(8,128)S(1)}) custom-call(s32[67]{0:T(128)S(1)} %pad_add_fusion.info_ref, bf16[2,208,384]{2,1,0:T(8,128)(2,1)S(1)} %collective-permute-done.17.other_ref, f32[3,8,128]{2,1,0:T(8,128)S(1)} %pad_maximum_fusion.3.stats_ref, ...), custom_call_target="tpu_custom_call" | custom-call | flops 1650000000 | tf_op jit(solution)/shard_map/queries/pallas_call | solution.py:653
  64.6 3.0 %attend_yours.2 = (bf16[1664,384]{1,0:T(8,128)(2,1)S(1)}, f32[416,128]{1,0:T(8,128)S(1)}, f32[416,128]{1,0:T(8,128)S(1)}, f32[416,384]{1,0:T(8,128)S(1)}) custom-call(s32[67]{0:T(128)S(1)} %pad_add_fusion.info_ref, f32[8,384]{1,0:T(8,128)S(1)} %get-tuple-element.52.rest_0_.means_ref, f32[8,384]{1,0:T(8,128)S(1)} %get-tuple-element.53.rest_1_.scales_ref, ...), custom_call_target="tpu_custom_call" | custom-call | flops 3960000000 | tf_op jit(solution)/shard_map/attend_yours/pallas_call | solution.py:653
  69.4 3.0 %attend_yours.3 = (bf16[1664,384]{1,0:T(8,128)(2,1)S(1)}, bf16[432,384]{1,0:T(8,128)(2,1)S(1)}) custom-call(s32[67]{0:T(128)S(1)} %pad_add_fusion.info_ref, f32[8,384]{1,0:T(8,128)S(1)} %get-tuple-element.52.rest_0_.means_ref, f32[8,384]{1,0:T(8,128)S(1)} %get-tuple-element.53.rest_1_.scales_ref, f32[1,384]{1,0:T(1,128)S(1)} %reshape.87.shift_ref.rest_2_, ...), custom_call_target="tpu_custom_call" | custom-call | flops 3960000000 | tf_op jit(solution)/shard_map/attend_yours/pallas_call | solution.py:653
  73.5 5.4 %attend_mine.1 = (f32[416,384]{1,0:T(8,128)S(1)}, f32[416,128]{1,0:T(8,128)S(1)}) custom-call(s32[67]{0:T(128)S(1)} %pad_add_fusion.info_ref, bf16[2,208,384]{2,1,0:T(8,128)(2,1)S(1)} %get-tuple-element.64.rest_5_.own_ref, f32[8,384]{1,0:T(8,128)S(1)} %get-tuple-element.52.rest_0_.means_ref, f32[8,384]{1,0:T(8,128)S(1)} %get-tuple-element.53.rest_1_.scales_ref, ...), custom_call_target="tpu_custom_call" | custom-call | flops 6600000000 | tf_op jit(solution)/shard_map/attend_mine/pallas_call | solution.py:653
  81.2 4.6 %collective-permute-start.25 = (bf16[1,104,384]{2,1,0:T(8,128)(2,1)S(1)}, bf16[1,104,384]{2,1,0:T(8,128)(2,1)S(1)}, u32[]{:S(2)}, u32[]{:S(2)}) collective-permute-start(bf16[1,104,384]{2,1,0:T(8,128)(2,1)S(1)} %get-tuple-element.69), channel_id=1, source_target_pairs={{2,4},{4,2},{6,8},{8,6},{10,12},{12,10},{14,16},{16,14},{18,20},{2... | collective-permute-start | bytes 239624 | tf_op jit(solution)/shard_map/ppermute | solution.py:809
  86.0 2.2 %upsample.1 = (bf16[6,192,208]{2,1,0:T(8,128)(2,1)S(1)}, f32[2,2,256,128]{3,2,1,0:T(8,128)S(1)}) custom-call(s32[67]{0:T(128)S(1)} %pad_add_fusion.info_ref, bf16[4,104,384]{2,1,0:T(8,128)(2,1)S(1)} %get-tuple-element.71.own_ref, bf16[2,2,2,192,768]{4,3,2,1,0:T(8,128)(2,1)S(1)} %fold.1.weight_ref, f32[1,256]{1,0:T(1,128)S(1)} %pad.4.bias_ref), custom_call_target="tpu_custom_call" | custom-call | flops 2200000000 | tf_op jit(solution)/shard_map/upsample/pallas_call | solution.py:653
  90.4 2.1 %close.1 = bf16[8,192,208]{2,1,0:T(8,128)(2,1)} custom-call(s32[67]{0:T(128)S(1)} %pad_add_fusion.info_ref, bf16[1,104,384]{2,1,0:T(8,128)(2,1)S(1)} %collective-permute-done.25.outer_ref, bf16[1,104,384]{2,1,0:T(8,128)(2,1)S(1)} %collective-permute-done.26.inner_ref, bf16[6,192,208]{2,1,0:T(8,128)(2,1)S(1)} %get-tuple-element.73.middle_ref, ...), custom_call_target="tpu_custom_call" | custom-call | flops 1100000000 | tf_op jit(solution)/shard_map/close/pallas_call | solution.py:653
  (92 shorter events, 28.8 us)
Async XLA Ops:
  0.9 8.6 %collective-permute-start = (bf16[1,104,384]{2,1,0:T(8,128)(2,1)S(1)}, bf16[1,104,384]{2,1,0:T(8,128)(2,1)S(1)}, u32[]{:S(2)}, u32[]{:S(2)}) collective-permute-start(bf16[1,104,384]{2,1,0:T(8,128)(2,1)S(1)} %get-tuple-element.87), channel_id=1, source_target_pairs={{2,4},{4,2},{6,8},{8,6},{10,12},{12,10},{14,16},{16,14},{18,20},{2... | collective-permute-start | bytes 239624 | tf_op jit(solution)/shard_map/ppermute | solution.py:671
  5.2 4.7 %collective-permute-start.1 = (bf16[1,104,384]{2,1,0:T(8,128)(2,1)S(1)}, bf16[1,104,384]{2,1,0:T(8,128)(2,1)S(1)}, u32[]{:S(2)}, u32[]{:S(2)}) collective-permute-start(bf16[1,104,384]{2,1,0:T(8,128)(2,1)S(1)} %get-tuple-element.86), channel_id=1, source_target_pairs={{0,2},{2,0},{4,6},{6,4},{8,10},{10,8},{12,14},{14,12},{16,18},{18,... | collective-permute-start | bytes 239624 | tf_op jit(solution)/shard_map/ppermute | solution.py:597
  9.9 6.7 %collective-permute-start.4 = (f32[3,8,128]{2,1,0:T(8,128)S(1)}, f32[3,8,128]{2,1,0:T(8,128)S(1)}, u32[]{:S(2)}, u32[]{:S(2)}) collective-permute-start(f32[3,8,128]{2,1,0:T(8,128)S(1)} %first_stats.1), channel_id=1, source_target_pairs={{0,24},{2,26},{4,28},{6,30},{8,16},{10,18},{12,20},{14,22},{16,8},... | collective-permute-start | bytes 36872 | tf_op jit(solution)/shard_map/ppermute | solution.py:597
  11.5 5.1 %collective-permute-start.3 = (f32[3,8,128]{2,1,0:T(8,128)S(1)}, f32[3,8,128]{2,1,0:T(8,128)S(1)}, u32[]{:S(2)}, u32[]{:S(2)}) collective-permute-start(f32[3,8,128]{2,1,0:T(8,128)S(1)} %first_stats.1), channel_id=1, source_target_pairs={{0,16},{2,18},{4,20},{6,22},{8,24},{10,26},{12,28},{14,30},{16,0},... | collective-permute-start | bytes 36872 | tf_op jit(solution)/shard_map/ppermute | solution.py:597
  12.5 4.1 %collective-permute-start.2 = (f32[3,8,128]{2,1,0:T(8,128)S(1)}, f32[3,8,128]{2,1,0:T(8,128)S(1)}, u32[]{:S(2)}, u32[]{:S(2)}) collective-permute-start(f32[3,8,128]{2,1,0:T(8,128)S(1)} %first_stats.1), channel_id=1, source_target_pairs={{0,8},{2,10},{4,12},{6,14},{8,0},{10,2},{12,4},{14,6},{16,24},{18,... | collective-permute-start | bytes 36872 | tf_op jit(solution)/shard_map/ppermute | solution.py:597
  16.7 4.7 %collective-permute-start.7 = (f32[3,8,128]{2,1,0:T(8,128)S(1)}, f32[3,8,128]{2,1,0:T(8,128)S(1)}, u32[]{:S(2)}, u32[]{:S(2)}) collective-permute-start(f32[3,8,128]{2,1,0:T(8,128)S(1)} %pad_maximum_fusion), channel_id=1, source_target_pairs={{0,6},{2,4},{4,2},{6,0},{8,14},{10,12},{12,10},{14,8},{16,22},{18,... | collective-permute-start | bytes 36872 | tf_op jit(solution)/shard_map/ppermute | solution.py:597
  32.0 9.5 %collective-permute-start.11 = (f32[3,8,128]{2,1,0:T(8,128)S(1)}, f32[3,8,128]{2,1,0:T(8,128)S(1)}, u32[]{:S(2)}, u32[]{:S(2)}) collective-permute-start(f32[3,8,128]{2,1,0:T(8,128)S(1)} %get-tuple-element.47), channel_id=1, source_target_pairs={{0,24},{2,26},{4,28},{6,30},{8,16},{10,18},{12,20},{14,22},{16,8},... | collective-permute-start | bytes 36872 | tf_op jit(solution)/shard_map/ppermute | solution.py:597
  34.2 7.3 %collective-permute-start.10 = (f32[3,8,128]{2,1,0:T(8,128)S(1)}, f32[3,8,128]{2,1,0:T(8,128)S(1)}, u32[]{:S(2)}, u32[]{:S(2)}) collective-permute-start(f32[3,8,128]{2,1,0:T(8,128)S(1)} %get-tuple-element.47), channel_id=1, source_target_pairs={{0,16},{2,18},{4,20},{6,22},{8,24},{10,26},{12,28},{14,30},{16,0},... | collective-permute-start | bytes 36872 | tf_op jit(solution)/shard_map/ppermute | solution.py:597
  36.0 5.5 %collective-permute-start.9 = (f32[3,8,128]{2,1,0:T(8,128)S(1)}, f32[3,8,128]{2,1,0:T(8,128)S(1)}, u32[]{:S(2)}, u32[]{:S(2)}) collective-permute-start(f32[3,8,128]{2,1,0:T(8,128)S(1)} %get-tuple-element.47), channel_id=1, source_target_pairs={{0,8},{2,10},{4,12},{6,14},{8,0},{10,2},{12,4},{14,6},{16,24},{18,... | collective-permute-start | bytes 36872 | tf_op jit(solution)/shard_map/ppermute | solution.py:597
  36.1 9.2 %collective-permute-start.13 = (bf16[2,208,384]{2,1,0:T(8,128)(2,1)S(1)}, bf16[2,208,384]{2,1,0:T(8,128)(2,1)S(1)}, u32[]{:S(2)}, u32[]{:S(2)}) collective-permute-start(bf16[2,208,384]{2,1,0:T(8,128)(2,1)S(1)} %get-tuple-element.64.rest_5_.own_ref), channel_id=1, source_target_pairs={{0,8},{2,10},{4,12},{6,14},{8,0},{10,2},{12,4},{14,6},{16,24},{18,... | collective-permute-start | bytes 958472 | tf_op jit(solution)/shard_map/ppermute | solution.py:597
  38.0 9.8 %collective-permute-start.14 = (bf16[2,208,384]{2,1,0:T(8,128)(2,1)S(1)}, bf16[2,208,384]{2,1,0:T(8,128)(2,1)S(1)}, u32[]{:S(2)}, u32[]{:S(2)}) collective-permute-start(bf16[2,208,384]{2,1,0:T(8,128)(2,1)S(1)} %get-tuple-element.64.rest_5_.own_ref), channel_id=1, source_target_pairs={{8,16},{10,18},{12,20},{14,22},{16,8},{18,10},{20,12},{22,14},{9,1... | collective-permute-start | bytes 958472 | tf_op jit(solution)/shard_map/ppermute | solution.py:597
  41.6 3.8 %collective-permute-start.12 = (f32[3,8,128]{2,1,0:T(8,128)S(1)}, f32[3,8,128]{2,1,0:T(8,128)S(1)}, u32[]{:S(2)}, u32[]{:S(2)}) collective-permute-start(f32[3,8,128]{2,1,0:T(8,128)S(1)} %pad_maximum_fusion.2), channel_id=1, source_target_pairs={{0,2},{2,0},{4,6},{6,4},{8,10},{10,8},{12,14},{14,12},{16,18},{18,... | collective-permute-start | bytes 36872 | tf_op jit(solution)/shard_map/ppermute | solution.py:597
  42.6 10.0 %collective-permute-start.16 = (f32[3,8,128]{2,1,0:T(8,128)S(1)}, f32[3,8,128]{2,1,0:T(8,128)S(1)}, u32[]{:S(2)}, u32[]{:S(2)}) collective-permute-start(f32[3,8,128]{2,1,0:T(8,128)S(1)} %pad_maximum_fusion.2), channel_id=1, source_target_pairs={{0,6},{2,4},{4,2},{6,0},{8,14},{10,12},{12,10},{14,8},{16,22},{18,... | collective-permute-start | bytes 36872 | tf_op jit(solution)/shard_map/ppermute | solution.py:597
  43.8 8.8 %collective-permute-start.15 = (f32[3,8,128]{2,1,0:T(8,128)S(1)}, f32[3,8,128]{2,1,0:T(8,128)S(1)}, u32[]{:S(2)}, u32[]{:S(2)}) collective-permute-start(f32[3,8,128]{2,1,0:T(8,128)S(1)} %pad_maximum_fusion.2), channel_id=1, source_target_pairs={{0,4},{2,6},{4,0},{6,2},{8,12},{10,14},{12,8},{14,10},{16,20},{18,... | collective-permute-start | bytes 36872 | tf_op jit(solution)/shard_map/ppermute | solution.py:597
  47.8 8.9 %collective-permute-start.19 = (bf16[2,208,384]{2,1,0:T(8,128)(2,1)S(1)}, bf16[2,208,384]{2,1,0:T(8,128)(2,1)S(1)}, u32[]{:S(2)}, u32[]{:S(2)}) collective-permute-start(bf16[2,208,384]{2,1,0:T(8,128)(2,1)S(1)} %collective-permute-done.13.rest_7_), channel_id=1, source_target_pairs={{8,16},{10,18},{12,20},{14,22},{16,8},{18,10},{20,12},{22,14},{9,1... | collective-permute-start | bytes 958472 | tf_op jit(solution)/shard_map/ppermute | solution.py:597
  51.3 5.8 %collective-permute-start.20 = (bf16[2,208,384]{2,1,0:T(8,128)(2,1)S(1)}, bf16[2,208,384]{2,1,0:T(8,128)(2,1)S(1)}, u32[]{:S(2)}, u32[]{:S(2)}) collective-permute-start(bf16[2,208,384]{2,1,0:T(8,128)(2,1)S(1)} %collective-permute-done.14.rest_8_), channel_id=1, source_target_pairs={{8,0},{10,2},{12,4},{14,6},{16,24},{18,26},{20,28},{22,30},{9,1},{... | collective-permute-start | bytes 958472 | tf_op jit(solution)/shard_map/ppermute | solution.py:597
  52.7 7.1 %collective-permute-start.18 = (bf16[2,208,384]{2,1,0:T(8,128)(2,1)S(1)}, bf16[2,208,384]{2,1,0:T(8,128)(2,1)S(1)}, u32[]{:S(2)}, u32[]{:S(2)}) collective-permute-start(bf16[2,208,384]{2,1,0:T(8,128)(2,1)S(1)} %get-tuple-element.64.rest_5_.own_ref), channel_id=1, source_target_pairs={{0,4},{2,6},{4,0},{6,2},{8,12},{10,14},{12,8},{14,10},{16,20},{18,... | collective-permute-start | bytes 958472 | tf_op jit(solution)/shard_map/ppermute | solution.py:597
  53.4 9.7 %collective-permute-start.17 = (bf16[2,208,384]{2,1,0:T(8,128)(2,1)S(1)}, bf16[2,208,384]{2,1,0:T(8,128)(2,1)S(1)}, u32[]{:S(2)}, u32[]{:S(2)}) collective-permute-start(bf16[2,208,384]{2,1,0:T(8,128)(2,1)S(1)} %get-tuple-element.64.rest_5_.own_ref), channel_id=1, source_target_pairs={{0,2},{2,0},{4,6},{6,4},{8,10},{10,8},{12,14},{14,12},{16,18},{18,... | collective-permute-start | bytes 958472 | tf_op jit(solution)/shard_map/ppermute | solution.py:597
  59.7 8.9 %collective-permute-start.21 = (bf16[2,208,384]{2,1,0:T(8,128)(2,1)S(1)}, bf16[2,208,384]{2,1,0:T(8,128)(2,1)S(1)}, u32[]{:S(2)}, u32[]{:S(2)}) collective-permute-start(bf16[2,208,384]{2,1,0:T(8,128)(2,1)S(1)} %collective-permute-done.18.rest_6_), channel_id=1, source_target_pairs={{8,16},{10,18},{12,20},{14,22},{16,8},{18,10},{20,12},{22,14},{9,1... | collective-permute-start | bytes 958472 | tf_op jit(solution)/shard_map/ppermute | solution.py:597
  62.3 7.1 %collective-permute-start.22 = (bf16[2,208,384]{2,1,0:T(8,128)(2,1)S(1)}, bf16[2,208,384]{2,1,0:T(8,128)(2,1)S(1)}, u32[]{:S(2)}, u32[]{:S(2)}) collective-permute-start(bf16[2,208,384]{2,1,0:T(8,128)(2,1)S(1)} %collective-permute-done.18.rest_6_), channel_id=1, source_target_pairs={{0,8},{2,10},{4,12},{6,14},{8,0},{10,2},{12,4},{14,6},{16,24},{18,... | collective-permute-start | bytes 958472 | tf_op jit(solution)/shard_map/ppermute | solution.py:597
  62.4 7.1 %collective-permute-start.23 = (bf16[2,208,384]{2,1,0:T(8,128)(2,1)S(1)}, bf16[2,208,384]{2,1,0:T(8,128)(2,1)S(1)}, u32[]{:S(2)}, u32[]{:S(2)}) collective-permute-start(bf16[2,208,384]{2,1,0:T(8,128)(2,1)S(1)} %broadcast_select_fusion.rest_5_), channel_id=1, source_target_pairs={{0,4},{2,6},{4,0},{6,2},{8,12},{10,14},{12,8},{14,10},{16,20},{18,... | collective-permute-start | bytes 958472 | tf_op jit(solution)/shard_map/ppermute | solution.py:597
  72.4 7.2 %collective-permute-start.24 = (bf16[432,384]{1,0:T(8,128)(2,1)S(1)}, bf16[432,384]{1,0:T(8,128)(2,1)S(1)}, u32[]{:S(2)}, u32[]{:S(2)}) collective-permute-start(bf16[432,384]{1,0:T(8,128)(2,1)S(1)} %get-tuple-element.63), channel_id=1, source_target_pairs={{0,2},{2,0},{4,6},{6,4},{8,10},{10,8},{12,14},{14,12},{16,18},{18,... | collective-permute-start | bytes 995336 | tf_op jit(solution)/shard_map/ppermute | solution.py:779
  81.2 8.2 %collective-permute-start.25 = (bf16[1,104,384]{2,1,0:T(8,128)(2,1)S(1)}, bf16[1,104,384]{2,1,0:T(8,128)(2,1)S(1)}, u32[]{:S(2)}, u32[]{:S(2)}) collective-permute-start(bf16[1,104,384]{2,1,0:T(8,128)(2,1)S(1)} %get-tuple-element.69), channel_id=1, source_target_pairs={{2,4},{4,2},{6,8},{8,6},{10,12},{12,10},{14,16},{16,14},{18,20},{2... | collective-permute-start | bytes 239624 | tf_op jit(solution)/shard_map/ppermute | solution.py:809
  85.9 4.5 %collective-permute-start.26 = (bf16[1,104,384]{2,1,0:T(8,128)(2,1)S(1)}, bf16[1,104,384]{2,1,0:T(8,128)(2,1)S(1)}, u32[]{:S(2)}, u32[]{:S(2)}) collective-permute-start(bf16[1,104,384]{2,1,0:T(8,128)(2,1)S(1)} %get-tuple-element.70), channel_id=1, source_target_pairs={{0,2},{2,0},{4,6},{6,4},{8,10},{10,8},{12,14},{14,12},{16,18},{18,... | collective-permute-start | bytes 239624 | tf_op jit(solution)/shard_map/ppermute | solution.py:597
  (16 other events, 224.7 us)

commit v7 on v6

--- a/solution.py
+++ b/solution.py
@@ -286,18 +286,22 @@
 
 
 def query_kernel(
-    rows, info_ref, other_ref, stats_ref, gain_ref, shift_ref, weight_ref, bias_ref, queries_ref,
-    constant_ref, means_ref, scales_ref,
+    rows, info_ref, own_ref, other_ref, stats_ref, gain_ref, shift_ref, weight_ref, bias_ref,
+    means_ref, scales_ref, *out_refs,
 ):
     info = Info(info_ref, rows)
     means, scales = norm_tables(stats_ref, gain_ref)
     means_ref[...] = means
     scales_ref[...] = scales
-    queries, constant = turned_queries(
-        info, info.tile() ^ 1, other_ref, means, scales, shift_ref, weight_ref, bias_ref
-    )
-    queries_ref[...] = queries
-    constant_ref[...] = jnp.broadcast_to(constant, constant_ref.shape)
+    for side, (tile, pairs_ref) in enumerate(
+        ((info.tile() ^ 1, other_ref), (info.tile(), own_ref))
+    ):
+        queries, constant = turned_queries(
+            info, tile, pairs_ref, means, scales, shift_ref, weight_ref, bias_ref
+        )
+        queries_ref, constant_ref = out_refs[2 * side : 2 * side + 2]
+        queries_ref[...] = queries
+        constant_ref[...] = jnp.broadcast_to(constant, constant_ref.shape)
 
 
 def key_codes(info, masks, span, cols):
@@ -400,15 +404,12 @@
 
 
 def attend_mine_kernel(
-    rows, groups, info_ref, own_ref, means_ref, scales_ref, shift_ref, weight_ref, bias_ref, *rest
+    rows, groups, info_ref, queries_ref, constant_ref, *rest
 ):
     key_refs, (mean_ref, level_ref) = rest[: len(groups)], rest[len(groups) :]
     info = Info(info_ref, rows)
     span = mean_ref.shape[0]
-    queries, constant = turned_queries(
-        info, info.tile(), own_ref, means_ref[...], scales_ref[...], shift_ref, weight_ref,
-        bias_ref,
-    )
+    queries, constant = queries_ref[...], constant_ref[:, 0:1]
     cols = span // ROWS_OF_TILE
     query_code = query_codes(info, info.tile(), span, cols)
     peak = jnp.full((span, 1), LOWEST, F32)
@@ -473,7 +474,8 @@
     outer_ref[0] = jnp.where(odd, value, top).astype(BF16)
 
 
-def fold_kernel(weight_ref, out_ref):
+def fold_kernel(weight_ref, output_ref, out_ref, output_copy_ref):
+    output_copy_ref[...] = output_ref[...]
     channels = weight_ref.shape[-1]
     wide = [[weight_ref[a, b].astype(F32) for b in range(3)] for a in range(3)]
 
@@ -515,7 +517,8 @@
 
 
 def upsample_kernel(
-    rows, info_ref, own_ref, weight_ref, bias_ref, out_ref, open_ref, columns_ref, wide_ref
+    rows, info_ref, own_ref, weight_ref, bias_ref, out_ref, open_ref, columns_ref, wide_ref,
+    turned_ref, sem,
 ):
     info = Info(info_ref, rows)
     row_count, cols, channels = own_ref.shape
@@ -549,12 +552,15 @@
     for r in range(1, 2 * row_count - 1):
         for part in range(parts_out):
             value = wide_ref[part, r] + bias_ref[:, part * LANES : (part + 1) * LANES]
-            write_turned(out_ref, r - 1, part, value, 2 * widths[r // 2])
+            write_turned(turned_ref, r - 1, part, value, 2 * widths[r // 2])
+    copy = pltpu.make_async_copy(turned_ref, out_ref.at[pl.ds(1, 2 * row_count - 2)], sem)
+    copy.start()
+    copy.wait()
 
 
 def close_kernel(
-    rows, info_ref, outer_ref, inner_ref, middle_ref, open_ref, weight_ref, bias_ref, out_ref,
-    columns_ref, wide_ref,
+    rows, info_ref, outer_ref, inner_ref, _, open_ref, weight_ref, bias_ref, out_ref, columns_ref,
+    wide_ref, turned_ref, sems,
 ):
     info = Info(info_ref, rows)
     wide_rows, _, wide_cols = out_ref.shape
@@ -572,15 +578,21 @@
                 weight_ref[down, down, right],
             )
             spread_columns(wide_ref, rim[:cols], down, right)
-    out_ref[1 : wide_rows - 1] = middle_ref[...]
+    copies = []
     for down in range(2):
         rim_row, own_row = (row_count + 1, row_count) if down else (0, 1)
         for part in range(wide_ref.shape[0]):
             rim = jnp.where(labels[rim_row] == labels[own_row], wide_ref[part, down], 0.0)
             value = open_ref[part, down] + rim + bias_ref[:, part * LANES : (part + 1) * LANES]
-            write_turned(
-                out_ref, down * (wide_rows - 1), part, value, 2 * widths[own_row]
+            write_turned(turned_ref, down, part, value, 2 * widths[own_row])
+        copies.append(
+            pltpu.make_async_copy(
+                turned_ref.at[down], out_ref.at[down * (wide_rows - 1)], sems.at[down]
             )
+        )
+        copies[-1].start()
+    for copy in copies:
+        copy.wait()
 
 
 def merge_stats(mine, other):
@@ -753,11 +765,22 @@
         groups = [list(range(i, i + 4)) for i in range(0, tiles // 2, 4)]
     gain, shift = row(second_gain), row(second_shift)
     table_shape = shape(SLOTS, channels, dtype=F32)
-    queries, constant, means, scales = call(
+    folded, out_weight = pl.pallas_call(
+        fold_kernel,
+        out_shape=(shape(2, 2, 2, out_channels, 2 * channels), shape(channels, channels)),
+        in_specs=[VMEM_SPEC, VMEM_SPEC],
+        out_specs=(VMEM_SPEC, VMEM_SPEC),
+        compiler_params=params(),
+        cost_estimate=cost(0.6),
+        name="fold",
+    )(jnp.swapaxes(upsample_weight, 2, 3), output_weight)
+    other, folded, out_weight = lax.optimization_barrier((other, folded, out_weight))
+    query_shapes = (shape(cells, channels), shape(cells, LANES, dtype=F32))
+    means, scales, queries, constant, mine_queries, mine_constant = call(
         functools.partial(query_kernel, rows),
-        [other, stats, gain, shift, triple_weight, row(triple_bias)],
-        (shape(cells, channels), shape(cells, LANES, dtype=F32), table_shape, table_shape),
-        cost_estimate=cost(1.5),
+        [own, other, stats, gain, shift, triple_weight, row(triple_bias)],
+        (table_shape, table_shape) + query_shapes * 2,
+        cost_estimate=cost(1.9),
         name="queries",
     )
     level_shape = shape(cells, LANES, dtype=F32)
@@ -777,29 +800,20 @@
         keys.append(normed)
     (sent,) = state
     received = lax.ppermute(sent, "tile", neighbour)
-    sent, own_late, upsample_weight = lax.optimization_barrier((sent, own, upsample_weight))
+    sent, mine_queries = lax.optimization_barrier((sent, mine_queries))
     mean, level = call(
         functools.partial(attend_mine_kernel, rows, tuple(tuple(masks) for masks in groups)),
-        [own_late, means, scales, shift, triple_weight, row(triple_bias)] + keys,
+        [mine_queries, mine_constant] + keys,
         (total_shape, level_shape),
-        cost_estimate=cost(6.0),
+        cost_estimate=cost(4.3),
         name="attend_mine",
     )
-    folded = pl.pallas_call(
-        fold_kernel,
-        out_shape=shape(2, 2, 2, out_channels, 2 * channels),
-        in_specs=[VMEM_SPEC],
-        out_specs=VMEM_SPEC,
-        compiler_params=params(),
-        cost_estimate=cost(0.5),
-        name="fold",
-    )(jnp.swapaxes(upsample_weight, 2, 3))
 
     rim_shape = shape(1, cols, channels)
     attended, inner, outer = call(
         functools.partial(finish_kernel, rows),
         [
-            mean, level, received, own, triple_weight, row(triple_bias), output_weight,
+            mean, level, received, own, triple_weight, row(triple_bias), out_weight,
             row(output_bias),
         ],
         (shape(row_count, cols, channels), rim_shape, rim_shape),
@@ -811,31 +825,39 @@
     parts_out = -(-out_channels // LANES)
     wide_cols = -(-2 * cols // LANES) * LANES
     wide_bias = jnp.pad(row(upsample_bias), ((0, 0), (0, -out_channels % LANES)))
-    middle, open_rows = call(
+    out_shape = shape(2 * row_count, out_channels, 2 * cols)
+    open_shape = shape(parts_out, 2, wide_cols, LANES, dtype=F32)
+    decoded, open_rows = pl.pallas_call(
         functools.partial(upsample_kernel, rows),
-        [attended, folded, wide_bias],
-        (
-            shape(2 * row_count - 2, out_channels, 2 * cols),
-            shape(parts_out, 2, wide_cols, LANES, dtype=F32),
-        ),
-        scratch=[
+        out_shape=(out_shape, open_shape),
+        in_specs=[SMEM_SPEC] + [VMEM_SPEC] * 3,
+        out_specs=(HBM_SPEC, VMEM_SPEC),
+        scratch_shapes=[
             pltpu.VMEM((row_count * padded, 3 * channels), BF16),
             pltpu.VMEM((parts_out, 2 * row_count, wide_cols, LANES), F32),
+            pltpu.VMEM((2 * row_count - 2, out_channels, 2 * cols), BF16),
+            pltpu.SemaphoreType.DMA,
         ],
+        compiler_params=params(),
         cost_estimate=cost(2.0),
         name="upsample",
-    )
-    decoded = call(
+    )(info, attended, folded, wide_bias)
+    decoded = pl.pallas_call(
         functools.partial(close_kernel, rows),
-        [outer, inner, middle, open_rows, folded, wide_bias],
-        shape(2 * row_count, out_channels, 2 * cols),
-        scratch=[
+        out_shape=out_shape,
+        in_specs=[SMEM_SPEC] + [VMEM_SPEC] * 2 + [HBM_SPEC] + [VMEM_SPEC] * 3,
+        out_specs=HBM_SPEC,
+        scratch_shapes=[
             pltpu.VMEM((2 * padded, 3 * channels), BF16),
             pltpu.VMEM((parts_out, 2, wide_cols, LANES), F32),
+            pltpu.VMEM((2, out_channels, 2 * cols), BF16),
+            pltpu.SemaphoreType.DMA((2,)),
         ],
+        input_output_aliases={3: 0},
+        compiler_params=params(),
         cost_estimate=cost(1.0),
         name="close",
-    )
+    )(info, outer, inner, decoded, open_rows, folded, wide_bias)
     return jnp.swapaxes(decoded, 1, 2).reshape(2 * row_count, 1, 2 * cols, out_channels)
 
 

time: 94.3 us -> 95.8 us (1.016)
  waiting for transfers between devices: 15 us -> 12.8 us
  Pallas kernels: 30.7 us -> 31.9 us
  other arithmetic: 1.9 us -> 2.86 us
    pallas_call x1 -> x3, Pallas kernels: 0.51 us -> 5.43 us  [the longest x1 3.02 us: shards(): pl.pallas_call(functools.partial(upsample_kernel, rows), out_shape=(out_s...]
    pallas_call x11 -> x9, Pallas kernels: 27.6 us -> 23.8 us  [call(): pl.pallas_call(kernel, out_shape=out_shape, in_specs=[SMEM_SPEC] + [VMEM_...]
    ppermute x23, waiting for transfers between devices: 13.6 us -> 12 us  [exchange(): return lax.ppermute(array, 'tile', moves)]
    ppermute x1, waiting for transfers between devices: 1.27 us -> 0.01 us  [shards(): outer = lax.ppermute(outer, 'tile', outer_moves)]
    select_n x1, other arithmetic: 0.05 us -> 1.01 us  [shards(): blocks[4] = jnp.where((tile // 4 == 1) | (tile // 4 == 2), inward, outward)]
  transfers between devices with their start and end apart: 27 -> 27, of which waited for: 15 -> 14; matrix products, arithmetic and copies ran while one was open for 1% -> 2% of each run, Pallas kernels for 21% -> 22%
where the time goes in v7:
time: 95.8 us; the launch traced here: 94 us
  starting transfers between devices  43.8 us (46%)
  Pallas kernels  31.9 us (33%)
  waiting for transfers between devices  12.8 us (13%)
  other arithmetic  2.86 us (3%)
  local copies, waits for them, and re-layouts  2.06 us (2%)
    ppermute x23, starting transfers between devices, exchange(): return lax.ppermute(array, 'tile', moves)  31.7 us
    pallas_call x9, Pallas kernels, call(): pl.pallas_call(kernel, out_shape=out_shape, in_specs=[SMEM_SPEC] + [VMEM_...  23.8 us
    ppermute x23, waiting for transfers between devices, exchange(): return lax.ppermute(array, 'tile', moves)  12 us
    ppermute x1, starting transfers between devices, shards(): outer = lax.ppermute(outer, 'tile', outer_moves)  5.05 us
    ppermute x1, starting transfers between devices, shards(): lax.ppermute(jnp.where(odd, source[row_count - 1:], source[:1]), 'tile',...  4.24 us
    pallas_call x1, Pallas kernels, shards(): pl.pallas_call(functools.partial(upsample_kernel, rows), out_shape=(out_s...  3.02 us
    pallas_call x1, Pallas kernels, shards(): pl.pallas_call(functools.partial(hold_kernel, taps), out_shape=shape(3 *...  2.63 us
    unnamed x26, local copies, waits for them, and re-layouts  2.03 us
  transfers between devices with their start and end apart: 27, of which 14 were waited for; matrix products, arithmetic and copies ran while one was open for 2% of the time, Pallas kernels for 22%

profile of v7, /device:TPU:8, one launch (start us, length us, event | category | flops | bytes accessed | tf_op | source)
XLA Modules:
  0.0 94.0 jit_solution(8174645340103140469)
XLA Ops:
  0.9 4.2 %collective-permute-start = (bf16[1,104,384]{2,1,0:T(8,128)(2,1)S(1)}, bf16[1,104,384]{2,1,0:T(8,128)(2,1)S(1)}, u32[]{:S(2)}, u32[]{:S(2)}) collective-permute-start(bf16[1,104,384]{2,1,0:T(8,128)(2,1)S(1)} %get-tuple-element.99), channel_id=1, source_target_pairs={{2,4},{4,2},{6,8},{8,6},{10,12},{12,10},{14,16},{16,14},{18,20},{2... | collective-permute-start | bytes 239624 | tf_op jit(solution)/shard_map/ppermute | solution.py:683
  7.6 1.8 %first_stats.1 = f32[3,8,128]{2,1,0:T(8,128)S(1)} custom-call(s32[67]{0:T(128)S(1)} %pad_add_fusion.info_ref, bf16[4,104,384]{2,1,0:T(8,128)(2,1)S(1)} %bitcast.13), custom_call_target="tpu_custom_call" | custom-call | flops 1650000000 | tf_op jit(solution)/shard_map/first_stats/pallas_call | solution.py:665
  10.1 2.9 %collective-permute-start.3 = (f32[3,8,128]{2,1,0:T(8,128)S(1)}, f32[3,8,128]{2,1,0:T(8,128)S(1)}, u32[]{:S(2)}, u32[]{:S(2)}) collective-permute-start(f32[3,8,128]{2,1,0:T(8,128)S(1)} %first_stats.1), channel_id=1, source_target_pairs={{0,16},{2,18},{4,20},{6,22},{8,24},{10,26},{12,28},{14,30},{16,0},... | collective-permute-start | bytes 36872 | tf_op jit(solution)/shard_map/ppermute | solution.py:609
  13.4 2.6 %hold.1.held_ref.rest_4_ = bf16[2304,1152]{1,0:T(8,128)(2,1)S(1)} custom-call(bf16[3,3,3,384,384]{4,3,2,1,0:T(8,128)(2,1)} %weight_ref.2), custom_call_target="tpu_custom_call" | custom-call | flops 3300000000 | tf_op jit(solution)/shard_map/hold/pallas_call | solution.py:689
  16.7 1.6 %collective-permute-start.5 = (f32[3,8,128]{2,1,0:T(8,128)S(1)}, f32[3,8,128]{2,1,0:T(8,128)S(1)}, u32[]{:S(2)}, u32[]{:S(2)}) collective-permute-start(f32[3,8,128]{2,1,0:T(8,128)S(1)} %pad_maximum_fusion), channel_id=1, source_target_pairs={{0,2},{2,0},{4,6},{6,4},{8,10},{10,8},{12,14},{14,12},{16,18},{18,... | collective-permute-start | bytes 36872 | tf_op jit(solution)/shard_map/ppermute | solution.py:609
  20.5 1.6 %collective-permute-done.6 = f32[3,8,128]{2,1,0:T(8,128)S(1)} collective-permute-done((f32[3,8,128]{2,1,0:T(8,128)S(1)}, f32[3,8,128]{2,1,0:T(8,128)S(1)}, u32[]{:S(2)}, u32[]{:S(2)}) %collective-permute-start.6) | collective-permute-done | bytes 12320 | tf_op jit(solution)/shard_map/ppermute | solution.py:609
  22.0 1.5 %collective-permute-done.7 = f32[3,8,128]{2,1,0:T(8,128)S(1)} collective-permute-done((f32[3,8,128]{2,1,0:T(8,128)S(1)}, f32[3,8,128]{2,1,0:T(8,128)S(1)}, u32[]{:S(2)}, u32[]{:S(2)}) %collective-permute-start.7) | collective-permute-done | bytes 12320 | tf_op jit(solution)/shard_map/ppermute | solution.py:609
  26.3 2.2 %own_conv.1.rest_1_ = f32[448,1152]{1,0:T(8,128)S(1)} custom-call(s32[67]{0:T(128)S(1)} %pad_add_fusion.info_ref, bf16[6,112,384]{2,1,0:T(8,128)(2,1)S(1)} %get-tuple-element.50.hidden_ref, bf16[2304,1152]{1,0:T(8,128)(2,1)S(1)} %hold.1.held_ref.rest_4_), custom_call_target="tpu_custom_call" | custom-call | flops 2420000000 | tf_op jit(solution)/shard_map/own_conv/pallas_call | solution.py:665
  28.6 3.7 %conv.1 = (bf16[2,208,384]{2,1,0:T(8,128)(2,1)S(1)}, f32[3,8,128]{2,1,0:T(8,128)S(1)}) custom-call(s32[67]{0:T(128)S(1)} %pad_add_fusion.info_ref, bf16[6,112,384]{2,1,0:T(8,128)(2,1)S(1)} %collective-permute-done.8.rest_0_, f32[448,1152]{1,0:T(8,128)S(1)} %own_conv.1.rest_1_, bf16[4,104,384]{2,1,0:T(8,128)(2,1)S(1)} %get-tuple-element.52.rest_2_, ...), custom_call_target="tpu_custom_call" | custom-call | flops 3849999872 | tf_op jit(solution)/shard_map/conv/pallas_call | solution.py:665
  32.3 2.5 %collective-permute-start.10 = (f32[3,8,128]{2,1,0:T(8,128)S(1)}, f32[3,8,128]{2,1,0:T(8,128)S(1)}, u32[]{:S(2)}, u32[]{:S(2)}) collective-permute-start(f32[3,8,128]{2,1,0:T(8,128)S(1)} %get-tuple-element.54), channel_id=1, source_target_pairs={{0,16},{2,18},{4,20},{6,22},{8,24},{10,26},{12,28},{14,30},{16,0},... | collective-permute-start | bytes 36872 | tf_op jit(solution)/shard_map/ppermute | solution.py:609
  34.8 1.9 %collective-permute-start.11 = (f32[3,8,128]{2,1,0:T(8,128)S(1)}, f32[3,8,128]{2,1,0:T(8,128)S(1)}, u32[]{:S(2)}, u32[]{:S(2)}) collective-permute-start(f32[3,8,128]{2,1,0:T(8,128)S(1)} %get-tuple-element.54), channel_id=1, source_target_pairs={{0,24},{2,26},{4,28},{6,30},{8,16},{10,18},{12,20},{14,22},{16,8},... | collective-permute-start | bytes 36872 | tf_op jit(solution)/shard_map/ppermute | solution.py:609
  36.8 2.0 %collective-permute-start.13 = (bf16[2,208,384]{2,1,0:T(8,128)(2,1)S(1)}, bf16[2,208,384]{2,1,0:T(8,128)(2,1)S(1)}, u32[]{:S(2)}, u32[]{:S(2)}) collective-permute-start(bf16[2,208,384]{2,1,0:T(8,128)(2,1)S(1)} %get-tuple-element.56.own_ref.rest_5_), channel_id=1, source_target_pairs={{0,8},{2,10},{4,12},{6,14},{8,0},{10,2},{12,4},{14,6},{16,24},{18,... | collective-permute-start | bytes 958472 | tf_op jit(solution)/shard_map/ppermute | solution.py:609
  38.8 2.0 %collective-permute-start.14 = (bf16[2,208,384]{2,1,0:T(8,128)(2,1)S(1)}, bf16[2,208,384]{2,1,0:T(8,128)(2,1)S(1)}, u32[]{:S(2)}, u32[]{:S(2)}) collective-permute-start(bf16[2,208,384]{2,1,0:T(8,128)(2,1)S(1)} %get-tuple-element.56.own_ref.rest_5_), channel_id=1, source_target_pairs={{8,16},{10,18},{12,20},{14,22},{16,8},{18,10},{20,12},{22,14},{9,1... | collective-permute-start | bytes 958472 | tf_op jit(solution)/shard_map/ppermute | solution.py:609
  45.6 3.0 %collective-permute-done.14.rest_8_ = bf16[2,208,384]{2,1,0:T(8,128)(2,1)S(1)} collective-permute-done((bf16[2,208,384]{2,1,0:T(8,128)(2,1)S(1)}, bf16[2,208,384]{2,1,0:T(8,128)(2,1)S(1)}, u32[]{:S(2)}, u32[]{:S(2)}) %collective-permute-start.14) | collective-permute-done | bytes 319520 | tf_op jit(solution)/shard_map/ppermute | solution.py:609
  48.6 2.2 %collective-permute-start.19 = (bf16[2,208,384]{2,1,0:T(8,128)(2,1)S(1)}, bf16[2,208,384]{2,1,0:T(8,128)(2,1)}, u32[]{:S(2)}, u32[]{:S(2)}) collective-permute-start(bf16[2,208,384]{2,1,0:T(8,128)(2,1)S(1)} %collective-permute-done.13.rest_7_), channel_id=1, source_target_pairs={{8,16},{10,18},{12,20},{14,22},{16,8},{18,10},{20,12},{22,14},{9,1... | collective-permute-start | bytes 958472 | tf_op jit(solution)/shard_map/ppermute | solution.py:609
  50.8 2.0 %collective-permute-start.20 = (bf16[2,208,384]{2,1,0:T(8,128)(2,1)S(1)}, bf16[2,208,384]{2,1,0:T(8,128)(2,1)}, u32[]{:S(2)}, u32[]{:S(2)}) collective-permute-start(bf16[2,208,384]{2,1,0:T(8,128)(2,1)S(1)} %collective-permute-done.14.rest_8_), channel_id=1, source_target_pairs={{8,0},{10,2},{12,4},{14,6},{16,24},{18,26},{20,28},{22,30},{9,1},{... | collective-permute-start | bytes 958472 | tf_op jit(solution)/shard_map/ppermute | solution.py:609
  59.9 3.8 %collective-permute-start.21 = (bf16[2,208,384]{2,1,0:T(8,128)(2,1)S(1)}, bf16[2,208,384]{2,1,0:T(8,128)(2,1)S(1)}, u32[]{:S(2)}, u32[]{:S(2)}) collective-permute-start(bf16[2,208,384]{2,1,0:T(8,128)(2,1)S(1)} %collective-permute-done.18.rest_6_), channel_id=1, source_target_pairs={{8,16},{10,18},{12,20},{14,22},{16,8},{18,10},{20,12},{22,14},{9,1... | collective-permute-start | bytes 958472 | tf_op jit(solution)/shard_map/ppermute | solution.py:609
  65.2 2.5 %queries.1 = (f32[8,384]{1,0:T(8,128)S(1)}, f32[8,384]{1,0:T(8,128)S(1)}, bf16[416,384]{1,0:T(8,128)(2,1)S(1)}, f32[416,128]{1,0:T(8,128)S(1)}, bf16[416,384]{1,0:T(8,128)(2,1)S(1)}, /*index=5*/f32[416,128]{1,0:T(8,128)S(1)}) custom-call(s32[67]{0:T(128)S(1)} %pad_add_fusion.info_ref, bf16[2,208,384]{2,1,0:T(8,128)(2,1)S(1)} %get-tuple-element.56.own_ref.rest_5_, ...), custom_call_target="tpu_custom_call" | custom-call | flops 2090000000 | tf_op jit(solution)/shard_map/queries/pallas_call | solution.py:665
  67.7 3.0 %attend_yours.2 = (bf16[1664,384]{1,0:T(8,128)(2,1)S(1)}, f32[416,128]{1,0:T(8,128)S(1)}, f32[416,128]{1,0:T(8,128)S(1)}, f32[416,384]{1,0:T(8,128)S(1)}) custom-call(s32[67]{0:T(128)S(1)} %pad_add_fusion.info_ref, f32[8,384]{1,0:T(8,128)S(1)} %get-tuple-element.61.rest_0_, f32[8,384]{1,0:T(8,128)S(1)} %get-tuple-element.62.rest_1_, ...), custom_call_target="tpu_custom_call" | custom-call | flops 3960000000 | tf_op jit(solution)/shard_map/attend_yours/pallas_call | solution.py:665
  70.9 3.0 %attend_yours.3 = (bf16[1664,384]{1,0:T(8,128)(2,1)S(1)}, bf16[432,384]{1,0:T(8,128)(2,1)S(1)}) custom-call(s32[67]{0:T(128)S(1)} %pad_add_fusion.info_ref, f32[8,384]{1,0:T(8,128)S(1)} %get-tuple-element.61.rest_0_, f32[8,384]{1,0:T(8,128)S(1)} %get-tuple-element.62.rest_1_, f32[1,384]{1,0:T(1,128)S(1)} %reshape.86.shift_ref.rest_2_, ...), custom_call_target="tpu_custom_call" | custom-call | flops 3960000000 | tf_op jit(solution)/shard_map/attend_yours/pallas_call | solution.py:665
  75.4 4.9 %attend_mine.1 = (f32[416,384]{1,0:T(8,128)S(1)}, f32[416,128]{1,0:T(8,128)S(1)}) custom-call(s32[67]{0:T(128)S(1)} %pad_add_fusion.info_ref, bf16[416,384]{1,0:T(8,128)(2,1)S(1)} %get-tuple-element.74.queries_ref, f32[416,128]{1,0:T(8,128)S(1)} %get-tuple-element.75.constant_ref, bf16[1664,384]{1,0:T(8,128)(2,1)S(1)} %get-tuple-element.76.rest_0_, ...), custom_call_target="tpu_custom_call" | custom-call | flops 4729999872 | tf_op jit(solution)/shard_map/attend_mine/pallas_call | solution.py:665
  82.5 5.1 %collective-permute-start.25 = (bf16[1,104,384]{2,1,0:T(8,128)(2,1)S(1)}, bf16[1,104,384]{2,1,0:T(8,128)(2,1)S(1)}, u32[]{:S(2)}, u32[]{:S(2)}) collective-permute-start(bf16[1,104,384]{2,1,0:T(8,128)(2,1)S(1)} %get-tuple-element.81), channel_id=1, source_target_pairs={{2,4},{4,2},{6,8},{8,6},{10,12},{12,10},{14,16},{16,14},{18,20},{2... | collective-permute-start | bytes 239624 | tf_op jit(solution)/shard_map/ppermute | solution.py:823
  87.6 3.0 %upsample.1 = (bf16[8,192,208]{2,1,0:T(8,128)(2,1)}, f32[2,2,256,128]{3,2,1,0:T(8,128)S(1)}) custom-call(s32[67]{0:T(128)S(1)} %pad_add_fusion.info_ref, bf16[4,104,384]{2,1,0:T(8,128)(2,1)S(1)} %get-tuple-element.83.own_ref, bf16[2,2,2,192,768]{4,3,2,1,0:T(8,128)(2,1)S(1)} %get-tuple-element.84.weight_ref, f32[1,256]{1,0:T(1,128)S(1)} %pad.4.bias_ref), custom_call_target="tpu_custom_call" | custom-call | flops 2200000000 | tf_op jit(solution)/shard_map/upsample/pallas_call | solution.py:830
  92.0 1.9 %close.1 = bf16[8,192,208]{2,1,0:T(8,128)(2,1)} custom-call(s32[67]{0:T(128)S(1)} %pad_add_fusion.info_ref, bf16[1,104,384]{2,1,0:T(8,128)(2,1)S(1)} %collective-permute-done.25.outer_ref, bf16[1,104,384]{2,1,0:T(8,128)(2,1)S(1)} %collective-permute-done.26.inner_ref, bf16[8,192,208]{2,1,0:T(8,128)(2,1)} %get-tuple-element.85._, ...), custom_call_target="tpu_custom_call", output_to_operand_aliasing={{}: (3, {})} | custom-call | flops 1100000000 | tf_op jit(solution)/shard_map/close/pallas_call | solution.py:845
  (92 shorter events, 28.5 us)
Async XLA Ops:
  0.9 8.6 %collective-permute-start = (bf16[1,104,384]{2,1,0:T(8,128)(2,1)S(1)}, bf16[1,104,384]{2,1,0:T(8,128)(2,1)S(1)}, u32[]{:S(2)}, u32[]{:S(2)}) collective-permute-start(bf16[1,104,384]{2,1,0:T(8,128)(2,1)S(1)} %get-tuple-element.99), channel_id=1, source_target_pairs={{2,4},{4,2},{6,8},{8,6},{10,12},{12,10},{14,16},{16,14},{18,20},{2... | collective-permute-start | bytes 239624 | tf_op jit(solution)/shard_map/ppermute | solution.py:683
  5.2 4.7 %collective-permute-start.1 = (bf16[1,104,384]{2,1,0:T(8,128)(2,1)S(1)}, bf16[1,104,384]{2,1,0:T(8,128)(2,1)S(1)}, u32[]{:S(2)}, u32[]{:S(2)}) collective-permute-start(bf16[1,104,384]{2,1,0:T(8,128)(2,1)S(1)} %get-tuple-element.98), channel_id=1, source_target_pairs={{0,2},{2,0},{4,6},{6,4},{8,10},{10,8},{12,14},{14,12},{16,18},{18,... | collective-permute-start | bytes 239624 | tf_op jit(solution)/shard_map/ppermute | solution.py:609
  9.9 6.1 %collective-permute-start.2 = (f32[3,8,128]{2,1,0:T(8,128)S(1)}, f32[3,8,128]{2,1,0:T(8,128)S(1)}, u32[]{:S(2)}, u32[]{:S(2)}) collective-permute-start(f32[3,8,128]{2,1,0:T(8,128)S(1)} %first_stats.1), channel_id=1, source_target_pairs={{0,8},{2,10},{4,12},{6,14},{8,0},{10,2},{12,4},{14,6},{16,24},{18,... | collective-permute-start | bytes 36872 | tf_op jit(solution)/shard_map/ppermute | solution.py:609
  10.1 6.0 %collective-permute-start.3 = (f32[3,8,128]{2,1,0:T(8,128)S(1)}, f32[3,8,128]{2,1,0:T(8,128)S(1)}, u32[]{:S(2)}, u32[]{:S(2)}) collective-permute-start(f32[3,8,128]{2,1,0:T(8,128)S(1)} %first_stats.1), channel_id=1, source_target_pairs={{0,16},{2,18},{4,20},{6,22},{8,24},{10,26},{12,28},{14,30},{16,0},... | collective-permute-start | bytes 36872 | tf_op jit(solution)/shard_map/ppermute | solution.py:609
  16.7 3.8 %collective-permute-start.5 = (f32[3,8,128]{2,1,0:T(8,128)S(1)}, f32[3,8,128]{2,1,0:T(8,128)S(1)}, u32[]{:S(2)}, u32[]{:S(2)}) collective-permute-start(f32[3,8,128]{2,1,0:T(8,128)S(1)} %pad_maximum_fusion), channel_id=1, source_target_pairs={{0,2},{2,0},{4,6},{6,4},{8,10},{10,8},{12,14},{14,12},{16,18},{18,... | collective-permute-start | bytes 36872 | tf_op jit(solution)/shard_map/ppermute | solution.py:609
  19.0 4.6 %collective-permute-start.7 = (f32[3,8,128]{2,1,0:T(8,128)S(1)}, f32[3,8,128]{2,1,0:T(8,128)S(1)}, u32[]{:S(2)}, u32[]{:S(2)}) collective-permute-start(f32[3,8,128]{2,1,0:T(8,128)S(1)} %pad_maximum_fusion), channel_id=1, source_target_pairs={{0,6},{2,4},{4,2},{6,0},{8,14},{10,12},{12,10},{14,8},{16,22},{18,... | collective-permute-start | bytes 36872 | tf_op jit(solution)/shard_map/ppermute | solution.py:609
  32.3 8.5 %collective-permute-start.10 = (f32[3,8,128]{2,1,0:T(8,128)S(1)}, f32[3,8,128]{2,1,0:T(8,128)S(1)}, u32[]{:S(2)}, u32[]{:S(2)}) collective-permute-start(f32[3,8,128]{2,1,0:T(8,128)S(1)} %get-tuple-element.54), channel_id=1, source_target_pairs={{0,16},{2,18},{4,20},{6,22},{8,24},{10,26},{12,28},{14,30},{16,0},... | collective-permute-start | bytes 36872 | tf_op jit(solution)/shard_map/ppermute | solution.py:609
  34.8 6.0 %collective-permute-start.11 = (f32[3,8,128]{2,1,0:T(8,128)S(1)}, f32[3,8,128]{2,1,0:T(8,128)S(1)}, u32[]{:S(2)}, u32[]{:S(2)}) collective-permute-start(f32[3,8,128]{2,1,0:T(8,128)S(1)} %get-tuple-element.54), channel_id=1, source_target_pairs={{0,24},{2,26},{4,28},{6,30},{8,16},{10,18},{12,20},{14,22},{16,8},... | collective-permute-start | bytes 36872 | tf_op jit(solution)/shard_map/ppermute | solution.py:609
  36.7 4.1 %collective-permute-start.9 = (f32[3,8,128]{2,1,0:T(8,128)S(1)}, f32[3,8,128]{2,1,0:T(8,128)S(1)}, u32[]{:S(2)}, u32[]{:S(2)}) collective-permute-start(f32[3,8,128]{2,1,0:T(8,128)S(1)} %get-tuple-element.54), channel_id=1, source_target_pairs={{0,8},{2,10},{4,12},{6,14},{8,0},{10,2},{12,4},{14,6},{16,24},{18,... | collective-permute-start | bytes 36872 | tf_op jit(solution)/shard_map/ppermute | solution.py:609
  36.8 8.8 %collective-permute-start.13 = (bf16[2,208,384]{2,1,0:T(8,128)(2,1)S(1)}, bf16[2,208,384]{2,1,0:T(8,128)(2,1)S(1)}, u32[]{:S(2)}, u32[]{:S(2)}) collective-permute-start(bf16[2,208,384]{2,1,0:T(8,128)(2,1)S(1)} %get-tuple-element.56.own_ref.rest_5_), channel_id=1, source_target_pairs={{0,8},{2,10},{4,12},{6,14},{8,0},{10,2},{12,4},{14,6},{16,24},{18,... | collective-permute-start | bytes 958472 | tf_op jit(solution)/shard_map/ppermute | solution.py:609
  38.8 9.8 %collective-permute-start.14 = (bf16[2,208,384]{2,1,0:T(8,128)(2,1)S(1)}, bf16[2,208,384]{2,1,0:T(8,128)(2,1)S(1)}, u32[]{:S(2)}, u32[]{:S(2)}) collective-permute-start(bf16[2,208,384]{2,1,0:T(8,128)(2,1)S(1)} %get-tuple-element.56.own_ref.rest_5_), channel_id=1, source_target_pairs={{8,16},{10,18},{12,20},{14,22},{16,8},{18,10},{20,12},{22,14},{9,1... | collective-permute-start | bytes 958472 | tf_op jit(solution)/shard_map/ppermute | solution.py:609
  40.9 3.8 %collective-permute-start.12 = (f32[3,8,128]{2,1,0:T(8,128)S(1)}, f32[3,8,128]{2,1,0:T(8,128)S(1)}, u32[]{:S(2)}, u32[]{:S(2)}) collective-permute-start(f32[3,8,128]{2,1,0:T(8,128)S(1)} %pad_maximum_fusion.2), channel_id=1, source_target_pairs={{0,2},{2,0},{4,6},{6,4},{8,10},{10,8},{12,14},{14,12},{16,18},{18,... | collective-permute-start | bytes 36872 | tf_op jit(solution)/shard_map/ppermute | solution.py:609
  42.4 10.4 %collective-permute-start.15 = (f32[3,8,128]{2,1,0:T(8,128)S(1)}, f32[3,8,128]{2,1,0:T(8,128)S(1)}, u32[]{:S(2)}, u32[]{:S(2)}) collective-permute-start(f32[3,8,128]{2,1,0:T(8,128)S(1)} %pad_maximum_fusion.2), channel_id=1, source_target_pairs={{0,4},{2,6},{4,0},{6,2},{8,12},{10,14},{12,8},{14,10},{16,20},{18,... | collective-permute-start | bytes 36872 | tf_op jit(solution)/shard_map/ppermute | solution.py:609
  43.3 9.5 %collective-permute-start.16 = (f32[3,8,128]{2,1,0:T(8,128)S(1)}, f32[3,8,128]{2,1,0:T(8,128)S(1)}, u32[]{:S(2)}, u32[]{:S(2)}) collective-permute-start(f32[3,8,128]{2,1,0:T(8,128)S(1)} %pad_maximum_fusion.2), channel_id=1, source_target_pairs={{0,6},{2,4},{4,2},{6,0},{8,14},{10,12},{12,10},{14,8},{16,22},{18,... | collective-permute-start | bytes 36872 | tf_op jit(solution)/shard_map/ppermute | solution.py:609
  48.6 9.0 %collective-permute-start.19 = (bf16[2,208,384]{2,1,0:T(8,128)(2,1)S(1)}, bf16[2,208,384]{2,1,0:T(8,128)(2,1)}, u32[]{:S(2)}, u32[]{:S(2)}) collective-permute-start(bf16[2,208,384]{2,1,0:T(8,128)(2,1)S(1)} %collective-permute-done.13.rest_7_), channel_id=1, source_target_pairs={{8,16},{10,18},{12,20},{14,22},{16,8},{18,10},{20,12},{22,14},{9,1... | collective-permute-start | bytes 958472 | tf_op jit(solution)/shard_map/ppermute | solution.py:609
  50.8 6.8 %collective-permute-start.20 = (bf16[2,208,384]{2,1,0:T(8,128)(2,1)S(1)}, bf16[2,208,384]{2,1,0:T(8,128)(2,1)}, u32[]{:S(2)}, u32[]{:S(2)}) collective-permute-start(bf16[2,208,384]{2,1,0:T(8,128)(2,1)S(1)} %collective-permute-done.14.rest_8_), channel_id=1, source_target_pairs={{8,0},{10,2},{12,4},{14,6},{16,24},{18,26},{20,28},{22,30},{9,1},{... | collective-permute-start | bytes 958472 | tf_op jit(solution)/shard_map/ppermute | solution.py:609
  52.8 7.1 %collective-permute-start.18 = (bf16[2,208,384]{2,1,0:T(8,128)(2,1)S(1)}, bf16[2,208,384]{2,1,0:T(8,128)(2,1)S(1)}, u32[]{:S(2)}, u32[]{:S(2)}) collective-permute-start(bf16[2,208,384]{2,1,0:T(8,128)(2,1)S(1)} %get-tuple-element.56.own_ref.rest_5_), channel_id=1, source_target_pairs={{0,4},{2,6},{4,0},{6,2},{8,12},{10,14},{12,8},{14,10},{16,20},{18,... | collective-permute-start | bytes 958472 | tf_op jit(solution)/shard_map/ppermute | solution.py:609
  54.3 9.5 %collective-permute-start.17 = (bf16[2,208,384]{2,1,0:T(8,128)(2,1)S(1)}, bf16[2,208,384]{2,1,0:T(8,128)(2,1)}, u32[]{:S(2)}, u32[]{:S(2)}) collective-permute-start(bf16[2,208,384]{2,1,0:T(8,128)(2,1)S(1)} %get-tuple-element.56.own_ref.rest_5_), channel_id=1, source_target_pairs={{0,2},{2,0},{4,6},{6,4},{8,10},{10,8},{12,14},{14,12},{16,18},{18,... | collective-permute-start | bytes 958472 | tf_op jit(solution)/shard_map/ppermute | solution.py:609
  59.9 10.8 %collective-permute-start.21 = (bf16[2,208,384]{2,1,0:T(8,128)(2,1)S(1)}, bf16[2,208,384]{2,1,0:T(8,128)(2,1)S(1)}, u32[]{:S(2)}, u32[]{:S(2)}) collective-permute-start(bf16[2,208,384]{2,1,0:T(8,128)(2,1)S(1)} %collective-permute-done.18.rest_6_), channel_id=1, source_target_pairs={{8,16},{10,18},{12,20},{14,22},{16,8},{18,10},{20,12},{22,14},{9,1... | collective-permute-start | bytes 958472 | tf_op jit(solution)/shard_map/ppermute | solution.py:609
  63.7 7.1 %collective-permute-start.22 = (bf16[2,208,384]{2,1,0:T(8,128)(2,1)S(1)}, bf16[2,208,384]{2,1,0:T(8,128)(2,1)S(1)}, u32[]{:S(2)}, u32[]{:S(2)}) collective-permute-start(bf16[2,208,384]{2,1,0:T(8,128)(2,1)S(1)} %collective-permute-done.18.rest_6_), channel_id=1, source_target_pairs={{0,8},{2,10},{4,12},{6,14},{8,0},{10,2},{12,4},{14,6},{16,24},{18,... | collective-permute-start | bytes 958472 | tf_op jit(solution)/shard_map/ppermute | solution.py:609
  63.8 7.1 %collective-permute-start.23 = (bf16[2,208,384]{2,1,0:T(8,128)(2,1)S(1)}, bf16[2,208,384]{2,1,0:T(8,128)(2,1)S(1)}, u32[]{:S(2)}, u32[]{:S(2)}) collective-permute-start(bf16[2,208,384]{2,1,0:T(8,128)(2,1)S(1)} %broadcast_select_fusion.rest_5_), channel_id=1, source_target_pairs={{0,4},{2,6},{4,0},{6,2},{8,12},{10,14},{12,8},{14,10},{16,20},{18,... | collective-permute-start | bytes 958472 | tf_op jit(solution)/shard_map/ppermute | solution.py:609
  73.9 7.2 %collective-permute-start.24 = (bf16[432,384]{1,0:T(8,128)(2,1)S(1)}, bf16[432,384]{1,0:T(8,128)(2,1)S(1)}, u32[]{:S(2)}, u32[]{:S(2)}) collective-permute-start(bf16[432,384]{1,0:T(8,128)(2,1)S(1)} %get-tuple-element.72), channel_id=1, source_target_pairs={{0,2},{2,0},{4,6},{6,4},{8,10},{10,8},{12,14},{14,12},{16,18},{18,... | collective-permute-start | bytes 995336 | tf_op jit(solution)/shard_map/ppermute | solution.py:802
  82.5 8.2 %collective-permute-start.25 = (bf16[1,104,384]{2,1,0:T(8,128)(2,1)S(1)}, bf16[1,104,384]{2,1,0:T(8,128)(2,1)S(1)}, u32[]{:S(2)}, u32[]{:S(2)}) collective-permute-start(bf16[1,104,384]{2,1,0:T(8,128)(2,1)S(1)} %get-tuple-element.81), channel_id=1, source_target_pairs={{2,4},{4,2},{6,8},{8,6},{10,12},{12,10},{14,16},{16,14},{18,20},{2... | collective-permute-start | bytes 239624 | tf_op jit(solution)/shard_map/ppermute | solution.py:823
  87.5 4.5 %collective-permute-start.26 = (bf16[1,104,384]{2,1,0:T(8,128)(2,1)S(1)}, bf16[1,104,384]{2,1,0:T(8,128)(2,1)S(1)}, u32[]{:S(2)}, u32[]{:S(2)}) collective-permute-start(bf16[1,104,384]{2,1,0:T(8,128)(2,1)S(1)} %get-tuple-element.82), channel_id=1, source_target_pairs={{0,2},{2,0},{4,6},{6,4},{8,10},{10,8},{12,14},{14,12},{16,18},{18,... | collective-permute-start | bytes 239624 | tf_op jit(solution)/shard_map/ppermute | solution.py:609
  (16 other events, 244.8 us)

commit v8 on v6

--- a/solution.py
+++ b/solution.py
@@ -597,13 +597,15 @@
     return lax.ppermute(array, "tile", moves)
 
 
-def merge_round(stats, tiles, masks, tied=()):
+def merge_round(stats, tiles, masks, tied=(), after=None):
     parts = [stats] + [exchange(stats, tiles, mask) for mask in masks]
+    free = ()
     if tied:
+        *parts[2:], free = lax.optimization_barrier((*parts[2:], after))
         parts[1], *tied = lax.optimization_barrier((parts[1], *tied))
     while len(parts) > 1:
         parts = [merge_stats(*parts[i : i + 2]) for i in range(0, len(parts), 2)]
-    return (parts[0], *tied) if tied else parts[0]
+    return (parts[0], *tied, free) if tied else parts[0]
 
 
 def merge_masks(tiles):
@@ -730,10 +732,9 @@
         stats = merge_round(stats, tiles, rounds[1])
         blocks[2] = exchange(own, tiles, 4)
         blocks[6] = exchange(own, tiles, 12, middle)
-        stats, blocks[2], blocks[6] = merge_round(
-            stats, tiles, rounds[0], (blocks[2], blocks[6])
+        stats, blocks[2], blocks[6], own_xy = merge_round(
+            stats, tiles, rounds[0], (blocks[2], blocks[6]), own
         )
-        stats, own_xy = lax.optimization_barrier((stats, own))
         inward = exchange(blocks[2], tiles, 12, middle)
         outward = exchange(blocks[6], tiles, 4, middle)
         other = exchange(own_xy, tiles, 1)

time: 94.3 us -> 94.3 us (level)
  starting transfers between devices: 43 us -> 44.9 us
  waiting for transfers between devices: 15 us -> 13.5 us
    ppermute x23, starting transfers between devices: 31.7 us -> 33 us  [exchange(): return lax.ppermute(array, 'tile', moves)]
  transfers between devices with their start and end apart: 27 -> 27, of which waited for: 15 -> 14; matrix products, arithmetic and copies ran while one was open for 1% -> 1% of each run, Pallas kernels for 21% -> 21%
where the time goes in v8:
time: 94.3 us; the launch traced here: 92.9 us
  starting transfers between devices  44.9 us (48%)
  Pallas kernels  30.7 us (33%)
  waiting for transfers between devices  13.5 us (14%)
  other arithmetic  1.9 us (2%)
  local copies, waits for them, and re-layouts  1.37 us (1%)
    ppermute x23, starting transfers between devices, exchange(): return lax.ppermute(array, 'tile', moves)  33 us
    pallas_call x11, Pallas kernels, call(): pl.pallas_call(kernel, out_shape=out_shape, in_specs=[SMEM_SPEC] + [VMEM_...  27.6 us
    ppermute x23, waiting for transfers between devices, exchange(): return lax.ppermute(array, 'tile', moves)  12.7 us
    ppermute x1, starting transfers between devices, shards(): outer = lax.ppermute(outer, 'tile', outer_moves)  5.25 us
    ppermute x1, starting transfers between devices, shards(): lax.ppermute(jnp.where(odd, source[row_count - 1:], source[:1]), 'tile',...  4.24 us
    pallas_call x1, Pallas kernels, shards(): pl.pallas_call(functools.partial(hold_kernel, taps), out_shape=shape(3 *...  2.63 us
  transfers between devices with their start and end apart: 27, of which 14 were waited for; matrix products, arithmetic and copies ran while one was open for 1% of the time, Pallas kernels for 21%

profile of v8, /device:TPU:8, one launch (start us, length us, event | category | flops | bytes accessed | tf_op | source)
XLA Modules:
  0.0 92.9 jit_solution(9014049915594213908)
XLA Ops:
  0.9 4.2 %collective-permute-start = (bf16[1,104,384]{2,1,0:T(8,128)(2,1)S(1)}, bf16[1,104,384]{2,1,0:T(8,128)(2,1)S(1)}, u32[]{:S(2)}, u32[]{:S(2)}) collective-permute-start(bf16[1,104,384]{2,1,0:T(8,128)(2,1)S(1)} %get-tuple-element.89), channel_id=1, source_target_pairs={{2,4},{4,2},{6,8},{8,6},{10,12},{12,10},{14,16},{16,14},{18,20},{2... | collective-permute-start | bytes 239624 | tf_op jit(solution)/shard_map/ppermute | solution.py:673
  7.6 1.8 %first_stats.1 = f32[3,8,128]{2,1,0:T(8,128)S(1)} custom-call(s32[67]{0:T(128)S(1)} %pad_add_fusion.info_ref, bf16[4,104,384]{2,1,0:T(8,128)(2,1)S(1)} %bitcast.14), custom_call_target="tpu_custom_call" | custom-call | flops 1650000000 | tf_op jit(solution)/shard_map/first_stats/pallas_call | solution.py:655
  9.9 1.6 %collective-permute-start.4 = (f32[3,8,128]{2,1,0:T(8,128)S(1)}, f32[3,8,128]{2,1,0:T(8,128)S(1)}, u32[]{:S(2)}, u32[]{:S(2)}) collective-permute-start(f32[3,8,128]{2,1,0:T(8,128)S(1)} %first_stats.1), channel_id=1, source_target_pairs={{0,24},{2,26},{4,28},{6,30},{8,16},{10,18},{12,20},{14,22},{16,8},... | collective-permute-start | bytes 36872 | tf_op jit(solution)/shard_map/ppermute | solution.py:597
  14.0 2.6 %hold.1.held_ref.rest_4_ = bf16[2304,1152]{1,0:T(8,128)(2,1)S(1)} custom-call(bf16[3,3,3,384,384]{4,3,2,1,0:T(8,128)(2,1)} %weight_ref.3), custom_call_target="tpu_custom_call" | custom-call | flops 3300000000 | tf_op jit(solution)/shard_map/hold/pallas_call | solution.py:679
  26.0 2.2 %own_conv.1.rest_1_ = f32[448,1152]{1,0:T(8,128)S(1)} custom-call(s32[67]{0:T(128)S(1)} %pad_add_fusion.info_ref, bf16[6,112,384]{2,1,0:T(8,128)(2,1)S(1)} %get-tuple-element.45.hidden_ref, bf16[2304,1152]{1,0:T(8,128)(2,1)S(1)} %hold.1.held_ref.rest_4_), custom_call_target="tpu_custom_call" | custom-call | flops 2420000000 | tf_op jit(solution)/shard_map/own_conv/pallas_call | solution.py:655
  28.2 3.7 %conv.1 = (bf16[2,208,384]{2,1,0:T(8,128)(2,1)S(1)}, f32[3,8,128]{2,1,0:T(8,128)S(1)}) custom-call(s32[67]{0:T(128)S(1)} %pad_add_fusion.info_ref, bf16[6,112,384]{2,1,0:T(8,128)(2,1)S(1)} %collective-permute-done.8.rest_0_, f32[448,1152]{1,0:T(8,128)S(1)} %own_conv.1.rest_1_, bf16[4,104,384]{2,1,0:T(8,128)(2,1)S(1)} %get-tuple-element.47.rest_2_, ...), custom_call_target="tpu_custom_call" | custom-call | flops 3849999872 | tf_op jit(solution)/shard_map/conv/pallas_call | solution.py:655
  32.0 2.2 %collective-permute-start.11 = (f32[3,8,128]{2,1,0:T(8,128)S(1)}, f32[3,8,128]{2,1,0:T(8,128)S(1)}, u32[]{:S(2)}, u32[]{:S(2)}) collective-permute-start(f32[3,8,128]{2,1,0:T(8,128)S(1)} %get-tuple-element.48), channel_id=1, source_target_pairs={{0,24},{2,26},{4,28},{6,30},{8,16},{10,18},{12,20},{14,22},{16,8},... | collective-permute-start | bytes 36872 | tf_op jit(solution)/shard_map/ppermute | solution.py:597
  34.2 1.8 %collective-permute-start.10 = (f32[3,8,128]{2,1,0:T(8,128)S(1)}, f32[3,8,128]{2,1,0:T(8,128)S(1)}, u32[]{:S(2)}, u32[]{:S(2)}) collective-permute-start(f32[3,8,128]{2,1,0:T(8,128)S(1)} %get-tuple-element.48), channel_id=1, source_target_pairs={{0,16},{2,18},{4,20},{6,22},{8,24},{10,26},{12,28},{14,30},{16,0},... | collective-permute-start | bytes 36872 | tf_op jit(solution)/shard_map/ppermute | solution.py:597
  36.1 1.9 %collective-permute-start.16 = (bf16[2,208,384]{2,1,0:T(8,128)(2,1)S(1)}, bf16[2,208,384]{2,1,0:T(8,128)(2,1)S(1)}, u32[]{:S(2)}, u32[]{:S(2)}) collective-permute-start(bf16[2,208,384]{2,1,0:T(8,128)(2,1)S(1)} %get-tuple-element.66.rest_5_.own_ref), channel_id=1, source_target_pairs={{0,8},{2,10},{4,12},{6,14},{8,0},{10,2},{12,4},{14,6},{16,24},{18,... | collective-permute-start | bytes 958472 | tf_op jit(solution)/shard_map/ppermute | solution.py:597
  38.0 3.5 %collective-permute-start.17 = (bf16[2,208,384]{2,1,0:T(8,128)(2,1)S(1)}, bf16[2,208,384]{2,1,0:T(8,128)(2,1)S(1)}, u32[]{:S(2)}, u32[]{:S(2)}) collective-permute-start(bf16[2,208,384]{2,1,0:T(8,128)(2,1)S(1)} %get-tuple-element.66.rest_5_.own_ref), channel_id=1, source_target_pairs={{8,16},{10,18},{12,20},{14,22},{16,8},{18,10},{20,12},{22,14},{9,1... | collective-permute-start | bytes 958472 | tf_op jit(solution)/shard_map/ppermute | solution.py:597
  42.3 1.8 %collective-permute-start.13 = (f32[3,8,128]{2,1,0:T(8,128)S(1)}, f32[3,8,128]{2,1,0:T(8,128)S(1)}, u32[]{:S(2)}, u32[]{:S(2)}) collective-permute-start(f32[3,8,128]{2,1,0:T(8,128)S(1)} %pad_maximum_fusion.2), channel_id=1, source_target_pairs={{0,6},{2,4},{4,2},{6,0},{8,14},{10,12},{12,10},{14,8},{16,22},{18,... | collective-permute-start | bytes 36872 | tf_op jit(solution)/shard_map/ppermute | solution.py:597
  45.3 1.6 %collective-permute-done.13 = f32[3,8,128]{2,1,0:T(8,128)S(1)} collective-permute-done((f32[3,8,128]{2,1,0:T(8,128)S(1)}, f32[3,8,128]{2,1,0:T(8,128)S(1)}, u32[]{:S(2)}, u32[]{:S(2)}) %collective-permute-start.13) | collective-permute-done | bytes 12320 | tf_op jit(solution)/shard_map/ppermute | solution.py:597
  46.9 1.6 %collective-permute-start.14 = (bf16[2,208,384]{2,1,0:T(8,128)(2,1)S(1)}, bf16[2,208,384]{2,1,0:T(8,128)(2,1)S(1)}, u32[]{:S(2)}, u32[]{:S(2)}) collective-permute-start(bf16[2,208,384]{2,1,0:T(8,128)(2,1)S(1)} %get-tuple-element.66.rest_5_.own_ref), channel_id=1, source_target_pairs={{0,2},{2,0},{4,6},{6,4},{8,10},{10,8},{12,14},{14,12},{16,18},{18,... | collective-permute-start | bytes 958472 | tf_op jit(solution)/shard_map/ppermute | solution.py:597
  49.3 2.4 %collective-permute-start.19 = (bf16[2,208,384]{2,1,0:T(8,128)(2,1)S(1)}, bf16[2,208,384]{2,1,0:T(8,128)(2,1)S(1)}, u32[]{:S(2)}, u32[]{:S(2)}) collective-permute-start(bf16[2,208,384]{2,1,0:T(8,128)(2,1)S(1)} %collective-permute-done.16.rest_7_), channel_id=1, source_target_pairs={{8,16},{10,18},{12,20},{14,22},{16,8},{18,10},{20,12},{22,14},{9,1... | collective-permute-start | bytes 958472 | tf_op jit(solution)/shard_map/ppermute | solution.py:597
  55.4 2.8 %collective-permute-done.19 = bf16[2,208,384]{2,1,0:T(8,128)(2,1)S(1)} collective-permute-done((bf16[2,208,384]{2,1,0:T(8,128)(2,1)S(1)}, bf16[2,208,384]{2,1,0:T(8,128)(2,1)S(1)}, u32[]{:S(2)}, u32[]{:S(2)}) %collective-permute-start.19) | collective-permute-done | bytes 319520 | tf_op jit(solution)/shard_map/ppermute | solution.py:597
  58.3 3.7 %collective-permute-start.21 = (bf16[2,208,384]{2,1,0:T(8,128)(2,1)S(1)}, bf16[2,208,384]{2,1,0:T(8,128)(2,1)S(1)}, u32[]{:S(2)}, u32[]{:S(2)}) collective-permute-start(bf16[2,208,384]{2,1,0:T(8,128)(2,1)S(1)} %collective-permute-done.18.rest_6_), channel_id=1, source_target_pairs={{8,16},{10,18},{12,20},{14,22},{16,8},{18,10},{20,12},{22,14},{9,1... | collective-permute-start | bytes 958472 | tf_op jit(solution)/shard_map/ppermute | solution.py:597
  62.1 1.6 %collective-permute-start.23 = (bf16[2,208,384]{2,1,0:T(8,128)(2,1)S(1)}, bf16[2,208,384]{2,1,0:T(8,128)(2,1)S(1)}, u32[]{:S(2)}, u32[]{:S(2)}) collective-permute-start(bf16[2,208,384]{2,1,0:T(8,128)(2,1)S(1)} %broadcast_select_fusion.rest_5_), channel_id=1, source_target_pairs={{0,4},{2,6},{4,0},{6,2},{8,12},{10,14},{12,8},{14,10},{16,20},{18,... | collective-permute-start | bytes 958472 | tf_op jit(solution)/shard_map/ppermute | solution.py:597
  63.7 3.0 %attend_yours.2 = (bf16[1664,384]{1,0:T(8,128)(2,1)S(1)}, f32[416,128]{1,0:T(8,128)S(1)}, f32[416,128]{1,0:T(8,128)S(1)}, f32[416,384]{1,0:T(8,128)S(1)}) custom-call(s32[67]{0:T(128)S(1)} %pad_add_fusion.info_ref, f32[8,384]{1,0:T(8,128)S(1)} %get-tuple-element.54.rest_0_.means_ref, f32[8,384]{1,0:T(8,128)S(1)} %get-tuple-element.55.rest_1_.scales_ref, ...), custom_call_target="tpu_custom_call" | custom-call | flops 3960000000 | tf_op jit(solution)/shard_map/attend_yours/pallas_call | solution.py:655
  67.1 1.9 %collective-permute-done.22.rest_7_ = bf16[2,208,384]{2,1,0:T(8,128)(2,1)S(1)} collective-permute-done((bf16[2,208,384]{2,1,0:T(8,128)(2,1)S(1)}, bf16[2,208,384]{2,1,0:T(8,128)(2,1)S(1)}, u32[]{:S(2)}, u32[]{:S(2)}) %collective-permute-start.22) | collective-permute-done | bytes 319520 | tf_op jit(solution)/shard_map/ppermute | solution.py:597
  69.2 3.0 %attend_yours.3 = (bf16[1664,384]{1,0:T(8,128)(2,1)S(1)}, bf16[432,384]{1,0:T(8,128)(2,1)S(1)}) custom-call(s32[67]{0:T(128)S(1)} %pad_add_fusion.info_ref, f32[8,384]{1,0:T(8,128)S(1)} %get-tuple-element.54.rest_0_.means_ref, f32[8,384]{1,0:T(8,128)S(1)} %get-tuple-element.55.rest_1_.scales_ref, f32[1,384]{1,0:T(1,128)S(1)} %reshape.87.shift_ref.rest_2_, ...), custom_call_target="tpu_custom_call" | custom-call | flops 3960000000 | tf_op jit(solution)/shard_map/attend_yours/pallas_call | solution.py:655
  73.3 5.4 %attend_mine.1 = (f32[416,384]{1,0:T(8,128)S(1)}, f32[416,128]{1,0:T(8,128)S(1)}) custom-call(s32[67]{0:T(128)S(1)} %pad_add_fusion.info_ref, bf16[2,208,384]{2,1,0:T(8,128)(2,1)S(1)} %get-tuple-element.66.rest_5_.own_ref, f32[8,384]{1,0:T(8,128)S(1)} %get-tuple-element.54.rest_0_.means_ref, f32[8,384]{1,0:T(8,128)S(1)} %get-tuple-element.55.rest_1_.scales_ref, ...), custom_call_target="tpu_custom_call" | custom-call | flops 6600000000 | tf_op jit(solution)/shard_map/attend_mine/pallas_call | solution.py:655
  81.0 5.3 %collective-permute-start.25 = (bf16[1,104,384]{2,1,0:T(8,128)(2,1)S(1)}, bf16[1,104,384]{2,1,0:T(8,128)(2,1)S(1)}, u32[]{:S(2)}, u32[]{:S(2)}) collective-permute-start(bf16[1,104,384]{2,1,0:T(8,128)(2,1)S(1)} %get-tuple-element.71), channel_id=1, source_target_pairs={{2,4},{4,2},{6,8},{8,6},{10,12},{12,10},{14,16},{16,14},{18,20},{2... | collective-permute-start | bytes 239624 | tf_op jit(solution)/shard_map/ppermute | solution.py:810
  86.4 2.2 %upsample.1 = (bf16[6,192,208]{2,1,0:T(8,128)(2,1)S(1)}, f32[2,2,256,128]{3,2,1,0:T(8,128)S(1)}) custom-call(s32[67]{0:T(128)S(1)} %pad_add_fusion.info_ref, bf16[4,104,384]{2,1,0:T(8,128)(2,1)S(1)} %get-tuple-element.73.own_ref, bf16[2,2,2,192,768]{4,3,2,1,0:T(8,128)(2,1)S(1)} %fold.1.weight_ref, f32[1,256]{1,0:T(1,128)S(1)} %pad.4.bias_ref), custom_call_target="tpu_custom_call" | custom-call | flops 2200000000 | tf_op jit(solution)/shard_map/upsample/pallas_call | solution.py:655
  90.8 2.1 %close.1 = bf16[8,192,208]{2,1,0:T(8,128)(2,1)} custom-call(s32[67]{0:T(128)S(1)} %pad_add_fusion.info_ref, bf16[1,104,384]{2,1,0:T(8,128)(2,1)S(1)} %collective-permute-done.25.outer_ref, bf16[1,104,384]{2,1,0:T(8,128)(2,1)S(1)} %collective-permute-done.26.inner_ref, bf16[6,192,208]{2,1,0:T(8,128)(2,1)S(1)} %get-tuple-element.75.middle_ref, ...), custom_call_target="tpu_custom_call" | custom-call | flops 1100000000 | tf_op jit(solution)/shard_map/close/pallas_call | solution.py:655
  (92 shorter events, 28.6 us)
Async XLA Ops:
  0.9 8.6 %collective-permute-start = (bf16[1,104,384]{2,1,0:T(8,128)(2,1)S(1)}, bf16[1,104,384]{2,1,0:T(8,128)(2,1)S(1)}, u32[]{:S(2)}, u32[]{:S(2)}) collective-permute-start(bf16[1,104,384]{2,1,0:T(8,128)(2,1)S(1)} %get-tuple-element.89), channel_id=1, source_target_pairs={{2,4},{4,2},{6,8},{8,6},{10,12},{12,10},{14,16},{16,14},{18,20},{2... | collective-permute-start | bytes 239624 | tf_op jit(solution)/shard_map/ppermute | solution.py:673
  5.2 4.7 %collective-permute-start.1 = (bf16[1,104,384]{2,1,0:T(8,128)(2,1)S(1)}, bf16[1,104,384]{2,1,0:T(8,128)(2,1)S(1)}, u32[]{:S(2)}, u32[]{:S(2)}) collective-permute-start(bf16[1,104,384]{2,1,0:T(8,128)(2,1)S(1)} %get-tuple-element.88), channel_id=1, source_target_pairs={{0,2},{2,0},{4,6},{6,4},{8,10},{10,8},{12,14},{14,12},{16,18},{18,... | collective-permute-start | bytes 239624 | tf_op jit(solution)/shard_map/ppermute | solution.py:597
  9.9 6.7 %collective-permute-start.4 = (f32[3,8,128]{2,1,0:T(8,128)S(1)}, f32[3,8,128]{2,1,0:T(8,128)S(1)}, u32[]{:S(2)}, u32[]{:S(2)}) collective-permute-start(f32[3,8,128]{2,1,0:T(8,128)S(1)} %first_stats.1), channel_id=1, source_target_pairs={{0,24},{2,26},{4,28},{6,30},{8,16},{10,18},{12,20},{14,22},{16,8},... | collective-permute-start | bytes 36872 | tf_op jit(solution)/shard_map/ppermute | solution.py:597
  11.5 5.1 %collective-permute-start.3 = (f32[3,8,128]{2,1,0:T(8,128)S(1)}, f32[3,8,128]{2,1,0:T(8,128)S(1)}, u32[]{:S(2)}, u32[]{:S(2)}) collective-permute-start(f32[3,8,128]{2,1,0:T(8,128)S(1)} %first_stats.1), channel_id=1, source_target_pairs={{0,16},{2,18},{4,20},{6,22},{8,24},{10,26},{12,28},{14,30},{16,0},... | collective-permute-start | bytes 36872 | tf_op jit(solution)/shard_map/ppermute | solution.py:597
  12.5 4.1 %collective-permute-start.2 = (f32[3,8,128]{2,1,0:T(8,128)S(1)}, f32[3,8,128]{2,1,0:T(8,128)S(1)}, u32[]{:S(2)}, u32[]{:S(2)}) collective-permute-start(f32[3,8,128]{2,1,0:T(8,128)S(1)} %first_stats.1), channel_id=1, source_target_pairs={{0,8},{2,10},{4,12},{6,14},{8,0},{10,2},{12,4},{14,6},{16,24},{18,... | collective-permute-start | bytes 36872 | tf_op jit(solution)/shard_map/ppermute | solution.py:597
  16.7 4.7 %collective-permute-start.7 = (f32[3,8,128]{2,1,0:T(8,128)S(1)}, f32[3,8,128]{2,1,0:T(8,128)S(1)}, u32[]{:S(2)}, u32[]{:S(2)}) collective-permute-start(f32[3,8,128]{2,1,0:T(8,128)S(1)} %pad_maximum_fusion), channel_id=1, source_target_pairs={{0,6},{2,4},{4,2},{6,0},{8,14},{10,12},{12,10},{14,8},{16,22},{18,... | collective-permute-start | bytes 36872 | tf_op jit(solution)/shard_map/ppermute | solution.py:597
  32.0 9.5 %collective-permute-start.11 = (f32[3,8,128]{2,1,0:T(8,128)S(1)}, f32[3,8,128]{2,1,0:T(8,128)S(1)}, u32[]{:S(2)}, u32[]{:S(2)}) collective-permute-start(f32[3,8,128]{2,1,0:T(8,128)S(1)} %get-tuple-element.48), channel_id=1, source_target_pairs={{0,24},{2,26},{4,28},{6,30},{8,16},{10,18},{12,20},{14,22},{16,8},... | collective-permute-start | bytes 36872 | tf_op jit(solution)/shard_map/ppermute | solution.py:597
  34.2 7.3 %collective-permute-start.10 = (f32[3,8,128]{2,1,0:T(8,128)S(1)}, f32[3,8,128]{2,1,0:T(8,128)S(1)}, u32[]{:S(2)}, u32[]{:S(2)}) collective-permute-start(f32[3,8,128]{2,1,0:T(8,128)S(1)} %get-tuple-element.48), channel_id=1, source_target_pairs={{0,16},{2,18},{4,20},{6,22},{8,24},{10,26},{12,28},{14,30},{16,0},... | collective-permute-start | bytes 36872 | tf_op jit(solution)/shard_map/ppermute | solution.py:597
  36.0 5.5 %collective-permute-start.9 = (f32[3,8,128]{2,1,0:T(8,128)S(1)}, f32[3,8,128]{2,1,0:T(8,128)S(1)}, u32[]{:S(2)}, u32[]{:S(2)}) collective-permute-start(f32[3,8,128]{2,1,0:T(8,128)S(1)} %get-tuple-element.48), channel_id=1, source_target_pairs={{0,8},{2,10},{4,12},{6,14},{8,0},{10,2},{12,4},{14,6},{16,24},{18,... | collective-permute-start | bytes 36872 | tf_op jit(solution)/shard_map/ppermute | solution.py:597
  36.1 13.2 %collective-permute-start.16 = (bf16[2,208,384]{2,1,0:T(8,128)(2,1)S(1)}, bf16[2,208,384]{2,1,0:T(8,128)(2,1)S(1)}, u32[]{:S(2)}, u32[]{:S(2)}) collective-permute-start(bf16[2,208,384]{2,1,0:T(8,128)(2,1)S(1)} %get-tuple-element.66.rest_5_.own_ref), channel_id=1, source_target_pairs={{0,8},{2,10},{4,12},{6,14},{8,0},{10,2},{12,4},{14,6},{16,24},{18,... | collective-permute-start | bytes 958472 | tf_op jit(solution)/shard_map/ppermute | solution.py:597
  38.0 11.3 %collective-permute-start.17 = (bf16[2,208,384]{2,1,0:T(8,128)(2,1)S(1)}, bf16[2,208,384]{2,1,0:T(8,128)(2,1)S(1)}, u32[]{:S(2)}, u32[]{:S(2)}) collective-permute-start(bf16[2,208,384]{2,1,0:T(8,128)(2,1)S(1)} %get-tuple-element.66.rest_5_.own_ref), channel_id=1, source_target_pairs={{8,16},{10,18},{12,20},{14,22},{16,8},{18,10},{20,12},{22,14},{9,1... | collective-permute-start | bytes 958472 | tf_op jit(solution)/shard_map/ppermute | solution.py:597
  41.6 3.8 %collective-permute-start.12 = (f32[3,8,128]{2,1,0:T(8,128)S(1)}, f32[3,8,128]{2,1,0:T(8,128)S(1)}, u32[]{:S(2)}, u32[]{:S(2)}) collective-permute-start(f32[3,8,128]{2,1,0:T(8,128)S(1)} %pad_maximum_fusion.2), channel_id=1, source_target_pairs={{0,4},{2,6},{4,0},{6,2},{8,12},{10,14},{12,8},{14,10},{16,20},{18,... | collective-permute-start | bytes 36872 | tf_op jit(solution)/shard_map/ppermute | solution.py:597
  42.3 4.6 %collective-permute-start.13 = (f32[3,8,128]{2,1,0:T(8,128)S(1)}, f32[3,8,128]{2,1,0:T(8,128)S(1)}, u32[]{:S(2)}, u32[]{:S(2)}) collective-permute-start(f32[3,8,128]{2,1,0:T(8,128)S(1)} %pad_maximum_fusion.2), channel_id=1, source_target_pairs={{0,6},{2,4},{4,2},{6,0},{8,14},{10,12},{12,10},{14,8},{16,22},{18,... | collective-permute-start | bytes 36872 | tf_op jit(solution)/shard_map/ppermute | solution.py:597
  44.1 5.2 %collective-permute-start.15 = (f32[3,8,128]{2,1,0:T(8,128)S(1)}, f32[3,8,128]{2,1,0:T(8,128)S(1)}, u32[]{:S(2)}, u32[]{:S(2)}) collective-permute-start(f32[3,8,128]{2,1,0:T(8,128)S(1)} %pad_maximum_fusion.2), channel_id=1, source_target_pairs={{0,2},{2,0},{4,6},{6,4},{8,10},{10,8},{12,14},{14,12},{16,18},{18,... | collective-permute-start | bytes 36872 | tf_op jit(solution)/shard_map/ppermute | solution.py:597
  46.9 7.0 %collective-permute-start.14 = (bf16[2,208,384]{2,1,0:T(8,128)(2,1)S(1)}, bf16[2,208,384]{2,1,0:T(8,128)(2,1)S(1)}, u32[]{:S(2)}, u32[]{:S(2)}) collective-permute-start(bf16[2,208,384]{2,1,0:T(8,128)(2,1)S(1)} %get-tuple-element.66.rest_5_.own_ref), channel_id=1, source_target_pairs={{0,2},{2,0},{4,6},{6,4},{8,10},{10,8},{12,14},{14,12},{16,18},{18,... | collective-permute-start | bytes 958472 | tf_op jit(solution)/shard_map/ppermute | solution.py:597
  48.5 9.8 %collective-permute-start.18 = (bf16[2,208,384]{2,1,0:T(8,128)(2,1)S(1)}, bf16[2,208,384]{2,1,0:T(8,128)(2,1)S(1)}, u32[]{:S(2)}, u32[]{:S(2)}) collective-permute-start(bf16[2,208,384]{2,1,0:T(8,128)(2,1)S(1)} %get-tuple-element.66.rest_5_.own_ref), channel_id=1, source_target_pairs={{0,4},{2,6},{4,0},{6,2},{8,12},{10,14},{12,8},{14,10},{16,20},{18,... | collective-permute-start | bytes 958472 | tf_op jit(solution)/shard_map/ppermute | solution.py:597
  49.3 8.9 %collective-permute-start.19 = (bf16[2,208,384]{2,1,0:T(8,128)(2,1)S(1)}, bf16[2,208,384]{2,1,0:T(8,128)(2,1)S(1)}, u32[]{:S(2)}, u32[]{:S(2)}) collective-permute-start(bf16[2,208,384]{2,1,0:T(8,128)(2,1)S(1)} %collective-permute-done.16.rest_7_), channel_id=1, source_target_pairs={{8,16},{10,18},{12,20},{14,22},{16,8},{18,10},{20,12},{22,14},{9,1... | collective-permute-start | bytes 958472 | tf_op jit(solution)/shard_map/ppermute | solution.py:597
  51.7 6.5 %collective-permute-start.20 = (bf16[2,208,384]{2,1,0:T(8,128)(2,1)S(1)}, bf16[2,208,384]{2,1,0:T(8,128)(2,1)S(1)}, u32[]{:S(2)}, u32[]{:S(2)}) collective-permute-start(bf16[2,208,384]{2,1,0:T(8,128)(2,1)S(1)} %collective-permute-done.17.rest_8_), channel_id=1, source_target_pairs={{8,0},{10,2},{12,4},{14,6},{16,24},{18,26},{20,28},{22,30},{9,1},{... | collective-permute-start | bytes 958472 | tf_op jit(solution)/shard_map/ppermute | solution.py:597
  58.3 8.9 %collective-permute-start.21 = (bf16[2,208,384]{2,1,0:T(8,128)(2,1)S(1)}, bf16[2,208,384]{2,1,0:T(8,128)(2,1)S(1)}, u32[]{:S(2)}, u32[]{:S(2)}) collective-permute-start(bf16[2,208,384]{2,1,0:T(8,128)(2,1)S(1)} %collective-permute-done.18.rest_6_), channel_id=1, source_target_pairs={{8,16},{10,18},{12,20},{14,22},{16,8},{18,10},{20,12},{22,14},{9,1... | collective-permute-start | bytes 958472 | tf_op jit(solution)/shard_map/ppermute | solution.py:597
  62.0 7.1 %collective-permute-start.22 = (bf16[2,208,384]{2,1,0:T(8,128)(2,1)S(1)}, bf16[2,208,384]{2,1,0:T(8,128)(2,1)S(1)}, u32[]{:S(2)}, u32[]{:S(2)}) collective-permute-start(bf16[2,208,384]{2,1,0:T(8,128)(2,1)S(1)} %collective-permute-done.18.rest_6_), channel_id=1, source_target_pairs={{0,8},{2,10},{4,12},{6,14},{8,0},{10,2},{12,4},{14,6},{16,24},{18,... | collective-permute-start | bytes 958472 | tf_op jit(solution)/shard_map/ppermute | solution.py:597
  62.1 7.1 %collective-permute-start.23 = (bf16[2,208,384]{2,1,0:T(8,128)(2,1)S(1)}, bf16[2,208,384]{2,1,0:T(8,128)(2,1)S(1)}, u32[]{:S(2)}, u32[]{:S(2)}) collective-permute-start(bf16[2,208,384]{2,1,0:T(8,128)(2,1)S(1)} %broadcast_select_fusion.rest_5_), channel_id=1, source_target_pairs={{0,4},{2,6},{4,0},{6,2},{8,12},{10,14},{12,8},{14,10},{16,20},{18,... | collective-permute-start | bytes 958472 | tf_op jit(solution)/shard_map/ppermute | solution.py:597
  72.1 7.2 %collective-permute-start.24 = (bf16[432,384]{1,0:T(8,128)(2,1)S(1)}, bf16[432,384]{1,0:T(8,128)(2,1)S(1)}, u32[]{:S(2)}, u32[]{:S(2)}) collective-permute-start(bf16[432,384]{1,0:T(8,128)(2,1)S(1)} %get-tuple-element.65), channel_id=1, source_target_pairs={{0,2},{2,0},{4,6},{6,4},{8,10},{10,8},{12,14},{14,12},{16,18},{18,... | collective-permute-start | bytes 995336 | tf_op jit(solution)/shard_map/ppermute | solution.py:780
  81.0 8.2 %collective-permute-start.25 = (bf16[1,104,384]{2,1,0:T(8,128)(2,1)S(1)}, bf16[1,104,384]{2,1,0:T(8,128)(2,1)S(1)}, u32[]{:S(2)}, u32[]{:S(2)}) collective-permute-start(bf16[1,104,384]{2,1,0:T(8,128)(2,1)S(1)} %get-tuple-element.71), channel_id=1, source_target_pairs={{2,4},{4,2},{6,8},{8,6},{10,12},{12,10},{14,16},{16,14},{18,20},{2... | collective-permute-start | bytes 239624 | tf_op jit(solution)/shard_map/ppermute | solution.py:810
  86.3 4.5 %collective-permute-start.26 = (bf16[1,104,384]{2,1,0:T(8,128)(2,1)S(1)}, bf16[1,104,384]{2,1,0:T(8,128)(2,1)S(1)}, u32[]{:S(2)}, u32[]{:S(2)}) collective-permute-start(bf16[1,104,384]{2,1,0:T(8,128)(2,1)S(1)} %get-tuple-element.72), channel_id=1, source_target_pairs={{0,2},{2,0},{4,6},{6,4},{8,10},{10,8},{12,14},{14,12},{16,18},{18,... | collective-permute-start | bytes 239624 | tf_op jit(solution)/shard_map/ppermute | solution.py:597
  (16 other events, 166.8 us)

commit v9 on v8

--- a/solution.py
+++ b/solution.py
@@ -56,17 +56,20 @@
 class Info:
     def __init__(self, ref, rows):
         self.ref, self.rows = ref, rows
-        self.videos = ref.shape[0] - 1 - rows
+        self.videos = ref.shape[0] - 2 - rows
 
     def tile(self):
         return self.ref[0]
 
+    def frame(self):
+        return self.ref[1]
+
     def label(self, row):
         inside = (row >= 0) & (row < self.rows)
-        return jnp.where(inside, self.ref[1 + jnp.clip(row, 0, self.rows - 1)], -1)
+        return jnp.where(inside, self.ref[2 + jnp.clip(row, 0, self.rows - 1)], -1)
 
     def width(self, label):
-        return jnp.where(label >= 0, self.ref[1 + self.rows + jnp.maximum(label, 0)], 0)
+        return jnp.where(label >= 0, self.ref[2 + self.rows + jnp.maximum(label, 0)], 0)
 
     def window(self, first, count):
         labels = [self.label(first + r) for r in range(count)]
@@ -222,26 +225,37 @@
 
 def conv_kernel(rows, taps, info_ref, *rest):
     hidden_refs, rest = rest[: taps - 1], rest[taps - 1 :]
-    product_ref, latents_ref, bias_ref, held_ref, own_ref, stats_ref, *inputs_refs = rest
+    product_ref, latents_ref, bias_ref, held_ref, own_ref, stats_ref, *rest = rest
+    branch_ref, inputs_refs = rest[0], rest[1:]
     row_count, cols, channels = latents_ref.shape
     info = Info(info_ref, rows)
     padded = product_ref.shape[0] // row_count
     labels, widths = info.window(info.tile() * row_count - 1, row_count + 2)
-    product = product_ref[...]
-    if hidden_refs:
-        (inputs_ref,) = inputs_refs
-        row_taps(info, hidden_refs, inputs_ref)
-        product = product + jnp.dot(
-            inputs_ref[...], held_ref[3 * channels :, :], preferred_element_type=F32
-        )
+    for active in range(taps):
+        frame = info.frame()
+
+        @pl.when(frame == active if active < taps - 1 else frame >= active)
+        def _(active=active):
+            product = product_ref[...]
+            if active:
+                depth = 3 * active * channels
+                row_taps(info, hidden_refs[:active], inputs_refs[0])
+                product = product + jnp.dot(
+                    inputs_refs[0][:, 0:depth],
+                    held_ref[3 * channels : 3 * channels + depth, :],
+                    preferred_element_type=F32,
+                )
+            for r in range(row_count):
+                lines = slice(r * padded, (r + 1) * padded)
+                branch = pltpu.roll(product[lines, 0:channels], 1, 0)
+                branch = branch + product[lines, channels : 2 * channels]
+                branch = branch + pltpu.roll(product[lines, 2 * channels :], padded - 1, 0)
+                branch_ref[r] = branch[:cols]
+
     column = lax.broadcasted_iota(jnp.int32, (cols, 1), 0)
     cells = []
     for r in range(row_count):
-        lines = slice(r * padded, (r + 1) * padded)
-        branch = pltpu.roll(product[lines, 0:channels], 1, 0)
-        branch = branch + product[lines, channels : 2 * channels]
-        branch = branch + pltpu.roll(product[lines, 2 * channels :], padded - 1, 0)
-        value = latents_ref[r].astype(F32) + branch[:cols] + bias_ref[...]
+        value = latents_ref[r].astype(F32) + branch_ref[r] + bias_ref[...]
         value = jnp.where(column < widths[r + 1], value, 0.0).astype(BF16)
         cells.append(value.astype(F32))
     for pair in range(row_count // 2):
@@ -642,7 +656,8 @@
     near_rows = row_count + 2
     source = latents.reshape(row_count, cols, channels)
     tile = lax.axis_index("tile").astype(jnp.int32)
-    info = jnp.concatenate([jnp.reshape(tile, (1,)), row_video, video_cols])
+    frame = lax.axis_index("frame").astype(jnp.int32)
+    info = jnp.concatenate([jnp.stack([tile, frame]), row_video, video_cols])
 
     def row(vector):
         return vector.reshape(1, -1)
@@ -713,12 +728,14 @@
         cost_estimate=cost(2.2),
         name="own_conv",
     )
-    scratch = [pltpu.VMEM((row_count * padded, 3 * (taps - 1) * channels), BF16)]
+    scratch = [pltpu.VMEM((row_count, cols, channels), F32)]
+    if taps > 1:
+        scratch.append(pltpu.VMEM((row_count * padded, 3 * (taps - 1) * channels), BF16))
     own, stats = call(
         functools.partial(conv_kernel, rows, taps),
         earlier + [product, source, row(conv_bias), held],
         (pair_shape, stats_shape),
-        scratch=scratch if taps > 1 else [],
+        scratch=scratch,
         cost_estimate=cost(1.5 + 2.0 * (taps - 1)),
         name="conv",
     )
@@ -763,6 +780,15 @@
     )
     level_shape = shape(cells, LANES, dtype=F32)
     total_shape = shape(cells, channels, dtype=F32)
+    folded = pl.pallas_call(
+        fold_kernel,
+        out_shape=shape(2, 2, 2, out_channels, 2 * channels),
+        in_specs=[VMEM_SPEC],
+        out_specs=VMEM_SPEC,
+        compiler_params=params(),
+        cost_estimate=cost(0.5),
+        name="fold",
+    )(jnp.swapaxes(upsample_weight, 2, 3))
     state, keys = (), []
     for index, masks in enumerate(groups):
         last = index == len(groups) - 1
@@ -776,9 +802,11 @@
             name="attend_yours",
         )
         keys.append(normed)
+        if index == len(groups) - 2:
+            *state, folded = lax.optimization_barrier((*state, folded))
     (sent,) = state
     received = lax.ppermute(sent, "tile", neighbour)
-    sent, own_late, upsample_weight = lax.optimization_barrier((sent, own, upsample_weight))
+    sent, own_late = lax.optimization_barrier((sent, own))
     mean, level = call(
         functools.partial(attend_mine_kernel, rows, tuple(tuple(masks) for masks in groups)),
         [own_late, means, scales, shift, triple_weight, row(triple_bias)] + keys,
@@ -786,16 +814,6 @@
         cost_estimate=cost(6.0),
         name="attend_mine",
     )
-    folded = pl.pallas_call(
-        fold_kernel,
-        out_shape=shape(2, 2, 2, out_channels, 2 * channels),
-        in_specs=[VMEM_SPEC],
-        out_specs=VMEM_SPEC,
-        compiler_params=params(),
-        cost_estimate=cost(0.5),
-        name="fold",
-    )(jnp.swapaxes(upsample_weight, 2, 3))
-
     rim_shape = shape(1, cols, channels)
     attended, inner, outer = call(
         functools.partial(finish_kernel, rows),

time: 94.3 us -> 94.8 us (level)
  waiting for transfers between devices: 13.5 us -> 15.5 us
  starting transfers between devices: 44.9 us -> 43.7 us
    ppermute x23, waiting for transfers between devices: 12.7 us -> 13.8 us  [exchange(): return lax.ppermute(array, 'tile', moves)]
  transfers between devices with their start and end apart: 27 -> 27, of which waited for: 14 -> 15; matrix products, arithmetic and copies ran while one was open for 1% -> 1% of each run, Pallas kernels for 21% -> 22%
where the time goes in v9:
time: 94.8 us; the launch traced here: 93.3 us
  starting transfers between devices  43.7 us (46%)
  Pallas kernels  30.6 us (32%)
  waiting for transfers between devices  15.5 us (16%)
  other arithmetic  1.9 us (2%)
  local copies, waits for them, and re-layouts  1.09 us (1%)
    ppermute x23, starting transfers between devices, exchange(): return lax.ppermute(array, 'tile', moves)  32.6 us
    pallas_call x11, Pallas kernels, call(): pl.pallas_call(kernel, out_shape=out_shape, in_specs=[SMEM_SPEC] + [VMEM_...  27.5 us
    ppermute x23, waiting for transfers between devices, exchange(): return lax.ppermute(array, 'tile', moves)  13.8 us
    ppermute x1, starting transfers between devices, shards(): outer = lax.ppermute(outer, 'tile', outer_moves)  4.52 us
    ppermute x1, starting transfers between devices, shards(): lax.ppermute(jnp.where(odd, source[row_count - 1:], source[:1]), 'tile',...  4.24 us
    pallas_call x1, Pallas kernels, shards(): pl.pallas_call(functools.partial(hold_kernel, taps), out_shape=shape(3 *...  2.63 us
  transfers between devices with their start and end apart: 27, of which 15 were waited for; matrix products, arithmetic and copies ran while one was open for 1% of the time, Pallas kernels for 22%

profile of v9, /device:TPU:8, one launch (start us, length us, event | category | flops | bytes accessed | tf_op | source)
XLA Modules:
  0.0 93.3 jit_solution(3692589142683323461)
XLA Ops:
  0.9 4.2 %collective-permute-start = (bf16[1,104,384]{2,1,0:T(8,128)(2,1)S(1)}, bf16[1,104,384]{2,1,0:T(8,128)(2,1)S(1)}, u32[]{:S(2)}, u32[]{:S(2)}) collective-permute-start(bf16[1,104,384]{2,1,0:T(8,128)(2,1)S(1)} %get-tuple-element.95), channel_id=1, source_target_pairs={{2,4},{4,2},{6,8},{8,6},{10,12},{12,10},{14,16},{16,14},{18,20},{2... | collective-permute-start | bytes 239624 | tf_op jit(solution)/shard_map/ppermute | solution.py:688
  7.6 1.8 %first_stats.1 = f32[3,8,128]{2,1,0:T(8,128)S(1)} custom-call(s32[68]{0:T(128)S(1)} %pad_add_fusion.info_ref, bf16[4,104,384]{2,1,0:T(8,128)(2,1)S(1)} %bitcast.15), custom_call_target="tpu_custom_call" | custom-call | flops 1650000000 | tf_op jit(solution)/shard_map/first_stats/pallas_call | solution.py:670
  9.9 1.6 %collective-permute-start.4 = (f32[3,8,128]{2,1,0:T(8,128)S(1)}, f32[3,8,128]{2,1,0:T(8,128)S(1)}, u32[]{:S(2)}, u32[]{:S(2)}) collective-permute-start(f32[3,8,128]{2,1,0:T(8,128)S(1)} %first_stats.1), channel_id=1, source_target_pairs={{0,24},{2,26},{4,28},{6,30},{8,16},{10,18},{12,20},{14,22},{16,8},... | collective-permute-start | bytes 36872 | tf_op jit(solution)/shard_map/ppermute | solution.py:611
  14.0 2.6 %hold.1.held_ref.rest_4_ = bf16[2304,1152]{1,0:T(8,128)(2,1)S(1)} custom-call(bf16[3,3,3,384,384]{4,3,2,1,0:T(8,128)(2,1)} %weight_ref.3), custom_call_target="tpu_custom_call" | custom-call | flops 3300000000 | tf_op jit(solution)/shard_map/hold/pallas_call | solution.py:694
  16.7 1.5 %collective-permute-start.7 = (f32[3,8,128]{2,1,0:T(8,128)S(1)}, f32[3,8,128]{2,1,0:T(8,128)S(1)}, u32[]{:S(2)}, u32[]{:S(2)}) collective-permute-start(f32[3,8,128]{2,1,0:T(8,128)S(1)} %pad_maximum_fusion), channel_id=1, source_target_pairs={{0,6},{2,4},{4,2},{6,0},{8,14},{10,12},{12,10},{14,8},{16,22},{18,... | collective-permute-start | bytes 36872 | tf_op jit(solution)/shard_map/ppermute | solution.py:611
  26.0 2.2 %own_conv.1.rest_1_ = f32[448,1152]{1,0:T(8,128)S(1)} custom-call(s32[68]{0:T(128)S(1)} %pad_add_fusion.info_ref, bf16[6,112,384]{2,1,0:T(8,128)(2,1)S(1)} %get-tuple-element.48.hidden_ref, bf16[2304,1152]{1,0:T(8,128)(2,1)S(1)} %hold.1.held_ref.rest_4_), custom_call_target="tpu_custom_call" | custom-call | flops 2420000000 | tf_op jit(solution)/shard_map/own_conv/pallas_call | solution.py:670
  28.2 2.1 %conv.1 = (bf16[2,208,384]{2,1,0:T(8,128)(2,1)}, f32[3,8,128]{2,1,0:T(8,128)S(1)}) custom-call(s32[68]{0:T(128)S(1)} %pad_add_fusion.info_ref, bf16[6,112,384]{2,1,0:T(8,128)(2,1)S(1)} %collective-permute-done.8.rest_0_, f32[448,1152]{1,0:T(8,128)S(1)} %own_conv.1.rest_1_, bf16[4,104,384]{2,1,0:T(8,128)(2,1)S(1)} %get-tuple-element.50.rest_2_, ...), custom_call_target="tpu_custom_call" | custom-call | flops 3849999872 | tf_op jit(solution)/shard_map/conv/pallas_call | solution.py:670
  30.4 2.3 %collective-permute-start.11 = (f32[3,8,128]{2,1,0:T(8,128)S(1)}, f32[3,8,128]{2,1,0:T(8,128)S(1)}, u32[]{:S(2)}, u32[]{:S(2)}) collective-permute-start(f32[3,8,128]{2,1,0:T(8,128)S(1)} %get-tuple-element.51), channel_id=1, source_target_pairs={{0,24},{2,26},{4,28},{6,30},{8,16},{10,18},{12,20},{14,22},{16,8},... | collective-permute-start | bytes 36872 | tf_op jit(solution)/shard_map/ppermute | solution.py:611
  32.6 1.8 %collective-permute-start.10 = (f32[3,8,128]{2,1,0:T(8,128)S(1)}, f32[3,8,128]{2,1,0:T(8,128)S(1)}, u32[]{:S(2)}, u32[]{:S(2)}) collective-permute-start(f32[3,8,128]{2,1,0:T(8,128)S(1)} %get-tuple-element.51), channel_id=1, source_target_pairs={{0,16},{2,18},{4,20},{6,22},{8,24},{10,26},{12,28},{14,30},{16,0},... | collective-permute-start | bytes 36872 | tf_op jit(solution)/shard_map/ppermute | solution.py:611
  34.5 1.9 %collective-permute-start.16 = (bf16[2,208,384]{2,1,0:T(8,128)(2,1)}, bf16[2,208,384]{2,1,0:T(8,128)(2,1)}, u32[]{:S(2)}, u32[]{:S(2)}) collective-permute-start(bf16[2,208,384]{2,1,0:T(8,128)(2,1)} %get-tuple-element.72.rest_5_.own_ref), channel_id=1, source_target_pairs={{0,8},{2,10},{4,12},{6,14},{8,0},{10,2},{12,4},{14,6},{16,24},{18,... | collective-permute-start | bytes 958472 | tf_op jit(solution)/shard_map/ppermute | solution.py:611
  36.5 3.5 %collective-permute-start.17 = (bf16[2,208,384]{2,1,0:T(8,128)(2,1)}, bf16[2,208,384]{2,1,0:T(8,128)(2,1)}, u32[]{:S(2)}, u32[]{:S(2)}) collective-permute-start(bf16[2,208,384]{2,1,0:T(8,128)(2,1)} %get-tuple-element.72.rest_5_.own_ref), channel_id=1, source_target_pairs={{8,16},{10,18},{12,20},{14,22},{16,8},{18,10},{20,12},{22,14},{9,1... | collective-permute-start | bytes 958472 | tf_op jit(solution)/shard_map/ppermute | solution.py:611
  40.8 1.8 %collective-permute-start.13 = (f32[3,8,128]{2,1,0:T(8,128)S(1)}, f32[3,8,128]{2,1,0:T(8,128)S(1)}, u32[]{:S(2)}, u32[]{:S(2)}) collective-permute-start(f32[3,8,128]{2,1,0:T(8,128)S(1)} %pad_maximum_fusion.2), channel_id=1, source_target_pairs={{0,6},{2,4},{4,2},{6,0},{8,14},{10,12},{12,10},{14,8},{16,22},{18,... | collective-permute-start | bytes 36872 | tf_op jit(solution)/shard_map/ppermute | solution.py:611
  48.1 3.5 %collective-permute-start.19 = (bf16[2,208,384]{2,1,0:T(8,128)(2,1)}, bf16[2,208,384]{2,1,0:T(8,128)(2,1)S(1)}, u32[]{:S(2)}, u32[]{:S(2)}) collective-permute-start(bf16[2,208,384]{2,1,0:T(8,128)(2,1)} %collective-permute-done.16.rest_7_), channel_id=1, source_target_pairs={{8,16},{10,18},{12,20},{14,22},{16,8},{18,10},{20,12},{22,14},{9,1... | collective-permute-start | bytes 958472 | tf_op jit(solution)/shard_map/ppermute | solution.py:611
  53.4 1.5 %queries.1 = (bf16[416,384]{1,0:T(8,128)(2,1)S(1)}, f32[416,128]{1,0:T(8,128)S(1)}, f32[8,384]{1,0:T(8,128)S(1)}, f32[8,384]{1,0:T(8,128)S(1)}) custom-call(s32[68]{0:T(128)S(1)} %pad_add_fusion.info_ref, bf16[2,208,384]{2,1,0:T(8,128)(2,1)S(1)} %collective-permute-done.14.other_ref, f32[3,8,128]{2,1,0:T(8,128)S(1)} %pad_maximum_fusion.3.stats_ref, ...), custom_call_target="tpu_custom_call" | custom-call | flops 1650000000 | tf_op jit(solution)/shard_map/queries/pallas_call | solution.py:670
  54.9 3.9 %collective-permute-done.19 = bf16[2,208,384]{2,1,0:T(8,128)(2,1)S(1)} collective-permute-done((bf16[2,208,384]{2,1,0:T(8,128)(2,1)}, bf16[2,208,384]{2,1,0:T(8,128)(2,1)S(1)}, u32[]{:S(2)}, u32[]{:S(2)}) %collective-permute-start.19) | collective-permute-done | bytes 319520 | tf_op jit(solution)/shard_map/ppermute | solution.py:611
  59.4 3.2 %collective-permute-start.21 = (bf16[2,208,384]{2,1,0:T(8,128)(2,1)S(1)}, bf16[2,208,384]{2,1,0:T(8,128)(2,1)S(1)}, u32[]{:S(2)}, u32[]{:S(2)}) collective-permute-start(bf16[2,208,384]{2,1,0:T(8,128)(2,1)S(1)} %collective-permute-done.18.rest_6_), channel_id=1, source_target_pairs={{8,16},{10,18},{12,20},{14,22},{16,8},{18,10},{20,12},{22,14},{9,1... | collective-permute-start | bytes 958472 | tf_op jit(solution)/shard_map/ppermute | solution.py:611
  63.4 3.6 %attend_yours.2 = (bf16[1664,384]{1,0:T(8,128)(2,1)S(1)}, f32[416,128]{1,0:T(8,128)S(1)}, f32[416,128]{1,0:T(8,128)S(1)}, f32[416,384]{1,0:T(8,128)S(1)}) custom-call(s32[68]{0:T(128)S(1)} %pad_add_fusion.info_ref, f32[8,384]{1,0:T(8,128)S(1)} %get-tuple-element.57.rest_0_.means_ref, f32[8,384]{1,0:T(8,128)S(1)} %get-tuple-element.58.rest_1_.scales_ref, ...), custom_call_target="tpu_custom_call" | custom-call | flops 3960000000 | tf_op jit(solution)/shard_map/attend_yours/pallas_call | solution.py:670
  67.0 2.0 %collective-permute-done.21.rest_6_ = bf16[2,208,384]{2,1,0:T(8,128)(2,1)S(1)} collective-permute-done((bf16[2,208,384]{2,1,0:T(8,128)(2,1)S(1)}, bf16[2,208,384]{2,1,0:T(8,128)(2,1)S(1)}, u32[]{:S(2)}, u32[]{:S(2)}) %collective-permute-start.21) | collective-permute-done | bytes 319520 | tf_op jit(solution)/shard_map/ppermute | solution.py:611
  70.1 3.0 %attend_yours.3 = (bf16[1664,384]{1,0:T(8,128)(2,1)S(1)}, bf16[432,384]{1,0:T(8,128)(2,1)S(1)}) custom-call(s32[68]{0:T(128)S(1)} %pad_add_fusion.info_ref, f32[8,384]{1,0:T(8,128)S(1)} %get-tuple-element.57.rest_0_.means_ref, f32[8,384]{1,0:T(8,128)S(1)} %get-tuple-element.58.rest_1_.scales_ref, f32[1,384]{1,0:T(1,128)S(1)} %reshape.83.shift_ref.rest_2_, ...), custom_call_target="tpu_custom_call" | custom-call | flops 3960000000 | tf_op jit(solution)/shard_map/attend_yours/pallas_call | solution.py:670
  74.2 5.8 %attend_mine.1 = (f32[416,384]{1,0:T(8,128)S(1)}, f32[416,128]{1,0:T(8,128)S(1)}) custom-call(s32[68]{0:T(128)S(1)} %pad_add_fusion.info_ref, bf16[2,208,384]{2,1,0:T(8,128)(2,1)} %get-tuple-element.72.rest_5_.own_ref, f32[8,384]{1,0:T(8,128)S(1)} %get-tuple-element.57.rest_0_.means_ref, f32[8,384]{1,0:T(8,128)S(1)} %get-tuple-element.58.rest_1_.scales_ref, ...), custom_call_target="tpu_custom_call" | custom-call | flops 6600000000 | tf_op jit(solution)/shard_map/attend_mine/pallas_call | solution.py:670
  80.3 1.9 %finish.1 = (bf16[4,104,384]{2,1,0:T(8,128)(2,1)S(1)}, bf16[1,104,384]{2,1,0:T(8,128)(2,1)S(1)}, bf16[1,104,384]{2,1,0:T(8,128)(2,1)S(1)}) custom-call(s32[68]{0:T(128)S(1)} %pad_add_fusion.info_ref, f32[416,384]{1,0:T(8,128)S(1)} %get-tuple-element.75.mean_ref, f32[416,128]{1,0:T(8,128)S(1)} %get-tuple-element.76.level_ref, ...), custom_call_target="tpu_custom_call" | custom-call | flops 1540000000 | tf_op jit(solution)/shard_map/finish/pallas_call | solution.py:670
  82.2 4.5 %collective-permute-start.25 = (bf16[1,104,384]{2,1,0:T(8,128)(2,1)S(1)}, bf16[1,104,384]{2,1,0:T(8,128)(2,1)S(1)}, u32[]{:S(2)}, u32[]{:S(2)}) collective-permute-start(bf16[1,104,384]{2,1,0:T(8,128)(2,1)S(1)} %get-tuple-element.77), channel_id=1, source_target_pairs={{2,4},{4,2},{6,8},{8,6},{10,12},{12,10},{14,16},{16,14},{18,20},{2... | collective-permute-start | bytes 239624 | tf_op jit(solution)/shard_map/ppermute | solution.py:828
  86.8 2.2 %upsample.1 = (bf16[6,192,208]{2,1,0:T(8,128)(2,1)S(1)}, f32[2,2,256,128]{3,2,1,0:T(8,128)S(1)}) custom-call(s32[68]{0:T(128)S(1)} %pad_add_fusion.info_ref, bf16[4,104,384]{2,1,0:T(8,128)(2,1)S(1)} %get-tuple-element.79.own_ref, bf16[2,2,2,192,768]{4,3,2,1,0:T(8,128)(2,1)S(1)} %fold.1.weight_ref, f32[1,256]{1,0:T(1,128)S(1)} %pad.4.bias_ref), custom_call_target="tpu_custom_call" | custom-call | flops 2200000000 | tf_op jit(solution)/shard_map/upsample/pallas_call | solution.py:670
  91.2 2.1 %close.1 = bf16[8,192,208]{2,1,0:T(8,128)(2,1)} custom-call(s32[68]{0:T(128)S(1)} %pad_add_fusion.info_ref, bf16[1,104,384]{2,1,0:T(8,128)(2,1)S(1)} %collective-permute-done.25.outer_ref, bf16[1,104,384]{2,1,0:T(8,128)(2,1)S(1)} %collective-permute-done.26.inner_ref, bf16[6,192,208]{2,1,0:T(8,128)(2,1)S(1)} %get-tuple-element.81.middle_ref, ...), custom_call_target="tpu_custom_call" | custom-call | flops 1100000000 | tf_op jit(solution)/shard_map/close/pallas_call | solution.py:670
  (92 shorter events, 28.4 us)
Async XLA Ops:
  0.9 8.6 %collective-permute-start = (bf16[1,104,384]{2,1,0:T(8,128)(2,1)S(1)}, bf16[1,104,384]{2,1,0:T(8,128)(2,1)S(1)}, u32[]{:S(2)}, u32[]{:S(2)}) collective-permute-start(bf16[1,104,384]{2,1,0:T(8,128)(2,1)S(1)} %get-tuple-element.95), channel_id=1, source_target_pairs={{2,4},{4,2},{6,8},{8,6},{10,12},{12,10},{14,16},{16,14},{18,20},{2... | collective-permute-start | bytes 239624 | tf_op jit(solution)/shard_map/ppermute | solution.py:688
  5.2 4.7 %collective-permute-start.1 = (bf16[1,104,384]{2,1,0:T(8,128)(2,1)S(1)}, bf16[1,104,384]{2,1,0:T(8,128)(2,1)S(1)}, u32[]{:S(2)}, u32[]{:S(2)}) collective-permute-start(bf16[1,104,384]{2,1,0:T(8,128)(2,1)S(1)} %get-tuple-element.94), channel_id=1, source_target_pairs={{0,2},{2,0},{4,6},{6,4},{8,10},{10,8},{12,14},{14,12},{16,18},{18,... | collective-permute-start | bytes 239624 | tf_op jit(solution)/shard_map/ppermute | solution.py:611
  9.9 6.7 %collective-permute-start.4 = (f32[3,8,128]{2,1,0:T(8,128)S(1)}, f32[3,8,128]{2,1,0:T(8,128)S(1)}, u32[]{:S(2)}, u32[]{:S(2)}) collective-permute-start(f32[3,8,128]{2,1,0:T(8,128)S(1)} %first_stats.1), channel_id=1, source_target_pairs={{0,24},{2,26},{4,28},{6,30},{8,16},{10,18},{12,20},{14,22},{16,8},... | collective-permute-start | bytes 36872 | tf_op jit(solution)/shard_map/ppermute | solution.py:611
  11.5 5.1 %collective-permute-start.3 = (f32[3,8,128]{2,1,0:T(8,128)S(1)}, f32[3,8,128]{2,1,0:T(8,128)S(1)}, u32[]{:S(2)}, u32[]{:S(2)}) collective-permute-start(f32[3,8,128]{2,1,0:T(8,128)S(1)} %first_stats.1), channel_id=1, source_target_pairs={{0,16},{2,18},{4,20},{6,22},{8,24},{10,26},{12,28},{14,30},{16,0},... | collective-permute-start | bytes 36872 | tf_op jit(solution)/shard_map/ppermute | solution.py:611
  12.5 4.1 %collective-permute-start.2 = (f32[3,8,128]{2,1,0:T(8,128)S(1)}, f32[3,8,128]{2,1,0:T(8,128)S(1)}, u32[]{:S(2)}, u32[]{:S(2)}) collective-permute-start(f32[3,8,128]{2,1,0:T(8,128)S(1)} %first_stats.1), channel_id=1, source_target_pairs={{0,8},{2,10},{4,12},{6,14},{8,0},{10,2},{12,4},{14,6},{16,24},{18,... | collective-permute-start | bytes 36872 | tf_op jit(solution)/shard_map/ppermute | solution.py:611
  16.7 4.7 %collective-permute-start.7 = (f32[3,8,128]{2,1,0:T(8,128)S(1)}, f32[3,8,128]{2,1,0:T(8,128)S(1)}, u32[]{:S(2)}, u32[]{:S(2)}) collective-permute-start(f32[3,8,128]{2,1,0:T(8,128)S(1)} %pad_maximum_fusion), channel_id=1, source_target_pairs={{0,6},{2,4},{4,2},{6,0},{8,14},{10,12},{12,10},{14,8},{16,22},{18,... | collective-permute-start | bytes 36872 | tf_op jit(solution)/shard_map/ppermute | solution.py:611
  30.4 9.6 %collective-permute-start.11 = (f32[3,8,128]{2,1,0:T(8,128)S(1)}, f32[3,8,128]{2,1,0:T(8,128)S(1)}, u32[]{:S(2)}, u32[]{:S(2)}) collective-permute-start(f32[3,8,128]{2,1,0:T(8,128)S(1)} %get-tuple-element.51), channel_id=1, source_target_pairs={{0,24},{2,26},{4,28},{6,30},{8,16},{10,18},{12,20},{14,22},{16,8},... | collective-permute-start | bytes 36872 | tf_op jit(solution)/shard_map/ppermute | solution.py:611
  32.6 7.3 %collective-permute-start.10 = (f32[3,8,128]{2,1,0:T(8,128)S(1)}, f32[3,8,128]{2,1,0:T(8,128)S(1)}, u32[]{:S(2)}, u32[]{:S(2)}) collective-permute-start(f32[3,8,128]{2,1,0:T(8,128)S(1)} %get-tuple-element.51), channel_id=1, source_target_pairs={{0,16},{2,18},{4,20},{6,22},{8,24},{10,26},{12,28},{14,30},{16,0},... | collective-permute-start | bytes 36872 | tf_op jit(solution)/shard_map/ppermute | solution.py:611
  34.4 5.5 %collective-permute-start.9 = (f32[3,8,128]{2,1,0:T(8,128)S(1)}, f32[3,8,128]{2,1,0:T(8,128)S(1)}, u32[]{:S(2)}, u32[]{:S(2)}) collective-permute-start(f32[3,8,128]{2,1,0:T(8,128)S(1)} %get-tuple-element.51), channel_id=1, source_target_pairs={{0,8},{2,10},{4,12},{6,14},{8,0},{10,2},{12,4},{14,6},{16,24},{18,... | collective-permute-start | bytes 36872 | tf_op jit(solution)/shard_map/ppermute | solution.py:611
  34.5 13.2 %collective-permute-start.16 = (bf16[2,208,384]{2,1,0:T(8,128)(2,1)}, bf16[2,208,384]{2,1,0:T(8,128)(2,1)}, u32[]{:S(2)}, u32[]{:S(2)}) collective-permute-start(bf16[2,208,384]{2,1,0:T(8,128)(2,1)} %get-tuple-element.72.rest_5_.own_ref), channel_id=1, source_target_pairs={{0,8},{2,10},{4,12},{6,14},{8,0},{10,2},{12,4},{14,6},{16,24},{18,... | collective-permute-start | bytes 958472 | tf_op jit(solution)/shard_map/ppermute | solution.py:611
  36.5 11.7 %collective-permute-start.17 = (bf16[2,208,384]{2,1,0:T(8,128)(2,1)}, bf16[2,208,384]{2,1,0:T(8,128)(2,1)}, u32[]{:S(2)}, u32[]{:S(2)}) collective-permute-start(bf16[2,208,384]{2,1,0:T(8,128)(2,1)} %get-tuple-element.72.rest_5_.own_ref), channel_id=1, source_target_pairs={{8,16},{10,18},{12,20},{14,22},{16,8},{18,10},{20,12},{22,14},{9,1... | collective-permute-start | bytes 958472 | tf_op jit(solution)/shard_map/ppermute | solution.py:611
  40.0 4.2 %collective-permute-start.12 = (f32[3,8,128]{2,1,0:T(8,128)S(1)}, f32[3,8,128]{2,1,0:T(8,128)S(1)}, u32[]{:S(2)}, u32[]{:S(2)}) collective-permute-start(f32[3,8,128]{2,1,0:T(8,128)S(1)} %pad_maximum_fusion.2), channel_id=1, source_target_pairs={{0,4},{2,6},{4,0},{6,2},{8,12},{10,14},{12,8},{14,10},{16,20},{18,... | collective-permute-start | bytes 36872 | tf_op jit(solution)/shard_map/ppermute | solution.py:611
  40.8 4.6 %collective-permute-start.13 = (f32[3,8,128]{2,1,0:T(8,128)S(1)}, f32[3,8,128]{2,1,0:T(8,128)S(1)}, u32[]{:S(2)}, u32[]{:S(2)}) collective-permute-start(f32[3,8,128]{2,1,0:T(8,128)S(1)} %pad_maximum_fusion.2), channel_id=1, source_target_pairs={{0,6},{2,4},{4,2},{6,0},{8,14},{10,12},{12,10},{14,8},{16,22},{18,... | collective-permute-start | bytes 36872 | tf_op jit(solution)/shard_map/ppermute | solution.py:611
  42.5 5.2 %collective-permute-start.15 = (f32[3,8,128]{2,1,0:T(8,128)S(1)}, f32[3,8,128]{2,1,0:T(8,128)S(1)}, u32[]{:S(2)}, u32[]{:S(2)}) collective-permute-start(f32[3,8,128]{2,1,0:T(8,128)S(1)} %pad_maximum_fusion.2), channel_id=1, source_target_pairs={{0,2},{2,0},{4,6},{6,4},{8,10},{10,8},{12,14},{14,12},{16,18},{18,... | collective-permute-start | bytes 36872 | tf_op jit(solution)/shard_map/ppermute | solution.py:611
  45.3 8.0 %collective-permute-start.14 = (bf16[2,208,384]{2,1,0:T(8,128)(2,1)}, bf16[2,208,384]{2,1,0:T(8,128)(2,1)S(1)}, u32[]{:S(2)}, u32[]{:S(2)}) collective-permute-start(bf16[2,208,384]{2,1,0:T(8,128)(2,1)} %get-tuple-element.72.rest_5_.own_ref), channel_id=1, source_target_pairs={{0,2},{2,0},{4,6},{6,4},{8,10},{10,8},{12,14},{14,12},{16,18},{18,... | collective-permute-start | bytes 958472 | tf_op jit(solution)/shard_map/ppermute | solution.py:611
  46.8 12.6 %collective-permute-start.18 = (bf16[2,208,384]{2,1,0:T(8,128)(2,1)}, bf16[2,208,384]{2,1,0:T(8,128)(2,1)S(1)}, u32[]{:S(2)}, u32[]{:S(2)}) collective-permute-start(bf16[2,208,384]{2,1,0:T(8,128)(2,1)} %get-tuple-element.72.rest_5_.own_ref), channel_id=1, source_target_pairs={{0,4},{2,6},{4,0},{6,2},{8,12},{10,14},{12,8},{14,10},{16,20},{18,... | collective-permute-start | bytes 958472 | tf_op jit(solution)/shard_map/ppermute | solution.py:611
  48.1 10.7 %collective-permute-start.19 = (bf16[2,208,384]{2,1,0:T(8,128)(2,1)}, bf16[2,208,384]{2,1,0:T(8,128)(2,1)S(1)}, u32[]{:S(2)}, u32[]{:S(2)}) collective-permute-start(bf16[2,208,384]{2,1,0:T(8,128)(2,1)} %collective-permute-done.16.rest_7_), channel_id=1, source_target_pairs={{8,16},{10,18},{12,20},{14,22},{16,8},{18,10},{20,12},{22,14},{9,1... | collective-permute-start | bytes 958472 | tf_op jit(solution)/shard_map/ppermute | solution.py:611
  51.6 7.7 %collective-permute-start.20 = (bf16[2,208,384]{2,1,0:T(8,128)(2,1)}, bf16[2,208,384]{2,1,0:T(8,128)(2,1)S(1)}, u32[]{:S(2)}, u32[]{:S(2)}) collective-permute-start(bf16[2,208,384]{2,1,0:T(8,128)(2,1)} %collective-permute-done.17.rest_8_), channel_id=1, source_target_pairs={{8,0},{10,2},{12,4},{14,6},{16,24},{18,26},{20,28},{22,30},{9,1},{... | collective-permute-start | bytes 958472 | tf_op jit(solution)/shard_map/ppermute | solution.py:611
  59.4 9.6 %collective-permute-start.21 = (bf16[2,208,384]{2,1,0:T(8,128)(2,1)S(1)}, bf16[2,208,384]{2,1,0:T(8,128)(2,1)S(1)}, u32[]{:S(2)}, u32[]{:S(2)}) collective-permute-start(bf16[2,208,384]{2,1,0:T(8,128)(2,1)S(1)} %collective-permute-done.18.rest_6_), channel_id=1, source_target_pairs={{8,16},{10,18},{12,20},{14,22},{16,8},{18,10},{20,12},{22,14},{9,1... | collective-permute-start | bytes 958472 | tf_op jit(solution)/shard_map/ppermute | solution.py:611
  62.6 7.5 %collective-permute-start.22 = (bf16[2,208,384]{2,1,0:T(8,128)(2,1)S(1)}, bf16[2,208,384]{2,1,0:T(8,128)(2,1)S(1)}, u32[]{:S(2)}, u32[]{:S(2)}) collective-permute-start(bf16[2,208,384]{2,1,0:T(8,128)(2,1)S(1)} %collective-permute-done.18.rest_6_), channel_id=1, source_target_pairs={{0,8},{2,10},{4,12},{6,14},{8,0},{10,2},{12,4},{14,6},{16,24},{18,... | collective-permute-start | bytes 958472 | tf_op jit(solution)/shard_map/ppermute | solution.py:611
  62.7 7.4 %collective-permute-start.23 = (bf16[2,208,384]{2,1,0:T(8,128)(2,1)S(1)}, bf16[2,208,384]{2,1,0:T(8,128)(2,1)S(1)}, u32[]{:S(2)}, u32[]{:S(2)}) collective-permute-start(bf16[2,208,384]{2,1,0:T(8,128)(2,1)S(1)} %broadcast_select_fusion.rest_5_), channel_id=1, source_target_pairs={{0,4},{2,6},{4,0},{6,2},{8,12},{10,14},{12,8},{14,10},{16,20},{18,... | collective-permute-start | bytes 958472 | tf_op jit(solution)/shard_map/ppermute | solution.py:611
  73.1 7.2 %collective-permute-start.24 = (bf16[432,384]{1,0:T(8,128)(2,1)S(1)}, bf16[432,384]{1,0:T(8,128)(2,1)S(1)}, u32[]{:S(2)}, u32[]{:S(2)}) collective-permute-start(bf16[432,384]{1,0:T(8,128)(2,1)S(1)} %get-tuple-element.71), channel_id=1, source_target_pairs={{0,2},{2,0},{4,6},{6,4},{8,10},{10,8},{12,14},{14,12},{16,18},{18,... | collective-permute-start | bytes 995336 | tf_op jit(solution)/shard_map/ppermute | solution.py:808
  82.2 8.2 %collective-permute-start.25 = (bf16[1,104,384]{2,1,0:T(8,128)(2,1)S(1)}, bf16[1,104,384]{2,1,0:T(8,128)(2,1)S(1)}, u32[]{:S(2)}, u32[]{:S(2)}) collective-permute-start(bf16[1,104,384]{2,1,0:T(8,128)(2,1)S(1)} %get-tuple-element.77), channel_id=1, source_target_pairs={{2,4},{4,2},{6,8},{8,6},{10,12},{12,10},{14,16},{16,14},{18,20},{2... | collective-permute-start | bytes 239624 | tf_op jit(solution)/shard_map/ppermute | solution.py:828
  86.7 4.5 %collective-permute-start.26 = (bf16[1,104,384]{2,1,0:T(8,128)(2,1)S(1)}, bf16[1,104,384]{2,1,0:T(8,128)(2,1)S(1)}, u32[]{:S(2)}, u32[]{:S(2)}) collective-permute-start(bf16[1,104,384]{2,1,0:T(8,128)(2,1)S(1)} %get-tuple-element.78), channel_id=1, source_target_pairs={{0,2},{2,0},{4,6},{6,4},{8,10},{10,8},{12,14},{14,12},{16,18},{18,... | collective-permute-start | bytes 239624 | tf_op jit(solution)/shard_map/ppermute | solution.py:611
  (16 other events, 163.7 us)

commit v10 on v8

--- a/solution.py
+++ b/solution.py
@@ -180,16 +180,19 @@
     source_ref[...] = latents_ref[...]
 
 
-def hold_kernel(taps, weight_ref, held_ref, sems):
+def hold_kernel(backs, weight_ref, held_ref, sems):
     channels = weight_ref.shape[-1]
     copies = [
         pltpu.make_async_copy(
-            weight_ref.at[2 - depth // 3, depth % 3, side],
-            held_ref.at[pl.ds(depth * channels, channels), pl.ds(side * channels, channels)],
-            sems.at[side, depth],
+            weight_ref.at[2 - back, tap, side],
+            held_ref.at[
+                pl.ds((3 * index + tap) * channels, channels), pl.ds(side * channels, channels)
+            ],
+            sems.at[index, tap, side],
         )
+        for index, back in enumerate(backs)
+        for tap in range(3)
         for side in range(3)
-        for depth in range(3 * taps)
     ]
     for copy in copies:
         copy.start()
@@ -214,15 +217,13 @@
 
 def own_conv_kernel(rows, info_ref, hidden_ref, held_ref, product_ref, inputs_ref):
     row_taps(Info(info_ref, rows), [hidden_ref], inputs_ref)
-    depth = inputs_ref.shape[1]
-    product_ref[...] = jnp.dot(
-        inputs_ref[...], held_ref[0:depth, :], preferred_element_type=F32
-    )
+    product_ref[...] = jnp.dot(inputs_ref[...], held_ref[...], preferred_element_type=F32)
 
 
 def conv_kernel(rows, taps, info_ref, *rest):
     hidden_refs, rest = rest[: taps - 1], rest[taps - 1 :]
-    product_ref, latents_ref, bias_ref, held_ref, own_ref, stats_ref, *inputs_refs = rest
+    product_ref, latents_ref, bias_ref, *rest = rest
+    held_refs, (own_ref, stats_ref, *inputs_refs) = rest[: taps > 1], rest[taps > 1 :]
     row_count, cols, channels = latents_ref.shape
     info = Info(info_ref, rows)
     padded = product_ref.shape[0] // row_count
@@ -232,7 +233,7 @@
         (inputs_ref,) = inputs_refs
         row_taps(info, hidden_refs, inputs_ref)
         product = product + jnp.dot(
-            inputs_ref[...], held_ref[3 * channels :, :], preferred_element_type=F32
+            inputs_ref[...], held_refs[0][...], preferred_element_type=F32
         )
     column = lax.broadcasted_iota(jnp.int32, (cols, 1), 0)
     cells = []
@@ -676,21 +677,25 @@
     inner = exchange(jnp.where(odd, source[:1], source[row_count - 1 :]), tiles, 1)
     stats, outer, inner = lax.optimization_barrier((stats, outer, inner))
     taps = min(3, frames)
-    held = pl.pallas_call(
-        functools.partial(hold_kernel, taps),
-        out_shape=shape(3 * taps * channels, 3 * channels),
-        in_specs=[HBM_SPEC],
-        out_specs=VMEM_SPEC,
-        scratch_shapes=[pltpu.SemaphoreType.DMA((3, 3 * taps))],
-        compiler_params=pltpu.CompilerParams(vmem_limit_bytes=HOLD_VMEM_BYTES),
-        cost_estimate=cost(1.5 * taps),
-        name="hold",
-    )(conv_weight)
+    held = [
+        pl.pallas_call(
+            functools.partial(hold_kernel, backs),
+            out_shape=shape(3 * len(backs) * channels, 3 * channels),
+            in_specs=[HBM_SPEC],
+            out_specs=VMEM_SPEC,
+            scratch_shapes=[pltpu.SemaphoreType.DMA((len(backs), 3, 3))],
+            compiler_params=pltpu.CompilerParams(vmem_limit_bytes=HOLD_VMEM_BYTES),
+            cost_estimate=cost(1.5 * len(backs)),
+            name="hold",
+        )(conv_weight)
+        for backs in ((0,), tuple(range(1, taps)))
+        if backs
+    ]
     rounds = merge_masks(tiles)
     for index, masks in enumerate(reversed(rounds)):
         stats = merge_round(stats, tiles, masks)
-        if index == len(rounds) - 2:
-            stats, held = lax.optimization_barrier((stats, held))
+        if index < len(held):
+            stats, held[index] = lax.optimization_barrier((stats, held[index]))
     hidden, source = call(
         functools.partial(hidden_kernel, rows),
         [outer, inner, source, stats, row(first_gain), row(first_shift)],
@@ -707,7 +712,7 @@
     pair_shape = shape(pairs, 2 * cols, channels)
     product = call(
         functools.partial(own_conv_kernel, rows),
-        [hidden, held],
+        [hidden, held[0]],
         shape(row_count * padded, 3 * channels, dtype=F32),
         scratch=[pltpu.VMEM((row_count * padded, 3 * channels), BF16)],
         cost_estimate=cost(2.2),
@@ -716,7 +721,7 @@
     scratch = [pltpu.VMEM((row_count * padded, 3 * (taps - 1) * channels), BF16)]
     own, stats = call(
         functools.partial(conv_kernel, rows, taps),
-        earlier + [product, source, row(conv_bias), held],
+        earlier + [product, source, row(conv_bias)] + held[1:],
         (pair_shape, stats_shape),
         scratch=scratch if taps > 1 else [],
         cost_estimate=cost(1.5 + 2.0 * (taps - 1)),
@@ -778,7 +783,7 @@
         keys.append(normed)
     (sent,) = state
     received = lax.ppermute(sent, "tile", neighbour)
-    sent, own_late, upsample_weight = lax.optimization_barrier((sent, own, upsample_weight))
+    sent, own_late = lax.optimization_barrier((sent, own))
     mean, level = call(
         functools.partial(attend_mine_kernel, rows, tuple(tuple(masks) for masks in groups)),
         [own_late, means, scales, shift, triple_weight, row(triple_bias)] + keys,
@@ -786,16 +791,6 @@
         cost_estimate=cost(6.0),
         name="attend_mine",
     )
-    folded = pl.pallas_call(
-        fold_kernel,
-        out_shape=shape(2, 2, 2, out_channels, 2 * channels),
-        in_specs=[VMEM_SPEC],
-        out_specs=VMEM_SPEC,
-        compiler_params=params(),
-        cost_estimate=cost(0.5),
-        name="fold",
-    )(jnp.swapaxes(upsample_weight, 2, 3))
-
     rim_shape = shape(1, cols, channels)
     attended, inner, outer = call(
         functools.partial(finish_kernel, rows),
@@ -809,6 +804,16 @@
     )
     outer = lax.ppermute(outer, "tile", outer_moves)
     inner = exchange(inner, tiles, 1)
+    attended, upsample_weight = lax.optimization_barrier((attended, upsample_weight))
+    folded = pl.pallas_call(
+        fold_kernel,
+        out_shape=shape(2, 2, 2, out_channels, 2 * channels),
+        in_specs=[VMEM_SPEC],
+        out_specs=VMEM_SPEC,
+        compiler_params=params(),
+        cost_estimate=cost(0.5),
+        name="fold",
+    )(jnp.swapaxes(upsample_weight, 2, 3))
     parts_out = -(-out_channels // LANES)
     wide_cols = -(-2 * cols // LANES) * LANES
     wide_bias = jnp.pad(row(upsample_bias), ((0, 0), (0, -out_channels % LANES)))

time: 94.3 us -> 94.2 us (level); the launches traced: 92.9 us -> 93.8 us
  waiting for transfers between devices: 13.5 us -> 19.3 us
  starting transfers between devices: 44.9 us -> 39.5 us
    ppermute x1, starting transfers between devices: 5.25 us -> 2.54 us  [shards(): outer = lax.ppermute(outer, 'tile', outer_moves)]
    ppermute x1, waiting for transfers between devices: 0.14 us -> 2.74 us  [shards(): received = lax.ppermute(sent, 'tile', neighbour)]
    ppermute x1, waiting for transfers between devices: 0.66 us -> 3.1 us  [shards(): outer = lax.ppermute(outer, 'tile', outer_moves)]
    ppermute x23, starting transfers between devices: 33 us -> 31.3 us  [exchange(): return lax.ppermute(array, 'tile', moves)]
    ppermute x1, starting transfers between devices: 1.12 us -> 0.07 us  [shards(): received = lax.ppermute(sent, 'tile', neighbour)]
    pallas_call x1 -> x2, Pallas kernels: 2.63 us -> 3.5 us  [shards(): pl.pallas_call(functools.partial(hold_kernel, backs), out_shape=shape(3 *...]
  transfers between devices with their start and end apart: 27 -> 27, of which waited for: 14 -> 12; matrix products, arithmetic and copies ran while one was open for 1% -> 1% of each run, Pallas kernels for 21% -> 21%
where the time goes in v10:
time: 94.2 us; the launch traced here: 93.8 us
  starting transfers between devices  39.5 us (42%)
  Pallas kernels  31.5 us (33%)
  waiting for transfers between devices  19.3 us (20%)
  other arithmetic  1.9 us (2%)
  local copies, waits for them, and re-layouts  1.07 us (1%)
    ppermute x23, starting transfers between devices, exchange(): return lax.ppermute(array, 'tile', moves)  31.3 us
    pallas_call x11, Pallas kernels, call(): pl.pallas_call(kernel, out_shape=out_shape, in_specs=[SMEM_SPEC] + [VMEM_...  27.5 us
    ppermute x23, waiting for transfers between devices, exchange(): return lax.ppermute(array, 'tile', moves)  13.4 us
    ppermute x1, starting transfers between devices, shards(): lax.ppermute(jnp.where(odd, source[row_count - 1:], source[:1]), 'tile',...  4.24 us
    pallas_call x2, Pallas kernels, shards(): pl.pallas_call(functools.partial(hold_kernel, backs), out_shape=shape(3 *...  3.5 us
    ppermute x1, waiting for transfers between devices, shards(): outer = lax.ppermute(outer, 'tile', outer_moves)  3.1 us
    ppermute x1, waiting for transfers between devices, shards(): received = lax.ppermute(sent, 'tile', neighbour)  2.74 us
    ppermute x1, starting transfers between devices, shards(): outer = lax.ppermute(outer, 'tile', outer_moves)  2.54 us
  transfers between devices with their start and end apart: 27, of which 12 were waited for; matrix products, arithmetic and copies ran while one was open for 1% of the time, Pallas kernels for 21%

profile of v10, /device:TPU:8, one launch (start us, length us, event | category | flops | bytes accessed | tf_op | source)
XLA Modules:
  0.0 93.8 jit_solution(3374006494647050738)
XLA Ops:
  0.9 4.2 %collective-permute-start = (bf16[1,104,384]{2,1,0:T(8,128)(2,1)S(1)}, bf16[1,104,384]{2,1,0:T(8,128)(2,1)S(1)}, u32[]{:S(2)}, u32[]{:S(2)}) collective-permute-start(bf16[1,104,384]{2,1,0:T(8,128)(2,1)S(1)} %get-tuple-element.95), channel_id=1, source_target_pairs={{2,4},{4,2},{6,8},{8,6},{10,12},{12,10},{14,16},{16,14},{18,20},{2... | collective-permute-start | bytes 239624 | tf_op jit(solution)/shard_map/ppermute | solution.py:674
  7.6 1.8 %first_stats.1 = f32[3,8,128]{2,1,0:T(8,128)S(1)} custom-call(s32[67]{0:T(128)S(1)} %pad_add_fusion.info_ref, bf16[4,104,384]{2,1,0:T(8,128)(2,1)S(1)} %bitcast.14), custom_call_target="tpu_custom_call" | custom-call | flops 1650000000 | tf_op jit(solution)/shard_map/first_stats/pallas_call | solution.py:656
  10.1 2.9 %collective-permute-start.3 = (f32[3,8,128]{2,1,0:T(8,128)S(1)}, f32[3,8,128]{2,1,0:T(8,128)S(1)}, u32[]{:S(2)}, u32[]{:S(2)}) collective-permute-start(f32[3,8,128]{2,1,0:T(8,128)S(1)} %first_stats.1), channel_id=1, source_target_pairs={{0,16},{2,18},{4,20},{6,22},{8,24},{10,26},{12,28},{14,30},{16,0},... | collective-permute-start | bytes 36872 | tf_op jit(solution)/shard_map/ppermute | solution.py:598
  13.4 1.7 %hold.2.held_ref = bf16[1152,1152]{1,0:T(8,128)(2,1)S(1)} custom-call(bf16[3,3,3,384,384]{4,3,2,1,0:T(8,128)(2,1)} %weight_ref.5), custom_call_target="tpu_custom_call" | custom-call | flops 1650000000 | tf_op jit(solution)/shard_map/hold/pallas_call | solution.py:681
  26.3 2.2 %own_conv.1.rest_1_ = f32[448,1152]{1,0:T(8,128)S(1)} custom-call(s32[67]{0:T(128)S(1)} %pad_add_fusion.info_ref, bf16[6,112,384]{2,1,0:T(8,128)(2,1)S(1)} %get-tuple-element.49.hidden_ref, bf16[1152,1152]{1,0:T(8,128)(2,1)S(1)} %hold.2.held_ref), custom_call_target="tpu_custom_call" | custom-call | flops 2420000000 | tf_op jit(solution)/shard_map/own_conv/pallas_call | solution.py:656
  28.6 3.7 %conv.1 = (bf16[2,208,384]{2,1,0:T(8,128)(2,1)S(1)}, f32[3,8,128]{2,1,0:T(8,128)S(1)}) custom-call(s32[67]{0:T(128)S(1)} %pad_add_fusion.info_ref, bf16[6,112,384]{2,1,0:T(8,128)(2,1)S(1)} %collective-permute-done.8.rest_0_, f32[448,1152]{1,0:T(8,128)S(1)} %own_conv.1.rest_1_, bf16[4,104,384]{2,1,0:T(8,128)(2,1)S(1)} %get-tuple-element.51.rest_2_, ...), custom_call_target="tpu_custom_call" | custom-call | flops 3849999872 | tf_op jit(solution)/shard_map/conv/pallas_call | solution.py:656
  32.3 2.2 %collective-permute-start.10 = (f32[3,8,128]{2,1,0:T(8,128)S(1)}, f32[3,8,128]{2,1,0:T(8,128)S(1)}, u32[]{:S(2)}, u32[]{:S(2)}) collective-permute-start(f32[3,8,128]{2,1,0:T(8,128)S(1)} %get-tuple-element.53), channel_id=1, source_target_pairs={{0,16},{2,18},{4,20},{6,22},{8,24},{10,26},{12,28},{14,30},{16,0},... | collective-permute-start | bytes 36872 | tf_op jit(solution)/shard_map/ppermute | solution.py:598
  34.5 2.2 %collective-permute-start.11 = (f32[3,8,128]{2,1,0:T(8,128)S(1)}, f32[3,8,128]{2,1,0:T(8,128)S(1)}, u32[]{:S(2)}, u32[]{:S(2)}) collective-permute-start(f32[3,8,128]{2,1,0:T(8,128)S(1)} %get-tuple-element.53), channel_id=1, source_target_pairs={{0,24},{2,26},{4,28},{6,30},{8,16},{10,18},{12,20},{14,22},{16,8},... | collective-permute-start | bytes 36872 | tf_op jit(solution)/shard_map/ppermute | solution.py:598
  36.7 2.0 %collective-permute-start.16 = (bf16[2,208,384]{2,1,0:T(8,128)(2,1)S(1)}, bf16[2,208,384]{2,1,0:T(8,128)(2,1)S(1)}, u32[]{:S(2)}, u32[]{:S(2)}) collective-permute-start(bf16[2,208,384]{2,1,0:T(8,128)(2,1)S(1)} %get-tuple-element.71.rest_5_.own_ref), channel_id=1, source_target_pairs={{0,8},{2,10},{4,12},{6,14},{8,0},{10,2},{12,4},{14,6},{16,24},{18,... | collective-permute-start | bytes 958472 | tf_op jit(solution)/shard_map/ppermute | solution.py:598
  38.7 1.9 %collective-permute-start.17 = (bf16[2,208,384]{2,1,0:T(8,128)(2,1)S(1)}, bf16[2,208,384]{2,1,0:T(8,128)(2,1)S(1)}, u32[]{:S(2)}, u32[]{:S(2)}) collective-permute-start(bf16[2,208,384]{2,1,0:T(8,128)(2,1)S(1)} %get-tuple-element.71.rest_5_.own_ref), channel_id=1, source_target_pairs={{8,16},{10,18},{12,20},{14,22},{16,8},{18,10},{20,12},{22,14},{9,1... | collective-permute-start | bytes 958472 | tf_op jit(solution)/shard_map/ppermute | solution.py:598
  44.5 2.3 %collective-permute-done.13 = f32[3,8,128]{2,1,0:T(8,128)S(1)} collective-permute-done((f32[3,8,128]{2,1,0:T(8,128)S(1)}, f32[3,8,128]{2,1,0:T(8,128)S(1)}, u32[]{:S(2)}, u32[]{:S(2)}) %collective-permute-start.13) | collective-permute-done | bytes 12320 | tf_op jit(solution)/shard_map/ppermute | solution.py:598
  48.9 4.0 %collective-permute-start.19 = (bf16[2,208,384]{2,1,0:T(8,128)(2,1)S(1)}, bf16[2,208,384]{2,1,0:T(8,128)(2,1)S(1)}, u32[]{:S(2)}, u32[]{:S(2)}) collective-permute-start(bf16[2,208,384]{2,1,0:T(8,128)(2,1)S(1)} %collective-permute-done.16.rest_7_), channel_id=1, source_target_pairs={{8,16},{10,18},{12,20},{14,22},{16,8},{18,10},{20,12},{22,14},{9,1... | collective-permute-start | bytes 958472 | tf_op jit(solution)/shard_map/ppermute | solution.py:598
  55.8 2.0 %collective-permute-done.19 = bf16[2,208,384]{2,1,0:T(8,128)(2,1)S(1)} collective-permute-done((bf16[2,208,384]{2,1,0:T(8,128)(2,1)S(1)}, bf16[2,208,384]{2,1,0:T(8,128)(2,1)S(1)}, u32[]{:S(2)}, u32[]{:S(2)}) %collective-permute-start.19) | collective-permute-done | bytes 319520 | tf_op jit(solution)/shard_map/ppermute | solution.py:598
  57.9 2.0 %collective-permute-done.20 = bf16[2,208,384]{2,1,0:T(8,128)(2,1)S(1)} collective-permute-done((bf16[2,208,384]{2,1,0:T(8,128)(2,1)S(1)}, bf16[2,208,384]{2,1,0:T(8,128)(2,1)S(1)}, u32[]{:S(2)}, u32[]{:S(2)}) %collective-permute-start.20) | collective-permute-done | bytes 319520 | tf_op jit(solution)/shard_map/ppermute | solution.py:598
  60.0 2.2 %collective-permute-start.21 = (bf16[2,208,384]{2,1,0:T(8,128)(2,1)S(1)}, bf16[2,208,384]{2,1,0:T(8,128)(2,1)S(1)}, u32[]{:S(2)}, u32[]{:S(2)}) collective-permute-start(bf16[2,208,384]{2,1,0:T(8,128)(2,1)S(1)} %collective-permute-done.18.rest_6_), channel_id=1, source_target_pairs={{8,16},{10,18},{12,20},{14,22},{16,8},{18,10},{20,12},{22,14},{9,1... | collective-permute-start | bytes 958472 | tf_op jit(solution)/shard_map/ppermute | solution.py:598
  63.9 3.0 %attend_yours.2 = (bf16[1664,384]{1,0:T(8,128)(2,1)S(1)}, f32[416,128]{1,0:T(8,128)S(1)}, f32[416,128]{1,0:T(8,128)S(1)}, f32[416,384]{1,0:T(8,128)S(1)}) custom-call(s32[67]{0:T(128)S(1)} %pad_add_fusion.info_ref, f32[8,384]{1,0:T(8,128)S(1)} %get-tuple-element.59.rest_0_.means_ref, f32[8,384]{1,0:T(8,128)S(1)} %get-tuple-element.60.rest_1_.scales_ref, ...), custom_call_target="tpu_custom_call" | custom-call | flops 3960000000 | tf_op jit(solution)/shard_map/attend_yours/pallas_call | solution.py:656
  66.9 1.9 %collective-permute-done.21.rest_6_ = bf16[2,208,384]{2,1,0:T(8,128)(2,1)S(1)} collective-permute-done((bf16[2,208,384]{2,1,0:T(8,128)(2,1)S(1)}, bf16[2,208,384]{2,1,0:T(8,128)(2,1)S(1)}, u32[]{:S(2)}, u32[]{:S(2)}) %collective-permute-start.21) | collective-permute-done | bytes 319520 | tf_op jit(solution)/shard_map/ppermute | solution.py:598
  70.4 3.0 %attend_yours.3 = (bf16[1664,384]{1,0:T(8,128)(2,1)S(1)}, bf16[432,384]{1,0:T(8,128)(2,1)S(1)}) custom-call(s32[67]{0:T(128)S(1)} %pad_add_fusion.info_ref, f32[8,384]{1,0:T(8,128)S(1)} %get-tuple-element.59.rest_0_.means_ref, f32[8,384]{1,0:T(8,128)S(1)} %get-tuple-element.60.rest_1_.scales_ref, f32[1,384]{1,0:T(1,128)S(1)} %reshape.87.shift_ref.rest_2_, ...), custom_call_target="tpu_custom_call" | custom-call | flops 3960000000 | tf_op jit(solution)/shard_map/attend_yours/pallas_call | solution.py:656
  73.4 5.4 %attend_mine.1 = (f32[416,384]{1,0:T(8,128)S(1)}, f32[416,128]{1,0:T(8,128)S(1)}) custom-call(s32[67]{0:T(128)S(1)} %pad_add_fusion.info_ref, bf16[2,208,384]{2,1,0:T(8,128)(2,1)S(1)} %get-tuple-element.71.rest_5_.own_ref, f32[8,384]{1,0:T(8,128)S(1)} %get-tuple-element.59.rest_0_.means_ref, f32[8,384]{1,0:T(8,128)S(1)} %get-tuple-element.60.rest_1_.scales_ref, ...), custom_call_target="tpu_custom_call" | custom-call | flops 6600000000 | tf_op jit(solution)/shard_map/attend_mine/pallas_call | solution.py:656
  78.8 2.7 %collective-permute-done.24.received_ref = bf16[432,384]{1,0:T(8,128)(2,1)S(1)} collective-permute-done((bf16[432,384]{1,0:T(8,128)(2,1)S(1)}, bf16[432,384]{1,0:T(8,128)(2,1)S(1)}, u32[]{:S(2)}, u32[]{:S(2)}) %collective-permute-start.24) | collective-permute-done | bytes 331808 | tf_op jit(solution)/shard_map/ppermute | solution.py:785
  83.5 2.5 %collective-permute-start.25 = (bf16[1,104,384]{2,1,0:T(8,128)(2,1)S(1)}, bf16[1,104,384]{2,1,0:T(8,128)(2,1)S(1)}, u32[]{:S(2)}, u32[]{:S(2)}) collective-permute-start(bf16[1,104,384]{2,1,0:T(8,128)(2,1)S(1)} %get-tuple-element.76), channel_id=1, source_target_pairs={{2,4},{4,2},{6,8},{8,6},{10,12},{12,10},{14,16},{16,14},{18,20},{2... | collective-permute-start | bytes 239624 | tf_op jit(solution)/shard_map/ppermute | solution.py:805
  86.4 2.2 %upsample.1 = (bf16[6,192,208]{2,1,0:T(8,128)(2,1)S(1)}, f32[2,2,256,128]{3,2,1,0:T(8,128)S(1)}) custom-call(s32[67]{0:T(128)S(1)} %pad_add_fusion.info_ref, bf16[4,104,384]{2,1,0:T(8,128)(2,1)S(1)} %get-tuple-element.79.own_ref, bf16[2,2,2,192,768]{4,3,2,1,0:T(8,128)(2,1)S(1)} %fold.1.weight_ref, f32[1,256]{1,0:T(1,128)S(1)} %pad.4.bias_ref), custom_call_target="tpu_custom_call" | custom-call | flops 2200000000 | tf_op jit(solution)/shard_map/upsample/pallas_call | solution.py:656
  88.6 3.1 %collective-permute-done.25.outer_ref = bf16[1,104,384]{2,1,0:T(8,128)(2,1)S(1)} collective-permute-done((bf16[1,104,384]{2,1,0:T(8,128)(2,1)S(1)}, bf16[1,104,384]{2,1,0:T(8,128)(2,1)S(1)}, u32[]{:S(2)}, u32[]{:S(2)}) %collective-permute-start.25) | collective-permute-done | bytes 79904 | tf_op jit(solution)/shard_map/ppermute | solution.py:805
  91.7 2.1 %close.1 = bf16[8,192,208]{2,1,0:T(8,128)(2,1)} custom-call(s32[67]{0:T(128)S(1)} %pad_add_fusion.info_ref, bf16[1,104,384]{2,1,0:T(8,128)(2,1)S(1)} %collective-permute-done.25.outer_ref, bf16[1,104,384]{2,1,0:T(8,128)(2,1)S(1)} %collective-permute-done.26.inner_ref, bf16[6,192,208]{2,1,0:T(8,128)(2,1)S(1)} %get-tuple-element.81.middle_ref, ...), custom_call_target="tpu_custom_call" | custom-call | flops 1100000000 | tf_op jit(solution)/shard_map/close/pallas_call | solution.py:656
  (93 shorter events, 29.9 us)
Async XLA Ops:
  0.9 8.5 %collective-permute-start = (bf16[1,104,384]{2,1,0:T(8,128)(2,1)S(1)}, bf16[1,104,384]{2,1,0:T(8,128)(2,1)S(1)}, u32[]{:S(2)}, u32[]{:S(2)}) collective-permute-start(bf16[1,104,384]{2,1,0:T(8,128)(2,1)S(1)} %get-tuple-element.95), channel_id=1, source_target_pairs={{2,4},{4,2},{6,8},{8,6},{10,12},{12,10},{14,16},{16,14},{18,20},{2... | collective-permute-start | bytes 239624 | tf_op jit(solution)/shard_map/ppermute | solution.py:674
  5.2 4.7 %collective-permute-start.1 = (bf16[1,104,384]{2,1,0:T(8,128)(2,1)S(1)}, bf16[1,104,384]{2,1,0:T(8,128)(2,1)S(1)}, u32[]{:S(2)}, u32[]{:S(2)}) collective-permute-start(bf16[1,104,384]{2,1,0:T(8,128)(2,1)S(1)} %get-tuple-element.94), channel_id=1, source_target_pairs={{0,2},{2,0},{4,6},{6,4},{8,10},{10,8},{12,14},{14,12},{16,18},{18,... | collective-permute-start | bytes 239624 | tf_op jit(solution)/shard_map/ppermute | solution.py:598
  9.9 5.2 %collective-permute-start.2 = (f32[3,8,128]{2,1,0:T(8,128)S(1)}, f32[3,8,128]{2,1,0:T(8,128)S(1)}, u32[]{:S(2)}, u32[]{:S(2)}) collective-permute-start(f32[3,8,128]{2,1,0:T(8,128)S(1)} %first_stats.1), channel_id=1, source_target_pairs={{0,8},{2,10},{4,12},{6,14},{8,0},{10,2},{12,4},{14,6},{16,24},{18,... | collective-permute-start | bytes 36872 | tf_op jit(solution)/shard_map/ppermute | solution.py:598
  10.1 5.1 %collective-permute-start.3 = (f32[3,8,128]{2,1,0:T(8,128)S(1)}, f32[3,8,128]{2,1,0:T(8,128)S(1)}, u32[]{:S(2)}, u32[]{:S(2)}) collective-permute-start(f32[3,8,128]{2,1,0:T(8,128)S(1)} %first_stats.1), channel_id=1, source_target_pairs={{0,16},{2,18},{4,20},{6,22},{8,24},{10,26},{12,28},{14,30},{16,0},... | collective-permute-start | bytes 36872 | tf_op jit(solution)/shard_map/ppermute | solution.py:598
  16.7 5.4 %collective-permute-start.5 = (f32[3,8,128]{2,1,0:T(8,128)S(1)}, f32[3,8,128]{2,1,0:T(8,128)S(1)}, u32[]{:S(2)}, u32[]{:S(2)}) collective-permute-start(f32[3,8,128]{2,1,0:T(8,128)S(1)} %pad_maximum_fusion), channel_id=1, source_target_pairs={{0,2},{2,0},{4,6},{6,4},{8,10},{10,8},{12,14},{14,12},{16,18},{18,... | collective-permute-start | bytes 36872 | tf_op jit(solution)/shard_map/ppermute | solution.py:598
  19.0 4.6 %collective-permute-start.7 = (f32[3,8,128]{2,1,0:T(8,128)S(1)}, f32[3,8,128]{2,1,0:T(8,128)S(1)}, u32[]{:S(2)}, u32[]{:S(2)}) collective-permute-start(f32[3,8,128]{2,1,0:T(8,128)S(1)} %pad_maximum_fusion), channel_id=1, source_target_pairs={{0,6},{2,4},{4,2},{6,0},{8,14},{10,12},{12,10},{14,8},{16,22},{18,... | collective-permute-start | bytes 36872 | tf_op jit(solution)/shard_map/ppermute | solution.py:598
  32.3 8.3 %collective-permute-start.10 = (f32[3,8,128]{2,1,0:T(8,128)S(1)}, f32[3,8,128]{2,1,0:T(8,128)S(1)}, u32[]{:S(2)}, u32[]{:S(2)}) collective-permute-start(f32[3,8,128]{2,1,0:T(8,128)S(1)} %get-tuple-element.53), channel_id=1, source_target_pairs={{0,16},{2,18},{4,20},{6,22},{8,24},{10,26},{12,28},{14,30},{16,0},... | collective-permute-start | bytes 36872 | tf_op jit(solution)/shard_map/ppermute | solution.py:598
  34.5 6.2 %collective-permute-start.11 = (f32[3,8,128]{2,1,0:T(8,128)S(1)}, f32[3,8,128]{2,1,0:T(8,128)S(1)}, u32[]{:S(2)}, u32[]{:S(2)}) collective-permute-start(f32[3,8,128]{2,1,0:T(8,128)S(1)} %get-tuple-element.53), channel_id=1, source_target_pairs={{0,24},{2,26},{4,28},{6,30},{8,16},{10,18},{12,20},{14,22},{16,8},... | collective-permute-start | bytes 36872 | tf_op jit(solution)/shard_map/ppermute | solution.py:598
  36.7 4.0 %collective-permute-start.9 = (f32[3,8,128]{2,1,0:T(8,128)S(1)}, f32[3,8,128]{2,1,0:T(8,128)S(1)}, u32[]{:S(2)}, u32[]{:S(2)}) collective-permute-start(f32[3,8,128]{2,1,0:T(8,128)S(1)} %get-tuple-element.53), channel_id=1, source_target_pairs={{0,8},{2,10},{4,12},{6,14},{8,0},{10,2},{12,4},{14,6},{16,24},{18,... | collective-permute-start | bytes 36872 | tf_op jit(solution)/shard_map/ppermute | solution.py:598
  36.7 12.1 %collective-permute-start.16 = (bf16[2,208,384]{2,1,0:T(8,128)(2,1)S(1)}, bf16[2,208,384]{2,1,0:T(8,128)(2,1)S(1)}, u32[]{:S(2)}, u32[]{:S(2)}) collective-permute-start(bf16[2,208,384]{2,1,0:T(8,128)(2,1)S(1)} %get-tuple-element.71.rest_5_.own_ref), channel_id=1, source_target_pairs={{0,8},{2,10},{4,12},{6,14},{8,0},{10,2},{12,4},{14,6},{16,24},{18,... | collective-permute-start | bytes 958472 | tf_op jit(solution)/shard_map/ppermute | solution.py:598
  38.7 10.1 %collective-permute-start.17 = (bf16[2,208,384]{2,1,0:T(8,128)(2,1)S(1)}, bf16[2,208,384]{2,1,0:T(8,128)(2,1)S(1)}, u32[]{:S(2)}, u32[]{:S(2)}) collective-permute-start(bf16[2,208,384]{2,1,0:T(8,128)(2,1)S(1)} %get-tuple-element.71.rest_5_.own_ref), channel_id=1, source_target_pairs={{8,16},{10,18},{12,20},{14,22},{16,8},{18,10},{20,12},{22,14},{9,1... | collective-permute-start | bytes 958472 | tf_op jit(solution)/shard_map/ppermute | solution.py:598
  40.7 3.8 %collective-permute-start.12 = (f32[3,8,128]{2,1,0:T(8,128)S(1)}, f32[3,8,128]{2,1,0:T(8,128)S(1)}, u32[]{:S(2)}, u32[]{:S(2)}) collective-permute-start(f32[3,8,128]{2,1,0:T(8,128)S(1)} %pad_maximum_fusion.2), channel_id=1, source_target_pairs={{0,4},{2,6},{4,0},{6,2},{8,12},{10,14},{12,8},{14,10},{16,20},{18,... | collective-permute-start | bytes 36872 | tf_op jit(solution)/shard_map/ppermute | solution.py:598
  42.1 4.7 %collective-permute-start.13 = (f32[3,8,128]{2,1,0:T(8,128)S(1)}, f32[3,8,128]{2,1,0:T(8,128)S(1)}, u32[]{:S(2)}, u32[]{:S(2)}) collective-permute-start(f32[3,8,128]{2,1,0:T(8,128)S(1)} %pad_maximum_fusion.2), channel_id=1, source_target_pairs={{0,6},{2,4},{4,2},{6,0},{8,14},{10,12},{12,10},{14,8},{16,22},{18,... | collective-permute-start | bytes 36872 | tf_op jit(solution)/shard_map/ppermute | solution.py:598
  43.7 5.2 %collective-permute-start.15 = (f32[3,8,128]{2,1,0:T(8,128)S(1)}, f32[3,8,128]{2,1,0:T(8,128)S(1)}, u32[]{:S(2)}, u32[]{:S(2)}) collective-permute-start(f32[3,8,128]{2,1,0:T(8,128)S(1)} %pad_maximum_fusion.2), channel_id=1, source_target_pairs={{0,2},{2,0},{4,6},{6,4},{8,10},{10,8},{12,14},{14,12},{16,18},{18,... | collective-permute-start | bytes 36872 | tf_op jit(solution)/shard_map/ppermute | solution.py:598
  46.8 7.5 %collective-permute-start.14 = (bf16[2,208,384]{2,1,0:T(8,128)(2,1)S(1)}, bf16[2,208,384]{2,1,0:T(8,128)(2,1)S(1)}, u32[]{:S(2)}, u32[]{:S(2)}) collective-permute-start(bf16[2,208,384]{2,1,0:T(8,128)(2,1)S(1)} %get-tuple-element.71.rest_5_.own_ref), channel_id=1, source_target_pairs={{0,2},{2,0},{4,6},{6,4},{8,10},{10,8},{12,14},{14,12},{16,18},{18,... | collective-permute-start | bytes 958472 | tf_op jit(solution)/shard_map/ppermute | solution.py:598
  47.7 12.2 %collective-permute-start.18 = (bf16[2,208,384]{2,1,0:T(8,128)(2,1)S(1)}, bf16[2,208,384]{2,1,0:T(8,128)(2,1)S(1)}, u32[]{:S(2)}, u32[]{:S(2)}) collective-permute-start(bf16[2,208,384]{2,1,0:T(8,128)(2,1)S(1)} %get-tuple-element.71.rest_5_.own_ref), channel_id=1, source_target_pairs={{0,4},{2,6},{4,0},{6,2},{8,12},{10,14},{12,8},{14,10},{16,20},{18,... | collective-permute-start | bytes 958472 | tf_op jit(solution)/shard_map/ppermute | solution.py:598
  48.9 9.0 %collective-permute-start.19 = (bf16[2,208,384]{2,1,0:T(8,128)(2,1)S(1)}, bf16[2,208,384]{2,1,0:T(8,128)(2,1)S(1)}, u32[]{:S(2)}, u32[]{:S(2)}) collective-permute-start(bf16[2,208,384]{2,1,0:T(8,128)(2,1)S(1)} %collective-permute-done.16.rest_7_), channel_id=1, source_target_pairs={{8,16},{10,18},{12,20},{14,22},{16,8},{18,10},{20,12},{22,14},{9,1... | collective-permute-start | bytes 958472 | tf_op jit(solution)/shard_map/ppermute | solution.py:598
  52.9 7.0 %collective-permute-start.20 = (bf16[2,208,384]{2,1,0:T(8,128)(2,1)S(1)}, bf16[2,208,384]{2,1,0:T(8,128)(2,1)S(1)}, u32[]{:S(2)}, u32[]{:S(2)}) collective-permute-start(bf16[2,208,384]{2,1,0:T(8,128)(2,1)S(1)} %collective-permute-done.17.rest_8_), channel_id=1, source_target_pairs={{8,0},{10,2},{12,4},{14,6},{16,24},{18,26},{20,28},{22,30},{9,1},{... | collective-permute-start | bytes 958472 | tf_op jit(solution)/shard_map/ppermute | solution.py:598
  60.0 8.9 %collective-permute-start.21 = (bf16[2,208,384]{2,1,0:T(8,128)(2,1)S(1)}, bf16[2,208,384]{2,1,0:T(8,128)(2,1)S(1)}, u32[]{:S(2)}, u32[]{:S(2)}) collective-permute-start(bf16[2,208,384]{2,1,0:T(8,128)(2,1)S(1)} %collective-permute-done.18.rest_6_), channel_id=1, source_target_pairs={{8,16},{10,18},{12,20},{14,22},{16,8},{18,10},{20,12},{22,14},{9,1... | collective-permute-start | bytes 958472 | tf_op jit(solution)/shard_map/ppermute | solution.py:598
  62.2 7.1 %collective-permute-start.22 = (bf16[2,208,384]{2,1,0:T(8,128)(2,1)S(1)}, bf16[2,208,384]{2,1,0:T(8,128)(2,1)S(1)}, u32[]{:S(2)}, u32[]{:S(2)}) collective-permute-start(bf16[2,208,384]{2,1,0:T(8,128)(2,1)S(1)} %collective-permute-done.18.rest_6_), channel_id=1, source_target_pairs={{0,8},{2,10},{4,12},{6,14},{8,0},{10,2},{12,4},{14,6},{16,24},{18,... | collective-permute-start | bytes 958472 | tf_op jit(solution)/shard_map/ppermute | solution.py:598
  63.4 7.0 %collective-permute-start.23 = (bf16[2,208,384]{2,1,0:T(8,128)(2,1)S(1)}, bf16[2,208,384]{2,1,0:T(8,128)(2,1)S(1)}, u32[]{:S(2)}, u32[]{:S(2)}) collective-permute-start(bf16[2,208,384]{2,1,0:T(8,128)(2,1)S(1)} %broadcast_select_fusion.rest_5_), channel_id=1, source_target_pairs={{0,4},{2,6},{4,0},{6,2},{8,12},{10,14},{12,8},{14,10},{16,20},{18,... | collective-permute-start | bytes 958472 | tf_op jit(solution)/shard_map/ppermute | solution.py:598
  73.3 8.2 %collective-permute-start.24 = (bf16[432,384]{1,0:T(8,128)(2,1)S(1)}, bf16[432,384]{1,0:T(8,128)(2,1)S(1)}, u32[]{:S(2)}, u32[]{:S(2)}) collective-permute-start(bf16[432,384]{1,0:T(8,128)(2,1)S(1)} %get-tuple-element.70), channel_id=1, source_target_pairs={{0,2},{2,0},{4,6},{6,4},{8,10},{10,8},{12,14},{14,12},{16,18},{18,... | collective-permute-start | bytes 995336 | tf_op jit(solution)/shard_map/ppermute | solution.py:785
  83.5 8.2 %collective-permute-start.25 = (bf16[1,104,384]{2,1,0:T(8,128)(2,1)S(1)}, bf16[1,104,384]{2,1,0:T(8,128)(2,1)S(1)}, u32[]{:S(2)}, u32[]{:S(2)}) collective-permute-start(bf16[1,104,384]{2,1,0:T(8,128)(2,1)S(1)} %get-tuple-element.76), channel_id=1, source_target_pairs={{2,4},{4,2},{6,8},{8,6},{10,12},{12,10},{14,16},{16,14},{18,20},{2... | collective-permute-start | bytes 239624 | tf_op jit(solution)/shard_map/ppermute | solution.py:805
  86.1 5.7 %collective-permute-start.26 = (bf16[1,104,384]{2,1,0:T(8,128)(2,1)S(1)}, bf16[1,104,384]{2,1,0:T(8,128)(2,1)S(1)}, u32[]{:S(2)}, u32[]{:S(2)}) collective-permute-start(bf16[1,104,384]{2,1,0:T(8,128)(2,1)S(1)} %get-tuple-element.77), channel_id=1, source_target_pairs={{0,2},{2,0},{4,6},{6,4},{8,10},{10,8},{12,14},{14,12},{16,18},{18,... | collective-permute-start | bytes 239624 | tf_op jit(solution)/shard_map/ppermute | solution.py:598
  (16 other events, 146.3 us)

commit v11 on v10

--- a/solution.py
+++ b/solution.py
@@ -749,7 +749,7 @@
         blocks[5] = exchange(blocks[4], tiles, 2)
         blocks[3] = exchange(passed, tiles, 4)
         blocks[7] = exchange(passed, tiles, 12, middle)
-        groups = [[0, 1, 2, 6], [4, 7, 3, 5]]
+        groups = [[0, 1, 2, 6, 4], [7, 3, 5]]
     else:
         for masks in rounds:
             stats = merge_round(stats, tiles, masks)
@@ -783,7 +783,7 @@
         keys.append(normed)
     (sent,) = state
     received = lax.ppermute(sent, "tile", neighbour)
-    sent, own_late = lax.optimization_barrier((sent, own))
+    sent, own_late, upsample_weight = lax.optimization_barrier((sent, own, upsample_weight))
     mean, level = call(
         functools.partial(attend_mine_kernel, rows, tuple(tuple(masks) for masks in groups)),
         [own_late, means, scales, shift, triple_weight, row(triple_bias)] + keys,
@@ -791,6 +791,16 @@
         cost_estimate=cost(6.0),
         name="attend_mine",
     )
+    folded = pl.pallas_call(
+        fold_kernel,
+        out_shape=shape(2, 2, 2, out_channels, 2 * channels),
+        in_specs=[VMEM_SPEC],
+        out_specs=VMEM_SPEC,
+        compiler_params=params(),
+        cost_estimate=cost(0.5),
+        name="fold",
+    )(jnp.swapaxes(upsample_weight, 2, 3))
+
     rim_shape = shape(1, cols, channels)
     attended, inner, outer = call(
         functools.partial(finish_kernel, rows),
@@ -804,16 +814,6 @@
     )
     outer = lax.ppermute(outer, "tile", outer_moves)
     inner = exchange(inner, tiles, 1)
-    attended, upsample_weight = lax.optimization_barrier((attended, upsample_weight))
-    folded = pl.pallas_call(
-        fold_kernel,
-        out_shape=shape(2, 2, 2, out_channels, 2 * channels),
-        in_specs=[VMEM_SPEC],
-        out_specs=VMEM_SPEC,
-        compiler_params=params(),
-        cost_estimate=cost(0.5),
-        name="fold",
-    )(jnp.swapaxes(upsample_weight, 2, 3))
     parts_out = -(-out_channels // LANES)
     wide_cols = -(-2 * cols // LANES) * LANES
     wide_bias = jnp.pad(row(upsample_bias), ((0, 0), (0, -out_channels % LANES)))

time: 94.2 us -> 93.7 us (level)
  waiting for transfers between devices: 19.3 us -> 16.6 us
    ppermute x1, waiting for transfers between devices: 2.74 us -> 1.71 us  [shards(): received = lax.ppermute(sent, 'tile', neighbour)]
  transfers between devices with their start and end apart: 27 -> 27, of which waited for: 12 -> 13; matrix products, arithmetic and copies ran while one was open for 1% -> 1% of each run, Pallas kernels for 21% -> 23%
where the time goes in v11:
time: 93.7 us; the launch traced here: 92.5 us
  starting transfers between devices  40.4 us (43%)
  Pallas kernels  32 us (34%)
  waiting for transfers between devices  16.6 us (18%)
  other arithmetic  1.9 us (2%)
  local copies, waits for them, and re-layouts  1.08 us (1%)
    ppermute x23, starting transfers between devices, exchange(): return lax.ppermute(array, 'tile', moves)  31.6 us
    pallas_call x11, Pallas kernels, call(): pl.pallas_call(kernel, out_shape=out_shape, in_specs=[SMEM_SPEC] + [VMEM_...  28 us
    ppermute x23, waiting for transfers between devices, exchange(): return lax.ppermute(array, 'tile', moves)  12.6 us
    ppermute x1, starting transfers between devices, shards(): lax.ppermute(jnp.where(odd, source[row_count - 1:], source[:1]), 'tile',...  4.24 us
    pallas_call x2, Pallas kernels, shards(): pl.pallas_call(functools.partial(hold_kernel, backs), out_shape=shape(3 *...  3.5 us
    ppermute x1, starting transfers between devices, shards(): outer = lax.ppermute(outer, 'tile', outer_moves)  3.19 us
    ppermute x1, waiting for transfers between devices, shards(): outer = lax.ppermute(outer, 'tile', outer_moves)  2.27 us
  transfers between devices with their start and end apart: 27, of which 13 were waited for; matrix products, arithmetic and copies ran while one was open for 1% of the time, Pallas kernels for 23%

profile of v11, /device:TPU:8, one launch (start us, length us, event | category | flops | bytes accessed | tf_op | source)
XLA Modules:
  0.0 92.5 jit_solution(2360752752800608512)
XLA Ops:
  0.9 4.2 %collective-permute-start = (bf16[1,104,384]{2,1,0:T(8,128)(2,1)S(1)}, bf16[1,104,384]{2,1,0:T(8,128)(2,1)S(1)}, u32[]{:S(2)}, u32[]{:S(2)}) collective-permute-start(bf16[1,104,384]{2,1,0:T(8,128)(2,1)S(1)} %get-tuple-element.93), channel_id=1, source_target_pairs={{2,4},{4,2},{6,8},{8,6},{10,12},{12,10},{14,16},{16,14},{18,20},{2... | collective-permute-start | bytes 239624 | tf_op jit(solution)/shard_map/ppermute | solution.py:674
  7.6 1.8 %first_stats.1 = f32[3,8,128]{2,1,0:T(8,128)S(1)} custom-call(s32[67]{0:T(128)S(1)} %pad_add_fusion.info_ref, bf16[4,104,384]{2,1,0:T(8,128)(2,1)S(1)} %bitcast.14), custom_call_target="tpu_custom_call" | custom-call | flops 1650000000 | tf_op jit(solution)/shard_map/first_stats/pallas_call | solution.py:656
  10.1 2.9 %collective-permute-start.3 = (f32[3,8,128]{2,1,0:T(8,128)S(1)}, f32[3,8,128]{2,1,0:T(8,128)S(1)}, u32[]{:S(2)}, u32[]{:S(2)}) collective-permute-start(f32[3,8,128]{2,1,0:T(8,128)S(1)} %first_stats.1), channel_id=1, source_target_pairs={{0,16},{2,18},{4,20},{6,22},{8,24},{10,26},{12,28},{14,30},{16,0},... | collective-permute-start | bytes 36872 | tf_op jit(solution)/shard_map/ppermute | solution.py:598
  13.4 1.7 %hold.2.held_ref = bf16[1152,1152]{1,0:T(8,128)(2,1)S(1)} custom-call(bf16[3,3,3,384,384]{4,3,2,1,0:T(8,128)(2,1)} %weight_ref.5), custom_call_target="tpu_custom_call" | custom-call | flops 1650000000 | tf_op jit(solution)/shard_map/hold/pallas_call | solution.py:681
  20.3 1.7 %hold.3.rest_4_ = bf16[1152,1152]{1,0:T(8,128)(2,1)S(1)} custom-call(bf16[3,3,3,384,384]{4,3,2,1,0:T(8,128)(2,1)} %weight_ref.5), custom_call_target="tpu_custom_call" | custom-call | flops 1650000000 | tf_op jit(solution)/shard_map/hold/pallas_call | solution.py:681
  26.3 2.2 %own_conv.1.rest_1_ = f32[448,1152]{1,0:T(8,128)S(1)} custom-call(s32[67]{0:T(128)S(1)} %pad_add_fusion.info_ref, bf16[6,112,384]{2,1,0:T(8,128)(2,1)S(1)} %get-tuple-element.48.hidden_ref, bf16[1152,1152]{1,0:T(8,128)(2,1)S(1)} %hold.2.held_ref), custom_call_target="tpu_custom_call" | custom-call | flops 2420000000 | tf_op jit(solution)/shard_map/own_conv/pallas_call | solution.py:656
  28.6 3.7 %conv.1 = (bf16[2,208,384]{2,1,0:T(8,128)(2,1)S(1)}, f32[3,8,128]{2,1,0:T(8,128)S(1)}) custom-call(s32[67]{0:T(128)S(1)} %pad_add_fusion.info_ref, bf16[6,112,384]{2,1,0:T(8,128)(2,1)S(1)} %collective-permute-done.8.rest_0_, f32[448,1152]{1,0:T(8,128)S(1)} %own_conv.1.rest_1_, bf16[4,104,384]{2,1,0:T(8,128)(2,1)S(1)} %get-tuple-element.50.rest_2_, ...), custom_call_target="tpu_custom_call" | custom-call | flops 3849999872 | tf_op jit(solution)/shard_map/conv/pallas_call | solution.py:656
  32.3 2.2 %collective-permute-start.10 = (f32[3,8,128]{2,1,0:T(8,128)S(1)}, f32[3,8,128]{2,1,0:T(8,128)S(1)}, u32[]{:S(2)}, u32[]{:S(2)}) collective-permute-start(f32[3,8,128]{2,1,0:T(8,128)S(1)} %get-tuple-element.52), channel_id=1, source_target_pairs={{0,16},{2,18},{4,20},{6,22},{8,24},{10,26},{12,28},{14,30},{16,0},... | collective-permute-start | bytes 36872 | tf_op jit(solution)/shard_map/ppermute | solution.py:598
  34.5 2.2 %collective-permute-start.11 = (f32[3,8,128]{2,1,0:T(8,128)S(1)}, f32[3,8,128]{2,1,0:T(8,128)S(1)}, u32[]{:S(2)}, u32[]{:S(2)}) collective-permute-start(f32[3,8,128]{2,1,0:T(8,128)S(1)} %get-tuple-element.52), channel_id=1, source_target_pairs={{0,24},{2,26},{4,28},{6,30},{8,16},{10,18},{12,20},{14,22},{16,8},... | collective-permute-start | bytes 36872 | tf_op jit(solution)/shard_map/ppermute | solution.py:598
  36.7 2.0 %collective-permute-start.16 = (bf16[2,208,384]{2,1,0:T(8,128)(2,1)S(1)}, bf16[2,208,384]{2,1,0:T(8,128)(2,1)S(1)}, u32[]{:S(2)}, u32[]{:S(2)}) collective-permute-start(bf16[2,208,384]{2,1,0:T(8,128)(2,1)S(1)} %get-tuple-element.70.rest_5_.own_ref), channel_id=1, source_target_pairs={{0,8},{2,10},{4,12},{6,14},{8,0},{10,2},{12,4},{14,6},{16,24},{18,... | collective-permute-start | bytes 958472 | tf_op jit(solution)/shard_map/ppermute | solution.py:598
  38.7 1.9 %collective-permute-start.17 = (bf16[2,208,384]{2,1,0:T(8,128)(2,1)S(1)}, bf16[2,208,384]{2,1,0:T(8,128)(2,1)S(1)}, u32[]{:S(2)}, u32[]{:S(2)}) collective-permute-start(bf16[2,208,384]{2,1,0:T(8,128)(2,1)S(1)} %get-tuple-element.70.rest_5_.own_ref), channel_id=1, source_target_pairs={{8,16},{10,18},{12,20},{14,22},{16,8},{18,10},{20,12},{22,14},{9,1... | collective-permute-start | bytes 958472 | tf_op jit(solution)/shard_map/ppermute | solution.py:598
  44.5 2.3 %collective-permute-done.13 = f32[3,8,128]{2,1,0:T(8,128)S(1)} collective-permute-done((f32[3,8,128]{2,1,0:T(8,128)S(1)}, f32[3,8,128]{2,1,0:T(8,128)S(1)}, u32[]{:S(2)}, u32[]{:S(2)}) %collective-permute-start.13) | collective-permute-done | bytes 12320 | tf_op jit(solution)/shard_map/ppermute | solution.py:598
  49.0 3.9 %collective-permute-start.19 = (bf16[2,208,384]{2,1,0:T(8,128)(2,1)S(1)}, bf16[2,208,384]{2,1,0:T(8,128)(2,1)S(1)}, u32[]{:S(2)}, u32[]{:S(2)}) collective-permute-start(bf16[2,208,384]{2,1,0:T(8,128)(2,1)S(1)} %collective-permute-done.16.rest_7_), channel_id=1, source_target_pairs={{8,16},{10,18},{12,20},{14,22},{16,8},{18,10},{20,12},{22,14},{9,1... | collective-permute-start | bytes 958472 | tf_op jit(solution)/shard_map/ppermute | solution.py:598
  56.0 1.8 %collective-permute-done.19 = bf16[2,208,384]{2,1,0:T(8,128)(2,1)S(1)} collective-permute-done((bf16[2,208,384]{2,1,0:T(8,128)(2,1)S(1)}, bf16[2,208,384]{2,1,0:T(8,128)(2,1)S(1)}, u32[]{:S(2)}, u32[]{:S(2)}) %collective-permute-start.19) | collective-permute-done | bytes 319520 | tf_op jit(solution)/shard_map/ppermute | solution.py:598
  57.9 2.0 %collective-permute-done.20 = bf16[2,208,384]{2,1,0:T(8,128)(2,1)S(1)} collective-permute-done((bf16[2,208,384]{2,1,0:T(8,128)(2,1)S(1)}, bf16[2,208,384]{2,1,0:T(8,128)(2,1)S(1)}, u32[]{:S(2)}, u32[]{:S(2)}) %collective-permute-start.20) | collective-permute-done | bytes 319520 | tf_op jit(solution)/shard_map/ppermute | solution.py:598
  59.9 2.2 %collective-permute-start.21 = (bf16[2,208,384]{2,1,0:T(8,128)(2,1)S(1)}, bf16[2,208,384]{2,1,0:T(8,128)(2,1)S(1)}, u32[]{:S(2)}, u32[]{:S(2)}) collective-permute-start(bf16[2,208,384]{2,1,0:T(8,128)(2,1)S(1)} %collective-permute-done.18.rest_6_), channel_id=1, source_target_pairs={{8,16},{10,18},{12,20},{14,22},{16,8},{18,10},{20,12},{22,14},{9,1... | collective-permute-start | bytes 958472 | tf_op jit(solution)/shard_map/ppermute | solution.py:598
  64.0 3.6 %attend_yours.2 = (bf16[2080,384]{1,0:T(8,128)(2,1)S(1)}, f32[416,128]{1,0:T(8,128)S(1)}, f32[416,128]{1,0:T(8,128)S(1)}, f32[416,384]{1,0:T(8,128)S(1)}) custom-call(s32[67]{0:T(128)S(1)} %pad_add_fusion.info_ref, f32[8,384]{1,0:T(8,128)S(1)} %get-tuple-element.58.rest_0_.means_ref, f32[8,384]{1,0:T(8,128)S(1)} %get-tuple-element.59.rest_1_.scales_ref, ...), custom_call_target="tpu_custom_call" | custom-call | flops 4950000128 | tf_op jit(solution)/shard_map/attend_yours/pallas_call | solution.py:656
  70.3 2.6 %attend_yours.3 = (bf16[1248,384]{1,0:T(8,128)(2,1)S(1)}, bf16[432,384]{1,0:T(8,128)(2,1)S(1)}) custom-call(s32[67]{0:T(128)S(1)} %pad_add_fusion.info_ref, f32[8,384]{1,0:T(8,128)S(1)} %get-tuple-element.58.rest_0_.means_ref, f32[8,384]{1,0:T(8,128)S(1)} %get-tuple-element.59.rest_1_.scales_ref, f32[1,384]{1,0:T(1,128)S(1)} %reshape.87.shift_ref.rest_2_, ...), custom_call_target="tpu_custom_call" | custom-call | flops 2969999872 | tf_op jit(solution)/shard_map/attend_yours/pallas_call | solution.py:656
  73.0 5.5 %attend_mine.1 = (f32[416,384]{1,0:T(8,128)S(1)}, f32[416,128]{1,0:T(8,128)S(1)}) custom-call(s32[67]{0:T(128)S(1)} %pad_add_fusion.info_ref, bf16[2,208,384]{2,1,0:T(8,128)(2,1)S(1)} %get-tuple-element.70.rest_5_.own_ref, f32[8,384]{1,0:T(8,128)S(1)} %get-tuple-element.58.rest_0_.means_ref, f32[8,384]{1,0:T(8,128)S(1)} %get-tuple-element.59.rest_1_.scales_ref, ...), custom_call_target="tpu_custom_call" | custom-call | flops 6600000000 | tf_op jit(solution)/shard_map/attend_mine/pallas_call | solution.py:656
  79.1 1.7 %collective-permute-done.24.received_ref = bf16[432,384]{1,0:T(8,128)(2,1)S(1)} collective-permute-done((bf16[432,384]{1,0:T(8,128)(2,1)S(1)}, bf16[432,384]{1,0:T(8,128)(2,1)S(1)}, u32[]{:S(2)}, u32[]{:S(2)}) %collective-permute-start.24) | collective-permute-done | bytes 331808 | tf_op jit(solution)/shard_map/ppermute | solution.py:785
  82.2 3.2 %collective-permute-start.25 = (bf16[1,104,384]{2,1,0:T(8,128)(2,1)S(1)}, bf16[1,104,384]{2,1,0:T(8,128)(2,1)S(1)}, u32[]{:S(2)}, u32[]{:S(2)}) collective-permute-start(bf16[1,104,384]{2,1,0:T(8,128)(2,1)S(1)} %get-tuple-element.75), channel_id=1, source_target_pairs={{2,4},{4,2},{6,8},{8,6},{10,12},{12,10},{14,16},{16,14},{18,20},{2... | collective-permute-start | bytes 239624 | tf_op jit(solution)/shard_map/ppermute | solution.py:815
  86.0 2.2 %upsample.1 = (bf16[6,192,208]{2,1,0:T(8,128)(2,1)S(1)}, f32[2,2,256,128]{3,2,1,0:T(8,128)S(1)}) custom-call(s32[67]{0:T(128)S(1)} %pad_add_fusion.info_ref, bf16[4,104,384]{2,1,0:T(8,128)(2,1)S(1)} %get-tuple-element.77.own_ref, bf16[2,2,2,192,768]{4,3,2,1,0:T(8,128)(2,1)S(1)} %fold.1.weight_ref, f32[1,256]{1,0:T(1,128)S(1)} %pad.4.bias_ref), custom_call_target="tpu_custom_call" | custom-call | flops 2200000000 | tf_op jit(solution)/shard_map/upsample/pallas_call | solution.py:656
  88.2 2.3 %collective-permute-done.25.outer_ref = bf16[1,104,384]{2,1,0:T(8,128)(2,1)S(1)} collective-permute-done((bf16[1,104,384]{2,1,0:T(8,128)(2,1)S(1)}, bf16[1,104,384]{2,1,0:T(8,128)(2,1)S(1)}, u32[]{:S(2)}, u32[]{:S(2)}) %collective-permute-start.25) | collective-permute-done | bytes 79904 | tf_op jit(solution)/shard_map/ppermute | solution.py:815
  90.4 2.1 %close.1 = bf16[8,192,208]{2,1,0:T(8,128)(2,1)} custom-call(s32[67]{0:T(128)S(1)} %pad_add_fusion.info_ref, bf16[1,104,384]{2,1,0:T(8,128)(2,1)S(1)} %collective-permute-done.25.outer_ref, bf16[1,104,384]{2,1,0:T(8,128)(2,1)S(1)} %collective-permute-done.26.inner_ref, bf16[6,192,208]{2,1,0:T(8,128)(2,1)S(1)} %get-tuple-element.79.middle_ref, ...), custom_call_target="tpu_custom_call" | custom-call | flops 1100000000 | tf_op jit(solution)/shard_map/close/pallas_call | solution.py:656
  (93 shorter events, 29.9 us)
Async XLA Ops:
  0.9 8.5 %collective-permute-start = (bf16[1,104,384]{2,1,0:T(8,128)(2,1)S(1)}, bf16[1,104,384]{2,1,0:T(8,128)(2,1)S(1)}, u32[]{:S(2)}, u32[]{:S(2)}) collective-permute-start(bf16[1,104,384]{2,1,0:T(8,128)(2,1)S(1)} %get-tuple-element.93), channel_id=1, source_target_pairs={{2,4},{4,2},{6,8},{8,6},{10,12},{12,10},{14,16},{16,14},{18,20},{2... | collective-permute-start | bytes 239624 | tf_op jit(solution)/shard_map/ppermute | solution.py:674
  5.2 4.7 %collective-permute-start.1 = (bf16[1,104,384]{2,1,0:T(8,128)(2,1)S(1)}, bf16[1,104,384]{2,1,0:T(8,128)(2,1)S(1)}, u32[]{:S(2)}, u32[]{:S(2)}) collective-permute-start(bf16[1,104,384]{2,1,0:T(8,128)(2,1)S(1)} %get-tuple-element.92), channel_id=1, source_target_pairs={{0,2},{2,0},{4,6},{6,4},{8,10},{10,8},{12,14},{14,12},{16,18},{18,... | collective-permute-start | bytes 239624 | tf_op jit(solution)/shard_map/ppermute | solution.py:598
  9.9 5.2 %collective-permute-start.2 = (f32[3,8,128]{2,1,0:T(8,128)S(1)}, f32[3,8,128]{2,1,0:T(8,128)S(1)}, u32[]{:S(2)}, u32[]{:S(2)}) collective-permute-start(f32[3,8,128]{2,1,0:T(8,128)S(1)} %first_stats.1), channel_id=1, source_target_pairs={{0,8},{2,10},{4,12},{6,14},{8,0},{10,2},{12,4},{14,6},{16,24},{18,... | collective-permute-start | bytes 36872 | tf_op jit(solution)/shard_map/ppermute | solution.py:598
  10.1 5.1 %collective-permute-start.3 = (f32[3,8,128]{2,1,0:T(8,128)S(1)}, f32[3,8,128]{2,1,0:T(8,128)S(1)}, u32[]{:S(2)}, u32[]{:S(2)}) collective-permute-start(f32[3,8,128]{2,1,0:T(8,128)S(1)} %first_stats.1), channel_id=1, source_target_pairs={{0,16},{2,18},{4,20},{6,22},{8,24},{10,26},{12,28},{14,30},{16,0},... | collective-permute-start | bytes 36872 | tf_op jit(solution)/shard_map/ppermute | solution.py:598
  16.7 5.4 %collective-permute-start.5 = (f32[3,8,128]{2,1,0:T(8,128)S(1)}, f32[3,8,128]{2,1,0:T(8,128)S(1)}, u32[]{:S(2)}, u32[]{:S(2)}) collective-permute-start(f32[3,8,128]{2,1,0:T(8,128)S(1)} %pad_maximum_fusion), channel_id=1, source_target_pairs={{0,2},{2,0},{4,6},{6,4},{8,10},{10,8},{12,14},{14,12},{16,18},{18,... | collective-permute-start | bytes 36872 | tf_op jit(solution)/shard_map/ppermute | solution.py:598
  19.0 4.6 %collective-permute-start.7 = (f32[3,8,128]{2,1,0:T(8,128)S(1)}, f32[3,8,128]{2,1,0:T(8,128)S(1)}, u32[]{:S(2)}, u32[]{:S(2)}) collective-permute-start(f32[3,8,128]{2,1,0:T(8,128)S(1)} %pad_maximum_fusion), channel_id=1, source_target_pairs={{0,6},{2,4},{4,2},{6,0},{8,14},{10,12},{12,10},{14,8},{16,22},{18,... | collective-permute-start | bytes 36872 | tf_op jit(solution)/shard_map/ppermute | solution.py:598
  32.3 8.3 %collective-permute-start.10 = (f32[3,8,128]{2,1,0:T(8,128)S(1)}, f32[3,8,128]{2,1,0:T(8,128)S(1)}, u32[]{:S(2)}, u32[]{:S(2)}) collective-permute-start(f32[3,8,128]{2,1,0:T(8,128)S(1)} %get-tuple-element.52), channel_id=1, source_target_pairs={{0,16},{2,18},{4,20},{6,22},{8,24},{10,26},{12,28},{14,30},{16,0},... | collective-permute-start | bytes 36872 | tf_op jit(solution)/shard_map/ppermute | solution.py:598
  34.5 6.2 %collective-permute-start.11 = (f32[3,8,128]{2,1,0:T(8,128)S(1)}, f32[3,8,128]{2,1,0:T(8,128)S(1)}, u32[]{:S(2)}, u32[]{:S(2)}) collective-permute-start(f32[3,8,128]{2,1,0:T(8,128)S(1)} %get-tuple-element.52), channel_id=1, source_target_pairs={{0,24},{2,26},{4,28},{6,30},{8,16},{10,18},{12,20},{14,22},{16,8},... | collective-permute-start | bytes 36872 | tf_op jit(solution)/shard_map/ppermute | solution.py:598
  36.7 4.0 %collective-permute-start.9 = (f32[3,8,128]{2,1,0:T(8,128)S(1)}, f32[3,8,128]{2,1,0:T(8,128)S(1)}, u32[]{:S(2)}, u32[]{:S(2)}) collective-permute-start(f32[3,8,128]{2,1,0:T(8,128)S(1)} %get-tuple-element.52), channel_id=1, source_target_pairs={{0,8},{2,10},{4,12},{6,14},{8,0},{10,2},{12,4},{14,6},{16,24},{18,... | collective-permute-start | bytes 36872 | tf_op jit(solution)/shard_map/ppermute | solution.py:598
  36.7 12.2 %collective-permute-start.16 = (bf16[2,208,384]{2,1,0:T(8,128)(2,1)S(1)}, bf16[2,208,384]{2,1,0:T(8,128)(2,1)S(1)}, u32[]{:S(2)}, u32[]{:S(2)}) collective-permute-start(bf16[2,208,384]{2,1,0:T(8,128)(2,1)S(1)} %get-tuple-element.70.rest_5_.own_ref), channel_id=1, source_target_pairs={{0,8},{2,10},{4,12},{6,14},{8,0},{10,2},{12,4},{14,6},{16,24},{18,... | collective-permute-start | bytes 958472 | tf_op jit(solution)/shard_map/ppermute | solution.py:598
  38.7 10.2 %collective-permute-start.17 = (bf16[2,208,384]{2,1,0:T(8,128)(2,1)S(1)}, bf16[2,208,384]{2,1,0:T(8,128)(2,1)S(1)}, u32[]{:S(2)}, u32[]{:S(2)}) collective-permute-start(bf16[2,208,384]{2,1,0:T(8,128)(2,1)S(1)} %get-tuple-element.70.rest_5_.own_ref), channel_id=1, source_target_pairs={{8,16},{10,18},{12,20},{14,22},{16,8},{18,10},{20,12},{22,14},{9,1... | collective-permute-start | bytes 958472 | tf_op jit(solution)/shard_map/ppermute | solution.py:598
  40.7 3.8 %collective-permute-start.12 = (f32[3,8,128]{2,1,0:T(8,128)S(1)}, f32[3,8,128]{2,1,0:T(8,128)S(1)}, u32[]{:S(2)}, u32[]{:S(2)}) collective-permute-start(f32[3,8,128]{2,1,0:T(8,128)S(1)} %pad_maximum_fusion.2), channel_id=1, source_target_pairs={{0,4},{2,6},{4,0},{6,2},{8,12},{10,14},{12,8},{14,10},{16,20},{18,... | collective-permute-start | bytes 36872 | tf_op jit(solution)/shard_map/ppermute | solution.py:598
  42.1 4.7 %collective-permute-start.13 = (f32[3,8,128]{2,1,0:T(8,128)S(1)}, f32[3,8,128]{2,1,0:T(8,128)S(1)}, u32[]{:S(2)}, u32[]{:S(2)}) collective-permute-start(f32[3,8,128]{2,1,0:T(8,128)S(1)} %pad_maximum_fusion.2), channel_id=1, source_target_pairs={{0,6},{2,4},{4,2},{6,0},{8,14},{10,12},{12,10},{14,8},{16,22},{18,... | collective-permute-start | bytes 36872 | tf_op jit(solution)/shard_map/ppermute | solution.py:598
  43.7 5.3 %collective-permute-start.15 = (f32[3,8,128]{2,1,0:T(8,128)S(1)}, f32[3,8,128]{2,1,0:T(8,128)S(1)}, u32[]{:S(2)}, u32[]{:S(2)}) collective-permute-start(f32[3,8,128]{2,1,0:T(8,128)S(1)} %pad_maximum_fusion.2), channel_id=1, source_target_pairs={{0,2},{2,0},{4,6},{6,4},{8,10},{10,8},{12,14},{14,12},{16,18},{18,... | collective-permute-start | bytes 36872 | tf_op jit(solution)/shard_map/ppermute | solution.py:598
  46.8 13.1 %collective-permute-start.18 = (bf16[2,208,384]{2,1,0:T(8,128)(2,1)S(1)}, bf16[2,208,384]{2,1,0:T(8,128)(2,1)S(1)}, u32[]{:S(2)}, u32[]{:S(2)}) collective-permute-start(bf16[2,208,384]{2,1,0:T(8,128)(2,1)S(1)} %get-tuple-element.70.rest_5_.own_ref), channel_id=1, source_target_pairs={{0,4},{2,6},{4,0},{6,2},{8,12},{10,14},{12,8},{14,10},{16,20},{18,... | collective-permute-start | bytes 958472 | tf_op jit(solution)/shard_map/ppermute | solution.py:598
  47.5 7.0 %collective-permute-start.14 = (bf16[2,208,384]{2,1,0:T(8,128)(2,1)S(1)}, bf16[2,208,384]{2,1,0:T(8,128)(2,1)S(1)}, u32[]{:S(2)}, u32[]{:S(2)}) collective-permute-start(bf16[2,208,384]{2,1,0:T(8,128)(2,1)S(1)} %get-tuple-element.70.rest_5_.own_ref), channel_id=1, source_target_pairs={{0,2},{2,0},{4,6},{6,4},{8,10},{10,8},{12,14},{14,12},{16,18},{18,... | collective-permute-start | bytes 958472 | tf_op jit(solution)/shard_map/ppermute | solution.py:598
  49.0 8.9 %collective-permute-start.19 = (bf16[2,208,384]{2,1,0:T(8,128)(2,1)S(1)}, bf16[2,208,384]{2,1,0:T(8,128)(2,1)S(1)}, u32[]{:S(2)}, u32[]{:S(2)}) collective-permute-start(bf16[2,208,384]{2,1,0:T(8,128)(2,1)S(1)} %collective-permute-done.16.rest_7_), channel_id=1, source_target_pairs={{8,16},{10,18},{12,20},{14,22},{16,8},{18,10},{20,12},{22,14},{9,1... | collective-permute-start | bytes 958472 | tf_op jit(solution)/shard_map/ppermute | solution.py:598
  52.9 6.9 %collective-permute-start.20 = (bf16[2,208,384]{2,1,0:T(8,128)(2,1)S(1)}, bf16[2,208,384]{2,1,0:T(8,128)(2,1)S(1)}, u32[]{:S(2)}, u32[]{:S(2)}) collective-permute-start(bf16[2,208,384]{2,1,0:T(8,128)(2,1)S(1)} %collective-permute-done.17.rest_8_), channel_id=1, source_target_pairs={{8,0},{10,2},{12,4},{14,6},{16,24},{18,26},{20,28},{22,30},{9,1},{... | collective-permute-start | bytes 958472 | tf_op jit(solution)/shard_map/ppermute | solution.py:598
  59.9 8.9 %collective-permute-start.21 = (bf16[2,208,384]{2,1,0:T(8,128)(2,1)S(1)}, bf16[2,208,384]{2,1,0:T(8,128)(2,1)S(1)}, u32[]{:S(2)}, u32[]{:S(2)}) collective-permute-start(bf16[2,208,384]{2,1,0:T(8,128)(2,1)S(1)} %collective-permute-done.18.rest_6_), channel_id=1, source_target_pairs={{8,16},{10,18},{12,20},{14,22},{16,8},{18,10},{20,12},{22,14},{9,1... | collective-permute-start | bytes 958472 | tf_op jit(solution)/shard_map/ppermute | solution.py:598
  62.2 7.1 %collective-permute-start.22 = (bf16[2,208,384]{2,1,0:T(8,128)(2,1)S(1)}, bf16[2,208,384]{2,1,0:T(8,128)(2,1)S(1)}, u32[]{:S(2)}, u32[]{:S(2)}) collective-permute-start(bf16[2,208,384]{2,1,0:T(8,128)(2,1)S(1)} %collective-permute-done.18.rest_6_), channel_id=1, source_target_pairs={{0,8},{2,10},{4,12},{6,14},{8,0},{10,2},{12,4},{14,6},{16,24},{18,... | collective-permute-start | bytes 958472 | tf_op jit(solution)/shard_map/ppermute | solution.py:598
  63.3 7.0 %collective-permute-start.23 = (bf16[2,208,384]{2,1,0:T(8,128)(2,1)S(1)}, bf16[2,208,384]{2,1,0:T(8,128)(2,1)S(1)}, u32[]{:S(2)}, u32[]{:S(2)}) collective-permute-start(bf16[2,208,384]{2,1,0:T(8,128)(2,1)S(1)} %broadcast_select_fusion.rest_9_), channel_id=1, source_target_pairs={{0,4},{2,6},{4,0},{6,2},{8,12},{10,14},{12,8},{14,10},{16,20},{18,... | collective-permute-start | bytes 958472 | tf_op jit(solution)/shard_map/ppermute | solution.py:598
  72.9 7.8 %collective-permute-start.24 = (bf16[432,384]{1,0:T(8,128)(2,1)S(1)}, bf16[432,384]{1,0:T(8,128)(2,1)S(1)}, u32[]{:S(2)}, u32[]{:S(2)}) collective-permute-start(bf16[432,384]{1,0:T(8,128)(2,1)S(1)} %get-tuple-element.69), channel_id=1, source_target_pairs={{0,2},{2,0},{4,6},{6,4},{8,10},{10,8},{12,14},{14,12},{16,18},{18,... | collective-permute-start | bytes 995336 | tf_op jit(solution)/shard_map/ppermute | solution.py:785
  82.2 8.2 %collective-permute-start.25 = (bf16[1,104,384]{2,1,0:T(8,128)(2,1)S(1)}, bf16[1,104,384]{2,1,0:T(8,128)(2,1)S(1)}, u32[]{:S(2)}, u32[]{:S(2)}) collective-permute-start(bf16[1,104,384]{2,1,0:T(8,128)(2,1)S(1)} %get-tuple-element.75), channel_id=1, source_target_pairs={{2,4},{4,2},{6,8},{8,6},{10,12},{12,10},{14,16},{16,14},{18,20},{2... | collective-permute-start | bytes 239624 | tf_op jit(solution)/shard_map/ppermute | solution.py:815
  85.4 5.0 %collective-permute-start.26 = (bf16[1,104,384]{2,1,0:T(8,128)(2,1)S(1)}, bf16[1,104,384]{2,1,0:T(8,128)(2,1)S(1)}, u32[]{:S(2)}, u32[]{:S(2)}) collective-permute-start(bf16[1,104,384]{2,1,0:T(8,128)(2,1)S(1)} %get-tuple-element.76), channel_id=1, source_target_pairs={{0,2},{2,0},{4,6},{6,4},{8,10},{10,8},{12,14},{14,12},{16,18},{18,... | collective-permute-start | bytes 239624 | tf_op jit(solution)/shard_map/ppermute | solution.py:598
  (16 other events, 144.8 us)

commit v12 on v11

--- a/solution.py
+++ b/solution.py
@@ -12,7 +12,6 @@
 EPSILON = 1e-05
 MASKED = -1e30
 LOWEST = -5e29
-HIGHEST = lax.Precision.HIGHEST
 SLOTS = 8
 ROWS_OF_TILE = 4
 LANES = 128
@@ -40,17 +39,32 @@
     per_group = channels // GROUPS
     group = lax.broadcasted_iota(jnp.int32, (LANES, channels), 0) * per_group
     channel = lax.broadcasted_iota(jnp.int32, (LANES, channels), 1)
-    return jnp.where((channel >= group) & (channel < group + per_group), 1.0, 0.0).astype(F32)
+    return jnp.where((channel >= group) & (channel < group + per_group), 1.0, 0.0).astype(BF16)
+
+
+def thirds(values):
+    parts = []
+    for _ in range(3):
+        parts.append(values.astype(BF16).astype(F32))
+        values = values - parts[-1]
+    return jnp.concatenate(parts, axis=0).astype(BF16)
+
+
+def added(products):
+    rows = products.shape[0] // 3
+    return (products[2 * rows :] + products[rows : 2 * rows]) + products[:rows]
 
 
 def to_groups(values, member):
-    return lax.dot_general(
-        values, member, (((1,), (1,)), ((), ())), precision=HIGHEST, preferred_element_type=F32
+    return added(
+        lax.dot_general(
+            thirds(values), member, (((1,), (1,)), ((), ())), preferred_element_type=F32
+        )
     )
 
 
 def to_channels(values, member):
-    return jnp.dot(values, member, precision=HIGHEST, preferred_element_type=F32)
+    return added(jnp.dot(thirds(values), member, preferred_element_type=F32))
 
 
 class Info:

time: 93.7 us -> 92.5 us (0.987)
  Pallas kernels: 32 us -> 30.1 us
    pallas_call x11, Pallas kernels: 28 us -> 26.1 us  [call(): pl.pallas_call(kernel, out_shape=out_shape, in_specs=[SMEM_SPEC] + [VMEM_...]
  transfers between devices with their start and end apart: 27 -> 27, of which waited for: 13 -> 14; matrix products, arithmetic and copies ran while one was open for 1% -> 1% of each run, Pallas kernels for 23% -> 22%
where the time goes in v12:
time: 92.5 us; the launch traced here: 91.5 us
  starting transfers between devices  40.8 us (44%)
  Pallas kernels  30.1 us (33%)
  waiting for transfers between devices  17.1 us (18%)
  other arithmetic  1.9 us (2%)
  local copies, waits for them, and re-layouts  1.08 us (1%)
    ppermute x23, starting transfers between devices, exchange(): return lax.ppermute(array, 'tile', moves)  31.8 us
    pallas_call x11, Pallas kernels, call(): pl.pallas_call(kernel, out_shape=out_shape, in_specs=[SMEM_SPEC] + [VMEM_...  26.1 us
    ppermute x23, waiting for transfers between devices, exchange(): return lax.ppermute(array, 'tile', moves)  12.8 us
    ppermute x1, starting transfers between devices, shards(): lax.ppermute(jnp.where(odd, source[row_count - 1:], source[:1]), 'tile',...  4.24 us
    pallas_call x2, Pallas kernels, shards(): pl.pallas_call(functools.partial(hold_kernel, backs), out_shape=shape(3 *...  3.5 us
    ppermute x1, starting transfers between devices, shards(): outer = lax.ppermute(outer, 'tile', outer_moves)  3.34 us
    ppermute x1, waiting for transfers between devices, shards(): outer = lax.ppermute(outer, 'tile', outer_moves)  2.34 us
  transfers between devices with their start and end apart: 27, of which 14 were waited for; matrix products, arithmetic and copies ran while one was open for 1% of the time, Pallas kernels for 22%

profile of v12, /device:TPU:8, one launch (start us, length us, event | category | flops | bytes accessed | tf_op | source)
XLA Modules:
  0.0 91.5 jit_solution(388533749259481305)
XLA Ops:
  0.9 4.2 %collective-permute-start = (bf16[1,104,384]{2,1,0:T(8,128)(2,1)S(1)}, bf16[1,104,384]{2,1,0:T(8,128)(2,1)S(1)}, u32[]{:S(2)}, u32[]{:S(2)}) collective-permute-start(bf16[1,104,384]{2,1,0:T(8,128)(2,1)S(1)} %get-tuple-element.93), channel_id=1, source_target_pairs={{2,4},{4,2},{6,8},{8,6},{10,12},{12,10},{14,16},{16,14},{18,20},{2... | collective-permute-start | bytes 239624 | tf_op jit(solution)/shard_map/ppermute | solution.py:688
  10.1 2.9 %collective-permute-start.3 = (f32[3,8,128]{2,1,0:T(8,128)S(1)}, f32[3,8,128]{2,1,0:T(8,128)S(1)}, u32[]{:S(2)}, u32[]{:S(2)}) collective-permute-start(f32[3,8,128]{2,1,0:T(8,128)S(1)} %first_stats.1), channel_id=1, source_target_pairs={{0,16},{2,18},{4,20},{6,22},{8,24},{10,26},{12,28},{14,30},{16,0},... | collective-permute-start | bytes 36872 | tf_op jit(solution)/shard_map/ppermute | solution.py:612
  13.4 1.7 %hold.2.held_ref = bf16[1152,1152]{1,0:T(8,128)(2,1)S(1)} custom-call(bf16[3,3,3,384,384]{4,3,2,1,0:T(8,128)(2,1)} %weight_ref.5), custom_call_target="tpu_custom_call" | custom-call | flops 1650000000 | tf_op jit(solution)/shard_map/hold/pallas_call | solution.py:695
  20.3 1.7 %hold.3.rest_4_ = bf16[1152,1152]{1,0:T(8,128)(2,1)S(1)} custom-call(bf16[3,3,3,384,384]{4,3,2,1,0:T(8,128)(2,1)} %weight_ref.5), custom_call_target="tpu_custom_call" | custom-call | flops 1650000000 | tf_op jit(solution)/shard_map/hold/pallas_call | solution.py:695
  26.2 2.2 %own_conv.1.rest_1_ = f32[448,1152]{1,0:T(8,128)S(1)} custom-call(s32[67]{0:T(128)S(1)} %pad_add_fusion.info_ref, bf16[6,112,384]{2,1,0:T(8,128)(2,1)S(1)} %get-tuple-element.48.hidden_ref, bf16[1152,1152]{1,0:T(8,128)(2,1)S(1)} %hold.2.held_ref), custom_call_target="tpu_custom_call" | custom-call | flops 2420000000 | tf_op jit(solution)/shard_map/own_conv/pallas_call | solution.py:670
  28.5 2.8 %conv.1 = (bf16[2,208,384]{2,1,0:T(8,128)(2,1)S(1)}, f32[3,8,128]{2,1,0:T(8,128)S(1)}) custom-call(s32[67]{0:T(128)S(1)} %pad_add_fusion.info_ref, bf16[6,112,384]{2,1,0:T(8,128)(2,1)S(1)} %collective-permute-done.8.rest_0_, f32[448,1152]{1,0:T(8,128)S(1)} %own_conv.1.rest_1_, bf16[4,104,384]{2,1,0:T(8,128)(2,1)S(1)} %get-tuple-element.50.rest_2_, ...), custom_call_target="tpu_custom_call" | custom-call | flops 3849999872 | tf_op jit(solution)/shard_map/conv/pallas_call | solution.py:670
  31.3 2.2 %collective-permute-start.10 = (f32[3,8,128]{2,1,0:T(8,128)S(1)}, f32[3,8,128]{2,1,0:T(8,128)S(1)}, u32[]{:S(2)}, u32[]{:S(2)}) collective-permute-start(f32[3,8,128]{2,1,0:T(8,128)S(1)} %get-tuple-element.52), channel_id=1, source_target_pairs={{0,16},{2,18},{4,20},{6,22},{8,24},{10,26},{12,28},{14,30},{16,0},... | collective-permute-start | bytes 36872 | tf_op jit(solution)/shard_map/ppermute | solution.py:612
  33.5 2.2 %collective-permute-start.11 = (f32[3,8,128]{2,1,0:T(8,128)S(1)}, f32[3,8,128]{2,1,0:T(8,128)S(1)}, u32[]{:S(2)}, u32[]{:S(2)}) collective-permute-start(f32[3,8,128]{2,1,0:T(8,128)S(1)} %get-tuple-element.52), channel_id=1, source_target_pairs={{0,24},{2,26},{4,28},{6,30},{8,16},{10,18},{12,20},{14,22},{16,8},... | collective-permute-start | bytes 36872 | tf_op jit(solution)/shard_map/ppermute | solution.py:612
  35.8 2.0 %collective-permute-start.16 = (bf16[2,208,384]{2,1,0:T(8,128)(2,1)S(1)}, bf16[2,208,384]{2,1,0:T(8,128)(2,1)S(1)}, u32[]{:S(2)}, u32[]{:S(2)}) collective-permute-start(bf16[2,208,384]{2,1,0:T(8,128)(2,1)S(1)} %get-tuple-element.70.rest_5_.own_ref), channel_id=1, source_target_pairs={{0,8},{2,10},{4,12},{6,14},{8,0},{10,2},{12,4},{14,6},{16,24},{18,... | collective-permute-start | bytes 958472 | tf_op jit(solution)/shard_map/ppermute | solution.py:612
  37.7 1.9 %collective-permute-start.17 = (bf16[2,208,384]{2,1,0:T(8,128)(2,1)S(1)}, bf16[2,208,384]{2,1,0:T(8,128)(2,1)S(1)}, u32[]{:S(2)}, u32[]{:S(2)}) collective-permute-start(bf16[2,208,384]{2,1,0:T(8,128)(2,1)S(1)} %get-tuple-element.70.rest_5_.own_ref), channel_id=1, source_target_pairs={{8,16},{10,18},{12,20},{14,22},{16,8},{18,10},{20,12},{22,14},{9,1... | collective-permute-start | bytes 958472 | tf_op jit(solution)/shard_map/ppermute | solution.py:612
  41.0 1.7 %collective-permute-start.13 = (f32[3,8,128]{2,1,0:T(8,128)S(1)}, f32[3,8,128]{2,1,0:T(8,128)S(1)}, u32[]{:S(2)}, u32[]{:S(2)}) collective-permute-start(f32[3,8,128]{2,1,0:T(8,128)S(1)} %pad_maximum_fusion.2), channel_id=1, source_target_pairs={{0,6},{2,4},{4,2},{6,0},{8,14},{10,12},{12,10},{14,8},{16,22},{18,... | collective-permute-start | bytes 36872 | tf_op jit(solution)/shard_map/ppermute | solution.py:612
  43.5 2.2 %collective-permute-done.13 = f32[3,8,128]{2,1,0:T(8,128)S(1)} collective-permute-done((f32[3,8,128]{2,1,0:T(8,128)S(1)}, f32[3,8,128]{2,1,0:T(8,128)S(1)}, u32[]{:S(2)}, u32[]{:S(2)}) %collective-permute-start.13) | collective-permute-done | bytes 12320 | tf_op jit(solution)/shard_map/ppermute | solution.py:612
  48.0 3.9 %collective-permute-start.19 = (bf16[2,208,384]{2,1,0:T(8,128)(2,1)S(1)}, bf16[2,208,384]{2,1,0:T(8,128)(2,1)S(1)}, u32[]{:S(2)}, u32[]{:S(2)}) collective-permute-start(bf16[2,208,384]{2,1,0:T(8,128)(2,1)S(1)} %collective-permute-done.16.rest_7_), channel_id=1, source_target_pairs={{8,16},{10,18},{12,20},{14,22},{16,8},{18,10},{20,12},{22,14},{9,1... | collective-permute-start | bytes 958472 | tf_op jit(solution)/shard_map/ppermute | solution.py:612
  54.9 2.0 %collective-permute-done.19 = bf16[2,208,384]{2,1,0:T(8,128)(2,1)S(1)} collective-permute-done((bf16[2,208,384]{2,1,0:T(8,128)(2,1)S(1)}, bf16[2,208,384]{2,1,0:T(8,128)(2,1)S(1)}, u32[]{:S(2)}, u32[]{:S(2)}) %collective-permute-start.19) | collective-permute-done | bytes 319520 | tf_op jit(solution)/shard_map/ppermute | solution.py:612
  56.9 2.0 %collective-permute-done.20 = bf16[2,208,384]{2,1,0:T(8,128)(2,1)S(1)} collective-permute-done((bf16[2,208,384]{2,1,0:T(8,128)(2,1)S(1)}, bf16[2,208,384]{2,1,0:T(8,128)(2,1)S(1)}, u32[]{:S(2)}, u32[]{:S(2)}) %collective-permute-start.20) | collective-permute-done | bytes 319520 | tf_op jit(solution)/shard_map/ppermute | solution.py:612
  58.9 2.2 %collective-permute-start.21 = (bf16[2,208,384]{2,1,0:T(8,128)(2,1)S(1)}, bf16[2,208,384]{2,1,0:T(8,128)(2,1)S(1)}, u32[]{:S(2)}, u32[]{:S(2)}) collective-permute-start(bf16[2,208,384]{2,1,0:T(8,128)(2,1)S(1)} %collective-permute-done.18.rest_6_), channel_id=1, source_target_pairs={{8,16},{10,18},{12,20},{14,22},{16,8},{18,10},{20,12},{22,14},{9,1... | collective-permute-start | bytes 958472 | tf_op jit(solution)/shard_map/ppermute | solution.py:612
  63.2 3.6 %attend_yours.2 = (bf16[2080,384]{1,0:T(8,128)(2,1)S(1)}, f32[416,128]{1,0:T(8,128)S(1)}, f32[416,128]{1,0:T(8,128)S(1)}, f32[416,384]{1,0:T(8,128)S(1)}) custom-call(s32[67]{0:T(128)S(1)} %pad_add_fusion.info_ref, f32[8,384]{1,0:T(8,128)S(1)} %get-tuple-element.58.rest_0_.means_ref, f32[8,384]{1,0:T(8,128)S(1)} %get-tuple-element.59.rest_1_.scales_ref, ...), custom_call_target="tpu_custom_call" | custom-call | flops 4950000128 | tf_op jit(solution)/shard_map/attend_yours/pallas_call | solution.py:670
  69.3 2.6 %attend_yours.3 = (bf16[1248,384]{1,0:T(8,128)(2,1)S(1)}, bf16[432,384]{1,0:T(8,128)(2,1)S(1)}) custom-call(s32[67]{0:T(128)S(1)} %pad_add_fusion.info_ref, f32[8,384]{1,0:T(8,128)S(1)} %get-tuple-element.58.rest_0_.means_ref, f32[8,384]{1,0:T(8,128)S(1)} %get-tuple-element.59.rest_1_.scales_ref, f32[1,384]{1,0:T(1,128)S(1)} %reshape.87.shift_ref.rest_2_, ...), custom_call_target="tpu_custom_call" | custom-call | flops 2969999872 | tf_op jit(solution)/shard_map/attend_yours/pallas_call | solution.py:670
  72.1 5.5 %attend_mine.1 = (f32[416,384]{1,0:T(8,128)S(1)}, f32[416,128]{1,0:T(8,128)S(1)}) custom-call(s32[67]{0:T(128)S(1)} %pad_add_fusion.info_ref, bf16[2,208,384]{2,1,0:T(8,128)(2,1)S(1)} %get-tuple-element.70.rest_5_.own_ref, f32[8,384]{1,0:T(8,128)S(1)} %get-tuple-element.58.rest_0_.means_ref, f32[8,384]{1,0:T(8,128)S(1)} %get-tuple-element.59.rest_1_.scales_ref, ...), custom_call_target="tpu_custom_call" | custom-call | flops 6600000000 | tf_op jit(solution)/shard_map/attend_mine/pallas_call | solution.py:670
  78.1 1.7 %collective-permute-done.24.received_ref = bf16[432,384]{1,0:T(8,128)(2,1)S(1)} collective-permute-done((bf16[432,384]{1,0:T(8,128)(2,1)S(1)}, bf16[432,384]{1,0:T(8,128)(2,1)S(1)}, u32[]{:S(2)}, u32[]{:S(2)}) %collective-permute-start.24) | collective-permute-done | bytes 331808 | tf_op jit(solution)/shard_map/ppermute | solution.py:799
  81.2 3.3 %collective-permute-start.25 = (bf16[1,104,384]{2,1,0:T(8,128)(2,1)S(1)}, bf16[1,104,384]{2,1,0:T(8,128)(2,1)S(1)}, u32[]{:S(2)}, u32[]{:S(2)}) collective-permute-start(bf16[1,104,384]{2,1,0:T(8,128)(2,1)S(1)} %get-tuple-element.75), channel_id=1, source_target_pairs={{2,4},{4,2},{6,8},{8,6},{10,12},{12,10},{14,16},{16,14},{18,20},{2... | collective-permute-start | bytes 239624 | tf_op jit(solution)/shard_map/ppermute | solution.py:829
  84.9 2.2 %upsample.1 = (bf16[6,192,208]{2,1,0:T(8,128)(2,1)S(1)}, f32[2,2,256,128]{3,2,1,0:T(8,128)S(1)}) custom-call(s32[67]{0:T(128)S(1)} %pad_add_fusion.info_ref, bf16[4,104,384]{2,1,0:T(8,128)(2,1)S(1)} %get-tuple-element.77.own_ref, bf16[2,2,2,192,768]{4,3,2,1,0:T(8,128)(2,1)S(1)} %fold.1.weight_ref, f32[1,256]{1,0:T(1,128)S(1)} %pad.4.bias_ref), custom_call_target="tpu_custom_call" | custom-call | flops 2200000000 | tf_op jit(solution)/shard_map/upsample/pallas_call | solution.py:670
  87.1 2.3 %collective-permute-done.25.outer_ref = bf16[1,104,384]{2,1,0:T(8,128)(2,1)S(1)} collective-permute-done((bf16[1,104,384]{2,1,0:T(8,128)(2,1)S(1)}, bf16[1,104,384]{2,1,0:T(8,128)(2,1)S(1)}, u32[]{:S(2)}, u32[]{:S(2)}) %collective-permute-start.25) | collective-permute-done | bytes 79904 | tf_op jit(solution)/shard_map/ppermute | solution.py:829
  89.4 2.1 %close.1 = bf16[8,192,208]{2,1,0:T(8,128)(2,1)} custom-call(s32[67]{0:T(128)S(1)} %pad_add_fusion.info_ref, bf16[1,104,384]{2,1,0:T(8,128)(2,1)S(1)} %collective-permute-done.25.outer_ref, bf16[1,104,384]{2,1,0:T(8,128)(2,1)S(1)} %collective-permute-done.26.inner_ref, bf16[6,192,208]{2,1,0:T(8,128)(2,1)S(1)} %get-tuple-element.79.middle_ref, ...), custom_call_target="tpu_custom_call" | custom-call | flops 1100000000 | tf_op jit(solution)/shard_map/close/pallas_call | solution.py:670
  (93 shorter events, 29.6 us)
Async XLA Ops:
  0.9 8.2 %collective-permute-start = (bf16[1,104,384]{2,1,0:T(8,128)(2,1)S(1)}, bf16[1,104,384]{2,1,0:T(8,128)(2,1)S(1)}, u32[]{:S(2)}, u32[]{:S(2)}) collective-permute-start(bf16[1,104,384]{2,1,0:T(8,128)(2,1)S(1)} %get-tuple-element.93), channel_id=1, source_target_pairs={{2,4},{4,2},{6,8},{8,6},{10,12},{12,10},{14,16},{16,14},{18,20},{2... | collective-permute-start | bytes 239624 | tf_op jit(solution)/shard_map/ppermute | solution.py:688
  5.2 4.7 %collective-permute-start.1 = (bf16[1,104,384]{2,1,0:T(8,128)(2,1)S(1)}, bf16[1,104,384]{2,1,0:T(8,128)(2,1)S(1)}, u32[]{:S(2)}, u32[]{:S(2)}) collective-permute-start(bf16[1,104,384]{2,1,0:T(8,128)(2,1)S(1)} %get-tuple-element.92), channel_id=1, source_target_pairs={{0,2},{2,0},{4,6},{6,4},{8,10},{10,8},{12,14},{14,12},{16,18},{18,... | collective-permute-start | bytes 239624 | tf_op jit(solution)/shard_map/ppermute | solution.py:612
  9.9 5.2 %collective-permute-start.2 = (f32[3,8,128]{2,1,0:T(8,128)S(1)}, f32[3,8,128]{2,1,0:T(8,128)S(1)}, u32[]{:S(2)}, u32[]{:S(2)}) collective-permute-start(f32[3,8,128]{2,1,0:T(8,128)S(1)} %first_stats.1), channel_id=1, source_target_pairs={{0,8},{2,10},{4,12},{6,14},{8,0},{10,2},{12,4},{14,6},{16,24},{18,... | collective-permute-start | bytes 36872 | tf_op jit(solution)/shard_map/ppermute | solution.py:612
  10.1 5.1 %collective-permute-start.3 = (f32[3,8,128]{2,1,0:T(8,128)S(1)}, f32[3,8,128]{2,1,0:T(8,128)S(1)}, u32[]{:S(2)}, u32[]{:S(2)}) collective-permute-start(f32[3,8,128]{2,1,0:T(8,128)S(1)} %first_stats.1), channel_id=1, source_target_pairs={{0,16},{2,18},{4,20},{6,22},{8,24},{10,26},{12,28},{14,30},{16,0},... | collective-permute-start | bytes 36872 | tf_op jit(solution)/shard_map/ppermute | solution.py:612
  16.7 5.4 %collective-permute-start.5 = (f32[3,8,128]{2,1,0:T(8,128)S(1)}, f32[3,8,128]{2,1,0:T(8,128)S(1)}, u32[]{:S(2)}, u32[]{:S(2)}) collective-permute-start(f32[3,8,128]{2,1,0:T(8,128)S(1)} %pad_maximum_fusion), channel_id=1, source_target_pairs={{0,2},{2,0},{4,6},{6,4},{8,10},{10,8},{12,14},{14,12},{16,18},{18,... | collective-permute-start | bytes 36872 | tf_op jit(solution)/shard_map/ppermute | solution.py:612
  19.0 4.6 %collective-permute-start.7 = (f32[3,8,128]{2,1,0:T(8,128)S(1)}, f32[3,8,128]{2,1,0:T(8,128)S(1)}, u32[]{:S(2)}, u32[]{:S(2)}) collective-permute-start(f32[3,8,128]{2,1,0:T(8,128)S(1)} %pad_maximum_fusion), channel_id=1, source_target_pairs={{0,6},{2,4},{4,2},{6,0},{8,14},{10,12},{12,10},{14,8},{16,22},{18,... | collective-permute-start | bytes 36872 | tf_op jit(solution)/shard_map/ppermute | solution.py:612
  31.3 8.4 %collective-permute-start.10 = (f32[3,8,128]{2,1,0:T(8,128)S(1)}, f32[3,8,128]{2,1,0:T(8,128)S(1)}, u32[]{:S(2)}, u32[]{:S(2)}) collective-permute-start(f32[3,8,128]{2,1,0:T(8,128)S(1)} %get-tuple-element.52), channel_id=1, source_target_pairs={{0,16},{2,18},{4,20},{6,22},{8,24},{10,26},{12,28},{14,30},{16,0},... | collective-permute-start | bytes 36872 | tf_op jit(solution)/shard_map/ppermute | solution.py:612
  33.5 6.2 %collective-permute-start.11 = (f32[3,8,128]{2,1,0:T(8,128)S(1)}, f32[3,8,128]{2,1,0:T(8,128)S(1)}, u32[]{:S(2)}, u32[]{:S(2)}) collective-permute-start(f32[3,8,128]{2,1,0:T(8,128)S(1)} %get-tuple-element.52), channel_id=1, source_target_pairs={{0,24},{2,26},{4,28},{6,30},{8,16},{10,18},{12,20},{14,22},{16,8},... | collective-permute-start | bytes 36872 | tf_op jit(solution)/shard_map/ppermute | solution.py:612
  35.7 4.0 %collective-permute-start.9 = (f32[3,8,128]{2,1,0:T(8,128)S(1)}, f32[3,8,128]{2,1,0:T(8,128)S(1)}, u32[]{:S(2)}, u32[]{:S(2)}) collective-permute-start(f32[3,8,128]{2,1,0:T(8,128)S(1)} %get-tuple-element.52), channel_id=1, source_target_pairs={{0,8},{2,10},{4,12},{6,14},{8,0},{10,2},{12,4},{14,6},{16,24},{18,... | collective-permute-start | bytes 36872 | tf_op jit(solution)/shard_map/ppermute | solution.py:612
  35.8 12.2 %collective-permute-start.16 = (bf16[2,208,384]{2,1,0:T(8,128)(2,1)S(1)}, bf16[2,208,384]{2,1,0:T(8,128)(2,1)S(1)}, u32[]{:S(2)}, u32[]{:S(2)}) collective-permute-start(bf16[2,208,384]{2,1,0:T(8,128)(2,1)S(1)} %get-tuple-element.70.rest_5_.own_ref), channel_id=1, source_target_pairs={{0,8},{2,10},{4,12},{6,14},{8,0},{10,2},{12,4},{14,6},{16,24},{18,... | collective-permute-start | bytes 958472 | tf_op jit(solution)/shard_map/ppermute | solution.py:612
  37.7 10.2 %collective-permute-start.17 = (bf16[2,208,384]{2,1,0:T(8,128)(2,1)S(1)}, bf16[2,208,384]{2,1,0:T(8,128)(2,1)S(1)}, u32[]{:S(2)}, u32[]{:S(2)}) collective-permute-start(bf16[2,208,384]{2,1,0:T(8,128)(2,1)S(1)} %get-tuple-element.70.rest_5_.own_ref), channel_id=1, source_target_pairs={{8,16},{10,18},{12,20},{14,22},{16,8},{18,10},{20,12},{22,14},{9,1... | collective-permute-start | bytes 958472 | tf_op jit(solution)/shard_map/ppermute | solution.py:612
  39.8 3.8 %collective-permute-start.12 = (f32[3,8,128]{2,1,0:T(8,128)S(1)}, f32[3,8,128]{2,1,0:T(8,128)S(1)}, u32[]{:S(2)}, u32[]{:S(2)}) collective-permute-start(f32[3,8,128]{2,1,0:T(8,128)S(1)} %pad_maximum_fusion.2), channel_id=1, source_target_pairs={{0,4},{2,6},{4,0},{6,2},{8,12},{10,14},{12,8},{14,10},{16,20},{18,... | collective-permute-start | bytes 36872 | tf_op jit(solution)/shard_map/ppermute | solution.py:612
  41.0 4.7 %collective-permute-start.13 = (f32[3,8,128]{2,1,0:T(8,128)S(1)}, f32[3,8,128]{2,1,0:T(8,128)S(1)}, u32[]{:S(2)}, u32[]{:S(2)}) collective-permute-start(f32[3,8,128]{2,1,0:T(8,128)S(1)} %pad_maximum_fusion.2), channel_id=1, source_target_pairs={{0,6},{2,4},{4,2},{6,0},{8,14},{10,12},{12,10},{14,8},{16,22},{18,... | collective-permute-start | bytes 36872 | tf_op jit(solution)/shard_map/ppermute | solution.py:612
  42.7 5.3 %collective-permute-start.15 = (f32[3,8,128]{2,1,0:T(8,128)S(1)}, f32[3,8,128]{2,1,0:T(8,128)S(1)}, u32[]{:S(2)}, u32[]{:S(2)}) collective-permute-start(f32[3,8,128]{2,1,0:T(8,128)S(1)} %pad_maximum_fusion.2), channel_id=1, source_target_pairs={{0,2},{2,0},{4,6},{6,4},{8,10},{10,8},{12,14},{14,12},{16,18},{18,... | collective-permute-start | bytes 36872 | tf_op jit(solution)/shard_map/ppermute | solution.py:612
  45.7 13.2 %collective-permute-start.18 = (bf16[2,208,384]{2,1,0:T(8,128)(2,1)S(1)}, bf16[2,208,384]{2,1,0:T(8,128)(2,1)S(1)}, u32[]{:S(2)}, u32[]{:S(2)}) collective-permute-start(bf16[2,208,384]{2,1,0:T(8,128)(2,1)S(1)} %get-tuple-element.70.rest_5_.own_ref), channel_id=1, source_target_pairs={{0,4},{2,6},{4,0},{6,2},{8,12},{10,14},{12,8},{14,10},{16,20},{18,... | collective-permute-start | bytes 958472 | tf_op jit(solution)/shard_map/ppermute | solution.py:612
  46.5 7.0 %collective-permute-start.14 = (bf16[2,208,384]{2,1,0:T(8,128)(2,1)S(1)}, bf16[2,208,384]{2,1,0:T(8,128)(2,1)S(1)}, u32[]{:S(2)}, u32[]{:S(2)}) collective-permute-start(bf16[2,208,384]{2,1,0:T(8,128)(2,1)S(1)} %get-tuple-element.70.rest_5_.own_ref), channel_id=1, source_target_pairs={{0,2},{2,0},{4,6},{6,4},{8,10},{10,8},{12,14},{14,12},{16,18},{18,... | collective-permute-start | bytes 958472 | tf_op jit(solution)/shard_map/ppermute | solution.py:612
  48.0 8.9 %collective-permute-start.19 = (bf16[2,208,384]{2,1,0:T(8,128)(2,1)S(1)}, bf16[2,208,384]{2,1,0:T(8,128)(2,1)S(1)}, u32[]{:S(2)}, u32[]{:S(2)}) collective-permute-start(bf16[2,208,384]{2,1,0:T(8,128)(2,1)S(1)} %collective-permute-done.16.rest_7_), channel_id=1, source_target_pairs={{8,16},{10,18},{12,20},{14,22},{16,8},{18,10},{20,12},{22,14},{9,1... | collective-permute-start | bytes 958472 | tf_op jit(solution)/shard_map/ppermute | solution.py:612
  51.9 6.9 %collective-permute-start.20 = (bf16[2,208,384]{2,1,0:T(8,128)(2,1)S(1)}, bf16[2,208,384]{2,1,0:T(8,128)(2,1)S(1)}, u32[]{:S(2)}, u32[]{:S(2)}) collective-permute-start(bf16[2,208,384]{2,1,0:T(8,128)(2,1)S(1)} %collective-permute-done.17.rest_8_), channel_id=1, source_target_pairs={{8,0},{10,2},{12,4},{14,6},{16,24},{18,26},{20,28},{22,30},{9,1},{... | collective-permute-start | bytes 958472 | tf_op jit(solution)/shard_map/ppermute | solution.py:612
  58.9 8.9 %collective-permute-start.21 = (bf16[2,208,384]{2,1,0:T(8,128)(2,1)S(1)}, bf16[2,208,384]{2,1,0:T(8,128)(2,1)S(1)}, u32[]{:S(2)}, u32[]{:S(2)}) collective-permute-start(bf16[2,208,384]{2,1,0:T(8,128)(2,1)S(1)} %collective-permute-done.18.rest_6_), channel_id=1, source_target_pairs={{8,16},{10,18},{12,20},{14,22},{16,8},{18,10},{20,12},{22,14},{9,1... | collective-permute-start | bytes 958472 | tf_op jit(solution)/shard_map/ppermute | solution.py:612
  61.2 7.1 %collective-permute-start.22 = (bf16[2,208,384]{2,1,0:T(8,128)(2,1)S(1)}, bf16[2,208,384]{2,1,0:T(8,128)(2,1)S(1)}, u32[]{:S(2)}, u32[]{:S(2)}) collective-permute-start(bf16[2,208,384]{2,1,0:T(8,128)(2,1)S(1)} %collective-permute-done.18.rest_6_), channel_id=1, source_target_pairs={{0,8},{2,10},{4,12},{6,14},{8,0},{10,2},{12,4},{14,6},{16,24},{18,... | collective-permute-start | bytes 958472 | tf_op jit(solution)/shard_map/ppermute | solution.py:612
  62.3 7.0 %collective-permute-start.23 = (bf16[2,208,384]{2,1,0:T(8,128)(2,1)S(1)}, bf16[2,208,384]{2,1,0:T(8,128)(2,1)S(1)}, u32[]{:S(2)}, u32[]{:S(2)}) collective-permute-start(bf16[2,208,384]{2,1,0:T(8,128)(2,1)S(1)} %broadcast_select_fusion.rest_9_), channel_id=1, source_target_pairs={{0,4},{2,6},{4,0},{6,2},{8,12},{10,14},{12,8},{14,10},{16,20},{18,... | collective-permute-start | bytes 958472 | tf_op jit(solution)/shard_map/ppermute | solution.py:612
  72.0 7.8 %collective-permute-start.24 = (bf16[432,384]{1,0:T(8,128)(2,1)S(1)}, bf16[432,384]{1,0:T(8,128)(2,1)S(1)}, u32[]{:S(2)}, u32[]{:S(2)}) collective-permute-start(bf16[432,384]{1,0:T(8,128)(2,1)S(1)} %get-tuple-element.69), channel_id=1, source_target_pairs={{0,2},{2,0},{4,6},{6,4},{8,10},{10,8},{12,14},{14,12},{16,18},{18,... | collective-permute-start | bytes 995336 | tf_op jit(solution)/shard_map/ppermute | solution.py:799
  81.2 8.2 %collective-permute-start.25 = (bf16[1,104,384]{2,1,0:T(8,128)(2,1)S(1)}, bf16[1,104,384]{2,1,0:T(8,128)(2,1)S(1)}, u32[]{:S(2)}, u32[]{:S(2)}) collective-permute-start(bf16[1,104,384]{2,1,0:T(8,128)(2,1)S(1)} %get-tuple-element.75), channel_id=1, source_target_pairs={{2,4},{4,2},{6,8},{8,6},{10,12},{12,10},{14,16},{16,14},{18,20},{2... | collective-permute-start | bytes 239624 | tf_op jit(solution)/shard_map/ppermute | solution.py:829
  84.6 4.9 %collective-permute-start.26 = (bf16[1,104,384]{2,1,0:T(8,128)(2,1)S(1)}, bf16[1,104,384]{2,1,0:T(8,128)(2,1)S(1)}, u32[]{:S(2)}, u32[]{:S(2)}) collective-permute-start(bf16[1,104,384]{2,1,0:T(8,128)(2,1)S(1)} %get-tuple-element.76), channel_id=1, source_target_pairs={{0,2},{2,0},{4,6},{6,4},{8,10},{10,8},{12,14},{14,12},{16,18},{18,... | collective-permute-start | bytes 239624 | tf_op jit(solution)/shard_map/ppermute | solution.py:612
  (16 other events, 139.6 us)

commit v13 on v12

--- a/solution.py
+++ b/solution.py
@@ -612,8 +612,9 @@
     return lax.ppermute(array, "tile", moves)
 
 
-def merge_round(stats, tiles, masks, tied=(), after=None):
-    parts = [stats] + [exchange(stats, tiles, mask) for mask in masks]
+def merge_round(stats, tiles, masks, tied=(), after=None, among=None):
+    limits = among or {}
+    parts = [stats] + [exchange(stats, tiles, mask, limits.get(mask)) for mask in masks]
     free = ()
     if tied:
         *parts[2:], free = lax.optimization_barrier((*parts[2:], after))
@@ -706,8 +707,14 @@
         if backs
     ]
     rounds = merge_masks(tiles)
+    layered = tiles == 16 and video_cols.shape[0] == 2
+
+    def middle(t):
+        return t // 4 in (1, 2)
+
+    among = {12: middle} if layered else {}
     for index, masks in enumerate(reversed(rounds)):
-        stats = merge_round(stats, tiles, masks)
+        stats = merge_round(stats, tiles, masks, among=among)
         if index < len(held):
             stats, held[index] = lax.optimization_barrier((stats, held[index]))
     hidden, source = call(
@@ -744,11 +751,8 @@
 
     blocks = {0: own}
     neighbour = [(i, i ^ 1) for i in range(tiles)]
-    if tiles == 16 and video_cols.shape[0] == 2:
-        def middle(t):
-            return t // 4 in (1, 2)
-
-        stats = merge_round(stats, tiles, rounds[1])
+    if layered:
+        stats = merge_round(stats, tiles, rounds[1], among=among)
         blocks[2] = exchange(own, tiles, 4)
         blocks[6] = exchange(own, tiles, 12, middle)
         stats, blocks[2], blocks[6], own_xy = merge_round(

time: 92.5 us -> 94.1 us (1.017)
  the two profiles are of different devices: /device:TPU:8 before, /device:TPU:0 now
where the time goes in v13:
time: 94.1 us; the launch traced here: 93.6 us
  starting transfers between devices  41.7 us (44%)
  Pallas kernels  30.1 us (32%)
  waiting for transfers between devices  17.9 us (19%)
  other arithmetic  1.9 us (2%)
  local copies, waits for them, and re-layouts  1.48 us (2%)
    ppermute x23, starting transfers between devices, exchange(): return lax.ppermute(array, 'tile', moves)  37.7 us
    pallas_call x11, Pallas kernels, call(): pl.pallas_call(kernel, out_shape=out_shape, in_specs=[SMEM_SPEC] + [VMEM_...  26.1 us
    ppermute x23, waiting for transfers between devices, exchange(): return lax.ppermute(array, 'tile', moves)  17.9 us
    pallas_call x2, Pallas kernels, shards(): pl.pallas_call(functools.partial(hold_kernel, backs), out_shape=shape(3 *...  3.5 us
  transfers between devices with their start and end apart: 27, of which 10 were waited for; matrix products, arithmetic and copies ran while one was open for 1% of the time, Pallas kernels for 21%

profile of v13, /device:TPU:0, one launch (start us, length us, event | category | flops | bytes accessed | tf_op | source)
XLA Modules:
  0.0 93.6 jit_solution(4644994691386561155)
XLA Ops:
  1.6 5.7 %collective-permute-start.1 = (bf16[1,104,384]{2,1,0:T(8,128)(2,1)S(1)}, bf16[1,104,384]{2,1,0:T(8,128)(2,1)S(1)}, u32[]{:S(2)}, u32[]{:S(2)}) collective-permute-start(bf16[1,104,384]{2,1,0:T(8,128)(2,1)S(1)} %get-tuple-element.92), channel_id=1, source_target_pairs={{0,2},{2,0},{4,6},{6,4},{8,10},{10,8},{12,14},{14,12},{16,18},{18,... | collective-permute-start | bytes 239624 | tf_op jit(solution)/shard_map/ppermute | solution.py:612
  11.1 1.9 %collective-permute-start.2 = (f32[3,8,128]{2,1,0:T(8,128)S(1)}, f32[3,8,128]{2,1,0:T(8,128)S(1)}, u32[]{:S(2)}, u32[]{:S(2)}) collective-permute-start(f32[3,8,128]{2,1,0:T(8,128)S(1)} %first_stats.1), channel_id=1, source_target_pairs={{0,8},{2,10},{4,12},{6,14},{8,0},{10,2},{12,4},{14,6},{16,24},{18,... | collective-permute-start | bytes 36872 | tf_op jit(solution)/shard_map/ppermute | solution.py:612
  13.0 2.6 %collective-permute-start.3 = (f32[3,8,128]{2,1,0:T(8,128)S(1)}, f32[3,8,128]{2,1,0:T(8,128)S(1)}, u32[]{:S(2)}, u32[]{:S(2)}) collective-permute-start(f32[3,8,128]{2,1,0:T(8,128)S(1)} %first_stats.1), channel_id=1, source_target_pairs={{0,16},{2,18},{4,20},{6,22},{8,24},{10,26},{12,28},{14,30},{16,0},... | collective-permute-start | bytes 36872 | tf_op jit(solution)/shard_map/ppermute | solution.py:612
  16.2 1.8 %hold.2.held_ref = bf16[1152,1152]{1,0:T(8,128)(2,1)S(1)} custom-call(bf16[3,3,3,384,384]{4,3,2,1,0:T(8,128)(2,1)} %weight_ref.5), custom_call_target="tpu_custom_call" | custom-call | flops 1650000000 | tf_op jit(solution)/shard_map/hold/pallas_call | solution.py:696
  19.9 1.7 %collective-permute-start.7 = (f32[3,8,128]{2,1,0:T(8,128)S(1)}, f32[3,8,128]{2,1,0:T(8,128)S(1)}, u32[]{:S(2)}, u32[]{:S(2)}) collective-permute-start(f32[3,8,128]{2,1,0:T(8,128)S(1)} %pad_maximum_fusion), channel_id=1, source_target_pairs={{0,6},{2,4},{4,2},{6,0},{8,14},{10,12},{12,10},{14,8},{16,22},{18,... | collective-permute-start | bytes 36872 | tf_op jit(solution)/shard_map/ppermute | solution.py:612
  21.6 1.7 %hold.3.rest_4_ = bf16[1152,1152]{1,0:T(8,128)(2,1)S(1)} custom-call(bf16[3,3,3,384,384]{4,3,2,1,0:T(8,128)(2,1)} %weight_ref.5), custom_call_target="tpu_custom_call" | custom-call | flops 1650000000 | tf_op jit(solution)/shard_map/hold/pallas_call | solution.py:696
  27.1 2.2 %own_conv.1.rest_1_ = f32[448,1152]{1,0:T(8,128)S(1)} custom-call(s32[67]{0:T(128)S(1)} %pad_add_fusion.info_ref, bf16[6,112,384]{2,1,0:T(8,128)(2,1)S(1)} %get-tuple-element.48.hidden_ref, bf16[1152,1152]{1,0:T(8,128)(2,1)S(1)} %hold.2.held_ref), custom_call_target="tpu_custom_call" | custom-call | flops 2420000000 | tf_op jit(solution)/shard_map/own_conv/pallas_call | solution.py:671
  29.4 2.8 %conv.1 = (bf16[2,208,384]{2,1,0:T(8,128)(2,1)S(1)}, f32[3,8,128]{2,1,0:T(8,128)S(1)}) custom-call(s32[67]{0:T(128)S(1)} %pad_add_fusion.info_ref, bf16[6,112,384]{2,1,0:T(8,128)(2,1)S(1)} %collective-permute-done.8.rest_0_, f32[448,1152]{1,0:T(8,128)S(1)} %own_conv.1.rest_1_, bf16[4,104,384]{2,1,0:T(8,128)(2,1)S(1)} %get-tuple-element.50.rest_2_, ...), custom_call_target="tpu_custom_call" | custom-call | flops 3849999872 | tf_op jit(solution)/shard_map/conv/pallas_call | solution.py:671
  32.2 4.0 %collective-permute-start.10 = (f32[3,8,128]{2,1,0:T(8,128)S(1)}, f32[3,8,128]{2,1,0:T(8,128)S(1)}, u32[]{:S(2)}, u32[]{:S(2)}) collective-permute-start(f32[3,8,128]{2,1,0:T(8,128)S(1)} %get-tuple-element.52), channel_id=1, source_target_pairs={{0,16},{2,18},{4,20},{6,22},{8,24},{10,26},{12,28},{14,30},{16,0},... | collective-permute-start | bytes 36872 | tf_op jit(solution)/shard_map/ppermute | solution.py:612
  36.8 1.9 %collective-permute-start.9 = (f32[3,8,128]{2,1,0:T(8,128)S(1)}, f32[3,8,128]{2,1,0:T(8,128)S(1)}, u32[]{:S(2)}, u32[]{:S(2)}) collective-permute-start(f32[3,8,128]{2,1,0:T(8,128)S(1)} %get-tuple-element.52), channel_id=1, source_target_pairs={{0,8},{2,10},{4,12},{6,14},{8,0},{10,2},{12,4},{14,6},{16,24},{18,... | collective-permute-start | bytes 36872 | tf_op jit(solution)/shard_map/ppermute | solution.py:612
  40.8 1.4 %collective-permute-start.12 = (f32[3,8,128]{2,1,0:T(8,128)S(1)}, f32[3,8,128]{2,1,0:T(8,128)S(1)}, u32[]{:S(2)}, u32[]{:S(2)}) collective-permute-start(f32[3,8,128]{2,1,0:T(8,128)S(1)} %pad_maximum_fusion.2), channel_id=1, source_target_pairs={{0,4},{2,6},{4,0},{6,2},{8,12},{10,14},{12,8},{14,10},{16,20},{18,... | collective-permute-start | bytes 36872 | tf_op jit(solution)/shard_map/ppermute | solution.py:612
  44.5 2.4 %collective-permute-done.13 = f32[3,8,128]{2,1,0:T(8,128)S(1)} collective-permute-done((f32[3,8,128]{2,1,0:T(8,128)S(1)}, f32[3,8,128]{2,1,0:T(8,128)S(1)}, u32[]{:S(2)}, u32[]{:S(2)}) %collective-permute-start.13) | collective-permute-done | bytes 12320 | tf_op jit(solution)/shard_map/ppermute | solution.py:612
  50.6 4.0 %collective-permute-done.14.other_ref = bf16[2,208,384]{2,1,0:T(8,128)(2,1)S(1)} collective-permute-done((bf16[2,208,384]{2,1,0:T(8,128)(2,1)S(1)}, bf16[2,208,384]{2,1,0:T(8,128)(2,1)S(1)}, u32[]{:S(2)}, u32[]{:S(2)}) %collective-permute-start.14) | collective-permute-done | bytes 319520 | tf_op jit(solution)/shard_map/ppermute | solution.py:612
  54.5 1.3 %queries.1 = (bf16[416,384]{1,0:T(8,128)(2,1)S(1)}, f32[416,128]{1,0:T(8,128)S(1)}, f32[8,384]{1,0:T(8,128)S(1)}, f32[8,384]{1,0:T(8,128)S(1)}) custom-call(s32[67]{0:T(128)S(1)} %pad_add_fusion.info_ref, bf16[2,208,384]{2,1,0:T(8,128)(2,1)S(1)} %collective-permute-done.14.other_ref, f32[3,8,128]{2,1,0:T(8,128)S(1)} %pad_maximum_fusion.3.stats_ref, ...), custom_call_target="tpu_custom_call" | custom-call | flops 1650000000 | tf_op jit(solution)/shard_map/queries/pallas_call | solution.py:671
  55.9 5.0 %collective-permute-done.20 = bf16[2,208,384]{2,1,0:T(8,128)(2,1)S(1)} collective-permute-done((bf16[2,208,384]{2,1,0:T(8,128)(2,1)S(1)}, bf16[2,208,384]{2,1,0:T(8,128)(2,1)S(1)}, u32[]{:S(2)}, u32[]{:S(2)}) %collective-permute-start.20) | collective-permute-done | bytes 319520 | tf_op jit(solution)/shard_map/ppermute | solution.py:612
  61.8 2.5 %collective-permute-start.22 = (bf16[2,208,384]{2,1,0:T(8,128)(2,1)S(1)}, bf16[2,208,384]{2,1,0:T(8,128)(2,1)S(1)}, u32[]{:S(2)}, u32[]{:S(2)}) collective-permute-start(bf16[2,208,384]{2,1,0:T(8,128)(2,1)S(1)} %collective-permute-done.18.rest_6_), channel_id=1, source_target_pairs={{0,8},{2,10},{4,12},{6,14},{8,0},{10,2},{12,4},{14,6},{16,24},{18,... | collective-permute-start | bytes 958472 | tf_op jit(solution)/shard_map/ppermute | solution.py:612
  65.2 3.7 %attend_yours.2 = (bf16[2080,384]{1,0:T(8,128)(2,1)S(1)}, f32[416,128]{1,0:T(8,128)S(1)}, f32[416,128]{1,0:T(8,128)S(1)}, f32[416,384]{1,0:T(8,128)S(1)}) custom-call(s32[67]{0:T(128)S(1)} %pad_add_fusion.info_ref, f32[8,384]{1,0:T(8,128)S(1)} %get-tuple-element.58.rest_0_.means_ref, f32[8,384]{1,0:T(8,128)S(1)} %get-tuple-element.59.rest_1_.scales_ref, ...), custom_call_target="tpu_custom_call" | custom-call | flops 4950000128 | tf_op jit(solution)/shard_map/attend_yours/pallas_call | solution.py:671
  69.3 2.0 %collective-permute-done.23.rest_7_ = bf16[2,208,384]{2,1,0:T(8,128)(2,1)S(1)} collective-permute-done((bf16[2,208,384]{2,1,0:T(8,128)(2,1)S(1)}, bf16[2,208,384]{2,1,0:T(8,128)(2,1)S(1)}, u32[]{:S(2)}, u32[]{:S(2)}) %collective-permute-start.23) | collective-permute-done | bytes 319520 | tf_op jit(solution)/shard_map/ppermute | solution.py:612
  71.3 2.6 %attend_yours.3 = (bf16[1248,384]{1,0:T(8,128)(2,1)S(1)}, bf16[432,384]{1,0:T(8,128)(2,1)S(1)}) custom-call(s32[67]{0:T(128)S(1)} %pad_add_fusion.info_ref, f32[8,384]{1,0:T(8,128)S(1)} %get-tuple-element.58.rest_0_.means_ref, f32[8,384]{1,0:T(8,128)S(1)} %get-tuple-element.59.rest_1_.scales_ref, f32[1,384]{1,0:T(1,128)S(1)} %reshape.87.shift_ref.rest_2_, ...), custom_call_target="tpu_custom_call" | custom-call | flops 2969999872 | tf_op jit(solution)/shard_map/attend_yours/pallas_call | solution.py:671
  75.2 5.5 %attend_mine.1 = (f32[416,384]{1,0:T(8,128)S(1)}, f32[416,128]{1,0:T(8,128)S(1)}) custom-call(s32[67]{0:T(128)S(1)} %pad_add_fusion.info_ref, bf16[2,208,384]{2,1,0:T(8,128)(2,1)S(1)} %get-tuple-element.70.rest_5_.own_ref, f32[8,384]{1,0:T(8,128)S(1)} %get-tuple-element.58.rest_0_.means_ref, f32[8,384]{1,0:T(8,128)S(1)} %get-tuple-element.59.rest_1_.scales_ref, ...), custom_call_target="tpu_custom_call" | custom-call | flops 6600000000 | tf_op jit(solution)/shard_map/attend_mine/pallas_call | solution.py:671
  81.7 1.4 %finish.1 = (bf16[4,104,384]{2,1,0:T(8,128)(2,1)S(1)}, bf16[1,104,384]{2,1,0:T(8,128)(2,1)S(1)}, bf16[1,104,384]{2,1,0:T(8,128)(2,1)S(1)}) custom-call(s32[67]{0:T(128)S(1)} %pad_add_fusion.info_ref, f32[416,384]{1,0:T(8,128)S(1)} %get-tuple-element.73.mean_ref, f32[416,128]{1,0:T(8,128)S(1)} %get-tuple-element.74.level_ref, ...), custom_call_target="tpu_custom_call" | custom-call | flops 1540000000 | tf_op jit(solution)/shard_map/finish/pallas_call | solution.py:671
  83.8 4.6 %collective-permute-start.26 = (bf16[1,104,384]{2,1,0:T(8,128)(2,1)S(1)}, bf16[1,104,384]{2,1,0:T(8,128)(2,1)S(1)}, u32[]{:S(2)}, u32[]{:S(2)}) collective-permute-start(bf16[1,104,384]{2,1,0:T(8,128)(2,1)S(1)} %get-tuple-element.76), channel_id=1, source_target_pairs={{0,2},{2,0},{4,6},{6,4},{8,10},{10,8},{12,14},{14,12},{16,18},{18,... | collective-permute-start | bytes 239624 | tf_op jit(solution)/shard_map/ppermute | solution.py:612
  88.4 2.2 %upsample.1 = (bf16[6,192,208]{2,1,0:T(8,128)(2,1)S(1)}, f32[2,2,256,128]{3,2,1,0:T(8,128)S(1)}) custom-call(s32[67]{0:T(128)S(1)} %pad_add_fusion.info_ref, bf16[4,104,384]{2,1,0:T(8,128)(2,1)S(1)} %get-tuple-element.77.own_ref, bf16[2,2,2,192,768]{4,3,2,1,0:T(8,128)(2,1)S(1)} %fold.1.weight_ref, f32[1,256]{1,0:T(1,128)S(1)} %pad.4.bias_ref), custom_call_target="tpu_custom_call" | custom-call | flops 2200000000 | tf_op jit(solution)/shard_map/upsample/pallas_call | solution.py:671
  91.5 2.1 %close.1 = bf16[8,192,208]{2,1,0:T(8,128)(2,1)} custom-call(s32[67]{0:T(128)S(1)} %pad_add_fusion.info_ref, bf16[1,104,384]{2,1,0:T(8,128)(2,1)S(1)} %collective-permute-done.25.outer_ref, bf16[1,104,384]{2,1,0:T(8,128)(2,1)S(1)} %collective-permute-done.26.inner_ref, bf16[6,192,208]{2,1,0:T(8,128)(2,1)S(1)} %get-tuple-element.79.middle_ref, ...), custom_call_target="tpu_custom_call" | custom-call | flops 1100000000 | tf_op jit(solution)/shard_map/close/pallas_call | solution.py:671
  (93 shorter events, 26.1 us)
Async XLA Ops:
  0.9 9.3 %collective-permute-start = (bf16[1,104,384]{2,1,0:T(8,128)(2,1)S(1)}, bf16[1,104,384]{2,1,0:T(8,128)(2,1)S(1)}, u32[]{:S(2)}, u32[]{:S(2)}) collective-permute-start(bf16[1,104,384]{2,1,0:T(8,128)(2,1)S(1)} %get-tuple-element.93), channel_id=1, source_target_pairs={{2,4},{4,2},{6,8},{8,6},{10,12},{12,10},{14,16},{16,14},{18,20},{2... | collective-permute-start | bytes 239624 | tf_op jit(solution)/shard_map/ppermute | solution.py:689
  1.6 9.5 %collective-permute-start.1 = (bf16[1,104,384]{2,1,0:T(8,128)(2,1)S(1)}, bf16[1,104,384]{2,1,0:T(8,128)(2,1)S(1)}, u32[]{:S(2)}, u32[]{:S(2)}) collective-permute-start(bf16[1,104,384]{2,1,0:T(8,128)(2,1)S(1)} %get-tuple-element.92), channel_id=1, source_target_pairs={{0,2},{2,0},{4,6},{6,4},{8,10},{10,8},{12,14},{14,12},{16,18},{18,... | collective-permute-start | bytes 239624 | tf_op jit(solution)/shard_map/ppermute | solution.py:612
  11.1 6.9 %collective-permute-start.2 = (f32[3,8,128]{2,1,0:T(8,128)S(1)}, f32[3,8,128]{2,1,0:T(8,128)S(1)}, u32[]{:S(2)}, u32[]{:S(2)}) collective-permute-start(f32[3,8,128]{2,1,0:T(8,128)S(1)} %first_stats.1), channel_id=1, source_target_pairs={{0,8},{2,10},{4,12},{6,14},{8,0},{10,2},{12,4},{14,6},{16,24},{18,... | collective-permute-start | bytes 36872 | tf_op jit(solution)/shard_map/ppermute | solution.py:612
  13.0 5.0 %collective-permute-start.3 = (f32[3,8,128]{2,1,0:T(8,128)S(1)}, f32[3,8,128]{2,1,0:T(8,128)S(1)}, u32[]{:S(2)}, u32[]{:S(2)}) collective-permute-start(f32[3,8,128]{2,1,0:T(8,128)S(1)} %first_stats.1), channel_id=1, source_target_pairs={{0,16},{2,18},{4,20},{6,22},{8,24},{10,26},{12,28},{14,30},{16,0},... | collective-permute-start | bytes 36872 | tf_op jit(solution)/shard_map/ppermute | solution.py:612
  18.1 5.4 %collective-permute-start.5 = (f32[3,8,128]{2,1,0:T(8,128)S(1)}, f32[3,8,128]{2,1,0:T(8,128)S(1)}, u32[]{:S(2)}, u32[]{:S(2)}) collective-permute-start(f32[3,8,128]{2,1,0:T(8,128)S(1)} %pad_maximum_fusion), channel_id=1, source_target_pairs={{0,2},{2,0},{4,6},{6,4},{8,10},{10,8},{12,14},{14,12},{16,18},{18,... | collective-permute-start | bytes 36872 | tf_op jit(solution)/shard_map/ppermute | solution.py:612
  19.3 4.2 %collective-permute-start.6 = (f32[3,8,128]{2,1,0:T(8,128)S(1)}, f32[3,8,128]{2,1,0:T(8,128)S(1)}, u32[]{:S(2)}, u32[]{:S(2)}) collective-permute-start(f32[3,8,128]{2,1,0:T(8,128)S(1)} %pad_maximum_fusion), channel_id=1, source_target_pairs={{0,4},{2,6},{4,0},{6,2},{8,12},{10,14},{12,8},{14,10},{16,20},{18,... | collective-permute-start | bytes 36872 | tf_op jit(solution)/shard_map/ppermute | solution.py:612
  19.9 4.6 %collective-permute-start.7 = (f32[3,8,128]{2,1,0:T(8,128)S(1)}, f32[3,8,128]{2,1,0:T(8,128)S(1)}, u32[]{:S(2)}, u32[]{:S(2)}) collective-permute-start(f32[3,8,128]{2,1,0:T(8,128)S(1)} %pad_maximum_fusion), channel_id=1, source_target_pairs={{0,6},{2,4},{4,2},{6,0},{8,14},{10,12},{12,10},{14,8},{16,22},{18,... | collective-permute-start | bytes 36872 | tf_op jit(solution)/shard_map/ppermute | solution.py:612
  32.2 7.4 %collective-permute-start.10 = (f32[3,8,128]{2,1,0:T(8,128)S(1)}, f32[3,8,128]{2,1,0:T(8,128)S(1)}, u32[]{:S(2)}, u32[]{:S(2)}) collective-permute-start(f32[3,8,128]{2,1,0:T(8,128)S(1)} %get-tuple-element.52), channel_id=1, source_target_pairs={{0,16},{2,18},{4,20},{6,22},{8,24},{10,26},{12,28},{14,30},{16,0},... | collective-permute-start | bytes 36872 | tf_op jit(solution)/shard_map/ppermute | solution.py:612
  36.8 3.9 %collective-permute-start.9 = (f32[3,8,128]{2,1,0:T(8,128)S(1)}, f32[3,8,128]{2,1,0:T(8,128)S(1)}, u32[]{:S(2)}, u32[]{:S(2)}) collective-permute-start(f32[3,8,128]{2,1,0:T(8,128)S(1)} %get-tuple-element.52), channel_id=1, source_target_pairs={{0,8},{2,10},{4,12},{6,14},{8,0},{10,2},{12,4},{14,6},{16,24},{18,... | collective-permute-start | bytes 36872 | tf_op jit(solution)/shard_map/ppermute | solution.py:612
  38.7 9.8 %collective-permute-start.16 = (bf16[2,208,384]{2,1,0:T(8,128)(2,1)S(1)}, bf16[2,208,384]{2,1,0:T(8,128)(2,1)S(1)}, u32[]{:S(2)}, u32[]{:S(2)}) collective-permute-start(bf16[2,208,384]{2,1,0:T(8,128)(2,1)S(1)} %get-tuple-element.70.rest_5_.own_ref), channel_id=1, source_target_pairs={{0,8},{2,10},{4,12},{6,14},{8,0},{10,2},{12,4},{14,6},{16,24},{18,... | collective-permute-start | bytes 958472 | tf_op jit(solution)/shard_map/ppermute | solution.py:612
  38.9 9.6 %collective-permute-start.17 = (bf16[2,208,384]{2,1,0:T(8,128)(2,1)S(1)}, bf16[2,208,384]{2,1,0:T(8,128)(2,1)S(1)}, u32[]{:S(2)}, u32[]{:S(2)}) collective-permute-start(bf16[2,208,384]{2,1,0:T(8,128)(2,1)S(1)} %get-tuple-element.70.rest_5_.own_ref), channel_id=1, source_target_pairs={{8,16},{10,18},{12,20},{14,22},{16,8},{18,10},{20,12},{22,14},{9,1... | collective-permute-start | bytes 958472 | tf_op jit(solution)/shard_map/ppermute | solution.py:612
  40.8 3.8 %collective-permute-start.12 = (f32[3,8,128]{2,1,0:T(8,128)S(1)}, f32[3,8,128]{2,1,0:T(8,128)S(1)}, u32[]{:S(2)}, u32[]{:S(2)}) collective-permute-start(f32[3,8,128]{2,1,0:T(8,128)S(1)} %pad_maximum_fusion.2), channel_id=1, source_target_pairs={{0,4},{2,6},{4,0},{6,2},{8,12},{10,14},{12,8},{14,10},{16,20},{18,... | collective-permute-start | bytes 36872 | tf_op jit(solution)/shard_map/ppermute | solution.py:612
  42.2 4.7 %collective-permute-start.13 = (f32[3,8,128]{2,1,0:T(8,128)S(1)}, f32[3,8,128]{2,1,0:T(8,128)S(1)}, u32[]{:S(2)}, u32[]{:S(2)}) collective-permute-start(f32[3,8,128]{2,1,0:T(8,128)S(1)} %pad_maximum_fusion.2), channel_id=1, source_target_pairs={{0,6},{2,4},{4,2},{6,0},{8,14},{10,12},{12,10},{14,8},{16,22},{18,... | collective-permute-start | bytes 36872 | tf_op jit(solution)/shard_map/ppermute | solution.py:612
  43.2 5.3 %collective-permute-start.15 = (f32[3,8,128]{2,1,0:T(8,128)S(1)}, f32[3,8,128]{2,1,0:T(8,128)S(1)}, u32[]{:S(2)}, u32[]{:S(2)}) collective-permute-start(f32[3,8,128]{2,1,0:T(8,128)S(1)} %pad_maximum_fusion.2), channel_id=1, source_target_pairs={{0,2},{2,0},{4,6},{6,4},{8,10},{10,8},{12,14},{14,12},{16,18},{18,... | collective-permute-start | bytes 36872 | tf_op jit(solution)/shard_map/ppermute | solution.py:612
  46.9 14.0 %collective-permute-start.18 = (bf16[2,208,384]{2,1,0:T(8,128)(2,1)S(1)}, bf16[2,208,384]{2,1,0:T(8,128)(2,1)S(1)}, u32[]{:S(2)}, u32[]{:S(2)}) collective-permute-start(bf16[2,208,384]{2,1,0:T(8,128)(2,1)S(1)} %get-tuple-element.70.rest_5_.own_ref), channel_id=1, source_target_pairs={{0,4},{2,6},{4,0},{6,2},{8,12},{10,14},{12,8},{14,10},{16,20},{18,... | collective-permute-start | bytes 958472 | tf_op jit(solution)/shard_map/ppermute | solution.py:612
  47.6 7.0 %collective-permute-start.14 = (bf16[2,208,384]{2,1,0:T(8,128)(2,1)S(1)}, bf16[2,208,384]{2,1,0:T(8,128)(2,1)S(1)}, u32[]{:S(2)}, u32[]{:S(2)}) collective-permute-start(bf16[2,208,384]{2,1,0:T(8,128)(2,1)S(1)} %get-tuple-element.70.rest_5_.own_ref), channel_id=1, source_target_pairs={{0,2},{2,0},{4,6},{6,4},{8,10},{10,8},{12,14},{14,12},{16,18},{18,... | collective-permute-start | bytes 958472 | tf_op jit(solution)/shard_map/ppermute | solution.py:612
  48.5 7.4 %collective-permute-start.19 = (bf16[2,208,384]{2,1,0:T(8,128)(2,1)S(1)}, bf16[2,208,384]{2,1,0:T(8,128)(2,1)S(1)}, u32[]{:S(2)}, u32[]{:S(2)}) collective-permute-start(bf16[2,208,384]{2,1,0:T(8,128)(2,1)S(1)} %collective-permute-done.16.rest_7_), channel_id=1, source_target_pairs={{8,16},{10,18},{12,20},{14,22},{16,8},{18,10},{20,12},{22,14},{9,1... | collective-permute-start | bytes 958472 | tf_op jit(solution)/shard_map/ppermute | solution.py:612
  49.2 11.6 %collective-permute-start.20 = (bf16[2,208,384]{2,1,0:T(8,128)(2,1)S(1)}, bf16[2,208,384]{2,1,0:T(8,128)(2,1)S(1)}, u32[]{:S(2)}, u32[]{:S(2)}) collective-permute-start(bf16[2,208,384]{2,1,0:T(8,128)(2,1)S(1)} %collective-permute-done.17.rest_8_), channel_id=1, source_target_pairs={{8,0},{10,2},{12,4},{14,6},{16,24},{18,26},{20,28},{22,30},{9,1},{... | collective-permute-start | bytes 958472 | tf_op jit(solution)/shard_map/ppermute | solution.py:612
  60.9 7.9 %collective-permute-start.21 = (bf16[2,208,384]{2,1,0:T(8,128)(2,1)S(1)}, bf16[2,208,384]{2,1,0:T(8,128)(2,1)S(1)}, u32[]{:S(2)}, u32[]{:S(2)}) collective-permute-start(bf16[2,208,384]{2,1,0:T(8,128)(2,1)S(1)} %collective-permute-done.18.rest_6_), channel_id=1, source_target_pairs={{8,16},{10,18},{12,20},{14,22},{16,8},{18,10},{20,12},{22,14},{9,1... | collective-permute-start | bytes 958472 | tf_op jit(solution)/shard_map/ppermute | solution.py:612
  61.8 7.5 %collective-permute-start.22 = (bf16[2,208,384]{2,1,0:T(8,128)(2,1)S(1)}, bf16[2,208,384]{2,1,0:T(8,128)(2,1)S(1)}, u32[]{:S(2)}, u32[]{:S(2)}) collective-permute-start(bf16[2,208,384]{2,1,0:T(8,128)(2,1)S(1)} %collective-permute-done.18.rest_6_), channel_id=1, source_target_pairs={{0,8},{2,10},{4,12},{6,14},{8,0},{10,2},{12,4},{14,6},{16,24},{18,... | collective-permute-start | bytes 958472 | tf_op jit(solution)/shard_map/ppermute | solution.py:612
  64.3 7.0 %collective-permute-start.23 = (bf16[2,208,384]{2,1,0:T(8,128)(2,1)S(1)}, bf16[2,208,384]{2,1,0:T(8,128)(2,1)S(1)}, u32[]{:S(2)}, u32[]{:S(2)}) collective-permute-start(bf16[2,208,384]{2,1,0:T(8,128)(2,1)S(1)} %broadcast_select_fusion.rest_9_), channel_id=1, source_target_pairs={{0,4},{2,6},{4,0},{6,2},{8,12},{10,14},{12,8},{14,10},{16,20},{18,... | collective-permute-start | bytes 958472 | tf_op jit(solution)/shard_map/ppermute | solution.py:612
  73.9 7.3 %collective-permute-start.24 = (bf16[432,384]{1,0:T(8,128)(2,1)S(1)}, bf16[432,384]{1,0:T(8,128)(2,1)S(1)}, u32[]{:S(2)}, u32[]{:S(2)}) collective-permute-start(bf16[432,384]{1,0:T(8,128)(2,1)S(1)} %get-tuple-element.69), channel_id=1, source_target_pairs={{0,2},{2,0},{4,6},{6,4},{8,10},{10,8},{12,14},{14,12},{16,18},{18,... | collective-permute-start | bytes 995336 | tf_op jit(solution)/shard_map/ppermute | solution.py:803
  83.1 7.5 %collective-permute-start.25 = (bf16[1,104,384]{2,1,0:T(8,128)(2,1)S(1)}, bf16[1,104,384]{2,1,0:T(8,128)(2,1)S(1)}, u32[]{:S(2)}, u32[]{:S(2)}) collective-permute-start(bf16[1,104,384]{2,1,0:T(8,128)(2,1)S(1)} %get-tuple-element.75), channel_id=1, source_target_pairs={{2,4},{4,2},{6,8},{8,6},{10,12},{12,10},{14,16},{16,14},{18,20},{2... | collective-permute-start | bytes 239624 | tf_op jit(solution)/shard_map/ppermute | solution.py:833
  83.8 7.8 %collective-permute-start.26 = (bf16[1,104,384]{2,1,0:T(8,128)(2,1)S(1)}, bf16[1,104,384]{2,1,0:T(8,128)(2,1)S(1)}, u32[]{:S(2)}, u32[]{:S(2)}) collective-permute-start(bf16[1,104,384]{2,1,0:T(8,128)(2,1)S(1)} %get-tuple-element.76), channel_id=1, source_target_pairs={{0,2},{2,0},{4,6},{6,4},{8,10},{10,8},{12,14},{14,12},{16,18},{18,... | collective-permute-start | bytes 239624 | tf_op jit(solution)/shard_map/ppermute | solution.py:612
  (16 other events, 136.9 us)

commit v14 on v13

--- a/solution.py
+++ b/solution.py
@@ -714,7 +714,7 @@
 
     among = {12: middle} if layered else {}
     for index, masks in enumerate(reversed(rounds)):
-        stats = merge_round(stats, tiles, masks, among=among)
+        stats = merge_round(stats, tiles, masks)
         if index < len(held):
             stats, held[index] = lax.optimization_barrier((stats, held[index]))
     hidden, source = call(

time: 94.1 us -> 94.5 us (level)
  the two profiles are of different devices: /device:TPU:0 before, /device:TPU:8 now
where the time goes in v14:
time: 94.5 us; the launch traced here: 93.5 us
  starting transfers between devices  42.8 us (45%)
  Pallas kernels  30.1 us (32%)
  waiting for transfers between devices  17.1 us (18%)
  other arithmetic  1.9 us (2%)
  local copies, waits for them, and re-layouts  1.08 us (1%)
    ppermute x23, starting transfers between devices, exchange(): return lax.ppermute(array, 'tile', moves)  33.8 us
    pallas_call x11, Pallas kernels, call(): pl.pallas_call(kernel, out_shape=out_shape, in_specs=[SMEM_SPEC] + [VMEM_...  26.1 us
    ppermute x23, waiting for transfers between devices, exchange(): return lax.ppermute(array, 'tile', moves)  12.8 us
    ppermute x1, starting transfers between devices, shards(): lax.ppermute(jnp.where(odd, source[row_count - 1:], source[:1]), 'tile',...  4.24 us
    pallas_call x2, Pallas kernels, shards(): pl.pallas_call(functools.partial(hold_kernel, backs), out_shape=shape(3 *...  3.5 us
    ppermute x1, starting transfers between devices, shards(): outer = lax.ppermute(outer, 'tile', outer_moves)  3.34 us
    ppermute x1, waiting for transfers between devices, shards(): outer = lax.ppermute(outer, 'tile', outer_moves)  2.32 us
  transfers between devices with their start and end apart: 27, of which 14 were waited for; matrix products, arithmetic and copies ran while one was open for 1% of the time, Pallas kernels for 21%

profile of v14, /device:TPU:8, one launch (start us, length us, event | category | flops | bytes accessed | tf_op | source)
XLA Modules:
  0.0 93.5 jit_solution(1994832388867144859)
XLA Ops:
  0.9 4.2 %collective-permute-start = (bf16[1,104,384]{2,1,0:T(8,128)(2,1)S(1)}, bf16[1,104,384]{2,1,0:T(8,128)(2,1)S(1)}, u32[]{:S(2)}, u32[]{:S(2)}) collective-permute-start(bf16[1,104,384]{2,1,0:T(8,128)(2,1)S(1)} %get-tuple-element.93), channel_id=1, source_target_pairs={{2,4},{4,2},{6,8},{8,6},{10,12},{12,10},{14,16},{16,14},{18,20},{2... | collective-permute-start | bytes 239624 | tf_op jit(solution)/shard_map/ppermute | solution.py:689
  10.1 2.9 %collective-permute-start.3 = (f32[3,8,128]{2,1,0:T(8,128)S(1)}, f32[3,8,128]{2,1,0:T(8,128)S(1)}, u32[]{:S(2)}, u32[]{:S(2)}) collective-permute-start(f32[3,8,128]{2,1,0:T(8,128)S(1)} %first_stats.1), channel_id=1, source_target_pairs={{0,16},{2,18},{4,20},{6,22},{8,24},{10,26},{12,28},{14,30},{16,0},... | collective-permute-start | bytes 36872 | tf_op jit(solution)/shard_map/ppermute | solution.py:612
  13.4 1.7 %hold.2.held_ref = bf16[1152,1152]{1,0:T(8,128)(2,1)S(1)} custom-call(bf16[3,3,3,384,384]{4,3,2,1,0:T(8,128)(2,1)} %weight_ref.5), custom_call_target="tpu_custom_call" | custom-call | flops 1650000000 | tf_op jit(solution)/shard_map/hold/pallas_call | solution.py:696
  20.3 1.7 %hold.3.rest_4_ = bf16[1152,1152]{1,0:T(8,128)(2,1)S(1)} custom-call(bf16[3,3,3,384,384]{4,3,2,1,0:T(8,128)(2,1)} %weight_ref.5), custom_call_target="tpu_custom_call" | custom-call | flops 1650000000 | tf_op jit(solution)/shard_map/hold/pallas_call | solution.py:696
  26.2 2.2 %own_conv.1.rest_1_ = f32[448,1152]{1,0:T(8,128)S(1)} custom-call(s32[67]{0:T(128)S(1)} %pad_add_fusion.info_ref, bf16[6,112,384]{2,1,0:T(8,128)(2,1)S(1)} %get-tuple-element.48.hidden_ref, bf16[1152,1152]{1,0:T(8,128)(2,1)S(1)} %hold.2.held_ref), custom_call_target="tpu_custom_call" | custom-call | flops 2420000000 | tf_op jit(solution)/shard_map/own_conv/pallas_call | solution.py:671
  28.5 2.8 %conv.1 = (bf16[2,208,384]{2,1,0:T(8,128)(2,1)S(1)}, f32[3,8,128]{2,1,0:T(8,128)S(1)}) custom-call(s32[67]{0:T(128)S(1)} %pad_add_fusion.info_ref, bf16[6,112,384]{2,1,0:T(8,128)(2,1)S(1)} %collective-permute-done.8.rest_0_, f32[448,1152]{1,0:T(8,128)S(1)} %own_conv.1.rest_1_, bf16[4,104,384]{2,1,0:T(8,128)(2,1)S(1)} %get-tuple-element.50.rest_2_, ...), custom_call_target="tpu_custom_call" | custom-call | flops 3849999872 | tf_op jit(solution)/shard_map/conv/pallas_call | solution.py:671
  31.3 2.2 %collective-permute-start.10 = (f32[3,8,128]{2,1,0:T(8,128)S(1)}, f32[3,8,128]{2,1,0:T(8,128)S(1)}, u32[]{:S(2)}, u32[]{:S(2)}) collective-permute-start(f32[3,8,128]{2,1,0:T(8,128)S(1)} %get-tuple-element.52), channel_id=1, source_target_pairs={{0,16},{2,18},{4,20},{6,22},{8,24},{10,26},{12,28},{14,30},{16,0},... | collective-permute-start | bytes 36872 | tf_op jit(solution)/shard_map/ppermute | solution.py:612
  33.5 4.1 %collective-permute-start.11 = (f32[3,8,128]{2,1,0:T(8,128)S(1)}, f32[3,8,128]{2,1,0:T(8,128)S(1)}, u32[]{:S(2)}, u32[]{:S(2)}) collective-permute-start(f32[3,8,128]{2,1,0:T(8,128)S(1)} %get-tuple-element.52), channel_id=1, source_target_pairs={{8,16},{10,18},{12,20},{14,22},{16,8},{18,10},{20,12},{22,14},{9,1... | collective-permute-start | bytes 36872 | tf_op jit(solution)/shard_map/ppermute | solution.py:612
  37.7 2.0 %collective-permute-start.16 = (bf16[2,208,384]{2,1,0:T(8,128)(2,1)S(1)}, bf16[2,208,384]{2,1,0:T(8,128)(2,1)S(1)}, u32[]{:S(2)}, u32[]{:S(2)}) collective-permute-start(bf16[2,208,384]{2,1,0:T(8,128)(2,1)S(1)} %get-tuple-element.70.rest_5_.own_ref), channel_id=1, source_target_pairs={{0,8},{2,10},{4,12},{6,14},{8,0},{10,2},{12,4},{14,6},{16,24},{18,... | collective-permute-start | bytes 958472 | tf_op jit(solution)/shard_map/ppermute | solution.py:612
  39.7 1.9 %collective-permute-start.17 = (bf16[2,208,384]{2,1,0:T(8,128)(2,1)S(1)}, bf16[2,208,384]{2,1,0:T(8,128)(2,1)S(1)}, u32[]{:S(2)}, u32[]{:S(2)}) collective-permute-start(bf16[2,208,384]{2,1,0:T(8,128)(2,1)S(1)} %get-tuple-element.70.rest_5_.own_ref), channel_id=1, source_target_pairs={{8,16},{10,18},{12,20},{14,22},{16,8},{18,10},{20,12},{22,14},{9,1... | collective-permute-start | bytes 958472 | tf_op jit(solution)/shard_map/ppermute | solution.py:612
  43.0 1.7 %collective-permute-start.13 = (f32[3,8,128]{2,1,0:T(8,128)S(1)}, f32[3,8,128]{2,1,0:T(8,128)S(1)}, u32[]{:S(2)}, u32[]{:S(2)}) collective-permute-start(f32[3,8,128]{2,1,0:T(8,128)S(1)} %pad_maximum_fusion.2), channel_id=1, source_target_pairs={{0,6},{2,4},{4,2},{6,0},{8,14},{10,12},{12,10},{14,8},{16,22},{18,... | collective-permute-start | bytes 36872 | tf_op jit(solution)/shard_map/ppermute | solution.py:612
  45.5 2.2 %collective-permute-done.13 = f32[3,8,128]{2,1,0:T(8,128)S(1)} collective-permute-done((f32[3,8,128]{2,1,0:T(8,128)S(1)}, f32[3,8,128]{2,1,0:T(8,128)S(1)}, u32[]{:S(2)}, u32[]{:S(2)}) %collective-permute-start.13) | collective-permute-done | bytes 12320 | tf_op jit(solution)/shard_map/ppermute | solution.py:612
  50.0 3.9 %collective-permute-start.19 = (bf16[2,208,384]{2,1,0:T(8,128)(2,1)S(1)}, bf16[2,208,384]{2,1,0:T(8,128)(2,1)S(1)}, u32[]{:S(2)}, u32[]{:S(2)}) collective-permute-start(bf16[2,208,384]{2,1,0:T(8,128)(2,1)S(1)} %collective-permute-done.16.rest_7_), channel_id=1, source_target_pairs={{8,16},{10,18},{12,20},{14,22},{16,8},{18,10},{20,12},{22,14},{9,1... | collective-permute-start | bytes 958472 | tf_op jit(solution)/shard_map/ppermute | solution.py:612
  56.8 2.0 %collective-permute-done.19 = bf16[2,208,384]{2,1,0:T(8,128)(2,1)S(1)} collective-permute-done((bf16[2,208,384]{2,1,0:T(8,128)(2,1)S(1)}, bf16[2,208,384]{2,1,0:T(8,128)(2,1)S(1)}, u32[]{:S(2)}, u32[]{:S(2)}) %collective-permute-start.19) | collective-permute-done | bytes 319520 | tf_op jit(solution)/shard_map/ppermute | solution.py:612
  58.8 2.0 %collective-permute-done.20 = bf16[2,208,384]{2,1,0:T(8,128)(2,1)S(1)} collective-permute-done((bf16[2,208,384]{2,1,0:T(8,128)(2,1)S(1)}, bf16[2,208,384]{2,1,0:T(8,128)(2,1)S(1)}, u32[]{:S(2)}, u32[]{:S(2)}) %collective-permute-start.20) | collective-permute-done | bytes 319520 | tf_op jit(solution)/shard_map/ppermute | solution.py:612
  60.9 2.2 %collective-permute-start.21 = (bf16[2,208,384]{2,1,0:T(8,128)(2,1)S(1)}, bf16[2,208,384]{2,1,0:T(8,128)(2,1)S(1)}, u32[]{:S(2)}, u32[]{:S(2)}) collective-permute-start(bf16[2,208,384]{2,1,0:T(8,128)(2,1)S(1)} %collective-permute-done.18.rest_6_), channel_id=1, source_target_pairs={{8,16},{10,18},{12,20},{14,22},{16,8},{18,10},{20,12},{22,14},{9,1... | collective-permute-start | bytes 958472 | tf_op jit(solution)/shard_map/ppermute | solution.py:612
  65.2 3.6 %attend_yours.2 = (bf16[2080,384]{1,0:T(8,128)(2,1)S(1)}, f32[416,128]{1,0:T(8,128)S(1)}, f32[416,128]{1,0:T(8,128)S(1)}, f32[416,384]{1,0:T(8,128)S(1)}) custom-call(s32[67]{0:T(128)S(1)} %pad_add_fusion.info_ref, f32[8,384]{1,0:T(8,128)S(1)} %get-tuple-element.58.rest_0_.means_ref, f32[8,384]{1,0:T(8,128)S(1)} %get-tuple-element.59.rest_1_.scales_ref, ...), custom_call_target="tpu_custom_call" | custom-call | flops 4950000128 | tf_op jit(solution)/shard_map/attend_yours/pallas_call | solution.py:671
  71.3 2.6 %attend_yours.3 = (bf16[1248,384]{1,0:T(8,128)(2,1)S(1)}, bf16[432,384]{1,0:T(8,128)(2,1)S(1)}) custom-call(s32[67]{0:T(128)S(1)} %pad_add_fusion.info_ref, f32[8,384]{1,0:T(8,128)S(1)} %get-tuple-element.58.rest_0_.means_ref, f32[8,384]{1,0:T(8,128)S(1)} %get-tuple-element.59.rest_1_.scales_ref, f32[1,384]{1,0:T(1,128)S(1)} %reshape.87.shift_ref.rest_2_, ...), custom_call_target="tpu_custom_call" | custom-call | flops 2969999872 | tf_op jit(solution)/shard_map/attend_yours/pallas_call | solution.py:671
  74.0 5.5 %attend_mine.1 = (f32[416,384]{1,0:T(8,128)S(1)}, f32[416,128]{1,0:T(8,128)S(1)}) custom-call(s32[67]{0:T(128)S(1)} %pad_add_fusion.info_ref, bf16[2,208,384]{2,1,0:T(8,128)(2,1)S(1)} %get-tuple-element.70.rest_5_.own_ref, f32[8,384]{1,0:T(8,128)S(1)} %get-tuple-element.58.rest_0_.means_ref, f32[8,384]{1,0:T(8,128)S(1)} %get-tuple-element.59.rest_1_.scales_ref, ...), custom_call_target="tpu_custom_call" | custom-call | flops 6600000000 | tf_op jit(solution)/shard_map/attend_mine/pallas_call | solution.py:671
  80.1 1.7 %collective-permute-done.24.received_ref = bf16[432,384]{1,0:T(8,128)(2,1)S(1)} collective-permute-done((bf16[432,384]{1,0:T(8,128)(2,1)S(1)}, bf16[432,384]{1,0:T(8,128)(2,1)S(1)}, u32[]{:S(2)}, u32[]{:S(2)}) %collective-permute-start.24) | collective-permute-done | bytes 331808 | tf_op jit(solution)/shard_map/ppermute | solution.py:803
  83.2 3.3 %collective-permute-start.25 = (bf16[1,104,384]{2,1,0:T(8,128)(2,1)S(1)}, bf16[1,104,384]{2,1,0:T(8,128)(2,1)S(1)}, u32[]{:S(2)}, u32[]{:S(2)}) collective-permute-start(bf16[1,104,384]{2,1,0:T(8,128)(2,1)S(1)} %get-tuple-element.75), channel_id=1, source_target_pairs={{2,4},{4,2},{6,8},{8,6},{10,12},{12,10},{14,16},{16,14},{18,20},{2... | collective-permute-start | bytes 239624 | tf_op jit(solution)/shard_map/ppermute | solution.py:833
  86.9 2.2 %upsample.1 = (bf16[6,192,208]{2,1,0:T(8,128)(2,1)S(1)}, f32[2,2,256,128]{3,2,1,0:T(8,128)S(1)}) custom-call(s32[67]{0:T(128)S(1)} %pad_add_fusion.info_ref, bf16[4,104,384]{2,1,0:T(8,128)(2,1)S(1)} %get-tuple-element.77.own_ref, bf16[2,2,2,192,768]{4,3,2,1,0:T(8,128)(2,1)S(1)} %fold.1.weight_ref, f32[1,256]{1,0:T(1,128)S(1)} %pad.4.bias_ref), custom_call_target="tpu_custom_call" | custom-call | flops 2200000000 | tf_op jit(solution)/shard_map/upsample/pallas_call | solution.py:671
  89.1 2.3 %collective-permute-done.25.outer_ref = bf16[1,104,384]{2,1,0:T(8,128)(2,1)S(1)} collective-permute-done((bf16[1,104,384]{2,1,0:T(8,128)(2,1)S(1)}, bf16[1,104,384]{2,1,0:T(8,128)(2,1)S(1)}, u32[]{:S(2)}, u32[]{:S(2)}) %collective-permute-start.25) | collective-permute-done | bytes 79904 | tf_op jit(solution)/shard_map/ppermute | solution.py:833
  91.4 2.1 %close.1 = bf16[8,192,208]{2,1,0:T(8,128)(2,1)} custom-call(s32[67]{0:T(128)S(1)} %pad_add_fusion.info_ref, bf16[1,104,384]{2,1,0:T(8,128)(2,1)S(1)} %collective-permute-done.25.outer_ref, bf16[1,104,384]{2,1,0:T(8,128)(2,1)S(1)} %collective-permute-done.26.inner_ref, bf16[6,192,208]{2,1,0:T(8,128)(2,1)S(1)} %get-tuple-element.79.middle_ref, ...), custom_call_target="tpu_custom_call" | custom-call | flops 1100000000 | tf_op jit(solution)/shard_map/close/pallas_call | solution.py:671
  (93 shorter events, 29.7 us)
Async XLA Ops:
  0.9 8.2 %collective-permute-start = (bf16[1,104,384]{2,1,0:T(8,128)(2,1)S(1)}, bf16[1,104,384]{2,1,0:T(8,128)(2,1)S(1)}, u32[]{:S(2)}, u32[]{:S(2)}) collective-permute-start(bf16[1,104,384]{2,1,0:T(8,128)(2,1)S(1)} %get-tuple-element.93), channel_id=1, source_target_pairs={{2,4},{4,2},{6,8},{8,6},{10,12},{12,10},{14,16},{16,14},{18,20},{2... | collective-permute-start | bytes 239624 | tf_op jit(solution)/shard_map/ppermute | solution.py:689
  5.2 4.7 %collective-permute-start.1 = (bf16[1,104,384]{2,1,0:T(8,128)(2,1)S(1)}, bf16[1,104,384]{2,1,0:T(8,128)(2,1)S(1)}, u32[]{:S(2)}, u32[]{:S(2)}) collective-permute-start(bf16[1,104,384]{2,1,0:T(8,128)(2,1)S(1)} %get-tuple-element.92), channel_id=1, source_target_pairs={{0,2},{2,0},{4,6},{6,4},{8,10},{10,8},{12,14},{14,12},{16,18},{18,... | collective-permute-start | bytes 239624 | tf_op jit(solution)/shard_map/ppermute | solution.py:612
  9.9 5.2 %collective-permute-start.2 = (f32[3,8,128]{2,1,0:T(8,128)S(1)}, f32[3,8,128]{2,1,0:T(8,128)S(1)}, u32[]{:S(2)}, u32[]{:S(2)}) collective-permute-start(f32[3,8,128]{2,1,0:T(8,128)S(1)} %first_stats.1), channel_id=1, source_target_pairs={{0,8},{2,10},{4,12},{6,14},{8,0},{10,2},{12,4},{14,6},{16,24},{18,... | collective-permute-start | bytes 36872 | tf_op jit(solution)/shard_map/ppermute | solution.py:612
  10.1 5.1 %collective-permute-start.3 = (f32[3,8,128]{2,1,0:T(8,128)S(1)}, f32[3,8,128]{2,1,0:T(8,128)S(1)}, u32[]{:S(2)}, u32[]{:S(2)}) collective-permute-start(f32[3,8,128]{2,1,0:T(8,128)S(1)} %first_stats.1), channel_id=1, source_target_pairs={{0,16},{2,18},{4,20},{6,22},{8,24},{10,26},{12,28},{14,30},{16,0},... | collective-permute-start | bytes 36872 | tf_op jit(solution)/shard_map/ppermute | solution.py:612
  16.7 5.4 %collective-permute-start.5 = (f32[3,8,128]{2,1,0:T(8,128)S(1)}, f32[3,8,128]{2,1,0:T(8,128)S(1)}, u32[]{:S(2)}, u32[]{:S(2)}) collective-permute-start(f32[3,8,128]{2,1,0:T(8,128)S(1)} %pad_maximum_fusion), channel_id=1, source_target_pairs={{0,2},{2,0},{4,6},{6,4},{8,10},{10,8},{12,14},{14,12},{16,18},{18,... | collective-permute-start | bytes 36872 | tf_op jit(solution)/shard_map/ppermute | solution.py:612
  19.0 4.6 %collective-permute-start.7 = (f32[3,8,128]{2,1,0:T(8,128)S(1)}, f32[3,8,128]{2,1,0:T(8,128)S(1)}, u32[]{:S(2)}, u32[]{:S(2)}) collective-permute-start(f32[3,8,128]{2,1,0:T(8,128)S(1)} %pad_maximum_fusion), channel_id=1, source_target_pairs={{0,6},{2,4},{4,2},{6,0},{8,14},{10,12},{12,10},{14,8},{16,22},{18,... | collective-permute-start | bytes 36872 | tf_op jit(solution)/shard_map/ppermute | solution.py:612
  31.3 10.3 %collective-permute-start.10 = (f32[3,8,128]{2,1,0:T(8,128)S(1)}, f32[3,8,128]{2,1,0:T(8,128)S(1)}, u32[]{:S(2)}, u32[]{:S(2)}) collective-permute-start(f32[3,8,128]{2,1,0:T(8,128)S(1)} %get-tuple-element.52), channel_id=1, source_target_pairs={{0,16},{2,18},{4,20},{6,22},{8,24},{10,26},{12,28},{14,30},{16,0},... | collective-permute-start | bytes 36872 | tf_op jit(solution)/shard_map/ppermute | solution.py:612
  33.5 8.1 %collective-permute-start.11 = (f32[3,8,128]{2,1,0:T(8,128)S(1)}, f32[3,8,128]{2,1,0:T(8,128)S(1)}, u32[]{:S(2)}, u32[]{:S(2)}) collective-permute-start(f32[3,8,128]{2,1,0:T(8,128)S(1)} %get-tuple-element.52), channel_id=1, source_target_pairs={{8,16},{10,18},{12,20},{14,22},{16,8},{18,10},{20,12},{22,14},{9,1... | collective-permute-start | bytes 36872 | tf_op jit(solution)/shard_map/ppermute | solution.py:612
  37.6 4.0 %collective-permute-start.9 = (f32[3,8,128]{2,1,0:T(8,128)S(1)}, f32[3,8,128]{2,1,0:T(8,128)S(1)}, u32[]{:S(2)}, u32[]{:S(2)}) collective-permute-start(f32[3,8,128]{2,1,0:T(8,128)S(1)} %get-tuple-element.52), channel_id=1, source_target_pairs={{0,8},{2,10},{4,12},{6,14},{8,0},{10,2},{12,4},{14,6},{16,24},{18,... | collective-permute-start | bytes 36872 | tf_op jit(solution)/shard_map/ppermute | solution.py:612
  37.7 12.3 %collective-permute-start.16 = (bf16[2,208,384]{2,1,0:T(8,128)(2,1)S(1)}, bf16[2,208,384]{2,1,0:T(8,128)(2,1)S(1)}, u32[]{:S(2)}, u32[]{:S(2)}) collective-permute-start(bf16[2,208,384]{2,1,0:T(8,128)(2,1)S(1)} %get-tuple-element.70.rest_5_.own_ref), channel_id=1, source_target_pairs={{0,8},{2,10},{4,12},{6,14},{8,0},{10,2},{12,4},{14,6},{16,24},{18,... | collective-permute-start | bytes 958472 | tf_op jit(solution)/shard_map/ppermute | solution.py:612
  39.7 10.2 %collective-permute-start.17 = (bf16[2,208,384]{2,1,0:T(8,128)(2,1)S(1)}, bf16[2,208,384]{2,1,0:T(8,128)(2,1)S(1)}, u32[]{:S(2)}, u32[]{:S(2)}) collective-permute-start(bf16[2,208,384]{2,1,0:T(8,128)(2,1)S(1)} %get-tuple-element.70.rest_5_.own_ref), channel_id=1, source_target_pairs={{8,16},{10,18},{12,20},{14,22},{16,8},{18,10},{20,12},{22,14},{9,1... | collective-permute-start | bytes 958472 | tf_op jit(solution)/shard_map/ppermute | solution.py:612
  41.7 3.8 %collective-permute-start.12 = (f32[3,8,128]{2,1,0:T(8,128)S(1)}, f32[3,8,128]{2,1,0:T(8,128)S(1)}, u32[]{:S(2)}, u32[]{:S(2)}) collective-permute-start(f32[3,8,128]{2,1,0:T(8,128)S(1)} %pad_maximum_fusion.2), channel_id=1, source_target_pairs={{0,4},{2,6},{4,0},{6,2},{8,12},{10,14},{12,8},{14,10},{16,20},{18,... | collective-permute-start | bytes 36872 | tf_op jit(solution)/shard_map/ppermute | solution.py:612
  43.0 4.7 %collective-permute-start.13 = (f32[3,8,128]{2,1,0:T(8,128)S(1)}, f32[3,8,128]{2,1,0:T(8,128)S(1)}, u32[]{:S(2)}, u32[]{:S(2)}) collective-permute-start(f32[3,8,128]{2,1,0:T(8,128)S(1)} %pad_maximum_fusion.2), channel_id=1, source_target_pairs={{0,6},{2,4},{4,2},{6,0},{8,14},{10,12},{12,10},{14,8},{16,22},{18,... | collective-permute-start | bytes 36872 | tf_op jit(solution)/shard_map/ppermute | solution.py:612
  44.7 5.3 %collective-permute-start.15 = (f32[3,8,128]{2,1,0:T(8,128)S(1)}, f32[3,8,128]{2,1,0:T(8,128)S(1)}, u32[]{:S(2)}, u32[]{:S(2)}) collective-permute-start(f32[3,8,128]{2,1,0:T(8,128)S(1)} %pad_maximum_fusion.2), channel_id=1, source_target_pairs={{0,2},{2,0},{4,6},{6,4},{8,10},{10,8},{12,14},{14,12},{16,18},{18,... | collective-permute-start | bytes 36872 | tf_op jit(solution)/shard_map/ppermute | solution.py:612
  47.7 13.2 %collective-permute-start.18 = (bf16[2,208,384]{2,1,0:T(8,128)(2,1)S(1)}, bf16[2,208,384]{2,1,0:T(8,128)(2,1)S(1)}, u32[]{:S(2)}, u32[]{:S(2)}) collective-permute-start(bf16[2,208,384]{2,1,0:T(8,128)(2,1)S(1)} %get-tuple-element.70.rest_5_.own_ref), channel_id=1, source_target_pairs={{0,4},{2,6},{4,0},{6,2},{8,12},{10,14},{12,8},{14,10},{16,20},{18,... | collective-permute-start | bytes 958472 | tf_op jit(solution)/shard_map/ppermute | solution.py:612
  48.5 7.0 %collective-permute-start.14 = (bf16[2,208,384]{2,1,0:T(8,128)(2,1)S(1)}, bf16[2,208,384]{2,1,0:T(8,128)(2,1)S(1)}, u32[]{:S(2)}, u32[]{:S(2)}) collective-permute-start(bf16[2,208,384]{2,1,0:T(8,128)(2,1)S(1)} %get-tuple-element.70.rest_5_.own_ref), channel_id=1, source_target_pairs={{0,2},{2,0},{4,6},{6,4},{8,10},{10,8},{12,14},{14,12},{16,18},{18,... | collective-permute-start | bytes 958472 | tf_op jit(solution)/shard_map/ppermute | solution.py:612
  50.0 8.9 %collective-permute-start.19 = (bf16[2,208,384]{2,1,0:T(8,128)(2,1)S(1)}, bf16[2,208,384]{2,1,0:T(8,128)(2,1)S(1)}, u32[]{:S(2)}, u32[]{:S(2)}) collective-permute-start(bf16[2,208,384]{2,1,0:T(8,128)(2,1)S(1)} %collective-permute-done.16.rest_7_), channel_id=1, source_target_pairs={{8,16},{10,18},{12,20},{14,22},{16,8},{18,10},{20,12},{22,14},{9,1... | collective-permute-start | bytes 958472 | tf_op jit(solution)/shard_map/ppermute | solution.py:612
  53.9 6.9 %collective-permute-start.20 = (bf16[2,208,384]{2,1,0:T(8,128)(2,1)S(1)}, bf16[2,208,384]{2,1,0:T(8,128)(2,1)S(1)}, u32[]{:S(2)}, u32[]{:S(2)}) collective-permute-start(bf16[2,208,384]{2,1,0:T(8,128)(2,1)S(1)} %collective-permute-done.17.rest_8_), channel_id=1, source_target_pairs={{8,0},{10,2},{12,4},{14,6},{16,24},{18,26},{20,28},{22,30},{9,1},{... | collective-permute-start | bytes 958472 | tf_op jit(solution)/shard_map/ppermute | solution.py:612
  60.9 8.9 %collective-permute-start.21 = (bf16[2,208,384]{2,1,0:T(8,128)(2,1)S(1)}, bf16[2,208,384]{2,1,0:T(8,128)(2,1)S(1)}, u32[]{:S(2)}, u32[]{:S(2)}) collective-permute-start(bf16[2,208,384]{2,1,0:T(8,128)(2,1)S(1)} %collective-permute-done.18.rest_6_), channel_id=1, source_target_pairs={{8,16},{10,18},{12,20},{14,22},{16,8},{18,10},{20,12},{22,14},{9,1... | collective-permute-start | bytes 958472 | tf_op jit(solution)/shard_map/ppermute | solution.py:612
  63.1 7.1 %collective-permute-start.22 = (bf16[2,208,384]{2,1,0:T(8,128)(2,1)S(1)}, bf16[2,208,384]{2,1,0:T(8,128)(2,1)S(1)}, u32[]{:S(2)}, u32[]{:S(2)}) collective-permute-start(bf16[2,208,384]{2,1,0:T(8,128)(2,1)S(1)} %collective-permute-done.18.rest_6_), channel_id=1, source_target_pairs={{0,8},{2,10},{4,12},{6,14},{8,0},{10,2},{12,4},{14,6},{16,24},{18,... | collective-permute-start | bytes 958472 | tf_op jit(solution)/shard_map/ppermute | solution.py:612
  64.3 7.0 %collective-permute-start.23 = (bf16[2,208,384]{2,1,0:T(8,128)(2,1)S(1)}, bf16[2,208,384]{2,1,0:T(8,128)(2,1)S(1)}, u32[]{:S(2)}, u32[]{:S(2)}) collective-permute-start(bf16[2,208,384]{2,1,0:T(8,128)(2,1)S(1)} %broadcast_select_fusion.rest_9_), channel_id=1, source_target_pairs={{0,4},{2,6},{4,0},{6,2},{8,12},{10,14},{12,8},{14,10},{16,20},{18,... | collective-permute-start | bytes 958472 | tf_op jit(solution)/shard_map/ppermute | solution.py:612
  73.9 7.8 %collective-permute-start.24 = (bf16[432,384]{1,0:T(8,128)(2,1)S(1)}, bf16[432,384]{1,0:T(8,128)(2,1)S(1)}, u32[]{:S(2)}, u32[]{:S(2)}) collective-permute-start(bf16[432,384]{1,0:T(8,128)(2,1)S(1)} %get-tuple-element.69), channel_id=1, source_target_pairs={{0,2},{2,0},{4,6},{6,4},{8,10},{10,8},{12,14},{14,12},{16,18},{18,... | collective-permute-start | bytes 995336 | tf_op jit(solution)/shard_map/ppermute | solution.py:803
  83.2 8.2 %collective-permute-start.25 = (bf16[1,104,384]{2,1,0:T(8,128)(2,1)S(1)}, bf16[1,104,384]{2,1,0:T(8,128)(2,1)S(1)}, u32[]{:S(2)}, u32[]{:S(2)}) collective-permute-start(bf16[1,104,384]{2,1,0:T(8,128)(2,1)S(1)} %get-tuple-element.75), channel_id=1, source_target_pairs={{2,4},{4,2},{6,8},{8,6},{10,12},{12,10},{14,16},{16,14},{18,20},{2... | collective-permute-start | bytes 239624 | tf_op jit(solution)/shard_map/ppermute | solution.py:833
  86.5 4.9 %collective-permute-start.26 = (bf16[1,104,384]{2,1,0:T(8,128)(2,1)S(1)}, bf16[1,104,384]{2,1,0:T(8,128)(2,1)S(1)}, u32[]{:S(2)}, u32[]{:S(2)}) collective-permute-start(bf16[1,104,384]{2,1,0:T(8,128)(2,1)S(1)} %get-tuple-element.76), channel_id=1, source_target_pairs={{0,2},{2,0},{4,6},{6,4},{8,10},{10,8},{12,14},{14,12},{16,18},{18,... | collective-permute-start | bytes 239624 | tf_op jit(solution)/shard_map/ppermute | solution.py:612
  (16 other events, 151.4 us)

commit v15 on v12

--- a/solution.py
+++ b/solution.py
@@ -756,7 +756,8 @@
         )
         inward = exchange(blocks[2], tiles, 12, middle)
         outward = exchange(blocks[6], tiles, 4, middle)
-        other = exchange(own_xy, tiles, 1)
+        own_x, stats = lax.optimization_barrier((own, stats))
+        other = exchange(own_x, tiles, 1)
         blocks[1] = exchange(own_xy, tiles, 2)
         blocks[4] = jnp.where((tile // 4 == 1) | (tile // 4 == 2), inward, outward)
         passed, blocks[4] = lax.optimization_barrier((blocks[1], blocks[4]))

time: 92.5 us -> 91.7 us (level)
  the two profiles are of different devices: /device:TPU:8 before, /device:TPU:0 now
where the time goes in v15:
time: 91.7 us; the launch traced here: 91.3 us
  starting transfers between devices  37.5 us (41%)
  Pallas kernels  30.1 us (33%)
  waiting for transfers between devices  19.8 us (22%)
  other arithmetic  1.89 us (2%)
  local copies, waits for them, and re-layouts  1.48 us (2%)
    ppermute x23, starting transfers between devices, exchange(): return lax.ppermute(array, 'tile', moves)  33.4 us
    pallas_call x11, Pallas kernels, call(): pl.pallas_call(kernel, out_shape=out_shape, in_specs=[SMEM_SPEC] + [VMEM_...  26.1 us
    ppermute x23, waiting for transfers between devices, exchange(): return lax.ppermute(array, 'tile', moves)  19.8 us
    pallas_call x2, Pallas kernels, shards(): pl.pallas_call(functools.partial(hold_kernel, backs), out_shape=shape(3 *...  3.5 us
  transfers between devices with their start and end apart: 27, of which 11 were waited for; matrix products, arithmetic and copies ran while one was open for 1% of the time, Pallas kernels for 22%

profile of v15, /device:TPU:0, one launch (start us, length us, event | category | flops | bytes accessed | tf_op | source)
XLA Modules:
  0.0 91.3 jit_solution(8013864364519549316)
XLA Ops:
  1.6 5.7 %collective-permute-start.1 = (bf16[1,104,384]{2,1,0:T(8,128)(2,1)S(1)}, bf16[1,104,384]{2,1,0:T(8,128)(2,1)S(1)}, u32[]{:S(2)}, u32[]{:S(2)}) collective-permute-start(bf16[1,104,384]{2,1,0:T(8,128)(2,1)S(1)} %get-tuple-element.96), channel_id=1, source_target_pairs={{0,2},{2,0},{4,6},{6,4},{8,10},{10,8},{12,14},{14,12},{16,18},{18,... | collective-permute-start | bytes 239624 | tf_op jit(solution)/shard_map/ppermute | solution.py:612
  11.1 1.9 %collective-permute-start.2 = (f32[3,8,128]{2,1,0:T(8,128)S(1)}, f32[3,8,128]{2,1,0:T(8,128)S(1)}, u32[]{:S(2)}, u32[]{:S(2)}) collective-permute-start(f32[3,8,128]{2,1,0:T(8,128)S(1)} %first_stats.1), channel_id=1, source_target_pairs={{0,8},{2,10},{4,12},{6,14},{8,0},{10,2},{12,4},{14,6},{16,24},{18,... | collective-permute-start | bytes 36872 | tf_op jit(solution)/shard_map/ppermute | solution.py:612
  13.0 2.6 %collective-permute-start.3 = (f32[3,8,128]{2,1,0:T(8,128)S(1)}, f32[3,8,128]{2,1,0:T(8,128)S(1)}, u32[]{:S(2)}, u32[]{:S(2)}) collective-permute-start(f32[3,8,128]{2,1,0:T(8,128)S(1)} %first_stats.1), channel_id=1, source_target_pairs={{0,16},{2,18},{4,20},{6,22},{8,24},{10,26},{12,28},{14,30},{16,0},... | collective-permute-start | bytes 36872 | tf_op jit(solution)/shard_map/ppermute | solution.py:612
  15.5 1.7 %hold.2.held_ref = bf16[1152,1152]{1,0:T(8,128)(2,1)S(1)} custom-call(bf16[3,3,3,384,384]{4,3,2,1,0:T(8,128)(2,1)} %weight_ref.5), custom_call_target="tpu_custom_call" | custom-call | flops 1650000000 | tf_op jit(solution)/shard_map/hold/pallas_call | solution.py:695
  17.5 3.5 %collective-permute-done.4 = f32[3,8,128]{2,1,0:T(8,128)S(1)} collective-permute-done((f32[3,8,128]{2,1,0:T(8,128)S(1)}, f32[3,8,128]{2,1,0:T(8,128)S(1)}, u32[]{:S(2)}, u32[]{:S(2)}) %collective-permute-start.4) | collective-permute-done | bytes 12320 | tf_op jit(solution)/shard_map/ppermute | solution.py:612
  22.9 1.8 %collective-permute-start.7 = (f32[3,8,128]{2,1,0:T(8,128)S(1)}, f32[3,8,128]{2,1,0:T(8,128)S(1)}, u32[]{:S(2)}, u32[]{:S(2)}) collective-permute-start(f32[3,8,128]{2,1,0:T(8,128)S(1)} %pad_maximum_fusion), channel_id=1, source_target_pairs={{0,6},{2,4},{4,2},{6,0},{8,14},{10,12},{12,10},{14,8},{16,22},{18,... | collective-permute-start | bytes 36872 | tf_op jit(solution)/shard_map/ppermute | solution.py:612
  24.7 1.7 %hold.3.rest_4_ = bf16[1152,1152]{1,0:T(8,128)(2,1)S(1)} custom-call(bf16[3,3,3,384,384]{4,3,2,1,0:T(8,128)(2,1)} %weight_ref.5), custom_call_target="tpu_custom_call" | custom-call | flops 1650000000 | tf_op jit(solution)/shard_map/hold/pallas_call | solution.py:695
  30.1 2.2 %own_conv.1.rest_1_ = f32[448,1152]{1,0:T(8,128)S(1)} custom-call(s32[67]{0:T(128)S(1)} %pad_add_fusion.info_ref, bf16[6,112,384]{2,1,0:T(8,128)(2,1)S(1)} %get-tuple-element.50.hidden_ref, bf16[1152,1152]{1,0:T(8,128)(2,1)S(1)} %hold.2.held_ref), custom_call_target="tpu_custom_call" | custom-call | flops 2420000000 | tf_op jit(solution)/shard_map/own_conv/pallas_call | solution.py:670
  32.3 2.8 %conv.1 = (bf16[2,208,384]{2,1,0:T(8,128)(2,1)S(1)}, f32[3,8,128]{2,1,0:T(8,128)S(1)}) custom-call(s32[67]{0:T(128)S(1)} %pad_add_fusion.info_ref, bf16[6,112,384]{2,1,0:T(8,128)(2,1)S(1)} %collective-permute-done.8.rest_0_, f32[448,1152]{1,0:T(8,128)S(1)} %own_conv.1.rest_1_, bf16[4,104,384]{2,1,0:T(8,128)(2,1)S(1)} %get-tuple-element.52.rest_2_, ...), custom_call_target="tpu_custom_call" | custom-call | flops 3849999872 | tf_op jit(solution)/shard_map/conv/pallas_call | solution.py:670
  35.3 1.5 %collective-permute-start.11 = (f32[3,8,128]{2,1,0:T(8,128)S(1)}, f32[3,8,128]{2,1,0:T(8,128)S(1)}, u32[]{:S(2)}, u32[]{:S(2)}) collective-permute-start(f32[3,8,128]{2,1,0:T(8,128)S(1)} %get-tuple-element.55), channel_id=1, source_target_pairs={{0,24},{2,26},{4,28},{6,30},{8,16},{10,18},{12,20},{14,22},{16,8},... | collective-permute-start | bytes 36872 | tf_op jit(solution)/shard_map/ppermute | solution.py:612
  36.8 2.0 %collective-permute-start.9 = (f32[3,8,128]{2,1,0:T(8,128)S(1)}, f32[3,8,128]{2,1,0:T(8,128)S(1)}, u32[]{:S(2)}, u32[]{:S(2)}) collective-permute-start(f32[3,8,128]{2,1,0:T(8,128)S(1)} %get-tuple-element.55), channel_id=1, source_target_pairs={{0,8},{2,10},{4,12},{6,14},{8,0},{10,2},{12,4},{14,6},{16,24},{18,... | collective-permute-start | bytes 36872 | tf_op jit(solution)/shard_map/ppermute | solution.py:612
  42.1 1.9 %collective-permute-start.16 = (f32[3,8,128]{2,1,0:T(8,128)S(1)}, f32[3,8,128]{2,1,0:T(8,128)S(1)}, u32[]{:S(2)}, u32[]{:S(2)}) collective-permute-start(f32[3,8,128]{2,1,0:T(8,128)S(1)} %pad_maximum_fusion.2), channel_id=1, source_target_pairs={{0,6},{2,4},{4,2},{6,0},{8,14},{10,12},{12,10},{14,8},{16,22},{18,... | collective-permute-start | bytes 36872 | tf_op jit(solution)/shard_map/ppermute | solution.py:612
  44.7 2.0 %collective-permute-done.16 = f32[3,8,128]{2,1,0:T(8,128)S(1)} collective-permute-done((f32[3,8,128]{2,1,0:T(8,128)S(1)}, f32[3,8,128]{2,1,0:T(8,128)S(1)}, u32[]{:S(2)}, u32[]{:S(2)}) %collective-permute-start.16) | collective-permute-done | bytes 12320 | tf_op jit(solution)/shard_map/ppermute | solution.py:612
  49.8 1.5 %collective-permute-start.17 = (bf16[2,208,384]{2,1,0:T(8,128)(2,1)S(1)}, bf16[2,208,384]{2,1,0:T(8,128)(2,1)S(1)}, u32[]{:S(2)}, u32[]{:S(2)}) collective-permute-start(bf16[2,208,384]{2,1,0:T(8,128)(2,1)S(1)} %get-tuple-element.74.rest_5_.own_ref), channel_id=1, source_target_pairs={{0,2},{2,0},{4,6},{6,4},{8,10},{10,8},{12,14},{14,12},{16,18},{18,... | collective-permute-start | bytes 958472 | tf_op jit(solution)/shard_map/ppermute | solution.py:612
  51.4 8.3 %collective-permute-done.20 = bf16[2,208,384]{2,1,0:T(8,128)(2,1)S(1)} collective-permute-done((bf16[2,208,384]{2,1,0:T(8,128)(2,1)S(1)}, bf16[2,208,384]{2,1,0:T(8,128)(2,1)S(1)}, u32[]{:S(2)}, u32[]{:S(2)}) %collective-permute-start.20) | collective-permute-done | bytes 319520 | tf_op jit(solution)/shard_map/ppermute | solution.py:612
  60.7 2.0 %collective-permute-start.22 = (bf16[2,208,384]{2,1,0:T(8,128)(2,1)S(1)}, bf16[2,208,384]{2,1,0:T(8,128)(2,1)S(1)}, u32[]{:S(2)}, u32[]{:S(2)}) collective-permute-start(bf16[2,208,384]{2,1,0:T(8,128)(2,1)S(1)} %collective-permute-done.18.rest_6_), channel_id=1, source_target_pairs={{0,8},{2,10},{4,12},{6,14},{8,0},{10,2},{12,4},{14,6},{16,24},{18,... | collective-permute-start | bytes 958472 | tf_op jit(solution)/shard_map/ppermute | solution.py:612
  64.8 3.6 %attend_yours.2 = (bf16[2080,384]{1,0:T(8,128)(2,1)S(1)}, f32[416,128]{1,0:T(8,128)S(1)}, f32[416,128]{1,0:T(8,128)S(1)}, f32[416,384]{1,0:T(8,128)S(1)}) custom-call(s32[67]{0:T(128)S(1)} %pad_add_fusion.info_ref, f32[8,384]{1,0:T(8,128)S(1)} %get-tuple-element.61.rest_0_.means_ref, f32[8,384]{1,0:T(8,128)S(1)} %get-tuple-element.62.rest_1_.scales_ref, ...), custom_call_target="tpu_custom_call" | custom-call | flops 4950000128 | tf_op jit(solution)/shard_map/attend_yours/pallas_call | solution.py:670
  69.7 2.6 %attend_yours.3 = (bf16[1248,384]{1,0:T(8,128)(2,1)S(1)}, bf16[432,384]{1,0:T(8,128)(2,1)S(1)}) custom-call(s32[67]{0:T(128)S(1)} %pad_add_fusion.info_ref, f32[8,384]{1,0:T(8,128)S(1)} %get-tuple-element.61.rest_0_.means_ref, f32[8,384]{1,0:T(8,128)S(1)} %get-tuple-element.62.rest_1_.scales_ref, f32[1,384]{1,0:T(1,128)S(1)} %reshape.87.shift_ref.rest_2_, ...), custom_call_target="tpu_custom_call" | custom-call | flops 2969999872 | tf_op jit(solution)/shard_map/attend_yours/pallas_call | solution.py:670
  72.3 1.5 %collective-permute-start.24 = (bf16[432,384]{1,0:T(8,128)(2,1)S(1)}, bf16[432,384]{1,0:T(8,128)(2,1)S(1)}, u32[]{:S(2)}, u32[]{:S(2)}) collective-permute-start(bf16[432,384]{1,0:T(8,128)(2,1)S(1)} %get-tuple-element.73), channel_id=1, source_target_pairs={{0,2},{2,0},{4,6},{6,4},{8,10},{10,8},{12,14},{14,12},{16,18},{18,... | collective-permute-start | bytes 995336 | tf_op jit(solution)/shard_map/ppermute | solution.py:800
  73.8 5.5 %attend_mine.1 = (f32[416,384]{1,0:T(8,128)S(1)}, f32[416,128]{1,0:T(8,128)S(1)}) custom-call(s32[67]{0:T(128)S(1)} %pad_add_fusion.info_ref, bf16[2,208,384]{2,1,0:T(8,128)(2,1)S(1)} %get-tuple-element.74.rest_5_.own_ref, f32[8,384]{1,0:T(8,128)S(1)} %get-tuple-element.61.rest_0_.means_ref, f32[8,384]{1,0:T(8,128)S(1)} %get-tuple-element.62.rest_1_.scales_ref, ...), custom_call_target="tpu_custom_call" | custom-call | flops 6600000000 | tf_op jit(solution)/shard_map/attend_mine/pallas_call | solution.py:670
  80.3 1.4 %finish.1 = (bf16[4,104,384]{2,1,0:T(8,128)(2,1)S(1)}, bf16[1,104,384]{2,1,0:T(8,128)(2,1)S(1)}, bf16[1,104,384]{2,1,0:T(8,128)(2,1)S(1)}) custom-call(s32[67]{0:T(128)S(1)} %pad_add_fusion.info_ref, f32[416,384]{1,0:T(8,128)S(1)} %get-tuple-element.77.mean_ref, f32[416,128]{1,0:T(8,128)S(1)} %get-tuple-element.78.level_ref, ...), custom_call_target="tpu_custom_call" | custom-call | flops 1540000000 | tf_op jit(solution)/shard_map/finish/pallas_call | solution.py:670
  82.4 3.7 %collective-permute-start.26 = (bf16[1,104,384]{2,1,0:T(8,128)(2,1)S(1)}, bf16[1,104,384]{2,1,0:T(8,128)(2,1)S(1)}, u32[]{:S(2)}, u32[]{:S(2)}) collective-permute-start(bf16[1,104,384]{2,1,0:T(8,128)(2,1)S(1)} %get-tuple-element.80), channel_id=1, source_target_pairs={{0,2},{2,0},{4,6},{6,4},{8,10},{10,8},{12,14},{14,12},{16,18},{18,... | collective-permute-start | bytes 239624 | tf_op jit(solution)/shard_map/ppermute | solution.py:612
  86.1 2.2 %upsample.1 = (bf16[6,192,208]{2,1,0:T(8,128)(2,1)S(1)}, f32[2,2,256,128]{3,2,1,0:T(8,128)S(1)}) custom-call(s32[67]{0:T(128)S(1)} %pad_add_fusion.info_ref, bf16[4,104,384]{2,1,0:T(8,128)(2,1)S(1)} %get-tuple-element.81.own_ref, bf16[2,2,2,192,768]{4,3,2,1,0:T(8,128)(2,1)S(1)} %fold.1.weight_ref, f32[1,256]{1,0:T(1,128)S(1)} %pad.4.bias_ref), custom_call_target="tpu_custom_call" | custom-call | flops 2200000000 | tf_op jit(solution)/shard_map/upsample/pallas_call | solution.py:670
  89.2 2.1 %close.1 = bf16[8,192,208]{2,1,0:T(8,128)(2,1)} custom-call(s32[67]{0:T(128)S(1)} %pad_add_fusion.info_ref, bf16[1,104,384]{2,1,0:T(8,128)(2,1)S(1)} %collective-permute-done.25.outer_ref, bf16[1,104,384]{2,1,0:T(8,128)(2,1)S(1)} %collective-permute-done.26.inner_ref, bf16[6,192,208]{2,1,0:T(8,128)(2,1)S(1)} %get-tuple-element.83.middle_ref, ...), custom_call_target="tpu_custom_call" | custom-call | flops 1100000000 | tf_op jit(solution)/shard_map/close/pallas_call | solution.py:670
  (93 shorter events, 25.0 us)
Async XLA Ops:
  0.9 9.3 %collective-permute-start = (bf16[1,104,384]{2,1,0:T(8,128)(2,1)S(1)}, bf16[1,104,384]{2,1,0:T(8,128)(2,1)S(1)}, u32[]{:S(2)}, u32[]{:S(2)}) collective-permute-start(bf16[1,104,384]{2,1,0:T(8,128)(2,1)S(1)} %get-tuple-element.97), channel_id=1, source_target_pairs={{2,4},{4,2},{6,8},{8,6},{10,12},{12,10},{14,16},{16,14},{18,20},{2... | collective-permute-start | bytes 239624 | tf_op jit(solution)/shard_map/ppermute | solution.py:688
  1.6 9.5 %collective-permute-start.1 = (bf16[1,104,384]{2,1,0:T(8,128)(2,1)S(1)}, bf16[1,104,384]{2,1,0:T(8,128)(2,1)S(1)}, u32[]{:S(2)}, u32[]{:S(2)}) collective-permute-start(bf16[1,104,384]{2,1,0:T(8,128)(2,1)S(1)} %get-tuple-element.96), channel_id=1, source_target_pairs={{0,2},{2,0},{4,6},{6,4},{8,10},{10,8},{12,14},{14,12},{16,18},{18,... | collective-permute-start | bytes 239624 | tf_op jit(solution)/shard_map/ppermute | solution.py:612
  11.1 6.2 %collective-permute-start.2 = (f32[3,8,128]{2,1,0:T(8,128)S(1)}, f32[3,8,128]{2,1,0:T(8,128)S(1)}, u32[]{:S(2)}, u32[]{:S(2)}) collective-permute-start(f32[3,8,128]{2,1,0:T(8,128)S(1)} %first_stats.1), channel_id=1, source_target_pairs={{0,8},{2,10},{4,12},{6,14},{8,0},{10,2},{12,4},{14,6},{16,24},{18,... | collective-permute-start | bytes 36872 | tf_op jit(solution)/shard_map/ppermute | solution.py:612
  13.0 4.6 %collective-permute-start.3 = (f32[3,8,128]{2,1,0:T(8,128)S(1)}, f32[3,8,128]{2,1,0:T(8,128)S(1)}, u32[]{:S(2)}, u32[]{:S(2)}) collective-permute-start(f32[3,8,128]{2,1,0:T(8,128)S(1)} %first_stats.1), channel_id=1, source_target_pairs={{0,16},{2,18},{4,20},{6,22},{8,24},{10,26},{12,28},{14,30},{16,0},... | collective-permute-start | bytes 36872 | tf_op jit(solution)/shard_map/ppermute | solution.py:612
  15.5 5.5 %collective-permute-start.4 = (f32[3,8,128]{2,1,0:T(8,128)S(1)}, f32[3,8,128]{2,1,0:T(8,128)S(1)}, u32[]{:S(2)}, u32[]{:S(2)}) collective-permute-start(f32[3,8,128]{2,1,0:T(8,128)S(1)} %first_stats.1), channel_id=1, source_target_pairs={{0,24},{2,26},{4,28},{6,30},{8,16},{10,18},{12,20},{14,22},{16,8},... | collective-permute-start | bytes 36872 | tf_op jit(solution)/shard_map/ppermute | solution.py:612
  21.1 5.4 %collective-permute-start.5 = (f32[3,8,128]{2,1,0:T(8,128)S(1)}, f32[3,8,128]{2,1,0:T(8,128)S(1)}, u32[]{:S(2)}, u32[]{:S(2)}) collective-permute-start(f32[3,8,128]{2,1,0:T(8,128)S(1)} %pad_maximum_fusion), channel_id=1, source_target_pairs={{0,2},{2,0},{4,6},{6,4},{8,10},{10,8},{12,14},{14,12},{16,18},{18,... | collective-permute-start | bytes 36872 | tf_op jit(solution)/shard_map/ppermute | solution.py:612
  21.6 4.9 %collective-permute-start.6 = (f32[3,8,128]{2,1,0:T(8,128)S(1)}, f32[3,8,128]{2,1,0:T(8,128)S(1)}, u32[]{:S(2)}, u32[]{:S(2)}) collective-permute-start(f32[3,8,128]{2,1,0:T(8,128)S(1)} %pad_maximum_fusion), channel_id=1, source_target_pairs={{0,4},{2,6},{4,0},{6,2},{8,12},{10,14},{12,8},{14,10},{16,20},{18,... | collective-permute-start | bytes 36872 | tf_op jit(solution)/shard_map/ppermute | solution.py:612
  22.9 4.6 %collective-permute-start.7 = (f32[3,8,128]{2,1,0:T(8,128)S(1)}, f32[3,8,128]{2,1,0:T(8,128)S(1)}, u32[]{:S(2)}, u32[]{:S(2)}) collective-permute-start(f32[3,8,128]{2,1,0:T(8,128)S(1)} %pad_maximum_fusion), channel_id=1, source_target_pairs={{0,6},{2,4},{4,2},{6,0},{8,14},{10,12},{12,10},{14,8},{16,22},{18,... | collective-permute-start | bytes 36872 | tf_op jit(solution)/shard_map/ppermute | solution.py:612
  35.2 4.7 %collective-permute-start.10 = (f32[3,8,128]{2,1,0:T(8,128)S(1)}, f32[3,8,128]{2,1,0:T(8,128)S(1)}, u32[]{:S(2)}, u32[]{:S(2)}) collective-permute-start(f32[3,8,128]{2,1,0:T(8,128)S(1)} %get-tuple-element.55), channel_id=1, source_target_pairs={{0,16},{2,18},{4,20},{6,22},{8,24},{10,26},{12,28},{14,30},{16,0},... | collective-permute-start | bytes 36872 | tf_op jit(solution)/shard_map/ppermute | solution.py:612
  35.3 5.7 %collective-permute-start.11 = (f32[3,8,128]{2,1,0:T(8,128)S(1)}, f32[3,8,128]{2,1,0:T(8,128)S(1)}, u32[]{:S(2)}, u32[]{:S(2)}) collective-permute-start(f32[3,8,128]{2,1,0:T(8,128)S(1)} %get-tuple-element.55), channel_id=1, source_target_pairs={{0,24},{2,26},{4,28},{6,30},{8,16},{10,18},{12,20},{14,22},{16,8},... | collective-permute-start | bytes 36872 | tf_op jit(solution)/shard_map/ppermute | solution.py:612
  36.8 4.2 %collective-permute-start.9 = (f32[3,8,128]{2,1,0:T(8,128)S(1)}, f32[3,8,128]{2,1,0:T(8,128)S(1)}, u32[]{:S(2)}, u32[]{:S(2)}) collective-permute-start(f32[3,8,128]{2,1,0:T(8,128)S(1)} %get-tuple-element.55), channel_id=1, source_target_pairs={{0,8},{2,10},{4,12},{6,14},{8,0},{10,2},{12,4},{14,6},{16,24},{18,... | collective-permute-start | bytes 36872 | tf_op jit(solution)/shard_map/ppermute | solution.py:612
  38.7 9.0 %collective-permute-start.13 = (bf16[2,208,384]{2,1,0:T(8,128)(2,1)S(1)}, bf16[2,208,384]{2,1,0:T(8,128)(2,1)S(1)}, u32[]{:S(2)}, u32[]{:S(2)}) collective-permute-start(bf16[2,208,384]{2,1,0:T(8,128)(2,1)S(1)} %get-tuple-element.74.rest_5_.own_ref), channel_id=1, source_target_pairs={{0,8},{2,10},{4,12},{6,14},{8,0},{10,2},{12,4},{14,6},{16,24},{18,... | collective-permute-start | bytes 958472 | tf_op jit(solution)/shard_map/ppermute | solution.py:612
  38.8 9.0 %collective-permute-start.14 = (bf16[2,208,384]{2,1,0:T(8,128)(2,1)S(1)}, bf16[2,208,384]{2,1,0:T(8,128)(2,1)S(1)}, u32[]{:S(2)}, u32[]{:S(2)}) collective-permute-start(bf16[2,208,384]{2,1,0:T(8,128)(2,1)S(1)} %get-tuple-element.74.rest_5_.own_ref), channel_id=1, source_target_pairs={{8,16},{10,18},{12,20},{14,22},{16,8},{18,10},{20,12},{22,14},{9,1... | collective-permute-start | bytes 958472 | tf_op jit(solution)/shard_map/ppermute | solution.py:612
  42.1 4.7 %collective-permute-start.16 = (f32[3,8,128]{2,1,0:T(8,128)S(1)}, f32[3,8,128]{2,1,0:T(8,128)S(1)}, u32[]{:S(2)}, u32[]{:S(2)}) collective-permute-start(f32[3,8,128]{2,1,0:T(8,128)S(1)} %pad_maximum_fusion.2), channel_id=1, source_target_pairs={{0,6},{2,4},{4,2},{6,0},{8,14},{10,12},{12,10},{14,8},{16,22},{18,... | collective-permute-start | bytes 36872 | tf_op jit(solution)/shard_map/ppermute | solution.py:612
  44.0 3.8 %collective-permute-start.12 = (f32[3,8,128]{2,1,0:T(8,128)S(1)}, f32[3,8,128]{2,1,0:T(8,128)S(1)}, u32[]{:S(2)}, u32[]{:S(2)}) collective-permute-start(f32[3,8,128]{2,1,0:T(8,128)S(1)} %pad_maximum_fusion.2), channel_id=1, source_target_pairs={{0,2},{2,0},{4,6},{6,4},{8,10},{10,8},{12,14},{14,12},{16,18},{18,... | collective-permute-start | bytes 36872 | tf_op jit(solution)/shard_map/ppermute | solution.py:612
  46.8 13.0 %collective-permute-start.18 = (bf16[2,208,384]{2,1,0:T(8,128)(2,1)S(1)}, bf16[2,208,384]{2,1,0:T(8,128)(2,1)S(1)}, u32[]{:S(2)}, u32[]{:S(2)}) collective-permute-start(bf16[2,208,384]{2,1,0:T(8,128)(2,1)S(1)} %get-tuple-element.74.rest_5_.own_ref), channel_id=1, source_target_pairs={{0,4},{2,6},{4,0},{6,2},{8,12},{10,14},{12,8},{14,10},{16,20},{18,... | collective-permute-start | bytes 958472 | tf_op jit(solution)/shard_map/ppermute | solution.py:612
  48.5 11.3 %collective-permute-start.20 = (bf16[2,208,384]{2,1,0:T(8,128)(2,1)S(1)}, bf16[2,208,384]{2,1,0:T(8,128)(2,1)S(1)}, u32[]{:S(2)}, u32[]{:S(2)}) collective-permute-start(bf16[2,208,384]{2,1,0:T(8,128)(2,1)S(1)} %collective-permute-done.14.rest_8_), channel_id=1, source_target_pairs={{8,0},{10,2},{12,4},{14,6},{16,24},{18,26},{20,28},{22,30},{9,1},{... | collective-permute-start | bytes 958472 | tf_op jit(solution)/shard_map/ppermute | solution.py:612
  49.8 13.6 %collective-permute-start.17 = (bf16[2,208,384]{2,1,0:T(8,128)(2,1)S(1)}, bf16[2,208,384]{2,1,0:T(8,128)(2,1)S(1)}, u32[]{:S(2)}, u32[]{:S(2)}) collective-permute-start(bf16[2,208,384]{2,1,0:T(8,128)(2,1)S(1)} %get-tuple-element.74.rest_5_.own_ref), channel_id=1, source_target_pairs={{0,2},{2,0},{4,6},{6,4},{8,10},{10,8},{12,14},{14,12},{16,18},{18,... | collective-permute-start | bytes 958472 | tf_op jit(solution)/shard_map/ppermute | solution.py:612
  59.8 8.6 %collective-permute-start.21 = (bf16[2,208,384]{2,1,0:T(8,128)(2,1)S(1)}, bf16[2,208,384]{2,1,0:T(8,128)(2,1)S(1)}, u32[]{:S(2)}, u32[]{:S(2)}) collective-permute-start(bf16[2,208,384]{2,1,0:T(8,128)(2,1)S(1)} %collective-permute-done.18.rest_6_), channel_id=1, source_target_pairs={{8,16},{10,18},{12,20},{14,22},{16,8},{18,10},{20,12},{22,14},{9,1... | collective-permute-start | bytes 958472 | tf_op jit(solution)/shard_map/ppermute | solution.py:612
  60.7 7.8 %collective-permute-start.22 = (bf16[2,208,384]{2,1,0:T(8,128)(2,1)S(1)}, bf16[2,208,384]{2,1,0:T(8,128)(2,1)S(1)}, u32[]{:S(2)}, u32[]{:S(2)}) collective-permute-start(bf16[2,208,384]{2,1,0:T(8,128)(2,1)S(1)} %collective-permute-done.18.rest_6_), channel_id=1, source_target_pairs={{0,8},{2,10},{4,12},{6,14},{8,0},{10,2},{12,4},{14,6},{16,24},{18,... | collective-permute-start | bytes 958472 | tf_op jit(solution)/shard_map/ppermute | solution.py:612
  62.7 7.0 %collective-permute-start.23 = (bf16[2,208,384]{2,1,0:T(8,128)(2,1)S(1)}, bf16[2,208,384]{2,1,0:T(8,128)(2,1)S(1)}, u32[]{:S(2)}, u32[]{:S(2)}) collective-permute-start(bf16[2,208,384]{2,1,0:T(8,128)(2,1)S(1)} %broadcast_select_fusion.rest_9_), channel_id=1, source_target_pairs={{0,4},{2,6},{4,0},{6,2},{8,12},{10,14},{12,8},{14,10},{16,20},{18,... | collective-permute-start | bytes 958472 | tf_op jit(solution)/shard_map/ppermute | solution.py:612
  72.3 7.5 %collective-permute-start.24 = (bf16[432,384]{1,0:T(8,128)(2,1)S(1)}, bf16[432,384]{1,0:T(8,128)(2,1)S(1)}, u32[]{:S(2)}, u32[]{:S(2)}) collective-permute-start(bf16[432,384]{1,0:T(8,128)(2,1)S(1)} %get-tuple-element.73), channel_id=1, source_target_pairs={{0,2},{2,0},{4,6},{6,4},{8,10},{10,8},{12,14},{14,12},{16,18},{18,... | collective-permute-start | bytes 995336 | tf_op jit(solution)/shard_map/ppermute | solution.py:800
  81.7 6.5 %collective-permute-start.25 = (bf16[1,104,384]{2,1,0:T(8,128)(2,1)S(1)}, bf16[1,104,384]{2,1,0:T(8,128)(2,1)S(1)}, u32[]{:S(2)}, u32[]{:S(2)}) collective-permute-start(bf16[1,104,384]{2,1,0:T(8,128)(2,1)S(1)} %get-tuple-element.79), channel_id=1, source_target_pairs={{2,4},{4,2},{6,8},{8,6},{10,12},{12,10},{14,16},{16,14},{18,20},{2... | collective-permute-start | bytes 239624 | tf_op jit(solution)/shard_map/ppermute | solution.py:830
  82.4 6.9 %collective-permute-start.26 = (bf16[1,104,384]{2,1,0:T(8,128)(2,1)S(1)}, bf16[1,104,384]{2,1,0:T(8,128)(2,1)S(1)}, u32[]{:S(2)}, u32[]{:S(2)}) collective-permute-start(bf16[1,104,384]{2,1,0:T(8,128)(2,1)S(1)} %get-tuple-element.80), channel_id=1, source_target_pairs={{0,2},{2,0},{4,6},{6,4},{8,10},{10,8},{12,14},{14,12},{16,18},{18,... | collective-permute-start | bytes 239624 | tf_op jit(solution)/shard_map/ppermute | solution.py:612
  (16 other events, 164.6 us)

commit v16 on v15

--- a/solution.py
+++ b/solution.py
@@ -798,7 +798,7 @@
         keys.append(normed)
     (sent,) = state
     received = lax.ppermute(sent, "tile", neighbour)
-    sent, own_late, upsample_weight = lax.optimization_barrier((sent, own, upsample_weight))
+    sent, own_late = lax.optimization_barrier((sent, own))
     mean, level = call(
         functools.partial(attend_mine_kernel, rows, tuple(tuple(masks) for masks in groups)),
         [own_late, means, scales, shift, triple_weight, row(triple_bias)] + keys,
@@ -806,16 +806,6 @@
         cost_estimate=cost(6.0),
         name="attend_mine",
     )
-    folded = pl.pallas_call(
-        fold_kernel,
-        out_shape=shape(2, 2, 2, out_channels, 2 * channels),
-        in_specs=[VMEM_SPEC],
-        out_specs=VMEM_SPEC,
-        compiler_params=params(),
-        cost_estimate=cost(0.5),
-        name="fold",
-    )(jnp.swapaxes(upsample_weight, 2, 3))
-
     rim_shape = shape(1, cols, channels)
     attended, inner, outer = call(
         functools.partial(finish_kernel, rows),
@@ -829,6 +819,16 @@
     )
     outer = lax.ppermute(outer, "tile", outer_moves)
     inner = exchange(inner, tiles, 1)
+    attended, upsample_weight = lax.optimization_barrier((attended, upsample_weight))
+    folded = pl.pallas_call(
+        fold_kernel,
+        out_shape=shape(2, 2, 2, out_channels, 2 * channels),
+        in_specs=[VMEM_SPEC],
+        out_specs=VMEM_SPEC,
+        compiler_params=params(),
+        cost_estimate=cost(0.1),
+        name="fold",
+    )(jnp.swapaxes(upsample_weight, 2, 3))
     parts_out = -(-out_channels // LANES)
     wide_cols = -(-2 * cols // LANES) * LANES
     wide_bias = jnp.pad(row(upsample_bias), ((0, 0), (0, -out_channels % LANES)))
@@ -843,7 +843,7 @@
             pltpu.VMEM((row_count * padded, 3 * channels), BF16),
             pltpu.VMEM((parts_out, 2 * row_count, wide_cols, LANES), F32),
         ],
-        cost_estimate=cost(2.0),
+        cost_estimate=cost(0.2),
         name="upsample",
     )
     decoded = call(

time: 91.7 us -> 90.8 us (level)
  the two profiles are of different devices: /device:TPU:0 before, /device:TPU:8 now
where the time goes in v16:
time: 90.8 us; the launch traced here: 89.9 us
  starting transfers between devices  42.6 us (47%)
  Pallas kernels  30.2 us (33%)
  waiting for transfers between devices  13.6 us (15%)
  other arithmetic  1.9 us (2%)
  local copies, waits for them, and re-layouts  1.07 us (1%)
    ppermute x23, starting transfers between devices, exchange(): return lax.ppermute(array, 'tile', moves)  30.3 us
    pallas_call x11, Pallas kernels, call(): pl.pallas_call(kernel, out_shape=out_shape, in_specs=[SMEM_SPEC] + [VMEM_...  26.1 us
    ppermute x23, waiting for transfers between devices, exchange(): return lax.ppermute(array, 'tile', moves)  13.1 us
    ppermute x1, starting transfers between devices, shards(): outer = lax.ppermute(outer, 'tile', outer_moves)  5.28 us
    ppermute x1, starting transfers between devices, shards(): lax.ppermute(jnp.where(odd, source[row_count - 1:], source[:1]), 'tile',...  4.24 us
    pallas_call x2, Pallas kernels, shards(): pl.pallas_call(functools.partial(hold_kernel, backs), out_shape=shape(3 *...  3.5 us
  transfers between devices with their start and end apart: 27, of which 12 were waited for; matrix products, arithmetic and copies ran while one was open for 1% of the time, Pallas kernels for 22%

profile of v16, /device:TPU:8, one launch (start us, length us, event | category | flops | bytes accessed | tf_op | source)
XLA Modules:
  0.0 89.9 jit_solution(5183581229551710695)
XLA Ops:
  0.9 4.2 %collective-permute-start = (bf16[1,104,384]{2,1,0:T(8,128)(2,1)S(1)}, bf16[1,104,384]{2,1,0:T(8,128)(2,1)S(1)}, u32[]{:S(2)}, u32[]{:S(2)}) collective-permute-start(bf16[1,104,384]{2,1,0:T(8,128)(2,1)S(1)} %get-tuple-element.99), channel_id=1, source_target_pairs={{2,4},{4,2},{6,8},{8,6},{10,12},{12,10},{14,16},{16,14},{18,20},{2... | collective-permute-start | bytes 239624 | tf_op jit(solution)/shard_map/ppermute | solution.py:688
  10.1 2.9 %collective-permute-start.3 = (f32[3,8,128]{2,1,0:T(8,128)S(1)}, f32[3,8,128]{2,1,0:T(8,128)S(1)}, u32[]{:S(2)}, u32[]{:S(2)}) collective-permute-start(f32[3,8,128]{2,1,0:T(8,128)S(1)} %first_stats.1), channel_id=1, source_target_pairs={{0,16},{2,18},{4,20},{6,22},{8,24},{10,26},{12,28},{14,30},{16,0},... | collective-permute-start | bytes 36872 | tf_op jit(solution)/shard_map/ppermute | solution.py:612
  13.4 1.7 %hold.2.held_ref = bf16[1152,1152]{1,0:T(8,128)(2,1)S(1)} custom-call(bf16[3,3,3,384,384]{4,3,2,1,0:T(8,128)(2,1)} %weight_ref.5), custom_call_target="tpu_custom_call" | custom-call | flops 1650000000 | tf_op jit(solution)/shard_map/hold/pallas_call | solution.py:695
  16.7 1.6 %collective-permute-start.5 = (f32[3,8,128]{2,1,0:T(8,128)S(1)}, f32[3,8,128]{2,1,0:T(8,128)S(1)}, u32[]{:S(2)}, u32[]{:S(2)}) collective-permute-start(f32[3,8,128]{2,1,0:T(8,128)S(1)} %pad_maximum_fusion), channel_id=1, source_target_pairs={{0,2},{2,0},{4,6},{6,4},{8,10},{10,8},{12,14},{14,12},{16,18},{18,... | collective-permute-start | bytes 36872 | tf_op jit(solution)/shard_map/ppermute | solution.py:612
  20.3 1.7 %hold.3.rest_4_ = bf16[1152,1152]{1,0:T(8,128)(2,1)S(1)} custom-call(bf16[3,3,3,384,384]{4,3,2,1,0:T(8,128)(2,1)} %weight_ref.5), custom_call_target="tpu_custom_call" | custom-call | flops 1650000000 | tf_op jit(solution)/shard_map/hold/pallas_call | solution.py:695
  26.2 2.2 %own_conv.1.rest_1_ = f32[448,1152]{1,0:T(8,128)S(1)} custom-call(s32[67]{0:T(128)S(1)} %pad_add_fusion.info_ref, bf16[6,112,384]{2,1,0:T(8,128)(2,1)S(1)} %get-tuple-element.51.hidden_ref, bf16[1152,1152]{1,0:T(8,128)(2,1)S(1)} %hold.2.held_ref), custom_call_target="tpu_custom_call" | custom-call | flops 2420000000 | tf_op jit(solution)/shard_map/own_conv/pallas_call | solution.py:670
  28.4 2.8 %conv.1 = (bf16[2,208,384]{2,1,0:T(8,128)(2,1)S(1)}, f32[3,8,128]{2,1,0:T(8,128)S(1)}) custom-call(s32[67]{0:T(128)S(1)} %pad_add_fusion.info_ref, bf16[6,112,384]{2,1,0:T(8,128)(2,1)S(1)} %collective-permute-done.8.rest_0_, f32[448,1152]{1,0:T(8,128)S(1)} %own_conv.1.rest_1_, bf16[4,104,384]{2,1,0:T(8,128)(2,1)S(1)} %get-tuple-element.53.rest_2_, ...), custom_call_target="tpu_custom_call" | custom-call | flops 3849999872 | tf_op jit(solution)/shard_map/conv/pallas_call | solution.py:670
  31.3 2.2 %collective-permute-start.10 = (f32[3,8,128]{2,1,0:T(8,128)S(1)}, f32[3,8,128]{2,1,0:T(8,128)S(1)}, u32[]{:S(2)}, u32[]{:S(2)}) collective-permute-start(f32[3,8,128]{2,1,0:T(8,128)S(1)} %get-tuple-element.56), channel_id=1, source_target_pairs={{0,16},{2,18},{4,20},{6,22},{8,24},{10,26},{12,28},{14,30},{16,0},... | collective-permute-start | bytes 36872 | tf_op jit(solution)/shard_map/ppermute | solution.py:612
  33.5 2.2 %collective-permute-start.11 = (f32[3,8,128]{2,1,0:T(8,128)S(1)}, f32[3,8,128]{2,1,0:T(8,128)S(1)}, u32[]{:S(2)}, u32[]{:S(2)}) collective-permute-start(f32[3,8,128]{2,1,0:T(8,128)S(1)} %get-tuple-element.56), channel_id=1, source_target_pairs={{0,24},{2,26},{4,28},{6,30},{8,16},{10,18},{12,20},{14,22},{16,8},... | collective-permute-start | bytes 36872 | tf_op jit(solution)/shard_map/ppermute | solution.py:612
  35.7 2.0 %collective-permute-start.13 = (bf16[2,208,384]{2,1,0:T(8,128)(2,1)S(1)}, bf16[2,208,384]{2,1,0:T(8,128)(2,1)S(1)}, u32[]{:S(2)}, u32[]{:S(2)}) collective-permute-start(bf16[2,208,384]{2,1,0:T(8,128)(2,1)S(1)} %get-tuple-element.75.rest_5_.own_ref), channel_id=1, source_target_pairs={{0,8},{2,10},{4,12},{6,14},{8,0},{10,2},{12,4},{14,6},{16,24},{18,... | collective-permute-start | bytes 958472 | tf_op jit(solution)/shard_map/ppermute | solution.py:612
  37.7 1.9 %collective-permute-start.14 = (bf16[2,208,384]{2,1,0:T(8,128)(2,1)S(1)}, bf16[2,208,384]{2,1,0:T(8,128)(2,1)S(1)}, u32[]{:S(2)}, u32[]{:S(2)}) collective-permute-start(bf16[2,208,384]{2,1,0:T(8,128)(2,1)S(1)} %get-tuple-element.75.rest_5_.own_ref), channel_id=1, source_target_pairs={{8,16},{10,18},{12,20},{14,22},{16,8},{18,10},{20,12},{22,14},{9,1... | collective-permute-start | bytes 958472 | tf_op jit(solution)/shard_map/ppermute | solution.py:612
  41.0 1.7 %collective-permute-start.16 = (f32[3,8,128]{2,1,0:T(8,128)S(1)}, f32[3,8,128]{2,1,0:T(8,128)S(1)}, u32[]{:S(2)}, u32[]{:S(2)}) collective-permute-start(f32[3,8,128]{2,1,0:T(8,128)S(1)} %pad_maximum_fusion.2), channel_id=1, source_target_pairs={{0,6},{2,4},{4,2},{6,0},{8,14},{10,12},{12,10},{14,8},{16,22},{18,... | collective-permute-start | bytes 36872 | tf_op jit(solution)/shard_map/ppermute | solution.py:612
  43.5 2.2 %collective-permute-done.16 = f32[3,8,128]{2,1,0:T(8,128)S(1)} collective-permute-done((f32[3,8,128]{2,1,0:T(8,128)S(1)}, f32[3,8,128]{2,1,0:T(8,128)S(1)}, u32[]{:S(2)}, u32[]{:S(2)}) %collective-permute-start.16) | collective-permute-done | bytes 12320 | tf_op jit(solution)/shard_map/ppermute | solution.py:612
  47.5 2.9 %collective-permute-start.19 = (bf16[2,208,384]{2,1,0:T(8,128)(2,1)S(1)}, bf16[2,208,384]{2,1,0:T(8,128)(2,1)S(1)}, u32[]{:S(2)}, u32[]{:S(2)}) collective-permute-start(bf16[2,208,384]{2,1,0:T(8,128)(2,1)S(1)} %collective-permute-done.13.rest_7_), channel_id=1, source_target_pairs={{8,16},{10,18},{12,20},{14,22},{16,8},{18,10},{20,12},{22,14},{9,1... | collective-permute-start | bytes 958472 | tf_op jit(solution)/shard_map/ppermute | solution.py:612
  51.8 1.5 %collective-permute-start.17 = (bf16[2,208,384]{2,1,0:T(8,128)(2,1)S(1)}, bf16[2,208,384]{2,1,0:T(8,128)(2,1)S(1)}, u32[]{:S(2)}, u32[]{:S(2)}) collective-permute-start(bf16[2,208,384]{2,1,0:T(8,128)(2,1)S(1)} %get-tuple-element.75.rest_5_.own_ref), channel_id=1, source_target_pairs={{0,2},{2,0},{4,6},{6,4},{8,10},{10,8},{12,14},{14,12},{16,18},{18,... | collective-permute-start | bytes 958472 | tf_op jit(solution)/shard_map/ppermute | solution.py:612
  53.4 3.0 %collective-permute-done.19 = bf16[2,208,384]{2,1,0:T(8,128)(2,1)S(1)} collective-permute-done((bf16[2,208,384]{2,1,0:T(8,128)(2,1)S(1)}, bf16[2,208,384]{2,1,0:T(8,128)(2,1)S(1)}, u32[]{:S(2)}, u32[]{:S(2)}) %collective-permute-start.19) | collective-permute-done | bytes 319520 | tf_op jit(solution)/shard_map/ppermute | solution.py:612
  56.5 3.1 %collective-permute-start.21 = (bf16[2,208,384]{2,1,0:T(8,128)(2,1)S(1)}, bf16[2,208,384]{2,1,0:T(8,128)(2,1)S(1)}, u32[]{:S(2)}, u32[]{:S(2)}) collective-permute-start(bf16[2,208,384]{2,1,0:T(8,128)(2,1)S(1)} %collective-permute-done.18.rest_6_), channel_id=1, source_target_pairs={{8,16},{10,18},{12,20},{14,22},{16,8},{18,10},{20,12},{22,14},{9,1... | collective-permute-start | bytes 958472 | tf_op jit(solution)/shard_map/ppermute | solution.py:612
  61.8 3.6 %attend_yours.2 = (bf16[2080,384]{1,0:T(8,128)(2,1)S(1)}, f32[416,128]{1,0:T(8,128)S(1)}, f32[416,128]{1,0:T(8,128)S(1)}, f32[416,384]{1,0:T(8,128)S(1)}) custom-call(s32[67]{0:T(128)S(1)} %pad_add_fusion.info_ref, f32[8,384]{1,0:T(8,128)S(1)} %get-tuple-element.62.rest_0_.means_ref, f32[8,384]{1,0:T(8,128)S(1)} %get-tuple-element.63.rest_1_.scales_ref, ...), custom_call_target="tpu_custom_call" | custom-call | flops 4950000128 | tf_op jit(solution)/shard_map/attend_yours/pallas_call | solution.py:670
  66.7 2.6 %attend_yours.3 = (bf16[1248,384]{1,0:T(8,128)(2,1)S(1)}, bf16[432,384]{1,0:T(8,128)(2,1)S(1)}) custom-call(s32[67]{0:T(128)S(1)} %pad_add_fusion.info_ref, f32[8,384]{1,0:T(8,128)S(1)} %get-tuple-element.62.rest_0_.means_ref, f32[8,384]{1,0:T(8,128)S(1)} %get-tuple-element.63.rest_1_.scales_ref, f32[1,384]{1,0:T(1,128)S(1)} %reshape.87.shift_ref.rest_2_, ...), custom_call_target="tpu_custom_call" | custom-call | flops 2969999872 | tf_op jit(solution)/shard_map/attend_yours/pallas_call | solution.py:670
  70.9 5.5 %attend_mine.1 = (f32[416,384]{1,0:T(8,128)S(1)}, f32[416,128]{1,0:T(8,128)S(1)}) custom-call(s32[67]{0:T(128)S(1)} %pad_add_fusion.info_ref, bf16[2,208,384]{2,1,0:T(8,128)(2,1)S(1)} %get-tuple-element.75.rest_5_.own_ref, f32[8,384]{1,0:T(8,128)S(1)} %get-tuple-element.62.rest_0_.means_ref, f32[8,384]{1,0:T(8,128)S(1)} %get-tuple-element.63.rest_1_.scales_ref, ...), custom_call_target="tpu_custom_call" | custom-call | flops 6600000000 | tf_op jit(solution)/shard_map/attend_mine/pallas_call | solution.py:670
  78.0 5.3 %collective-permute-start.25 = (bf16[1,104,384]{2,1,0:T(8,128)(2,1)S(1)}, bf16[1,104,384]{2,1,0:T(8,128)(2,1)S(1)}, u32[]{:S(2)}, u32[]{:S(2)}) collective-permute-start(bf16[1,104,384]{2,1,0:T(8,128)(2,1)S(1)} %get-tuple-element.80), channel_id=1, source_target_pairs={{2,4},{4,2},{6,8},{8,6},{10,12},{12,10},{14,16},{16,14},{18,20},{2... | collective-permute-start | bytes 239624 | tf_op jit(solution)/shard_map/ppermute | solution.py:820
  83.9 2.2 %upsample.1 = (bf16[6,192,208]{2,1,0:T(8,128)(2,1)S(1)}, f32[2,2,256,128]{3,2,1,0:T(8,128)S(1)}) custom-call(s32[67]{0:T(128)S(1)} %pad_add_fusion.info_ref, bf16[4,104,384]{2,1,0:T(8,128)(2,1)S(1)} %get-tuple-element.83.own_ref, bf16[2,2,2,192,768]{4,3,2,1,0:T(8,128)(2,1)S(1)} %fold.1.weight_ref, f32[1,256]{1,0:T(1,128)S(1)} %pad.4.bias_ref), custom_call_target="tpu_custom_call" | custom-call | flops 220000000 | tf_op jit(solution)/shard_map/upsample/pallas_call | solution.py:670
  86.1 1.7 %collective-permute-done.26.inner_ref = bf16[1,104,384]{2,1,0:T(8,128)(2,1)S(1)} collective-permute-done((bf16[1,104,384]{2,1,0:T(8,128)(2,1)S(1)}, bf16[1,104,384]{2,1,0:T(8,128)(2,1)S(1)}, u32[]{:S(2)}, u32[]{:S(2)}) %collective-permute-start.26) | collective-permute-done | bytes 79904 | tf_op jit(solution)/shard_map/ppermute | solution.py:612
  87.8 2.1 %close.1 = bf16[8,192,208]{2,1,0:T(8,128)(2,1)} custom-call(s32[67]{0:T(128)S(1)} %pad_add_fusion.info_ref, bf16[1,104,384]{2,1,0:T(8,128)(2,1)S(1)} %collective-permute-done.25.outer_ref, bf16[1,104,384]{2,1,0:T(8,128)(2,1)S(1)} %collective-permute-done.26.inner_ref, bf16[6,192,208]{2,1,0:T(8,128)(2,1)S(1)} %get-tuple-element.85.middle_ref, ...), custom_call_target="tpu_custom_call" | custom-call | flops 1100000000 | tf_op jit(solution)/shard_map/close/pallas_call | solution.py:670
  (93 shorter events, 26.4 us)
Async XLA Ops:
  0.9 8.2 %collective-permute-start = (bf16[1,104,384]{2,1,0:T(8,128)(2,1)S(1)}, bf16[1,104,384]{2,1,0:T(8,128)(2,1)S(1)}, u32[]{:S(2)}, u32[]{:S(2)}) collective-permute-start(bf16[1,104,384]{2,1,0:T(8,128)(2,1)S(1)} %get-tuple-element.99), channel_id=1, source_target_pairs={{2,4},{4,2},{6,8},{8,6},{10,12},{12,10},{14,16},{16,14},{18,20},{2... | collective-permute-start | bytes 239624 | tf_op jit(solution)/shard_map/ppermute | solution.py:688
  5.2 4.7 %collective-permute-start.1 = (bf16[1,104,384]{2,1,0:T(8,128)(2,1)S(1)}, bf16[1,104,384]{2,1,0:T(8,128)(2,1)S(1)}, u32[]{:S(2)}, u32[]{:S(2)}) collective-permute-start(bf16[1,104,384]{2,1,0:T(8,128)(2,1)S(1)} %get-tuple-element.98), channel_id=1, source_target_pairs={{0,2},{2,0},{4,6},{6,4},{8,10},{10,8},{12,14},{14,12},{16,18},{18,... | collective-permute-start | bytes 239624 | tf_op jit(solution)/shard_map/ppermute | solution.py:612
  9.9 5.2 %collective-permute-start.2 = (f32[3,8,128]{2,1,0:T(8,128)S(1)}, f32[3,8,128]{2,1,0:T(8,128)S(1)}, u32[]{:S(2)}, u32[]{:S(2)}) collective-permute-start(f32[3,8,128]{2,1,0:T(8,128)S(1)} %first_stats.1), channel_id=1, source_target_pairs={{0,8},{2,10},{4,12},{6,14},{8,0},{10,2},{12,4},{14,6},{16,24},{18,... | collective-permute-start | bytes 36872 | tf_op jit(solution)/shard_map/ppermute | solution.py:612
  10.1 5.1 %collective-permute-start.3 = (f32[3,8,128]{2,1,0:T(8,128)S(1)}, f32[3,8,128]{2,1,0:T(8,128)S(1)}, u32[]{:S(2)}, u32[]{:S(2)}) collective-permute-start(f32[3,8,128]{2,1,0:T(8,128)S(1)} %first_stats.1), channel_id=1, source_target_pairs={{0,16},{2,18},{4,20},{6,22},{8,24},{10,26},{12,28},{14,30},{16,0},... | collective-permute-start | bytes 36872 | tf_op jit(solution)/shard_map/ppermute | solution.py:612
  16.7 5.4 %collective-permute-start.5 = (f32[3,8,128]{2,1,0:T(8,128)S(1)}, f32[3,8,128]{2,1,0:T(8,128)S(1)}, u32[]{:S(2)}, u32[]{:S(2)}) collective-permute-start(f32[3,8,128]{2,1,0:T(8,128)S(1)} %pad_maximum_fusion), channel_id=1, source_target_pairs={{0,2},{2,0},{4,6},{6,4},{8,10},{10,8},{12,14},{14,12},{16,18},{18,... | collective-permute-start | bytes 36872 | tf_op jit(solution)/shard_map/ppermute | solution.py:612
  19.0 4.6 %collective-permute-start.7 = (f32[3,8,128]{2,1,0:T(8,128)S(1)}, f32[3,8,128]{2,1,0:T(8,128)S(1)}, u32[]{:S(2)}, u32[]{:S(2)}) collective-permute-start(f32[3,8,128]{2,1,0:T(8,128)S(1)} %pad_maximum_fusion), channel_id=1, source_target_pairs={{0,6},{2,4},{4,2},{6,0},{8,14},{10,12},{12,10},{14,8},{16,22},{18,... | collective-permute-start | bytes 36872 | tf_op jit(solution)/shard_map/ppermute | solution.py:612
  31.3 8.4 %collective-permute-start.10 = (f32[3,8,128]{2,1,0:T(8,128)S(1)}, f32[3,8,128]{2,1,0:T(8,128)S(1)}, u32[]{:S(2)}, u32[]{:S(2)}) collective-permute-start(f32[3,8,128]{2,1,0:T(8,128)S(1)} %get-tuple-element.56), channel_id=1, source_target_pairs={{0,16},{2,18},{4,20},{6,22},{8,24},{10,26},{12,28},{14,30},{16,0},... | collective-permute-start | bytes 36872 | tf_op jit(solution)/shard_map/ppermute | solution.py:612
  33.5 6.2 %collective-permute-start.11 = (f32[3,8,128]{2,1,0:T(8,128)S(1)}, f32[3,8,128]{2,1,0:T(8,128)S(1)}, u32[]{:S(2)}, u32[]{:S(2)}) collective-permute-start(f32[3,8,128]{2,1,0:T(8,128)S(1)} %get-tuple-element.56), channel_id=1, source_target_pairs={{0,24},{2,26},{4,28},{6,30},{8,16},{10,18},{12,20},{14,22},{16,8},... | collective-permute-start | bytes 36872 | tf_op jit(solution)/shard_map/ppermute | solution.py:612
  35.7 4.0 %collective-permute-start.9 = (f32[3,8,128]{2,1,0:T(8,128)S(1)}, f32[3,8,128]{2,1,0:T(8,128)S(1)}, u32[]{:S(2)}, u32[]{:S(2)}) collective-permute-start(f32[3,8,128]{2,1,0:T(8,128)S(1)} %get-tuple-element.56), channel_id=1, source_target_pairs={{0,8},{2,10},{4,12},{6,14},{8,0},{10,2},{12,4},{14,6},{16,24},{18,... | collective-permute-start | bytes 36872 | tf_op jit(solution)/shard_map/ppermute | solution.py:612
  35.7 10.8 %collective-permute-start.13 = (bf16[2,208,384]{2,1,0:T(8,128)(2,1)S(1)}, bf16[2,208,384]{2,1,0:T(8,128)(2,1)S(1)}, u32[]{:S(2)}, u32[]{:S(2)}) collective-permute-start(bf16[2,208,384]{2,1,0:T(8,128)(2,1)S(1)} %get-tuple-element.75.rest_5_.own_ref), channel_id=1, source_target_pairs={{0,8},{2,10},{4,12},{6,14},{8,0},{10,2},{12,4},{14,6},{16,24},{18,... | collective-permute-start | bytes 958472 | tf_op jit(solution)/shard_map/ppermute | solution.py:612
  37.7 9.8 %collective-permute-start.14 = (bf16[2,208,384]{2,1,0:T(8,128)(2,1)S(1)}, bf16[2,208,384]{2,1,0:T(8,128)(2,1)S(1)}, u32[]{:S(2)}, u32[]{:S(2)}) collective-permute-start(bf16[2,208,384]{2,1,0:T(8,128)(2,1)S(1)} %get-tuple-element.75.rest_5_.own_ref), channel_id=1, source_target_pairs={{8,16},{10,18},{12,20},{14,22},{16,8},{18,10},{20,12},{22,14},{9,1... | collective-permute-start | bytes 958472 | tf_op jit(solution)/shard_map/ppermute | solution.py:612
  39.7 3.8 %collective-permute-start.15 = (f32[3,8,128]{2,1,0:T(8,128)S(1)}, f32[3,8,128]{2,1,0:T(8,128)S(1)}, u32[]{:S(2)}, u32[]{:S(2)}) collective-permute-start(f32[3,8,128]{2,1,0:T(8,128)S(1)} %pad_maximum_fusion.2), channel_id=1, source_target_pairs={{0,4},{2,6},{4,0},{6,2},{8,12},{10,14},{12,8},{14,10},{16,20},{18,... | collective-permute-start | bytes 36872 | tf_op jit(solution)/shard_map/ppermute | solution.py:612
  41.0 4.7 %collective-permute-start.16 = (f32[3,8,128]{2,1,0:T(8,128)S(1)}, f32[3,8,128]{2,1,0:T(8,128)S(1)}, u32[]{:S(2)}, u32[]{:S(2)}) collective-permute-start(f32[3,8,128]{2,1,0:T(8,128)S(1)} %pad_maximum_fusion.2), channel_id=1, source_target_pairs={{0,6},{2,4},{4,2},{6,0},{8,14},{10,12},{12,10},{14,8},{16,22},{18,... | collective-permute-start | bytes 36872 | tf_op jit(solution)/shard_map/ppermute | solution.py:612
  42.7 3.8 %collective-permute-start.12 = (f32[3,8,128]{2,1,0:T(8,128)S(1)}, f32[3,8,128]{2,1,0:T(8,128)S(1)}, u32[]{:S(2)}, u32[]{:S(2)}) collective-permute-start(f32[3,8,128]{2,1,0:T(8,128)S(1)} %pad_maximum_fusion.2), channel_id=1, source_target_pairs={{0,2},{2,0},{4,6},{6,4},{8,10},{10,8},{12,14},{14,12},{16,18},{18,... | collective-permute-start | bytes 36872 | tf_op jit(solution)/shard_map/ppermute | solution.py:612
  45.7 10.8 %collective-permute-start.18 = (bf16[2,208,384]{2,1,0:T(8,128)(2,1)S(1)}, bf16[2,208,384]{2,1,0:T(8,128)(2,1)S(1)}, u32[]{:S(2)}, u32[]{:S(2)}) collective-permute-start(bf16[2,208,384]{2,1,0:T(8,128)(2,1)S(1)} %get-tuple-element.75.rest_5_.own_ref), channel_id=1, source_target_pairs={{0,4},{2,6},{4,0},{6,2},{8,12},{10,14},{12,8},{14,10},{16,20},{18,... | collective-permute-start | bytes 958472 | tf_op jit(solution)/shard_map/ppermute | solution.py:612
  47.5 8.9 %collective-permute-start.19 = (bf16[2,208,384]{2,1,0:T(8,128)(2,1)S(1)}, bf16[2,208,384]{2,1,0:T(8,128)(2,1)S(1)}, u32[]{:S(2)}, u32[]{:S(2)}) collective-permute-start(bf16[2,208,384]{2,1,0:T(8,128)(2,1)S(1)} %collective-permute-done.13.rest_7_), channel_id=1, source_target_pairs={{8,16},{10,18},{12,20},{14,22},{16,8},{18,10},{20,12},{22,14},{9,1... | collective-permute-start | bytes 958472 | tf_op jit(solution)/shard_map/ppermute | solution.py:612
  50.5 6.0 %collective-permute-start.20 = (bf16[2,208,384]{2,1,0:T(8,128)(2,1)S(1)}, bf16[2,208,384]{2,1,0:T(8,128)(2,1)S(1)}, u32[]{:S(2)}, u32[]{:S(2)}) collective-permute-start(bf16[2,208,384]{2,1,0:T(8,128)(2,1)S(1)} %collective-permute-done.14.rest_8_), channel_id=1, source_target_pairs={{8,0},{10,2},{12,4},{14,6},{16,24},{18,26},{20,28},{22,30},{9,1},{... | collective-permute-start | bytes 958472 | tf_op jit(solution)/shard_map/ppermute | solution.py:612
  51.8 8.6 %collective-permute-start.17 = (bf16[2,208,384]{2,1,0:T(8,128)(2,1)S(1)}, bf16[2,208,384]{2,1,0:T(8,128)(2,1)S(1)}, u32[]{:S(2)}, u32[]{:S(2)}) collective-permute-start(bf16[2,208,384]{2,1,0:T(8,128)(2,1)S(1)} %get-tuple-element.75.rest_5_.own_ref), channel_id=1, source_target_pairs={{0,2},{2,0},{4,6},{6,4},{8,10},{10,8},{12,14},{14,12},{16,18},{18,... | collective-permute-start | bytes 958472 | tf_op jit(solution)/shard_map/ppermute | solution.py:612
  56.5 9.0 %collective-permute-start.21 = (bf16[2,208,384]{2,1,0:T(8,128)(2,1)S(1)}, bf16[2,208,384]{2,1,0:T(8,128)(2,1)S(1)}, u32[]{:S(2)}, u32[]{:S(2)}) collective-permute-start(bf16[2,208,384]{2,1,0:T(8,128)(2,1)S(1)} %collective-permute-done.18.rest_6_), channel_id=1, source_target_pairs={{8,16},{10,18},{12,20},{14,22},{16,8},{18,10},{20,12},{22,14},{9,1... | collective-permute-start | bytes 958472 | tf_op jit(solution)/shard_map/ppermute | solution.py:612
  59.6 7.1 %collective-permute-start.22 = (bf16[2,208,384]{2,1,0:T(8,128)(2,1)S(1)}, bf16[2,208,384]{2,1,0:T(8,128)(2,1)S(1)}, u32[]{:S(2)}, u32[]{:S(2)}) collective-permute-start(bf16[2,208,384]{2,1,0:T(8,128)(2,1)S(1)} %collective-permute-done.18.rest_6_), channel_id=1, source_target_pairs={{0,8},{2,10},{4,12},{6,14},{8,0},{10,2},{12,4},{14,6},{16,24},{18,... | collective-permute-start | bytes 958472 | tf_op jit(solution)/shard_map/ppermute | solution.py:612
  59.7 7.0 %collective-permute-start.23 = (bf16[2,208,384]{2,1,0:T(8,128)(2,1)S(1)}, bf16[2,208,384]{2,1,0:T(8,128)(2,1)S(1)}, u32[]{:S(2)}, u32[]{:S(2)}) collective-permute-start(bf16[2,208,384]{2,1,0:T(8,128)(2,1)S(1)} %broadcast_select_fusion.rest_9_), channel_id=1, source_target_pairs={{0,4},{2,6},{4,0},{6,2},{8,12},{10,14},{12,8},{14,10},{16,20},{18,... | collective-permute-start | bytes 958472 | tf_op jit(solution)/shard_map/ppermute | solution.py:612
  69.4 7.2 %collective-permute-start.24 = (bf16[432,384]{1,0:T(8,128)(2,1)S(1)}, bf16[432,384]{1,0:T(8,128)(2,1)S(1)}, u32[]{:S(2)}, u32[]{:S(2)}) collective-permute-start(bf16[432,384]{1,0:T(8,128)(2,1)S(1)} %get-tuple-element.74), channel_id=1, source_target_pairs={{0,2},{2,0},{4,6},{6,4},{8,10},{10,8},{12,14},{14,12},{16,18},{18,... | collective-permute-start | bytes 995336 | tf_op jit(solution)/shard_map/ppermute | solution.py:800
  78.0 8.1 %collective-permute-start.25 = (bf16[1,104,384]{2,1,0:T(8,128)(2,1)S(1)}, bf16[1,104,384]{2,1,0:T(8,128)(2,1)S(1)}, u32[]{:S(2)}, u32[]{:S(2)}) collective-permute-start(bf16[1,104,384]{2,1,0:T(8,128)(2,1)S(1)} %get-tuple-element.80), channel_id=1, source_target_pairs={{2,4},{4,2},{6,8},{8,6},{10,12},{12,10},{14,16},{16,14},{18,20},{2... | collective-permute-start | bytes 239624 | tf_op jit(solution)/shard_map/ppermute | solution.py:820
  83.3 4.5 %collective-permute-start.26 = (bf16[1,104,384]{2,1,0:T(8,128)(2,1)S(1)}, bf16[1,104,384]{2,1,0:T(8,128)(2,1)S(1)}, u32[]{:S(2)}, u32[]{:S(2)}) collective-permute-start(bf16[1,104,384]{2,1,0:T(8,128)(2,1)S(1)} %get-tuple-element.81), channel_id=1, source_target_pairs={{0,2},{2,0},{4,6},{6,4},{8,10},{10,8},{12,14},{14,12},{16,18},{18,... | collective-permute-start | bytes 239624 | tf_op jit(solution)/shard_map/ppermute | solution.py:612
  (16 other events, 183.4 us)

commit v17 on v16

--- a/solution.py
+++ b/solution.py
@@ -301,18 +301,22 @@
 
 
 def query_kernel(
-    rows, info_ref, other_ref, stats_ref, gain_ref, shift_ref, weight_ref, bias_ref, queries_ref,
-    constant_ref, means_ref, scales_ref,
+    rows, info_ref, own_ref, other_ref, stats_ref, gain_ref, shift_ref, weight_ref, bias_ref,
+    means_ref, scales_ref, *out_refs,
 ):
     info = Info(info_ref, rows)
     means, scales = norm_tables(stats_ref, gain_ref)
     means_ref[...] = means
     scales_ref[...] = scales
-    queries, constant = turned_queries(
-        info, info.tile() ^ 1, other_ref, means, scales, shift_ref, weight_ref, bias_ref
-    )
-    queries_ref[...] = queries
-    constant_ref[...] = jnp.broadcast_to(constant, constant_ref.shape)
+    for side, (tile, pairs_ref) in enumerate(
+        ((info.tile() ^ 1, other_ref), (info.tile(), own_ref))
+    ):
+        queries, constant = turned_queries(
+            info, tile, pairs_ref, means, scales, shift_ref, weight_ref, bias_ref
+        )
+        queries_ref, constant_ref = out_refs[2 * side : 2 * side + 2]
+        queries_ref[...] = queries
+        constant_ref[...] = jnp.broadcast_to(constant, constant_ref.shape)
 
 
 def key_codes(info, masks, span, cols):
@@ -415,15 +419,12 @@
 
 
 def attend_mine_kernel(
-    rows, groups, info_ref, own_ref, means_ref, scales_ref, shift_ref, weight_ref, bias_ref, *rest
+    rows, groups, info_ref, queries_ref, constant_ref, *rest
 ):
     key_refs, (mean_ref, level_ref) = rest[: len(groups)], rest[len(groups) :]
     info = Info(info_ref, rows)
     span = mean_ref.shape[0]
-    queries, constant = turned_queries(
-        info, info.tile(), own_ref, means_ref[...], scales_ref[...], shift_ref, weight_ref,
-        bias_ref,
-    )
+    queries, constant = queries_ref[...], constant_ref[:, 0:1]
     cols = span // ROWS_OF_TILE
     query_code = query_codes(info, info.tile(), span, cols)
     peak = jnp.full((span, 1), LOWEST, F32)
@@ -774,11 +775,12 @@
         groups = [list(range(i, i + 4)) for i in range(0, tiles // 2, 4)]
     gain, shift = row(second_gain), row(second_shift)
     table_shape = shape(SLOTS, channels, dtype=F32)
-    queries, constant, means, scales = call(
+    query_shapes = (shape(cells, channels), shape(cells, LANES, dtype=F32))
+    means, scales, queries, constant, mine_queries, mine_constant = call(
         functools.partial(query_kernel, rows),
-        [other, stats, gain, shift, triple_weight, row(triple_bias)],
-        (shape(cells, channels), shape(cells, LANES, dtype=F32), table_shape, table_shape),
-        cost_estimate=cost(1.5),
+        [own, other, stats, gain, shift, triple_weight, row(triple_bias)],
+        (table_shape, table_shape) + query_shapes * 2,
+        cost_estimate=cost(1.9),
         name="queries",
     )
     level_shape = shape(cells, LANES, dtype=F32)
@@ -798,10 +800,10 @@
         keys.append(normed)
     (sent,) = state
     received = lax.ppermute(sent, "tile", neighbour)
-    sent, own_late = lax.optimization_barrier((sent, own))
+    sent, mine_queries = lax.optimization_barrier((sent, mine_queries))
     mean, level = call(
         functools.partial(attend_mine_kernel, rows, tuple(tuple(masks) for masks in groups)),
-        [own_late, means, scales, shift, triple_weight, row(triple_bias)] + keys,
+        [mine_queries, mine_constant] + keys,
         (total_shape, level_shape),
         cost_estimate=cost(6.0),
         name="attend_mine",

time: 90.8 us -> 90.8 us (level)
  no operation moved by 1% of the time
where the time goes in v17:
time: 90.8 us; the launch traced here: 89.9 us
  starting transfers between devices  42.7 us (47%)
  Pallas kernels  30.2 us (33%)
  waiting for transfers between devices  13.5 us (15%)
  other arithmetic  1.9 us (2%)
  local copies, waits for them, and re-layouts  1.07 us (1%)
    ppermute x23, starting transfers between devices, exchange(): return lax.ppermute(array, 'tile', moves)  30.3 us
    pallas_call x11, Pallas kernels, call(): pl.pallas_call(kernel, out_shape=out_shape, in_specs=[SMEM_SPEC] + [VMEM_...  26.2 us
    ppermute x23, waiting for transfers between devices, exchange(): return lax.ppermute(array, 'tile', moves)  12.6 us
    ppermute x1, starting transfers between devices, shards(): outer = lax.ppermute(outer, 'tile', outer_moves)  5.3 us
    ppermute x1, starting transfers between devices, shards(): lax.ppermute(jnp.where(odd, source[row_count - 1:], source[:1]), 'tile',...  4.24 us
    pallas_call x2, Pallas kernels, shards(): pl.pallas_call(functools.partial(hold_kernel, backs), out_shape=shape(3 *...  3.5 us
  transfers between devices with their start and end apart: 27, of which 12 were waited for; matrix products, arithmetic and copies ran while one was open for 1% of the time, Pallas kernels for 22%

profile of v17, /device:TPU:8, one launch (start us, length us, event | category | flops | bytes accessed | tf_op | source)
XLA Modules:
  0.0 89.9 jit_solution(3475716764454471680)
XLA Ops:
  0.9 4.2 %collective-permute-start = (bf16[1,104,384]{2,1,0:T(8,128)(2,1)S(1)}, bf16[1,104,384]{2,1,0:T(8,128)(2,1)S(1)}, u32[]{:S(2)}, u32[]{:S(2)}) collective-permute-start(bf16[1,104,384]{2,1,0:T(8,128)(2,1)S(1)} %get-tuple-element.103), channel_id=1, source_target_pairs={{2,4},{4,2},{6,8},{8,6},{10,12},{12,10},{14,16},{16,14},{18,20},{2... | collective-permute-start | bytes 239624 | tf_op jit(solution)/shard_map/ppermute | solution.py:689
  10.1 2.9 %collective-permute-start.3 = (f32[3,8,128]{2,1,0:T(8,128)S(1)}, f32[3,8,128]{2,1,0:T(8,128)S(1)}, u32[]{:S(2)}, u32[]{:S(2)}) collective-permute-start(f32[3,8,128]{2,1,0:T(8,128)S(1)} %first_stats.1), channel_id=1, source_target_pairs={{0,16},{2,18},{4,20},{6,22},{8,24},{10,26},{12,28},{14,30},{16,0},... | collective-permute-start | bytes 36872 | tf_op jit(solution)/shard_map/ppermute | solution.py:613
  13.4 1.7 %hold.2.held_ref = bf16[1152,1152]{1,0:T(8,128)(2,1)S(1)} custom-call(bf16[3,3,3,384,384]{4,3,2,1,0:T(8,128)(2,1)} %weight_ref.4), custom_call_target="tpu_custom_call" | custom-call | flops 1650000000 | tf_op jit(solution)/shard_map/hold/pallas_call | solution.py:696
  16.7 1.6 %collective-permute-start.5 = (f32[3,8,128]{2,1,0:T(8,128)S(1)}, f32[3,8,128]{2,1,0:T(8,128)S(1)}, u32[]{:S(2)}, u32[]{:S(2)}) collective-permute-start(f32[3,8,128]{2,1,0:T(8,128)S(1)} %pad_maximum_fusion), channel_id=1, source_target_pairs={{0,2},{2,0},{4,6},{6,4},{8,10},{10,8},{12,14},{14,12},{16,18},{18,... | collective-permute-start | bytes 36872 | tf_op jit(solution)/shard_map/ppermute | solution.py:613
  20.3 1.7 %hold.3.rest_4_ = bf16[1152,1152]{1,0:T(8,128)(2,1)S(1)} custom-call(bf16[3,3,3,384,384]{4,3,2,1,0:T(8,128)(2,1)} %weight_ref.4), custom_call_target="tpu_custom_call" | custom-call | flops 1650000000 | tf_op jit(solution)/shard_map/hold/pallas_call | solution.py:696
  26.2 2.2 %own_conv.1.rest_1_ = f32[448,1152]{1,0:T(8,128)S(1)} custom-call(s32[67]{0:T(128)S(1)} %pad_add_fusion.info_ref, bf16[6,112,384]{2,1,0:T(8,128)(2,1)S(1)} %get-tuple-element.53.hidden_ref, bf16[1152,1152]{1,0:T(8,128)(2,1)S(1)} %hold.2.held_ref), custom_call_target="tpu_custom_call" | custom-call | flops 2420000000 | tf_op jit(solution)/shard_map/own_conv/pallas_call | solution.py:671
  28.4 2.8 %conv.1 = (bf16[2,208,384]{2,1,0:T(8,128)(2,1)S(1)}, f32[3,8,128]{2,1,0:T(8,128)S(1)}) custom-call(s32[67]{0:T(128)S(1)} %pad_add_fusion.info_ref, bf16[6,112,384]{2,1,0:T(8,128)(2,1)S(1)} %collective-permute-done.8.rest_0_, f32[448,1152]{1,0:T(8,128)S(1)} %own_conv.1.rest_1_, bf16[4,104,384]{2,1,0:T(8,128)(2,1)S(1)} %get-tuple-element.55.rest_2_, ...), custom_call_target="tpu_custom_call" | custom-call | flops 3849999872 | tf_op jit(solution)/shard_map/conv/pallas_call | solution.py:671
  31.3 2.2 %collective-permute-start.10 = (f32[3,8,128]{2,1,0:T(8,128)S(1)}, f32[3,8,128]{2,1,0:T(8,128)S(1)}, u32[]{:S(2)}, u32[]{:S(2)}) collective-permute-start(f32[3,8,128]{2,1,0:T(8,128)S(1)} %get-tuple-element.58), channel_id=1, source_target_pairs={{0,16},{2,18},{4,20},{6,22},{8,24},{10,26},{12,28},{14,30},{16,0},... | collective-permute-start | bytes 36872 | tf_op jit(solution)/shard_map/ppermute | solution.py:613
  33.5 2.2 %collective-permute-start.11 = (f32[3,8,128]{2,1,0:T(8,128)S(1)}, f32[3,8,128]{2,1,0:T(8,128)S(1)}, u32[]{:S(2)}, u32[]{:S(2)}) collective-permute-start(f32[3,8,128]{2,1,0:T(8,128)S(1)} %get-tuple-element.58), channel_id=1, source_target_pairs={{0,24},{2,26},{4,28},{6,30},{8,16},{10,18},{12,20},{14,22},{16,8},... | collective-permute-start | bytes 36872 | tf_op jit(solution)/shard_map/ppermute | solution.py:613
  35.7 2.0 %collective-permute-start.13 = (bf16[2,208,384]{2,1,0:T(8,128)(2,1)S(1)}, bf16[2,208,384]{2,1,0:T(8,128)(2,1)S(1)}, u32[]{:S(2)}, u32[]{:S(2)}) collective-permute-start(bf16[2,208,384]{2,1,0:T(8,128)(2,1)S(1)} %get-tuple-element.68.own_ref.rest_5_), channel_id=1, source_target_pairs={{0,8},{2,10},{4,12},{6,14},{8,0},{10,2},{12,4},{14,6},{16,24},{18,... | collective-permute-start | bytes 958472 | tf_op jit(solution)/shard_map/ppermute | solution.py:613
  37.7 1.9 %collective-permute-start.14 = (bf16[2,208,384]{2,1,0:T(8,128)(2,1)S(1)}, bf16[2,208,384]{2,1,0:T(8,128)(2,1)S(1)}, u32[]{:S(2)}, u32[]{:S(2)}) collective-permute-start(bf16[2,208,384]{2,1,0:T(8,128)(2,1)S(1)} %get-tuple-element.68.own_ref.rest_5_), channel_id=1, source_target_pairs={{8,16},{10,18},{12,20},{14,22},{16,8},{18,10},{20,12},{22,14},{9,1... | collective-permute-start | bytes 958472 | tf_op jit(solution)/shard_map/ppermute | solution.py:613
  41.0 1.7 %collective-permute-start.16 = (f32[3,8,128]{2,1,0:T(8,128)S(1)}, f32[3,8,128]{2,1,0:T(8,128)S(1)}, u32[]{:S(2)}, u32[]{:S(2)}) collective-permute-start(f32[3,8,128]{2,1,0:T(8,128)S(1)} %pad_maximum_fusion.2), channel_id=1, source_target_pairs={{0,6},{2,4},{4,2},{6,0},{8,14},{10,12},{12,10},{14,8},{16,22},{18,... | collective-permute-start | bytes 36872 | tf_op jit(solution)/shard_map/ppermute | solution.py:613
  43.5 2.2 %collective-permute-done.16 = f32[3,8,128]{2,1,0:T(8,128)S(1)} collective-permute-done((f32[3,8,128]{2,1,0:T(8,128)S(1)}, f32[3,8,128]{2,1,0:T(8,128)S(1)}, u32[]{:S(2)}, u32[]{:S(2)}) %collective-permute-start.16) | collective-permute-done | bytes 12320 | tf_op jit(solution)/shard_map/ppermute | solution.py:613
  47.5 2.9 %collective-permute-start.19 = (bf16[2,208,384]{2,1,0:T(8,128)(2,1)S(1)}, bf16[2,208,384]{2,1,0:T(8,128)(2,1)S(1)}, u32[]{:S(2)}, u32[]{:S(2)}) collective-permute-start(bf16[2,208,384]{2,1,0:T(8,128)(2,1)S(1)} %collective-permute-done.13.rest_7_), channel_id=1, source_target_pairs={{8,16},{10,18},{12,20},{14,22},{16,8},{18,10},{20,12},{22,14},{9,1... | collective-permute-start | bytes 958472 | tf_op jit(solution)/shard_map/ppermute | solution.py:613
  53.4 3.0 %collective-permute-done.19 = bf16[2,208,384]{2,1,0:T(8,128)(2,1)S(1)} collective-permute-done((bf16[2,208,384]{2,1,0:T(8,128)(2,1)S(1)}, bf16[2,208,384]{2,1,0:T(8,128)(2,1)S(1)}, u32[]{:S(2)}, u32[]{:S(2)}) %collective-permute-start.19) | collective-permute-done | bytes 319520 | tf_op jit(solution)/shard_map/ppermute | solution.py:613
  56.5 3.1 %collective-permute-start.21 = (bf16[2,208,384]{2,1,0:T(8,128)(2,1)S(1)}, bf16[2,208,384]{2,1,0:T(8,128)(2,1)S(1)}, u32[]{:S(2)}, u32[]{:S(2)}) collective-permute-start(bf16[2,208,384]{2,1,0:T(8,128)(2,1)S(1)} %collective-permute-done.18.rest_6_), channel_id=1, source_target_pairs={{8,16},{10,18},{12,20},{14,22},{16,8},{18,10},{20,12},{22,14},{9,1... | collective-permute-start | bytes 958472 | tf_op jit(solution)/shard_map/ppermute | solution.py:613
  60.5 1.8 %queries.1 = (f32[8,384]{1,0:T(8,128)S(1)}, f32[8,384]{1,0:T(8,128)S(1)}, bf16[416,384]{1,0:T(8,128)(2,1)S(1)}, f32[416,128]{1,0:T(8,128)S(1)}, bf16[416,384]{1,0:T(8,128)(2,1)S(1)}, /*index=5*/f32[416,128]{1,0:T(8,128)S(1)}) custom-call(s32[67]{0:T(128)S(1)} %pad_add_fusion.info_ref, bf16[2,208,384]{2,1,0:T(8,128)(2,1)S(1)} %get-tuple-element.68.own_ref.rest_5_, ...), custom_call_target="tpu_custom_call" | custom-call | flops 2090000000 | tf_op jit(solution)/shard_map/queries/pallas_call | solution.py:671
  62.3 3.6 %attend_yours.2 = (bf16[2080,384]{1,0:T(8,128)(2,1)S(1)}, f32[416,128]{1,0:T(8,128)S(1)}, f32[416,128]{1,0:T(8,128)S(1)}, f32[416,384]{1,0:T(8,128)S(1)}) custom-call(s32[67]{0:T(128)S(1)} %pad_add_fusion.info_ref, f32[8,384]{1,0:T(8,128)S(1)} %get-tuple-element.64.rest_0_, f32[8,384]{1,0:T(8,128)S(1)} %get-tuple-element.65.rest_1_, ...), custom_call_target="tpu_custom_call" | custom-call | flops 4950000128 | tf_op jit(solution)/shard_map/attend_yours/pallas_call | solution.py:671
  66.7 2.6 %attend_yours.3 = (bf16[1248,384]{1,0:T(8,128)(2,1)S(1)}, bf16[432,384]{1,0:T(8,128)(2,1)S(1)}) custom-call(s32[67]{0:T(128)S(1)} %pad_add_fusion.info_ref, f32[8,384]{1,0:T(8,128)S(1)} %get-tuple-element.64.rest_0_, f32[8,384]{1,0:T(8,128)S(1)} %get-tuple-element.65.rest_1_, f32[1,384]{1,0:T(1,128)S(1)} %reshape.86.shift_ref.rest_2_, ...), custom_call_target="tpu_custom_call" | custom-call | flops 2969999872 | tf_op jit(solution)/shard_map/attend_yours/pallas_call | solution.py:671
  70.9 5.1 %attend_mine.1 = (f32[416,384]{1,0:T(8,128)S(1)}, f32[416,128]{1,0:T(8,128)S(1)}) custom-call(s32[67]{0:T(128)S(1)} %pad_add_fusion.info_ref, bf16[416,384]{1,0:T(8,128)(2,1)S(1)} %get-tuple-element.78.queries_ref, f32[416,128]{1,0:T(8,128)S(1)} %get-tuple-element.79.constant_ref, bf16[2080,384]{1,0:T(8,128)(2,1)S(1)} %get-tuple-element.80.rest_0_, ...), custom_call_target="tpu_custom_call" | custom-call | flops 6600000000 | tf_op jit(solution)/shard_map/attend_mine/pallas_call | solution.py:671
  78.0 5.3 %collective-permute-start.25 = (bf16[1,104,384]{2,1,0:T(8,128)(2,1)S(1)}, bf16[1,104,384]{2,1,0:T(8,128)(2,1)S(1)}, u32[]{:S(2)}, u32[]{:S(2)}) collective-permute-start(bf16[1,104,384]{2,1,0:T(8,128)(2,1)S(1)} %get-tuple-element.84), channel_id=1, source_target_pairs={{2,4},{4,2},{6,8},{8,6},{10,12},{12,10},{14,16},{16,14},{18,20},{2... | collective-permute-start | bytes 239624 | tf_op jit(solution)/shard_map/ppermute | solution.py:822
  83.9 2.2 %upsample.1 = (bf16[6,192,208]{2,1,0:T(8,128)(2,1)S(1)}, f32[2,2,256,128]{3,2,1,0:T(8,128)S(1)}) custom-call(s32[67]{0:T(128)S(1)} %pad_add_fusion.info_ref, bf16[4,104,384]{2,1,0:T(8,128)(2,1)S(1)} %get-tuple-element.87.own_ref, bf16[2,2,2,192,768]{4,3,2,1,0:T(8,128)(2,1)S(1)} %fold.1.weight_ref, f32[1,256]{1,0:T(1,128)S(1)} %pad.4.bias_ref), custom_call_target="tpu_custom_call" | custom-call | flops 220000000 | tf_op jit(solution)/shard_map/upsample/pallas_call | solution.py:671
  86.1 1.7 %collective-permute-done.26.inner_ref = bf16[1,104,384]{2,1,0:T(8,128)(2,1)S(1)} collective-permute-done((bf16[1,104,384]{2,1,0:T(8,128)(2,1)S(1)}, bf16[1,104,384]{2,1,0:T(8,128)(2,1)S(1)}, u32[]{:S(2)}, u32[]{:S(2)}) %collective-permute-start.26) | collective-permute-done | bytes 79904 | tf_op jit(solution)/shard_map/ppermute | solution.py:613
  87.8 2.1 %close.1 = bf16[8,192,208]{2,1,0:T(8,128)(2,1)} custom-call(s32[67]{0:T(128)S(1)} %pad_add_fusion.info_ref, bf16[1,104,384]{2,1,0:T(8,128)(2,1)S(1)} %collective-permute-done.25.outer_ref, bf16[1,104,384]{2,1,0:T(8,128)(2,1)S(1)} %collective-permute-done.26.inner_ref, bf16[6,192,208]{2,1,0:T(8,128)(2,1)S(1)} %get-tuple-element.89.middle_ref, ...), custom_call_target="tpu_custom_call" | custom-call | flops 1100000000 | tf_op jit(solution)/shard_map/close/pallas_call | solution.py:671
  (93 shorter events, 26.5 us)
Async XLA Ops:
  0.9 8.2 %collective-permute-start = (bf16[1,104,384]{2,1,0:T(8,128)(2,1)S(1)}, bf16[1,104,384]{2,1,0:T(8,128)(2,1)S(1)}, u32[]{:S(2)}, u32[]{:S(2)}) collective-permute-start(bf16[1,104,384]{2,1,0:T(8,128)(2,1)S(1)} %get-tuple-element.103), channel_id=1, source_target_pairs={{2,4},{4,2},{6,8},{8,6},{10,12},{12,10},{14,16},{16,14},{18,20},{2... | collective-permute-start | bytes 239624 | tf_op jit(solution)/shard_map/ppermute | solution.py:689
  5.2 4.7 %collective-permute-start.1 = (bf16[1,104,384]{2,1,0:T(8,128)(2,1)S(1)}, bf16[1,104,384]{2,1,0:T(8,128)(2,1)S(1)}, u32[]{:S(2)}, u32[]{:S(2)}) collective-permute-start(bf16[1,104,384]{2,1,0:T(8,128)(2,1)S(1)} %get-tuple-element.102), channel_id=1, source_target_pairs={{0,2},{2,0},{4,6},{6,4},{8,10},{10,8},{12,14},{14,12},{16,18},{18,... | collective-permute-start | bytes 239624 | tf_op jit(solution)/shard_map/ppermute | solution.py:613
  9.9 5.2 %collective-permute-start.2 = (f32[3,8,128]{2,1,0:T(8,128)S(1)}, f32[3,8,128]{2,1,0:T(8,128)S(1)}, u32[]{:S(2)}, u32[]{:S(2)}) collective-permute-start(f32[3,8,128]{2,1,0:T(8,128)S(1)} %first_stats.1), channel_id=1, source_target_pairs={{0,8},{2,10},{4,12},{6,14},{8,0},{10,2},{12,4},{14,6},{16,24},{18,... | collective-permute-start | bytes 36872 | tf_op jit(solution)/shard_map/ppermute | solution.py:613
  10.1 5.1 %collective-permute-start.3 = (f32[3,8,128]{2,1,0:T(8,128)S(1)}, f32[3,8,128]{2,1,0:T(8,128)S(1)}, u32[]{:S(2)}, u32[]{:S(2)}) collective-permute-start(f32[3,8,128]{2,1,0:T(8,128)S(1)} %first_stats.1), channel_id=1, source_target_pairs={{0,16},{2,18},{4,20},{6,22},{8,24},{10,26},{12,28},{14,30},{16,0},... | collective-permute-start | bytes 36872 | tf_op jit(solution)/shard_map/ppermute | solution.py:613
  16.7 5.4 %collective-permute-start.5 = (f32[3,8,128]{2,1,0:T(8,128)S(1)}, f32[3,8,128]{2,1,0:T(8,128)S(1)}, u32[]{:S(2)}, u32[]{:S(2)}) collective-permute-start(f32[3,8,128]{2,1,0:T(8,128)S(1)} %pad_maximum_fusion), channel_id=1, source_target_pairs={{0,2},{2,0},{4,6},{6,4},{8,10},{10,8},{12,14},{14,12},{16,18},{18,... | collective-permute-start | bytes 36872 | tf_op jit(solution)/shard_map/ppermute | solution.py:613
  19.0 4.6 %collective-permute-start.7 = (f32[3,8,128]{2,1,0:T(8,128)S(1)}, f32[3,8,128]{2,1,0:T(8,128)S(1)}, u32[]{:S(2)}, u32[]{:S(2)}) collective-permute-start(f32[3,8,128]{2,1,0:T(8,128)S(1)} %pad_maximum_fusion), channel_id=1, source_target_pairs={{0,6},{2,4},{4,2},{6,0},{8,14},{10,12},{12,10},{14,8},{16,22},{18,... | collective-permute-start | bytes 36872 | tf_op jit(solution)/shard_map/ppermute | solution.py:613
  31.3 8.4 %collective-permute-start.10 = (f32[3,8,128]{2,1,0:T(8,128)S(1)}, f32[3,8,128]{2,1,0:T(8,128)S(1)}, u32[]{:S(2)}, u32[]{:S(2)}) collective-permute-start(f32[3,8,128]{2,1,0:T(8,128)S(1)} %get-tuple-element.58), channel_id=1, source_target_pairs={{0,16},{2,18},{4,20},{6,22},{8,24},{10,26},{12,28},{14,30},{16,0},... | collective-permute-start | bytes 36872 | tf_op jit(solution)/shard_map/ppermute | solution.py:613
  33.5 6.2 %collective-permute-start.11 = (f32[3,8,128]{2,1,0:T(8,128)S(1)}, f32[3,8,128]{2,1,0:T(8,128)S(1)}, u32[]{:S(2)}, u32[]{:S(2)}) collective-permute-start(f32[3,8,128]{2,1,0:T(8,128)S(1)} %get-tuple-element.58), channel_id=1, source_target_pairs={{0,24},{2,26},{4,28},{6,30},{8,16},{10,18},{12,20},{14,22},{16,8},... | collective-permute-start | bytes 36872 | tf_op jit(solution)/shard_map/ppermute | solution.py:613
  35.7 4.0 %collective-permute-start.9 = (f32[3,8,128]{2,1,0:T(8,128)S(1)}, f32[3,8,128]{2,1,0:T(8,128)S(1)}, u32[]{:S(2)}, u32[]{:S(2)}) collective-permute-start(f32[3,8,128]{2,1,0:T(8,128)S(1)} %get-tuple-element.58), channel_id=1, source_target_pairs={{0,8},{2,10},{4,12},{6,14},{8,0},{10,2},{12,4},{14,6},{16,24},{18,... | collective-permute-start | bytes 36872 | tf_op jit(solution)/shard_map/ppermute | solution.py:613
  35.7 10.8 %collective-permute-start.13 = (bf16[2,208,384]{2,1,0:T(8,128)(2,1)S(1)}, bf16[2,208,384]{2,1,0:T(8,128)(2,1)S(1)}, u32[]{:S(2)}, u32[]{:S(2)}) collective-permute-start(bf16[2,208,384]{2,1,0:T(8,128)(2,1)S(1)} %get-tuple-element.68.own_ref.rest_5_), channel_id=1, source_target_pairs={{0,8},{2,10},{4,12},{6,14},{8,0},{10,2},{12,4},{14,6},{16,24},{18,... | collective-permute-start | bytes 958472 | tf_op jit(solution)/shard_map/ppermute | solution.py:613
  37.7 9.8 %collective-permute-start.14 = (bf16[2,208,384]{2,1,0:T(8,128)(2,1)S(1)}, bf16[2,208,384]{2,1,0:T(8,128)(2,1)S(1)}, u32[]{:S(2)}, u32[]{:S(2)}) collective-permute-start(bf16[2,208,384]{2,1,0:T(8,128)(2,1)S(1)} %get-tuple-element.68.own_ref.rest_5_), channel_id=1, source_target_pairs={{8,16},{10,18},{12,20},{14,22},{16,8},{18,10},{20,12},{22,14},{9,1... | collective-permute-start | bytes 958472 | tf_op jit(solution)/shard_map/ppermute | solution.py:613
  39.7 3.8 %collective-permute-start.15 = (f32[3,8,128]{2,1,0:T(8,128)S(1)}, f32[3,8,128]{2,1,0:T(8,128)S(1)}, u32[]{:S(2)}, u32[]{:S(2)}) collective-permute-start(f32[3,8,128]{2,1,0:T(8,128)S(1)} %pad_maximum_fusion.2), channel_id=1, source_target_pairs={{0,4},{2,6},{4,0},{6,2},{8,12},{10,14},{12,8},{14,10},{16,20},{18,... | collective-permute-start | bytes 36872 | tf_op jit(solution)/shard_map/ppermute | solution.py:613
  41.0 4.7 %collective-permute-start.16 = (f32[3,8,128]{2,1,0:T(8,128)S(1)}, f32[3,8,128]{2,1,0:T(8,128)S(1)}, u32[]{:S(2)}, u32[]{:S(2)}) collective-permute-start(f32[3,8,128]{2,1,0:T(8,128)S(1)} %pad_maximum_fusion.2), channel_id=1, source_target_pairs={{0,6},{2,4},{4,2},{6,0},{8,14},{10,12},{12,10},{14,8},{16,22},{18,... | collective-permute-start | bytes 36872 | tf_op jit(solution)/shard_map/ppermute | solution.py:613
  42.7 3.8 %collective-permute-start.12 = (f32[3,8,128]{2,1,0:T(8,128)S(1)}, f32[3,8,128]{2,1,0:T(8,128)S(1)}, u32[]{:S(2)}, u32[]{:S(2)}) collective-permute-start(f32[3,8,128]{2,1,0:T(8,128)S(1)} %pad_maximum_fusion.2), channel_id=1, source_target_pairs={{0,2},{2,0},{4,6},{6,4},{8,10},{10,8},{12,14},{14,12},{16,18},{18,... | collective-permute-start | bytes 36872 | tf_op jit(solution)/shard_map/ppermute | solution.py:613
  45.7 10.8 %collective-permute-start.18 = (bf16[2,208,384]{2,1,0:T(8,128)(2,1)S(1)}, bf16[2,208,384]{2,1,0:T(8,128)(2,1)S(1)}, u32[]{:S(2)}, u32[]{:S(2)}) collective-permute-start(bf16[2,208,384]{2,1,0:T(8,128)(2,1)S(1)} %get-tuple-element.68.own_ref.rest_5_), channel_id=1, source_target_pairs={{0,4},{2,6},{4,0},{6,2},{8,12},{10,14},{12,8},{14,10},{16,20},{18,... | collective-permute-start | bytes 958472 | tf_op jit(solution)/shard_map/ppermute | solution.py:613
  47.5 8.9 %collective-permute-start.19 = (bf16[2,208,384]{2,1,0:T(8,128)(2,1)S(1)}, bf16[2,208,384]{2,1,0:T(8,128)(2,1)S(1)}, u32[]{:S(2)}, u32[]{:S(2)}) collective-permute-start(bf16[2,208,384]{2,1,0:T(8,128)(2,1)S(1)} %collective-permute-done.13.rest_7_), channel_id=1, source_target_pairs={{8,16},{10,18},{12,20},{14,22},{16,8},{18,10},{20,12},{22,14},{9,1... | collective-permute-start | bytes 958472 | tf_op jit(solution)/shard_map/ppermute | solution.py:613
  50.5 6.0 %collective-permute-start.20 = (bf16[2,208,384]{2,1,0:T(8,128)(2,1)S(1)}, bf16[2,208,384]{2,1,0:T(8,128)(2,1)S(1)}, u32[]{:S(2)}, u32[]{:S(2)}) collective-permute-start(bf16[2,208,384]{2,1,0:T(8,128)(2,1)S(1)} %collective-permute-done.14.rest_8_), channel_id=1, source_target_pairs={{8,0},{10,2},{12,4},{14,6},{16,24},{18,26},{20,28},{22,30},{9,1},{... | collective-permute-start | bytes 958472 | tf_op jit(solution)/shard_map/ppermute | solution.py:613
  51.8 8.6 %collective-permute-start.17 = (bf16[2,208,384]{2,1,0:T(8,128)(2,1)S(1)}, bf16[2,208,384]{2,1,0:T(8,128)(2,1)S(1)}, u32[]{:S(2)}, u32[]{:S(2)}) collective-permute-start(bf16[2,208,384]{2,1,0:T(8,128)(2,1)S(1)} %get-tuple-element.68.own_ref.rest_5_), channel_id=1, source_target_pairs={{0,2},{2,0},{4,6},{6,4},{8,10},{10,8},{12,14},{14,12},{16,18},{18,... | collective-permute-start | bytes 958472 | tf_op jit(solution)/shard_map/ppermute | solution.py:613
  56.5 9.5 %collective-permute-start.21 = (bf16[2,208,384]{2,1,0:T(8,128)(2,1)S(1)}, bf16[2,208,384]{2,1,0:T(8,128)(2,1)S(1)}, u32[]{:S(2)}, u32[]{:S(2)}) collective-permute-start(bf16[2,208,384]{2,1,0:T(8,128)(2,1)S(1)} %collective-permute-done.18.rest_6_), channel_id=1, source_target_pairs={{8,16},{10,18},{12,20},{14,22},{16,8},{18,10},{20,12},{22,14},{9,1... | collective-permute-start | bytes 958472 | tf_op jit(solution)/shard_map/ppermute | solution.py:613
  59.6 7.1 %collective-permute-start.22 = (bf16[2,208,384]{2,1,0:T(8,128)(2,1)S(1)}, bf16[2,208,384]{2,1,0:T(8,128)(2,1)S(1)}, u32[]{:S(2)}, u32[]{:S(2)}) collective-permute-start(bf16[2,208,384]{2,1,0:T(8,128)(2,1)S(1)} %collective-permute-done.18.rest_6_), channel_id=1, source_target_pairs={{0,8},{2,10},{4,12},{6,14},{8,0},{10,2},{12,4},{14,6},{16,24},{18,... | collective-permute-start | bytes 958472 | tf_op jit(solution)/shard_map/ppermute | solution.py:613
  59.7 7.0 %collective-permute-start.23 = (bf16[2,208,384]{2,1,0:T(8,128)(2,1)S(1)}, bf16[2,208,384]{2,1,0:T(8,128)(2,1)S(1)}, u32[]{:S(2)}, u32[]{:S(2)}) collective-permute-start(bf16[2,208,384]{2,1,0:T(8,128)(2,1)S(1)} %broadcast_select_fusion.rest_9_), channel_id=1, source_target_pairs={{0,4},{2,6},{4,0},{6,2},{8,12},{10,14},{12,8},{14,10},{16,20},{18,... | collective-permute-start | bytes 958472 | tf_op jit(solution)/shard_map/ppermute | solution.py:613
  69.4 7.2 %collective-permute-start.24 = (bf16[432,384]{1,0:T(8,128)(2,1)S(1)}, bf16[432,384]{1,0:T(8,128)(2,1)S(1)}, u32[]{:S(2)}, u32[]{:S(2)}) collective-permute-start(bf16[432,384]{1,0:T(8,128)(2,1)S(1)} %get-tuple-element.76), channel_id=1, source_target_pairs={{0,2},{2,0},{4,6},{6,4},{8,10},{10,8},{12,14},{14,12},{16,18},{18,... | collective-permute-start | bytes 995336 | tf_op jit(solution)/shard_map/ppermute | solution.py:802
  78.0 8.1 %collective-permute-start.25 = (bf16[1,104,384]{2,1,0:T(8,128)(2,1)S(1)}, bf16[1,104,384]{2,1,0:T(8,128)(2,1)S(1)}, u32[]{:S(2)}, u32[]{:S(2)}) collective-permute-start(bf16[1,104,384]{2,1,0:T(8,128)(2,1)S(1)} %get-tuple-element.84), channel_id=1, source_target_pairs={{2,4},{4,2},{6,8},{8,6},{10,12},{12,10},{14,16},{16,14},{18,20},{2... | collective-permute-start | bytes 239624 | tf_op jit(solution)/shard_map/ppermute | solution.py:822
  83.3 4.5 %collective-permute-start.26 = (bf16[1,104,384]{2,1,0:T(8,128)(2,1)S(1)}, bf16[1,104,384]{2,1,0:T(8,128)(2,1)S(1)}, u32[]{:S(2)}, u32[]{:S(2)}) collective-permute-start(bf16[1,104,384]{2,1,0:T(8,128)(2,1)S(1)} %get-tuple-element.85), channel_id=1, source_target_pairs={{0,2},{2,0},{4,6},{6,4},{8,10},{10,8},{12,14},{14,12},{16,18},{18,... | collective-permute-start | bytes 239624 | tf_op jit(solution)/shard_map/ppermute | solution.py:613
  (16 other events, 183.4 us)

commit v18 on v17

--- a/solution.py
+++ b/solution.py
@@ -531,7 +531,8 @@
 
 
 def upsample_kernel(
-    rows, info_ref, own_ref, weight_ref, bias_ref, out_ref, open_ref, columns_ref, wide_ref
+    rows, info_ref, own_ref, weight_ref, bias_ref, out_ref, open_ref, columns_ref, wide_ref,
+    turned_ref, sem,
 ):
     info = Info(info_ref, rows)
     row_count, cols, channels = own_ref.shape
@@ -565,12 +566,15 @@
     for r in range(1, 2 * row_count - 1):
         for part in range(parts_out):
             value = wide_ref[part, r] + bias_ref[:, part * LANES : (part + 1) * LANES]
-            write_turned(out_ref, r - 1, part, value, 2 * widths[r // 2])
+            write_turned(turned_ref, r - 1, part, value, 2 * widths[r // 2])
+    copy = pltpu.make_async_copy(turned_ref, out_ref.at[pl.ds(1, 2 * row_count - 2)], sem)
+    copy.start()
+    copy.wait()
 
 
 def close_kernel(
-    rows, info_ref, outer_ref, inner_ref, middle_ref, open_ref, weight_ref, bias_ref, out_ref,
-    columns_ref, wide_ref,
+    rows, info_ref, outer_ref, inner_ref, _, open_ref, weight_ref, bias_ref, out_ref, columns_ref,
+    wide_ref, turned_ref, sems,
 ):
     info = Info(info_ref, rows)
     wide_rows, _, wide_cols = out_ref.shape
@@ -588,15 +592,21 @@
                 weight_ref[down, down, right],
             )
             spread_columns(wide_ref, rim[:cols], down, right)
-    out_ref[1 : wide_rows - 1] = middle_ref[...]
+    copies = []
     for down in range(2):
         rim_row, own_row = (row_count + 1, row_count) if down else (0, 1)
         for part in range(wide_ref.shape[0]):
             rim = jnp.where(labels[rim_row] == labels[own_row], wide_ref[part, down], 0.0)
             value = open_ref[part, down] + rim + bias_ref[:, part * LANES : (part + 1) * LANES]
-            write_turned(
-                out_ref, down * (wide_rows - 1), part, value, 2 * widths[own_row]
+            write_turned(turned_ref, down, part, value, 2 * widths[own_row])
+        copies.append(
+            pltpu.make_async_copy(
+                turned_ref.at[down], out_ref.at[down * (wide_rows - 1)], sems.at[down]
             )
+        )
+        copies[-1].start()
+    for copy in copies:
+        copy.wait()
 
 
 def merge_stats(mine, other):
@@ -834,31 +844,39 @@
     parts_out = -(-out_channels // LANES)
     wide_cols = -(-2 * cols // LANES) * LANES
     wide_bias = jnp.pad(row(upsample_bias), ((0, 0), (0, -out_channels % LANES)))
-    middle, open_rows = call(
+    out_shape = shape(2 * row_count, out_channels, 2 * cols)
+    open_shape = shape(parts_out, 2, wide_cols, LANES, dtype=F32)
+    decoded, open_rows = pl.pallas_call(
         functools.partial(upsample_kernel, rows),
-        [attended, folded, wide_bias],
-        (
-            shape(2 * row_count - 2, out_channels, 2 * cols),
-            shape(parts_out, 2, wide_cols, LANES, dtype=F32),
-        ),
-        scratch=[
+        out_shape=(out_shape, open_shape),
+        in_specs=[SMEM_SPEC] + [VMEM_SPEC] * 3,
+        out_specs=(HBM_SPEC, VMEM_SPEC),
+        scratch_shapes=[
             pltpu.VMEM((row_count * padded, 3 * channels), BF16),
             pltpu.VMEM((parts_out, 2 * row_count, wide_cols, LANES), F32),
+            pltpu.VMEM((2 * row_count - 2, out_channels, 2 * cols), BF16),
+            pltpu.SemaphoreType.DMA,
         ],
+        compiler_params=params(),
         cost_estimate=cost(0.2),
         name="upsample",
-    )
-    decoded = call(
+    )(info, attended, folded, wide_bias)
+    decoded = pl.pallas_call(
         functools.partial(close_kernel, rows),
-        [outer, inner, middle, open_rows, folded, wide_bias],
-        shape(2 * row_count, out_channels, 2 * cols),
-        scratch=[
+        out_shape=out_shape,
+        in_specs=[SMEM_SPEC] + [VMEM_SPEC] * 2 + [HBM_SPEC] + [VMEM_SPEC] * 3,
+        out_specs=HBM_SPEC,
+        scratch_shapes=[
             pltpu.VMEM((2 * padded, 3 * channels), BF16),
             pltpu.VMEM((parts_out, 2, wide_cols, LANES), F32),
+            pltpu.VMEM((2, out_channels, 2 * cols), BF16),
+            pltpu.SemaphoreType.DMA((2,)),
         ],
+        input_output_aliases={3: 0},
+        compiler_params=params(),
         cost_estimate=cost(1.0),
         name="close",
-    )
+    )(info, outer, inner, decoded, open_rows, folded, wide_bias)
     return jnp.swapaxes(decoded, 1, 2).reshape(2 * row_count, 1, 2 * cols, out_channels)
 
 

time: 90.8 us -> 91.4 us (level)
    pallas_call x0 -> x2, Pallas kernels: none -> 4.86 us  [the longest x1 3.01 us: shards(): pl.pallas_call(functools.partial(upsample_kernel, rows), out_shape=(out_s...]
    pallas_call x11 -> x9, Pallas kernels: 26.2 us -> 22 us  [call(): pl.pallas_call(kernel, out_shape=out_shape, in_specs=[SMEM_SPEC] + [VMEM_...]
  transfers between devices with their start and end apart: 27 -> 27, of which waited for: 12 -> 12; matrix products, arithmetic and copies ran while one was open for 1% -> 1% of each run, Pallas kernels for 22% -> 23%
where the time goes in v18:
time: 91.4 us; the launch traced here: 89.8 us
  starting transfers between devices  42.7 us (47%)
  Pallas kernels  30.9 us (34%)
  waiting for transfers between devices  12.6 us (14%)
  other arithmetic  1.9 us (2%)
  local copies, waits for them, and re-layouts  1.07 us (1%)
    ppermute x23, starting transfers between devices, exchange(): return lax.ppermute(array, 'tile', moves)  30.3 us
    pallas_call x9, Pallas kernels, call(): pl.pallas_call(kernel, out_shape=out_shape, in_specs=[SMEM_SPEC] + [VMEM_...  22 us
    ppermute x23, waiting for transfers between devices, exchange(): return lax.ppermute(array, 'tile', moves)  11.8 us
    ppermute x1, starting transfers between devices, shards(): outer = lax.ppermute(outer, 'tile', outer_moves)  5.29 us
    ppermute x1, starting transfers between devices, shards(): lax.ppermute(jnp.where(odd, source[row_count - 1:], source[:1]), 'tile',...  4.24 us
    pallas_call x2, Pallas kernels, shards(): pl.pallas_call(functools.partial(hold_kernel, backs), out_shape=shape(3 *...  3.5 us
    pallas_call x1, Pallas kernels, shards(): pl.pallas_call(functools.partial(upsample_kernel, rows), out_shape=(out_s...  3.01 us
    pallas_call x1, Pallas kernels, shards(): pl.pallas_call(functools.partial(close_kernel, rows), out_shape=out_shape...  1.86 us
  transfers between devices with their start and end apart: 27, of which 12 were waited for; matrix products, arithmetic and copies ran while one was open for 1% of the time, Pallas kernels for 23%

profile of v18, /device:TPU:8, one launch (start us, length us, event | category | flops | bytes accessed | tf_op | source)
XLA Modules:
  0.0 89.8 jit_solution(14220994666280551659)
XLA Ops:
  0.9 4.2 %collective-permute-start = (bf16[1,104,384]{2,1,0:T(8,128)(2,1)S(1)}, bf16[1,104,384]{2,1,0:T(8,128)(2,1)S(1)}, u32[]{:S(2)}, u32[]{:S(2)}) collective-permute-start(bf16[1,104,384]{2,1,0:T(8,128)(2,1)S(1)} %get-tuple-element.103), channel_id=1, source_target_pairs={{2,4},{4,2},{6,8},{8,6},{10,12},{12,10},{14,16},{16,14},{18,20},{2... | collective-permute-start | bytes 239624 | tf_op jit(solution)/shard_map/ppermute | solution.py:699
  10.1 2.9 %collective-permute-start.3 = (f32[3,8,128]{2,1,0:T(8,128)S(1)}, f32[3,8,128]{2,1,0:T(8,128)S(1)}, u32[]{:S(2)}, u32[]{:S(2)}) collective-permute-start(f32[3,8,128]{2,1,0:T(8,128)S(1)} %first_stats.1), channel_id=1, source_target_pairs={{0,16},{2,18},{4,20},{6,22},{8,24},{10,26},{12,28},{14,30},{16,0},... | collective-permute-start | bytes 36872 | tf_op jit(solution)/shard_map/ppermute | solution.py:623
  13.4 1.7 %hold.2.held_ref = bf16[1152,1152]{1,0:T(8,128)(2,1)S(1)} custom-call(bf16[3,3,3,384,384]{4,3,2,1,0:T(8,128)(2,1)} %weight_ref.4), custom_call_target="tpu_custom_call" | custom-call | flops 1650000000 | tf_op jit(solution)/shard_map/hold/pallas_call | solution.py:706
  16.7 1.6 %collective-permute-start.5 = (f32[3,8,128]{2,1,0:T(8,128)S(1)}, f32[3,8,128]{2,1,0:T(8,128)S(1)}, u32[]{:S(2)}, u32[]{:S(2)}) collective-permute-start(f32[3,8,128]{2,1,0:T(8,128)S(1)} %pad_maximum_fusion), channel_id=1, source_target_pairs={{0,2},{2,0},{4,6},{6,4},{8,10},{10,8},{12,14},{14,12},{16,18},{18,... | collective-permute-start | bytes 36872 | tf_op jit(solution)/shard_map/ppermute | solution.py:623
  20.3 1.7 %hold.3.rest_4_ = bf16[1152,1152]{1,0:T(8,128)(2,1)S(1)} custom-call(bf16[3,3,3,384,384]{4,3,2,1,0:T(8,128)(2,1)} %weight_ref.4), custom_call_target="tpu_custom_call" | custom-call | flops 1650000000 | tf_op jit(solution)/shard_map/hold/pallas_call | solution.py:706
  26.2 2.2 %own_conv.1.rest_1_ = f32[448,1152]{1,0:T(8,128)S(1)} custom-call(s32[67]{0:T(128)S(1)} %pad_add_fusion.info_ref, bf16[6,112,384]{2,1,0:T(8,128)(2,1)S(1)} %get-tuple-element.53.hidden_ref, bf16[1152,1152]{1,0:T(8,128)(2,1)S(1)} %hold.2.held_ref), custom_call_target="tpu_custom_call" | custom-call | flops 2420000000 | tf_op jit(solution)/shard_map/own_conv/pallas_call | solution.py:681
  28.4 2.8 %conv.1 = (bf16[2,208,384]{2,1,0:T(8,128)(2,1)S(1)}, f32[3,8,128]{2,1,0:T(8,128)S(1)}) custom-call(s32[67]{0:T(128)S(1)} %pad_add_fusion.info_ref, bf16[6,112,384]{2,1,0:T(8,128)(2,1)S(1)} %collective-permute-done.8.rest_0_, f32[448,1152]{1,0:T(8,128)S(1)} %own_conv.1.rest_1_, bf16[4,104,384]{2,1,0:T(8,128)(2,1)S(1)} %get-tuple-element.55.rest_2_, ...), custom_call_target="tpu_custom_call" | custom-call | flops 3849999872 | tf_op jit(solution)/shard_map/conv/pallas_call | solution.py:681
  31.3 2.2 %collective-permute-start.10 = (f32[3,8,128]{2,1,0:T(8,128)S(1)}, f32[3,8,128]{2,1,0:T(8,128)S(1)}, u32[]{:S(2)}, u32[]{:S(2)}) collective-permute-start(f32[3,8,128]{2,1,0:T(8,128)S(1)} %get-tuple-element.58), channel_id=1, source_target_pairs={{0,16},{2,18},{4,20},{6,22},{8,24},{10,26},{12,28},{14,30},{16,0},... | collective-permute-start | bytes 36872 | tf_op jit(solution)/shard_map/ppermute | solution.py:623
  33.5 2.2 %collective-permute-start.11 = (f32[3,8,128]{2,1,0:T(8,128)S(1)}, f32[3,8,128]{2,1,0:T(8,128)S(1)}, u32[]{:S(2)}, u32[]{:S(2)}) collective-permute-start(f32[3,8,128]{2,1,0:T(8,128)S(1)} %get-tuple-element.58), channel_id=1, source_target_pairs={{0,24},{2,26},{4,28},{6,30},{8,16},{10,18},{12,20},{14,22},{16,8},... | collective-permute-start | bytes 36872 | tf_op jit(solution)/shard_map/ppermute | solution.py:623
  35.7 2.0 %collective-permute-start.13 = (bf16[2,208,384]{2,1,0:T(8,128)(2,1)S(1)}, bf16[2,208,384]{2,1,0:T(8,128)(2,1)S(1)}, u32[]{:S(2)}, u32[]{:S(2)}) collective-permute-start(bf16[2,208,384]{2,1,0:T(8,128)(2,1)S(1)} %get-tuple-element.68.own_ref.rest_5_), channel_id=1, source_target_pairs={{0,8},{2,10},{4,12},{6,14},{8,0},{10,2},{12,4},{14,6},{16,24},{18,... | collective-permute-start | bytes 958472 | tf_op jit(solution)/shard_map/ppermute | solution.py:623
  37.7 1.9 %collective-permute-start.14 = (bf16[2,208,384]{2,1,0:T(8,128)(2,1)S(1)}, bf16[2,208,384]{2,1,0:T(8,128)(2,1)S(1)}, u32[]{:S(2)}, u32[]{:S(2)}) collective-permute-start(bf16[2,208,384]{2,1,0:T(8,128)(2,1)S(1)} %get-tuple-element.68.own_ref.rest_5_), channel_id=1, source_target_pairs={{8,16},{10,18},{12,20},{14,22},{16,8},{18,10},{20,12},{22,14},{9,1... | collective-permute-start | bytes 958472 | tf_op jit(solution)/shard_map/ppermute | solution.py:623
  41.0 1.7 %collective-permute-start.16 = (f32[3,8,128]{2,1,0:T(8,128)S(1)}, f32[3,8,128]{2,1,0:T(8,128)S(1)}, u32[]{:S(2)}, u32[]{:S(2)}) collective-permute-start(f32[3,8,128]{2,1,0:T(8,128)S(1)} %pad_maximum_fusion.2), channel_id=1, source_target_pairs={{0,6},{2,4},{4,2},{6,0},{8,14},{10,12},{12,10},{14,8},{16,22},{18,... | collective-permute-start | bytes 36872 | tf_op jit(solution)/shard_map/ppermute | solution.py:623
  43.5 2.2 %collective-permute-done.16 = f32[3,8,128]{2,1,0:T(8,128)S(1)} collective-permute-done((f32[3,8,128]{2,1,0:T(8,128)S(1)}, f32[3,8,128]{2,1,0:T(8,128)S(1)}, u32[]{:S(2)}, u32[]{:S(2)}) %collective-permute-start.16) | collective-permute-done | bytes 12320 | tf_op jit(solution)/shard_map/ppermute | solution.py:623
  47.5 2.9 %collective-permute-start.19 = (bf16[2,208,384]{2,1,0:T(8,128)(2,1)S(1)}, bf16[2,208,384]{2,1,0:T(8,128)(2,1)S(1)}, u32[]{:S(2)}, u32[]{:S(2)}) collective-permute-start(bf16[2,208,384]{2,1,0:T(8,128)(2,1)S(1)} %collective-permute-done.13.rest_7_), channel_id=1, source_target_pairs={{8,16},{10,18},{12,20},{14,22},{16,8},{18,10},{20,12},{22,14},{9,1... | collective-permute-start | bytes 958472 | tf_op jit(solution)/shard_map/ppermute | solution.py:623
  53.4 3.0 %collective-permute-done.19 = bf16[2,208,384]{2,1,0:T(8,128)(2,1)S(1)} collective-permute-done((bf16[2,208,384]{2,1,0:T(8,128)(2,1)S(1)}, bf16[2,208,384]{2,1,0:T(8,128)(2,1)S(1)}, u32[]{:S(2)}, u32[]{:S(2)}) %collective-permute-start.19) | collective-permute-done | bytes 319520 | tf_op jit(solution)/shard_map/ppermute | solution.py:623
  56.5 3.1 %collective-permute-start.21 = (bf16[2,208,384]{2,1,0:T(8,128)(2,1)S(1)}, bf16[2,208,384]{2,1,0:T(8,128)(2,1)S(1)}, u32[]{:S(2)}, u32[]{:S(2)}) collective-permute-start(bf16[2,208,384]{2,1,0:T(8,128)(2,1)S(1)} %collective-permute-done.18.rest_6_), channel_id=1, source_target_pairs={{8,16},{10,18},{12,20},{14,22},{16,8},{18,10},{20,12},{22,14},{9,1... | collective-permute-start | bytes 958472 | tf_op jit(solution)/shard_map/ppermute | solution.py:623
  60.5 1.8 %queries.1 = (f32[8,384]{1,0:T(8,128)S(1)}, f32[8,384]{1,0:T(8,128)S(1)}, bf16[416,384]{1,0:T(8,128)(2,1)S(1)}, f32[416,128]{1,0:T(8,128)S(1)}, bf16[416,384]{1,0:T(8,128)(2,1)S(1)}, /*index=5*/f32[416,128]{1,0:T(8,128)S(1)}) custom-call(s32[67]{0:T(128)S(1)} %pad_add_fusion.info_ref, bf16[2,208,384]{2,1,0:T(8,128)(2,1)S(1)} %get-tuple-element.68.own_ref.rest_5_, ...), custom_call_target="tpu_custom_call" | custom-call | flops 2090000000 | tf_op jit(solution)/shard_map/queries/pallas_call | solution.py:681
  62.3 3.6 %attend_yours.2 = (bf16[2080,384]{1,0:T(8,128)(2,1)S(1)}, f32[416,128]{1,0:T(8,128)S(1)}, f32[416,128]{1,0:T(8,128)S(1)}, f32[416,384]{1,0:T(8,128)S(1)}) custom-call(s32[67]{0:T(128)S(1)} %pad_add_fusion.info_ref, f32[8,384]{1,0:T(8,128)S(1)} %get-tuple-element.64.rest_0_, f32[8,384]{1,0:T(8,128)S(1)} %get-tuple-element.65.rest_1_, ...), custom_call_target="tpu_custom_call" | custom-call | flops 4950000128 | tf_op jit(solution)/shard_map/attend_yours/pallas_call | solution.py:681
  66.7 2.6 %attend_yours.3 = (bf16[1248,384]{1,0:T(8,128)(2,1)S(1)}, bf16[432,384]{1,0:T(8,128)(2,1)S(1)}) custom-call(s32[67]{0:T(128)S(1)} %pad_add_fusion.info_ref, f32[8,384]{1,0:T(8,128)S(1)} %get-tuple-element.64.rest_0_, f32[8,384]{1,0:T(8,128)S(1)} %get-tuple-element.65.rest_1_, f32[1,384]{1,0:T(1,128)S(1)} %reshape.86.shift_ref.rest_2_, ...), custom_call_target="tpu_custom_call" | custom-call | flops 2969999872 | tf_op jit(solution)/shard_map/attend_yours/pallas_call | solution.py:681
  69.4 1.5 %collective-permute-start.24 = (bf16[432,384]{1,0:T(8,128)(2,1)S(1)}, bf16[432,384]{1,0:T(8,128)(2,1)S(1)}, u32[]{:S(2)}, u32[]{:S(2)}) collective-permute-start(bf16[432,384]{1,0:T(8,128)(2,1)S(1)} %get-tuple-element.76), channel_id=1, source_target_pairs={{0,2},{2,0},{4,6},{6,4},{8,10},{10,8},{12,14},{14,12},{16,18},{18,... | collective-permute-start | bytes 995336 | tf_op jit(solution)/shard_map/ppermute | solution.py:812
  70.9 5.1 %attend_mine.1 = (f32[416,384]{1,0:T(8,128)S(1)}, f32[416,128]{1,0:T(8,128)S(1)}) custom-call(s32[67]{0:T(128)S(1)} %pad_add_fusion.info_ref, bf16[416,384]{1,0:T(8,128)(2,1)S(1)} %get-tuple-element.78.queries_ref, f32[416,128]{1,0:T(8,128)S(1)} %get-tuple-element.79.constant_ref, bf16[2080,384]{1,0:T(8,128)(2,1)S(1)} %get-tuple-element.80.rest_0_, ...), custom_call_target="tpu_custom_call" | custom-call | flops 6600000000 | tf_op jit(solution)/shard_map/attend_mine/pallas_call | solution.py:681
  78.0 5.3 %collective-permute-start.25 = (bf16[1,104,384]{2,1,0:T(8,128)(2,1)S(1)}, bf16[1,104,384]{2,1,0:T(8,128)(2,1)S(1)}, u32[]{:S(2)}, u32[]{:S(2)}) collective-permute-start(bf16[1,104,384]{2,1,0:T(8,128)(2,1)S(1)} %get-tuple-element.84), channel_id=1, source_target_pairs={{2,4},{4,2},{6,8},{8,6},{10,12},{12,10},{14,16},{16,14},{18,20},{2... | collective-permute-start | bytes 239624 | tf_op jit(solution)/shard_map/ppermute | solution.py:832
  83.9 3.0 %upsample.1 = (bf16[8,192,208]{2,1,0:T(8,128)(2,1)}, f32[2,2,256,128]{3,2,1,0:T(8,128)S(1)}) custom-call(s32[67]{0:T(128)S(1)} %pad_add_fusion.info_ref, bf16[4,104,384]{2,1,0:T(8,128)(2,1)S(1)} %get-tuple-element.87.own_ref, bf16[2,2,2,192,768]{4,3,2,1,0:T(8,128)(2,1)S(1)} %fold.1.weight_ref, f32[1,256]{1,0:T(1,128)S(1)} %pad.4.bias_ref), custom_call_target="tpu_custom_call" | custom-call | flops 220000000 | tf_op jit(solution)/shard_map/upsample/pallas_call | solution.py:849
  87.8 1.9 %close.1 = bf16[8,192,208]{2,1,0:T(8,128)(2,1)} custom-call(s32[67]{0:T(128)S(1)} %pad_add_fusion.info_ref, bf16[1,104,384]{2,1,0:T(8,128)(2,1)S(1)} %collective-permute-done.25.outer_ref, bf16[1,104,384]{2,1,0:T(8,128)(2,1)S(1)} %collective-permute-done.26.inner_ref, bf16[8,192,208]{2,1,0:T(8,128)(2,1)} %get-tuple-element.89._, ...), custom_call_target="tpu_custom_call", output_to_operand_aliasing={{}: (3, {})} | custom-call | flops 1100000000 | tf_op jit(solution)/shard_map/close/pallas_call | solution.py:864
  (93 shorter events, 25.8 us)
Async XLA Ops:
  0.9 8.2 %collective-permute-start = (bf16[1,104,384]{2,1,0:T(8,128)(2,1)S(1)}, bf16[1,104,384]{2,1,0:T(8,128)(2,1)S(1)}, u32[]{:S(2)}, u32[]{:S(2)}) collective-permute-start(bf16[1,104,384]{2,1,0:T(8,128)(2,1)S(1)} %get-tuple-element.103), channel_id=1, source_target_pairs={{2,4},{4,2},{6,8},{8,6},{10,12},{12,10},{14,16},{16,14},{18,20},{2... | collective-permute-start | bytes 239624 | tf_op jit(solution)/shard_map/ppermute | solution.py:699
  5.2 4.7 %collective-permute-start.1 = (bf16[1,104,384]{2,1,0:T(8,128)(2,1)S(1)}, bf16[1,104,384]{2,1,0:T(8,128)(2,1)S(1)}, u32[]{:S(2)}, u32[]{:S(2)}) collective-permute-start(bf16[1,104,384]{2,1,0:T(8,128)(2,1)S(1)} %get-tuple-element.102), channel_id=1, source_target_pairs={{0,2},{2,0},{4,6},{6,4},{8,10},{10,8},{12,14},{14,12},{16,18},{18,... | collective-permute-start | bytes 239624 | tf_op jit(solution)/shard_map/ppermute | solution.py:623
  9.9 5.2 %collective-permute-start.2 = (f32[3,8,128]{2,1,0:T(8,128)S(1)}, f32[3,8,128]{2,1,0:T(8,128)S(1)}, u32[]{:S(2)}, u32[]{:S(2)}) collective-permute-start(f32[3,8,128]{2,1,0:T(8,128)S(1)} %first_stats.1), channel_id=1, source_target_pairs={{0,8},{2,10},{4,12},{6,14},{8,0},{10,2},{12,4},{14,6},{16,24},{18,... | collective-permute-start | bytes 36872 | tf_op jit(solution)/shard_map/ppermute | solution.py:623
  10.1 5.1 %collective-permute-start.3 = (f32[3,8,128]{2,1,0:T(8,128)S(1)}, f32[3,8,128]{2,1,0:T(8,128)S(1)}, u32[]{:S(2)}, u32[]{:S(2)}) collective-permute-start(f32[3,8,128]{2,1,0:T(8,128)S(1)} %first_stats.1), channel_id=1, source_target_pairs={{0,16},{2,18},{4,20},{6,22},{8,24},{10,26},{12,28},{14,30},{16,0},... | collective-permute-start | bytes 36872 | tf_op jit(solution)/shard_map/ppermute | solution.py:623
  16.7 5.4 %collective-permute-start.5 = (f32[3,8,128]{2,1,0:T(8,128)S(1)}, f32[3,8,128]{2,1,0:T(8,128)S(1)}, u32[]{:S(2)}, u32[]{:S(2)}) collective-permute-start(f32[3,8,128]{2,1,0:T(8,128)S(1)} %pad_maximum_fusion), channel_id=1, source_target_pairs={{0,2},{2,0},{4,6},{6,4},{8,10},{10,8},{12,14},{14,12},{16,18},{18,... | collective-permute-start | bytes 36872 | tf_op jit(solution)/shard_map/ppermute | solution.py:623
  19.0 4.6 %collective-permute-start.7 = (f32[3,8,128]{2,1,0:T(8,128)S(1)}, f32[3,8,128]{2,1,0:T(8,128)S(1)}, u32[]{:S(2)}, u32[]{:S(2)}) collective-permute-start(f32[3,8,128]{2,1,0:T(8,128)S(1)} %pad_maximum_fusion), channel_id=1, source_target_pairs={{0,6},{2,4},{4,2},{6,0},{8,14},{10,12},{12,10},{14,8},{16,22},{18,... | collective-permute-start | bytes 36872 | tf_op jit(solution)/shard_map/ppermute | solution.py:623
  31.3 8.4 %collective-permute-start.10 = (f32[3,8,128]{2,1,0:T(8,128)S(1)}, f32[3,8,128]{2,1,0:T(8,128)S(1)}, u32[]{:S(2)}, u32[]{:S(2)}) collective-permute-start(f32[3,8,128]{2,1,0:T(8,128)S(1)} %get-tuple-element.58), channel_id=1, source_target_pairs={{0,16},{2,18},{4,20},{6,22},{8,24},{10,26},{12,28},{14,30},{16,0},... | collective-permute-start | bytes 36872 | tf_op jit(solution)/shard_map/ppermute | solution.py:623
  33.5 6.2 %collective-permute-start.11 = (f32[3,8,128]{2,1,0:T(8,128)S(1)}, f32[3,8,128]{2,1,0:T(8,128)S(1)}, u32[]{:S(2)}, u32[]{:S(2)}) collective-permute-start(f32[3,8,128]{2,1,0:T(8,128)S(1)} %get-tuple-element.58), channel_id=1, source_target_pairs={{0,24},{2,26},{4,28},{6,30},{8,16},{10,18},{12,20},{14,22},{16,8},... | collective-permute-start | bytes 36872 | tf_op jit(solution)/shard_map/ppermute | solution.py:623
  35.7 4.0 %collective-permute-start.9 = (f32[3,8,128]{2,1,0:T(8,128)S(1)}, f32[3,8,128]{2,1,0:T(8,128)S(1)}, u32[]{:S(2)}, u32[]{:S(2)}) collective-permute-start(f32[3,8,128]{2,1,0:T(8,128)S(1)} %get-tuple-element.58), channel_id=1, source_target_pairs={{0,8},{2,10},{4,12},{6,14},{8,0},{10,2},{12,4},{14,6},{16,24},{18,... | collective-permute-start | bytes 36872 | tf_op jit(solution)/shard_map/ppermute | solution.py:623
  35.7 10.8 %collective-permute-start.13 = (bf16[2,208,384]{2,1,0:T(8,128)(2,1)S(1)}, bf16[2,208,384]{2,1,0:T(8,128)(2,1)S(1)}, u32[]{:S(2)}, u32[]{:S(2)}) collective-permute-start(bf16[2,208,384]{2,1,0:T(8,128)(2,1)S(1)} %get-tuple-element.68.own_ref.rest_5_), channel_id=1, source_target_pairs={{0,8},{2,10},{4,12},{6,14},{8,0},{10,2},{12,4},{14,6},{16,24},{18,... | collective-permute-start | bytes 958472 | tf_op jit(solution)/shard_map/ppermute | solution.py:623
  37.7 9.8 %collective-permute-start.14 = (bf16[2,208,384]{2,1,0:T(8,128)(2,1)S(1)}, bf16[2,208,384]{2,1,0:T(8,128)(2,1)S(1)}, u32[]{:S(2)}, u32[]{:S(2)}) collective-permute-start(bf16[2,208,384]{2,1,0:T(8,128)(2,1)S(1)} %get-tuple-element.68.own_ref.rest_5_), channel_id=1, source_target_pairs={{8,16},{10,18},{12,20},{14,22},{16,8},{18,10},{20,12},{22,14},{9,1... | collective-permute-start | bytes 958472 | tf_op jit(solution)/shard_map/ppermute | solution.py:623
  39.7 3.8 %collective-permute-start.15 = (f32[3,8,128]{2,1,0:T(8,128)S(1)}, f32[3,8,128]{2,1,0:T(8,128)S(1)}, u32[]{:S(2)}, u32[]{:S(2)}) collective-permute-start(f32[3,8,128]{2,1,0:T(8,128)S(1)} %pad_maximum_fusion.2), channel_id=1, source_target_pairs={{0,4},{2,6},{4,0},{6,2},{8,12},{10,14},{12,8},{14,10},{16,20},{18,... | collective-permute-start | bytes 36872 | tf_op jit(solution)/shard_map/ppermute | solution.py:623
  41.0 4.7 %collective-permute-start.16 = (f32[3,8,128]{2,1,0:T(8,128)S(1)}, f32[3,8,128]{2,1,0:T(8,128)S(1)}, u32[]{:S(2)}, u32[]{:S(2)}) collective-permute-start(f32[3,8,128]{2,1,0:T(8,128)S(1)} %pad_maximum_fusion.2), channel_id=1, source_target_pairs={{0,6},{2,4},{4,2},{6,0},{8,14},{10,12},{12,10},{14,8},{16,22},{18,... | collective-permute-start | bytes 36872 | tf_op jit(solution)/shard_map/ppermute | solution.py:623
  42.7 3.8 %collective-permute-start.12 = (f32[3,8,128]{2,1,0:T(8,128)S(1)}, f32[3,8,128]{2,1,0:T(8,128)S(1)}, u32[]{:S(2)}, u32[]{:S(2)}) collective-permute-start(f32[3,8,128]{2,1,0:T(8,128)S(1)} %pad_maximum_fusion.2), channel_id=1, source_target_pairs={{0,2},{2,0},{4,6},{6,4},{8,10},{10,8},{12,14},{14,12},{16,18},{18,... | collective-permute-start | bytes 36872 | tf_op jit(solution)/shard_map/ppermute | solution.py:623
  45.7 10.8 %collective-permute-start.18 = (bf16[2,208,384]{2,1,0:T(8,128)(2,1)S(1)}, bf16[2,208,384]{2,1,0:T(8,128)(2,1)S(1)}, u32[]{:S(2)}, u32[]{:S(2)}) collective-permute-start(bf16[2,208,384]{2,1,0:T(8,128)(2,1)S(1)} %get-tuple-element.68.own_ref.rest_5_), channel_id=1, source_target_pairs={{0,4},{2,6},{4,0},{6,2},{8,12},{10,14},{12,8},{14,10},{16,20},{18,... | collective-permute-start | bytes 958472 | tf_op jit(solution)/shard_map/ppermute | solution.py:623
  47.5 8.9 %collective-permute-start.19 = (bf16[2,208,384]{2,1,0:T(8,128)(2,1)S(1)}, bf16[2,208,384]{2,1,0:T(8,128)(2,1)S(1)}, u32[]{:S(2)}, u32[]{:S(2)}) collective-permute-start(bf16[2,208,384]{2,1,0:T(8,128)(2,1)S(1)} %collective-permute-done.13.rest_7_), channel_id=1, source_target_pairs={{8,16},{10,18},{12,20},{14,22},{16,8},{18,10},{20,12},{22,14},{9,1... | collective-permute-start | bytes 958472 | tf_op jit(solution)/shard_map/ppermute | solution.py:623
  50.5 6.0 %collective-permute-start.20 = (bf16[2,208,384]{2,1,0:T(8,128)(2,1)S(1)}, bf16[2,208,384]{2,1,0:T(8,128)(2,1)S(1)}, u32[]{:S(2)}, u32[]{:S(2)}) collective-permute-start(bf16[2,208,384]{2,1,0:T(8,128)(2,1)S(1)} %collective-permute-done.14.rest_8_), channel_id=1, source_target_pairs={{8,0},{10,2},{12,4},{14,6},{16,24},{18,26},{20,28},{22,30},{9,1},{... | collective-permute-start | bytes 958472 | tf_op jit(solution)/shard_map/ppermute | solution.py:623
  51.8 8.6 %collective-permute-start.17 = (bf16[2,208,384]{2,1,0:T(8,128)(2,1)S(1)}, bf16[2,208,384]{2,1,0:T(8,128)(2,1)S(1)}, u32[]{:S(2)}, u32[]{:S(2)}) collective-permute-start(bf16[2,208,384]{2,1,0:T(8,128)(2,1)S(1)} %get-tuple-element.68.own_ref.rest_5_), channel_id=1, source_target_pairs={{0,2},{2,0},{4,6},{6,4},{8,10},{10,8},{12,14},{14,12},{16,18},{18,... | collective-permute-start | bytes 958472 | tf_op jit(solution)/shard_map/ppermute | solution.py:623
  56.5 9.5 %collective-permute-start.21 = (bf16[2,208,384]{2,1,0:T(8,128)(2,1)S(1)}, bf16[2,208,384]{2,1,0:T(8,128)(2,1)S(1)}, u32[]{:S(2)}, u32[]{:S(2)}) collective-permute-start(bf16[2,208,384]{2,1,0:T(8,128)(2,1)S(1)} %collective-permute-done.18.rest_6_), channel_id=1, source_target_pairs={{8,16},{10,18},{12,20},{14,22},{16,8},{18,10},{20,12},{22,14},{9,1... | collective-permute-start | bytes 958472 | tf_op jit(solution)/shard_map/ppermute | solution.py:623
  59.6 7.1 %collective-permute-start.22 = (bf16[2,208,384]{2,1,0:T(8,128)(2,1)S(1)}, bf16[2,208,384]{2,1,0:T(8,128)(2,1)S(1)}, u32[]{:S(2)}, u32[]{:S(2)}) collective-permute-start(bf16[2,208,384]{2,1,0:T(8,128)(2,1)S(1)} %collective-permute-done.18.rest_6_), channel_id=1, source_target_pairs={{0,8},{2,10},{4,12},{6,14},{8,0},{10,2},{12,4},{14,6},{16,24},{18,... | collective-permute-start | bytes 958472 | tf_op jit(solution)/shard_map/ppermute | solution.py:623
  59.7 7.0 %collective-permute-start.23 = (bf16[2,208,384]{2,1,0:T(8,128)(2,1)S(1)}, bf16[2,208,384]{2,1,0:T(8,128)(2,1)S(1)}, u32[]{:S(2)}, u32[]{:S(2)}) collective-permute-start(bf16[2,208,384]{2,1,0:T(8,128)(2,1)S(1)} %broadcast_select_fusion.rest_9_), channel_id=1, source_target_pairs={{0,4},{2,6},{4,0},{6,2},{8,12},{10,14},{12,8},{14,10},{16,20},{18,... | collective-permute-start | bytes 958472 | tf_op jit(solution)/shard_map/ppermute | solution.py:623
  69.4 7.2 %collective-permute-start.24 = (bf16[432,384]{1,0:T(8,128)(2,1)S(1)}, bf16[432,384]{1,0:T(8,128)(2,1)S(1)}, u32[]{:S(2)}, u32[]{:S(2)}) collective-permute-start(bf16[432,384]{1,0:T(8,128)(2,1)S(1)} %get-tuple-element.76), channel_id=1, source_target_pairs={{0,2},{2,0},{4,6},{6,4},{8,10},{10,8},{12,14},{14,12},{16,18},{18,... | collective-permute-start | bytes 995336 | tf_op jit(solution)/shard_map/ppermute | solution.py:812
  78.0 8.9 %collective-permute-start.25 = (bf16[1,104,384]{2,1,0:T(8,128)(2,1)S(1)}, bf16[1,104,384]{2,1,0:T(8,128)(2,1)S(1)}, u32[]{:S(2)}, u32[]{:S(2)}) collective-permute-start(bf16[1,104,384]{2,1,0:T(8,128)(2,1)S(1)} %get-tuple-element.84), channel_id=1, source_target_pairs={{2,4},{4,2},{6,8},{8,6},{10,12},{12,10},{14,16},{16,14},{18,20},{2... | collective-permute-start | bytes 239624 | tf_op jit(solution)/shard_map/ppermute | solution.py:832
  83.3 4.5 %collective-permute-start.26 = (bf16[1,104,384]{2,1,0:T(8,128)(2,1)S(1)}, bf16[1,104,384]{2,1,0:T(8,128)(2,1)S(1)}, u32[]{:S(2)}, u32[]{:S(2)}) collective-permute-start(bf16[1,104,384]{2,1,0:T(8,128)(2,1)S(1)} %get-tuple-element.85), channel_id=1, source_target_pairs={{0,2},{2,0},{4,6},{6,4},{8,10},{10,8},{12,14},{14,12},{16,18},{18,... | collective-permute-start | bytes 239624 | tf_op jit(solution)/shard_map/ppermute | solution.py:623
  (16 other events, 183.4 us)
